TPU v7x, 128 devices: a whole 4x4x4 slice. The times are simulated.
128 devices in a mesh: dp: 16 (over x, y), expert: 8 (over z, core).
Axes of the slice: x: 4, y: 4, z: 4, core: 2. Of those that a mesh axis runs over, the one named last changes fastest.
Arguments:
- block_input: bfloat16 [16384, 512], P(('dp', 'expert')), may hold values from -6 to 6
- gain_one: float32 [512], replicated, may hold values from 0.5 to 1.5
- gain_two: float32 [512], replicated, may hold values from 0.5 to 1.5
- moa_router: bfloat16 [512, 8], replicated, may hold values from -0.125 to 0.125
- key_proj: bfloat16 [512, 512], replicated, may hold values from -0.25 to 0.25
- value_proj: bfloat16 [512, 512], replicated, may hold values from -0.25 to 0.25
- query_proj: bfloat16 [8, 512, 512], P('expert'), may hold values from -0.25 to 0.25
- out_proj: bfloat16 [8, 512, 512], P('expert'), may hold values from -1.5 to 1.5
- moe_router: bfloat16 [512, 8], replicated, may hold values from -0.25 to 0.25
- ffn_in: bfloat16 [8, 512, 2048], P('expert'), may hold values from -0.25 to 0.25
- ffn_out: bfloat16 [8, 2048, 512], P('expert'), may hold values from -0.1875 to 0.1875
- halt_weight: float32 [512], replicated, may hold values from -0.25 to 0.25
- depths: int32 [16384], P(('dp', 'expert')), may hold values from 1 to 3, as said below
- moa_choice: int32 [3, 16384, 4], P(None, 'dp'), may hold values from 0 to 7, all different within a row
- moe_choice: int32 [3, 16384, 2], P(None, ('dp', 'expert')), may hold values from 0 to 7, all different within a row; in each aligned block of 128 rows (0 to 127, 128 to 255, ..., all dimensions but the last counted through in order) at most 40 rows name the same one
- cotangent: bfloat16 [16384, 512], P(('dp', 'expert')), may hold values from -6 to 6
Outputs:
- block_output: float32 [16384, 512], P(('dp', 'expert'))
- grad_input: float32 [16384, 512], P(('dp', 'expert'))
- grad_gain_one: float32 [512], P(('dp', 'expert'))
- grad_gain_two: float32 [512], P(('dp', 'expert'))
- grad_moa_router: float32 [512, 8], P(('dp', 'expert'))
- grad_key_proj: float32 [512, 512], P(('dp', 'expert'))
- grad_value_proj: float32 [512, 512], P(('dp', 'expert'))
- grad_query_proj: float32 [8, 512, 512], P('expert', 'dp')
- grad_out_proj: float32 [8, 512, 512], P('expert', 'dp')
- grad_moe_router: float32 [512, 8], P(('dp', 'expert'))
- grad_ffn_in: float32 [8, 512, 2048], P('expert', 'dp')
- grad_ffn_out: float32 [8, 2048, 512], P('expert', 'dp')
- grad_halt_weight: float32 [512], P(('dp', 'expert'))
Inputs may be any that keep to these rules, and one draw needn't show every extreme that they name: `depths`: at least one token has 3 steps and one has 1. `moa_choice`: each row names 4 different experts. `moe_choice`: each row names 2 different experts; in every step, among the rows of one device no expert is named by more than 40 rows, and some device reaches 40.
All inputs are finite; a program needn't handle non-finite values.
Results may differ from a plain program's by a relative error of at most 0.035.
Values may be sent and summed in bfloat16 or wider, within the bound.
No kernel may reach another device: no remote copies, remote signals or barrier semaphores. Data moves between devices by JAX's collectives and lax.ppermute only.
A program may use at most 384 MiB of HBM per device.

v0:
```python
import jax
import jax.numpy as jnp
from jax import lax
from jax.sharding import PartitionSpec as P

HEADS = 8


highest = lax.Precision.HIGHEST


def layer_norm(inputs, norm_gain):
    average = jnp.mean(inputs, -1, keepdims=True)
    centred = inputs - average
    spread = jnp.mean(centred * centred, -1, keepdims=True)
    return centred * lax.rsqrt(spread + 1e-05) * norm_gain


def slot_index(chosen, running, experts, capacity):
    flat_ids = chosen.reshape(-1)
    live_rows = jnp.repeat(running, chosen.shape[1])
    onehot = (flat_ids[:, None] == jnp.arange(experts, dtype=jnp.int32)[None, :]).astype(
        jnp.int32
    ) * live_rows[:, None]
    earlier = jnp.cumsum(onehot, 0) - onehot
    position = jnp.sum(earlier * onehot, -1)
    target = jnp.where(live_rows > 0, flat_ids * capacity + position, experts * capacity)
    return (target, live_rows)


def combine(stacked, halt_vec, depth_rows):
    remain = jnp.ones(depth_rows.shape, jnp.float32)
    output = jnp.zeros(stacked.shape[1:], jnp.float32)
    for section_index in range(stacked.shape[0]):
        halt_prob = jax.nn.sigmoid(jnp.dot(stacked[section_index], halt_vec, precision=highest))
        continues = depth_rows > section_index + 1
        stops_here = depth_rows == section_index + 1
        weight_now = jnp.where(continues, halt_prob * remain, jnp.where(stops_here, remain, 0.0))
        output = output + weight_now[:, None] * stacked[section_index]
        remain = remain * (1.0 - halt_prob)
    return output


def score_block(queries, key_rows, row_start):
    block_rows = queries.shape[0]
    head_width = queries.shape[1] // HEADS
    span = key_rows.shape[0]
    query_heads = queries.reshape(block_rows, HEADS, head_width)
    key_heads = key_rows.reshape(span, HEADS, head_width)
    scores = jnp.einsum(
        "qhd,khd->hqk", query_heads, key_heads, preferred_element_type=jnp.float32
    ) * head_width ** (-0.5)
    allowed = jnp.arange(span)[None, :] <= (row_start + jnp.arange(block_rows))[:, None]
    return jnp.where(allowed[None], scores, -jnp.inf)


def attend_forward(queries, key_rows, value_rows):
    total_rows = queries.shape[0]
    block_rows = min(512, total_rows)
    head_width = value_rows.shape[1] // HEADS
    outputs = []
    row_sums = []
    for row_start in range(0, total_rows, block_rows):
        row_stop = row_start + block_rows
        scores = score_block(queries[row_start:row_stop], key_rows[:row_stop], row_start)
        row_peak = jnp.max(scores, -1, keepdims=True)
        exp_scores = jnp.exp(scores - row_peak)
        row_total = jnp.sum(exp_scores, -1, keepdims=True)
        weights_low = (exp_scores / row_total).astype(jnp.bfloat16)
        value_heads = value_rows[:row_stop].reshape(row_stop, HEADS, head_width)
        mixed_rows = jnp.einsum(
            "hqk,khd->qhd", weights_low, value_heads, preferred_element_type=jnp.float32
        )
        outputs.append(mixed_rows.reshape(block_rows, HEADS * head_width).astype(jnp.bfloat16))
        row_sums.append(row_peak[..., 0] + jnp.log(row_total[..., 0]))
    return (jnp.concatenate(outputs, 0), row_sums)


def attend_backward(queries, key_rows, value_rows, grad_out, row_sums):
    total_rows = queries.shape[0]
    block_rows = min(512, total_rows)
    head_width = queries.shape[1] // HEADS
    score_scale = head_width ** (-0.5)
    grad_queries = []
    grad_keys = jnp.zeros(key_rows.shape, jnp.float32)
    grad_values = jnp.zeros(value_rows.shape, jnp.float32)
    for number, row_start in enumerate(range(0, total_rows, block_rows)):
        row_stop = row_start + block_rows
        scores = score_block(queries[row_start:row_stop], key_rows[:row_stop], row_start)
        probs_raw = jnp.exp(scores - row_sums[number][..., None])
        weights_low = probs_raw.astype(jnp.bfloat16)
        upstream = grad_out[row_start:row_stop].reshape(block_rows, HEADS, head_width)
        value_heads = value_rows[:row_stop].reshape(row_stop, HEADS, head_width)
        key_heads = key_rows[:row_stop].reshape(row_stop, HEADS, head_width)
        query_heads = queries[row_start:row_stop].reshape(block_rows, HEADS, head_width)
        grad_probs = jnp.einsum(
            "qhd,khd->hqk", upstream, value_heads, preferred_element_type=jnp.float32
        )
        inner_sum = jnp.sum(probs_raw * grad_probs, -1, keepdims=True)
        grad_scores = (probs_raw * (grad_probs - inner_sum)).astype(jnp.bfloat16)
        block_queries = (
            jnp.einsum("hqk,khd->qhd", grad_scores, key_heads, preferred_element_type=jnp.float32)
            * score_scale
        )
        grad_queries.append(block_queries.reshape(block_rows, HEADS * head_width))
        part_keys = (
            jnp.einsum("hqk,qhd->khd", grad_scores, query_heads, preferred_element_type=jnp.float32)
            * score_scale
        )
        part_values = jnp.einsum(
            "hqk,qhd->khd", weights_low, upstream, preferred_element_type=jnp.float32
        )
        grad_keys = grad_keys.at[:row_stop].add(part_keys.reshape(row_stop, HEADS * head_width))
        grad_values = grad_values.at[:row_stop].add(
            part_values.reshape(row_stop, HEADS * head_width)
        )
    return (jnp.concatenate(grad_queries, 0), grad_keys, grad_values)


def local(
    block_input,
    gain_one,
    gain_two,
    moa_router,
    key_proj,
    value_proj,
    query_proj,
    out_proj,
    moe_router,
    ffn_in,
    ffn_out,
    halt_weight,
    depths,
    moa_choice,
    moe_choice,
    cotangent,
):
    peer_count = lax.axis_size("expert")
    member = lax.axis_index("expert")
    tok_rows = block_input.shape[0]
    model_width = block_input.shape[1]
    moa_count = moa_router.shape[1]
    moe_count = moe_router.shape[1]
    moa_local = query_proj.shape[0]
    moe_local = ffn_in.shape[0]
    moe_top = moe_choice.shape[2]
    sections = moa_choice.shape[0]
    capacity = max(2, 5 * tok_rows * moe_top // (4 * moe_count))
    moa_ids = jnp.arange(moa_count, dtype=jnp.int32)
    moe_ids = jnp.arange(moe_count, dtype=jnp.int32)
    key_wide = key_proj.astype(jnp.float32)
    value_wide = value_proj.astype(jnp.float32)
    current = block_input.astype(jnp.float32)
    saved_steps = []
    history = []
    for section_index in range(sections):
        running = (depths > section_index).astype(jnp.int32)
        normed = layer_norm(current, gain_one).astype(jnp.bfloat16)
        group_rows = lax.all_gather(normed, "expert", axis=0, tiled=True)
        group_keys = jnp.dot(group_rows, key_proj, preferred_element_type=jnp.float32).astype(
            jnp.bfloat16
        )
        group_values = jnp.dot(group_rows, value_proj, preferred_element_type=jnp.float32).astype(
            jnp.bfloat16
        )
        chosen_group = jnp.any(moa_choice[section_index][:, :, None] == moa_ids, axis=1)
        group_logits = jnp.dot(group_rows, moa_router, preferred_element_type=jnp.float32)
        group_gates = jax.nn.softmax(jnp.where(chosen_group, group_logits, -jnp.inf), axis=-1)
        expert_saved = []
        local_index = 0
        expert_id = member * moa_local + local_index
        column = jnp.sum(jnp.where(moa_ids == expert_id, group_gates, 0.0), -1)
        queries = jnp.dot(
            group_rows, query_proj[local_index], preferred_element_type=jnp.float32
        ).astype(jnp.bfloat16)
        attended, row_sums = attend_forward(queries, group_keys, group_values)
        projected = jnp.dot(attended, out_proj[local_index], preferred_element_type=jnp.float32)
        gated_sum = column[:, None] * projected
        expert_saved.append((expert_id, column, queries, attended, row_sums, projected))
        attention = lax.psum_scatter(
            gated_sum.astype(jnp.bfloat16), "expert", scatter_dimension=0, tiled=True
        ).astype(jnp.float32)
        mixed_state = current + attention
        normed_two = layer_norm(mixed_state, gain_two).astype(jnp.bfloat16)
        chosen_moe = moe_choice[section_index]
        onehot_moe = (chosen_moe[:, :, None] == moe_ids).astype(jnp.float32)
        moe_logits = jnp.dot(normed_two, moe_router, preferred_element_type=jnp.float32)
        moe_gates = jax.nn.softmax(jnp.sum(onehot_moe * moe_logits[:, None, :], -1), axis=-1)
        target, live_rows = slot_index(chosen_moe, running, moe_count, capacity)
        safe_target = jnp.minimum(target, moe_count * capacity - 1)
        live_mask = live_rows.astype(jnp.float32).reshape(tok_rows, moe_top, 1)
        send_rows = jnp.zeros((moe_count * capacity, model_width), jnp.bfloat16)
        send_rows = send_rows.at[target].set(jnp.repeat(normed_two, moe_top, axis=0), mode="drop")
        received = lax.all_to_all(
            send_rows.reshape(peer_count, moe_local * capacity, model_width),
            "expert",
            split_axis=0,
            concat_axis=0,
            tiled=True,
        )
        received = received.reshape(peer_count, moe_local, capacity, model_width)
        pre_act = jnp.einsum("smcd,mdf->smcf", received, ffn_in, preferred_element_type=jnp.float32)
        activated = jax.nn.gelu(pre_act, approximate=True).astype(jnp.bfloat16)
        expert_out = jnp.einsum(
            "smcf,mfd->smcd", activated, ffn_out, preferred_element_type=jnp.float32
        ).astype(jnp.bfloat16)
        returned = lax.all_to_all(
            expert_out.reshape(peer_count, moe_local * capacity, model_width),
            "expert",
            split_axis=0,
            concat_axis=0,
            tiled=True,
        )
        returned = returned.reshape(moe_count * capacity, model_width)
        moe_rows = (
            returned[safe_target].astype(jnp.float32).reshape(tok_rows, moe_top, model_width)
            * live_mask
        )
        moe_part = jnp.sum(moe_gates[:, :, None] * moe_rows, 1)
        new_state = jnp.where(running[:, None] > 0, mixed_state + moe_part, current)
        saved_steps.append(
            (
                current,
                running,
                normed,
                group_rows,
                group_keys,
                group_values,
                group_gates,
                expert_saved,
                mixed_state,
                normed_two,
                onehot_moe,
                moe_gates,
                target,
                safe_target,
                live_mask,
                received,
                pre_act,
                activated,
                moe_rows,
            )
        )
        history.append(new_state)
        current = new_state

    def combine_local(stacked, halt_vec):
        return combine(stacked, halt_vec, depths)

    output, combine_pull = jax.vjp(combine_local, jnp.stack(history), halt_weight)
    grad_stack, grad_halt = combine_pull(cotangent.astype(jnp.float32))
    carry_grad = jnp.zeros((tok_rows, model_width), jnp.float32)
    grad_gain_one = jnp.zeros(gain_one.shape, jnp.float32)
    grad_gain_two = jnp.zeros(gain_two.shape, jnp.float32)
    grad_moa_router = jnp.zeros(moa_router.shape, jnp.float32)
    grad_moe_router = jnp.zeros(moe_router.shape, jnp.float32)
    grad_key_proj = jnp.zeros(key_proj.shape, jnp.float32)
    grad_value_proj = jnp.zeros(value_proj.shape, jnp.float32)
    expert_parts = []
    for section_index in reversed(range(sections)):
        (
            previous,
            running,
            normed,
            group_rows,
            group_keys,
            group_values,
            group_gates,
            expert_saved,
            mixed_state,
            normed_two,
            onehot_moe,
            moe_gates,
            target,
            safe_target,
            live_mask,
            received,
            pre_act,
            activated,
            moe_rows,
        ) = saved_steps[section_index]
        upstream = grad_stack[section_index] + carry_grad
        run_mask = running.astype(jnp.float32)[:, None]
        grad_z = run_mask * upstream
        keep_grad = (1.0 - run_mask) * upstream
        grad_moe_gates = jnp.sum(moe_rows * grad_z[:, None, :], -1)
        grad_slots = (moe_gates[:, :, None] * grad_z[:, None, :] * live_mask).reshape(
            tok_rows * moe_top, model_width
        )
        grad_send = jnp.zeros((moe_count * capacity, model_width), jnp.bfloat16)
        grad_send = grad_send.at[target].set(grad_slots.astype(jnp.bfloat16), mode="drop")
        grad_recv = lax.all_to_all(
            grad_send.reshape(peer_count, moe_local * capacity, model_width),
            "expert",
            split_axis=0,
            concat_axis=0,
            tiled=True,
        )
        grad_recv = grad_recv.reshape(peer_count, moe_local, capacity, model_width)
        grad_act = jnp.einsum(
            "smcd,mfd->smcf", grad_recv, ffn_out, preferred_element_type=jnp.float32
        )
        step_ffn_out = jnp.einsum(
            "smcf,smcd->mfd", activated, grad_recv, preferred_element_type=jnp.float32
        )

        def gelu_local(inner_values):
            return jax.nn.gelu(inner_values, approximate=True)

        gelu_pull = jax.vjp(gelu_local, pre_act)[1]
        grad_pre = gelu_pull(grad_act)[0].astype(jnp.bfloat16)
        step_ffn_in = jnp.einsum(
            "smcd,smcf->mdf", received, grad_pre, preferred_element_type=jnp.float32
        )
        grad_recv_rows = jnp.einsum(
            "smcf,mdf->smcd", grad_pre, ffn_in, preferred_element_type=jnp.float32
        )
        grad_back = lax.all_to_all(
            grad_recv_rows.reshape(peer_count, moe_local * capacity, model_width).astype(
                jnp.bfloat16
            ),
            "expert",
            split_axis=0,
            concat_axis=0,
            tiled=True,
        ).astype(jnp.float32)
        grad_back = grad_back.reshape(moe_count * capacity, model_width)
        grad_normed_two = jnp.sum(
            grad_back[safe_target].reshape(tok_rows, moe_top, model_width) * live_mask, 1
        )
        grad_picked = moe_gates * (
            grad_moe_gates - jnp.sum(moe_gates * grad_moe_gates, -1, keepdims=True)
        )
        grad_moe_logits = jnp.sum(onehot_moe * grad_picked[:, :, None], 1)
        grad_moe_router = grad_moe_router + jnp.dot(
            normed_two.astype(jnp.float32).T, grad_moe_logits, precision=highest
        )
        grad_normed_two = grad_normed_two + jnp.dot(
            grad_moe_logits, moe_router.astype(jnp.float32).T, precision=highest
        )
        norm_pull_two = jax.vjp(layer_norm, mixed_state, gain_two)[1]
        grad_mixed, grad_gain_part = norm_pull_two(grad_normed_two)
        grad_gain_two = grad_gain_two + grad_gain_part
        grad_mixed = grad_mixed + grad_z
        grad_group = lax.all_gather(
            grad_mixed.astype(jnp.bfloat16), "expert", axis=0, tiled=True
        ).astype(grad_mixed.dtype)
        step_query = jnp.zeros(query_proj.shape, jnp.float32)
        step_out = jnp.zeros(out_proj.shape, jnp.float32)
        local_index = 0
        expert_id, column, queries, attended, row_sums, projected = expert_saved[local_index]
        grad_column = jnp.sum(projected * grad_group, -1)
        grad_columns = jnp.where(moa_ids == expert_id, grad_column[:, None], 0.0)
        grad_proj = (column[:, None] * grad_group).astype(jnp.bfloat16)
        step_out = step_out.at[local_index].add(
            jnp.einsum("sf,sd->fd", attended, grad_proj, preferred_element_type=jnp.float32)
        )
        grad_attended = jnp.einsum(
            "sd,fd->sf", grad_proj, out_proj[local_index], preferred_element_type=jnp.float32
        ).astype(jnp.bfloat16)
        grad_queries, part_keys, part_values = attend_backward(
            queries, group_keys, group_values, grad_attended, row_sums
        )
        grad_queries = grad_queries.astype(jnp.bfloat16)
        step_query = step_query.at[local_index].add(
            jnp.einsum("sd,sf->df", group_rows, grad_queries, preferred_element_type=jnp.float32)
        )
        grad_query_rows = jnp.einsum(
            "sf,df->sd", grad_queries, query_proj[local_index], preferred_element_type=jnp.float32
        )
        own_rows, own_keys, own_values, own_columns = (
            lax.psum_scatter(
                grad_query_rows.astype(jnp.bfloat16), "expert", scatter_dimension=0, tiled=True
            ).astype(jnp.float32),
            lax.psum_scatter(
                part_keys.astype(jnp.bfloat16), "expert", scatter_dimension=0, tiled=True
            ).astype(jnp.float32),
            lax.psum_scatter(
                part_values.astype(jnp.bfloat16), "expert", scatter_dimension=0, tiled=True
            ).astype(jnp.float32),
            lax.psum_scatter(
                grad_columns.astype(jnp.bfloat16), "expert", scatter_dimension=0, tiled=True
            ).astype(jnp.float32),
        )
        normed_wide = normed.astype(jnp.float32)
        grad_key_proj = grad_key_proj + jnp.dot(normed_wide.T, own_keys, precision=highest)
        grad_value_proj = grad_value_proj + jnp.dot(normed_wide.T, own_values, precision=highest)
        grad_normed = own_rows + jnp.dot(own_keys, key_wide.T, precision=highest)
        grad_normed = grad_normed + jnp.dot(own_values, value_wide.T, precision=highest)
        own_gates = lax.dynamic_slice_in_dim(group_gates, member * tok_rows, tok_rows, 0)
        grad_moa_logits = own_gates * (
            own_columns - jnp.sum(own_gates * own_columns, -1, keepdims=True)
        )
        grad_moa_router = grad_moa_router + jnp.dot(
            normed.astype(jnp.float32).T, grad_moa_logits, precision=highest
        )
        grad_normed = grad_normed + jnp.dot(
            grad_moa_logits, moa_router.astype(jnp.float32).T, precision=highest
        )
        norm_pull_one = jax.vjp(layer_norm, previous, gain_one)[1]
        grad_previous, grad_gain_part = norm_pull_one(grad_normed)
        grad_gain_one = grad_gain_one + grad_gain_part
        carry_grad = keep_grad + grad_mixed + grad_previous
        expert_parts.append(
            (
                lax.psum_scatter(
                    step_query.astype(jnp.bfloat16), "dp", scatter_dimension=1, tiled=True
                ).astype(jnp.float32),
                lax.psum_scatter(
                    step_out.astype(jnp.bfloat16), "dp", scatter_dimension=1, tiled=True
                ).astype(jnp.float32),
                lax.psum_scatter(
                    step_ffn_in.astype(jnp.bfloat16), "dp", scatter_dimension=1, tiled=True
                ).astype(jnp.float32),
                lax.psum_scatter(
                    step_ffn_out.astype(jnp.bfloat16), "dp", scatter_dimension=1, tiled=True
                ).astype(jnp.float32),
            )
        )
    summed_parts = expert_parts[0]
    for extra_part in expert_parts[1:]:
        summed_parts = (
            summed_parts[0] + extra_part[0],
            summed_parts[1] + extra_part[1],
            summed_parts[2] + extra_part[2],
            summed_parts[3] + extra_part[3],
        )
    shared = (
        lax.psum_scatter(grad_gain_one, ("dp", "expert"), scatter_dimension=0, tiled=True),
        lax.psum_scatter(grad_gain_two, ("dp", "expert"), scatter_dimension=0, tiled=True),
        lax.psum_scatter(grad_moa_router, ("dp", "expert"), scatter_dimension=0, tiled=True),
        lax.psum_scatter(grad_key_proj, ("dp", "expert"), scatter_dimension=0, tiled=True),
        lax.psum_scatter(grad_value_proj, ("dp", "expert"), scatter_dimension=0, tiled=True),
        lax.psum_scatter(grad_moe_router, ("dp", "expert"), scatter_dimension=0, tiled=True),
        lax.psum_scatter(grad_halt, ("dp", "expert"), scatter_dimension=0, tiled=True),
    )
    return (
        output,
        carry_grad,
        shared[0],
        shared[1],
        shared[2],
        shared[3],
        shared[4],
        summed_parts[0],
        summed_parts[1],
        shared[5],
        summed_parts[2],
        summed_parts[3],
        shared[6],
    )


def solution(mesh):
    in_specs = (
        P(("dp", "expert"), None),
        P(),
        P(),
        P(),
        P(),
        P(),
        P("expert", None, None),
        P("expert", None, None),
        P(),
        P("expert", None, None),
        P("expert", None, None),
        P(),
        P(("dp", "expert")),
        P(None, "dp", None),
        P(None, ("dp", "expert"), None),
        P(("dp", "expert"), None),
    )
    out_specs = (
        P(("dp", "expert"), None),
        P(("dp", "expert"), None),
        P(("dp", "expert")),
        P(("dp", "expert")),
        P(("dp", "expert"), None),
        P(("dp", "expert"), None),
        P(("dp", "expert"), None),
        P("expert", "dp", None),
        P("expert", "dp", None),
        P(("dp", "expert"), None),
        P("expert", "dp", None),
        P("expert", "dp", None),
        P(("dp", "expert")),
    )
    return jax.shard_map(local, mesh=mesh, in_specs=in_specs, out_specs=out_specs, check_vma=False)
```

profile of v0, /device:TPU:1, one launch (start us, length us, event | category | flops | bytes accessed | tf_op | source)
XLA Modules:
  0.0 2140.7 jit_solution(16625106948746379786)
XLA Ops:
  13.2 25.4 %all-gather.7.cloned.1.call-done = bf16[1024,512]{0,1:T(8,128)(2,1)} async-done(((bf16[128,512]{0,1:T(8,128)(2,1)}), bf16[1024,512]{0,1:T(8,128)(2,1)}) %all-gather.7.cloned.1.call-update) | async-done | bytes 1048592 | tf_op jit(solution)/shard_map/all_gather | solution.py:159
  73.3 25.5 %reduce-scatter.82.cloned.1.call-done = bf16[128,512]{1,0:T(8,128)(2,1)} async-done(((bf16[1024,512]{1,0:T(8,128)(2,1)}), bf16[128,512]{1,0:T(8,128)(2,1)}) %reduce-scatter.82.cloned.1.call-update) | async-done | bytes 131088
  103.9 7.0 all-to-all-start
  111.6 6.4 all-to-all-done
  130.0 5.7 all-to-all-done.1
  143.3 23.3 %all-gather.9.cloned.1.call-done = bf16[1024,512]{0,1:T(8,128)(2,1)} async-done(((bf16[128,512]{0,1:T(8,128)(2,1)}), bf16[1024,512]{0,1:T(8,128)(2,1)}) %all-gather.9.cloned.1.call-update) | async-done | bytes 1048592 | tf_op jit(solution)/shard_map/all_gather | solution.py:159
  202.6 23.2 %reduce-scatter.84.cloned.1.call-done = bf16[128,512]{1,0:T(8,128)(2,1)} async-done(((bf16[1024,512]{1,0:T(8,128)(2,1)}), bf16[128,512]{1,0:T(8,128)(2,1)}) %reduce-scatter.84.cloned.1.call-update) | async-done | bytes 131088
  231.1 7.0 all-to-all-start.2
  238.3 6.9 all-to-all-done.2
  256.0 7.0 all-to-all-done.3
  272.6 22.8 %all-gather.11.cloned.1.call-done = bf16[1024,512]{0,1:T(8,128)(2,1)} async-done(((bf16[128,512]{0,1:T(8,128)(2,1)}), bf16[1024,512]{0,1:T(8,128)(2,1)}) %all-gather.11.cloned.1.call-update) | async-done | bytes 1048592 | tf_op jit(solution)/shard_map/all_gather | solution.py:159
  328.9 27.4 %reduce-scatter.86.cloned.1.call-done = bf16[128,512]{1,0:T(8,128)(2,1)} async-done(((bf16[1024,512]{1,0:T(8,128)(2,1)}), bf16[128,512]{1,0:T(8,128)(2,1)}) %reduce-scatter.86.cloned.1.call-update) | async-done | bytes 131088
  361.7 7.0 all-to-all-start.4
  368.9 7.0 all-to-all-done.4
  387.2 6.3 all-to-all-done.5
  409.2 12.1 all_to_all.60
  426.1 10.6 all_to_all.61
  455.3 22.8 %all-gather.13.cloned.1.call-done = bf16[1024,512]{0,1:T(8,128)(2,1)} async-done(((bf16[128,512]{0,1:T(8,128)(2,1)}), bf16[1024,512]{0,1:T(8,128)(2,1)}) %all-gather.13.cloned.1.call-update) | async-done | bytes 1048592 | tf_op jit(solution)/shard_map/all_gather | solution.py:345
  482.5 8.7 multiply_reduce_fusion.5
  491.2 7.0 multiply_convert_fusion.5
  500.9 10.0 multiply_reduce_fusion.2
  510.9 10.4 multiply_convert_fusion.2
  521.3 6.1 fusion.114
  542.5 5.1 fusion.28
  547.6 7.8 fusion.10
  565.9 27.1 %reduce-scatter.90.cloned.1.call-done = bf16[128,512]{1,0:T(8,128)(2,1)} async-done(((bf16[1024,512]{1,0:T(8,128)(2,1)}), bf16[128,512]{1,0:T(8,128)(2,1)}) %reduce-scatter.90.cloned.1.call-update) | async-done | bytes 131088
  595.1 31.2 %reduce-scatter.92.cloned.1.call-done = bf16[128,512]{1,0:T(8,128)(2,1)} async-done(((bf16[1024,512]{1,0:T(8,128)(2,1)}), bf16[128,512]{1,0:T(8,128)(2,1)}) %reduce-scatter.92.cloned.1.call-update) | async-done | bytes 131088
  636.6 14.5 all_to_all.62
  655.9 10.6 all_to_all.63
  684.8 22.8 %all-gather.15.cloned.1.call-done = bf16[1024,512]{0,1:T(8,128)(2,1)} async-done(((bf16[128,512]{0,1:T(8,128)(2,1)}), bf16[1024,512]{0,1:T(8,128)(2,1)}) %all-gather.15.cloned.1.call-update) | async-done | bytes 1048592 | tf_op jit(solution)/shard_map/all_gather | solution.py:345
  712.2 8.7 multiply_reduce_fusion.4
  720.9 6.8 multiply_convert_fusion.4
  731.0 10.0 multiply_reduce_fusion.1
  741.0 10.4 multiply_convert_fusion.1
  751.4 6.1 fusion.115
  773.0 5.0 fusion.26
  778.1 7.3 fusion.8
  796.1 26.9 %reduce-scatter.98.cloned.1.call-done = bf16[128,512]{1,0:T(8,128)(2,1)} async-done(((bf16[1024,512]{1,0:T(8,128)(2,1)}), bf16[128,512]{1,0:T(8,128)(2,1)}) %reduce-scatter.98.cloned.1.call-update) | async-done | bytes 131088
  825.0 31.1 %reduce-scatter.100.cloned.1.call-done = bf16[128,512]{1,0:T(8,128)(2,1)} async-done(((bf16[1024,512]{1,0:T(8,128)(2,1)}), bf16[128,512]{1,0:T(8,128)(2,1)}) %reduce-scatter.100.cloned.1.call-update) | async-done | bytes 131088
  865.7 14.5 all_to_all.64
  885.0 10.6 all_to_all.65
  906.3 23.4 %all-gather.17.cloned.1.call-done = bf16[1024,512]{0,1:T(8,128)(2,1)} async-done(((bf16[128,512]{0,1:T(8,128)(2,1)}), bf16[1024,512]{0,1:T(8,128)(2,1)}) %all-gather.17.cloned.1.call-update) | async-done | bytes 1048592 | tf_op jit(solution)/shard_map/all_gather | solution.py:345
  951.7 5.5 multiply_reduce_fusion.3
  957.3 6.0 multiply_convert_fusion.3
  964.8 10.0 multiply_reduce_fusion
  974.8 11.1 multiply_convert_fusion
  987.2 6.4 fusion.116
  1058.9 7.3 fusion.6
  1075.8 35.7 %reduce-scatter.66.cloned.1.call-done = bf16[1,32,512]{2,1,0:T(8,128)(2,1)} async-done(((bf16[1,512,512]{2,1,0:T(8,128)(2,1)}), bf16[1,32,512]{2,1,0:T(8,128)(2,1)}) %reduce-scatter.66.cloned.1.call-update) | async-done | bytes 32784 | tf_op jit(solution)/shard_map/reduce_scatter | solution.py:409
  1111.5 75.1 %reduce-scatter.68.cloned.1.call-done = bf16[1,32,512]{2,1,0:T(8,128)(2,1)} async-done(((bf16[1,512,512]{2,1,0:T(8,128)(2,1)}), bf16[1,32,512]{2,1,0:T(8,128)(2,1)}) %reduce-scatter.68.cloned.1.call-update) | async-done | bytes 32784 | tf_op jit(solution)/shard_map/reduce_scatter | solution.py:409
  1188.0 73.3 %reduce-scatter.58.cloned.1.call-done = bf16[1,32,512]{2,1,0:T(8,128)(2,1)} async-done(((bf16[1,512,512]{2,1,0:T(8,128)(2,1)}), bf16[1,32,512]{2,1,0:T(8,128)(2,1)}) %reduce-scatter.58.cloned.1.call-update) | async-done | bytes 32784 | tf_op jit(solution)/shard_map/reduce_scatter | solution.py:406
  1261.4 75.1 %reduce-scatter.60.cloned.1.call-done = bf16[1,32,512]{2,1,0:T(8,128)(2,1)} async-done(((bf16[1,512,512]{2,1,0:T(8,128)(2,1)}), bf16[1,32,512]{2,1,0:T(8,128)(2,1)}) %reduce-scatter.60.cloned.1.call-update) | async-done | bytes 32784 | tf_op jit(solution)/shard_map/reduce_scatter | solution.py:406
  1336.5 74.6 %reduce-scatter.62.cloned.1.call-done = bf16[1,32,512]{2,1,0:T(8,128)(2,1)} async-done(((bf16[1,512,512]{2,1,0:T(8,128)(2,1)}), bf16[1,32,512]{2,1,0:T(8,128)(2,1)}) %reduce-scatter.62.cloned.1.call-update) | async-done | bytes 32784 | tf_op jit(solution)/shard_map/reduce_scatter | solution.py:406
  1412.5 75.8 %reduce-scatter.76.cloned.1.call-done = bf16[1,128,512]{2,1,0:T(8,128)(2,1)} async-done(((bf16[1,2048,512]{2,1,0:T(8,128)(2,1)}), bf16[1,128,512]{2,1,0:T(8,128)(2,1)}) %reduce-scatter.76.cloned.1.call-update) | async-done | bytes 131088 | tf_op jit(solution)/shard_map/reduce_scatter | solution.py:415
  1488.4 76.7 %reduce-scatter.78.cloned.1.call-done = bf16[1,128,512]{2,1,0:T(8,128)(2,1)} async-done(((bf16[1,2048,512]{2,1,0:T(8,128)(2,1)}), bf16[1,128,512]{2,1,0:T(8,128)(2,1)}) %reduce-scatter.78.cloned.1.call-update) | async-done | bytes 131088 | tf_op jit(solution)/shard_map/reduce_scatter | solution.py:415
  1565.1 77.1 %reduce-scatter.80.cloned.1.call-done = bf16[1,128,512]{2,1,0:T(8,128)(2,1)} async-done(((bf16[1,2048,512]{2,1,0:T(8,128)(2,1)}), bf16[1,128,512]{2,1,0:T(8,128)(2,1)}) %reduce-scatter.80.cloned.1.call-update) | async-done | bytes 131088 | tf_op jit(solution)/shard_map/reduce_scatter | solution.py:415
  1644.0 75.0 %reduce-scatter.70.cloned.1.call-done = bf16[1,32,2048]{2,1,0:T(8,128)(2,1)} async-done(((bf16[1,512,2048]{2,1,0:T(8,128)(2,1)}), bf16[1,32,2048]{2,1,0:T(8,128)(2,1)}) %reduce-scatter.70.cloned.1.call-update) | async-done | bytes 131088 | tf_op jit(solution)/shard_map/reduce_scatter | solution.py:412
  1719.0 77.1 %reduce-scatter.72.cloned.1.call-done = bf16[1,32,2048]{2,1,0:T(8,128)(2,1)} async-done(((bf16[1,512,2048]{2,1,0:T(8,128)(2,1)}), bf16[1,32,2048]{2,1,0:T(8,128)(2,1)}) %reduce-scatter.72.cloned.1.call-update) | async-done | bytes 131088 | tf_op jit(solution)/shard_map/reduce_scatter | solution.py:412
  1796.0 76.6 %reduce-scatter.74.cloned.1.call-done = bf16[1,32,2048]{2,1,0:T(8,128)(2,1)} async-done(((bf16[1,512,2048]{2,1,0:T(8,128)(2,1)}), bf16[1,32,2048]{2,1,0:T(8,128)(2,1)}) %reduce-scatter.74.cloned.1.call-update) | async-done | bytes 131088 | tf_op jit(solution)/shard_map/reduce_scatter | solution.py:412
  1874.4 30.8 %reduce-scatter.104.cloned.1.call-done = bf16[128,512]{1,0:T(8,128)(2,1)} async-done(((bf16[1024,512]{1,0:T(8,128)(2,1)}), bf16[128,512]{1,0:T(8,128)(2,1)}) %reduce-scatter.104.cloned.1.call-update) | async-done | bytes 131088
  1906.9 31.6 %reduce-scatter.106.cloned.1.call-done = bf16[128,512]{1,0:T(8,128)(2,1)} async-done(((bf16[1024,512]{1,0:T(8,128)(2,1)}), bf16[128,512]{1,0:T(8,128)(2,1)}) %reduce-scatter.106.cloned.1.call-update) | async-done | bytes 131088
  1940.5 31.1 %reduce-scatter.108.cloned.1.call-done = bf16[128,512]{1,0:T(8,128)(2,1)} async-done(((bf16[1024,512]{1,0:T(8,128)(2,1)}), bf16[128,512]{1,0:T(8,128)(2,1)}) %reduce-scatter.108.cloned.1.call-update) | async-done | bytes 131088
  1981.0 72.2 %all-reduce.19 = (f32[512]{0:T(512)}, f32[512]{0:T(512)}, f32[512,8]{1,0:T(8,128)}, f32[512,8]{1,0:T(8,128)}, f32[512]{0:T(512)S(1)}) all-reduce(f32[512]{0:T(512)} %add_add_fusion.12, f32[512]{0:T(512)} %add_add_fusion.11, f32[512,8]{1,0:T(8,128)S(1)} %copy-done.123, ...), channel_id=17, replica_groups=mesh['dp'=16,'expert'=8] {'dp','expert'}, use_global_device_ids=true, to_apply=%region_120.121.clone | all-reduce | flops 9728 | bytes 77824
  2061.1 69.6 %all-reduce.23.cloned.1.call-done = (f32[512,512]{1,0:T(8,128)}, f32[512,512]{1,0:T(8,128)}) async-done(((f32[512,512]{1,0:T(8,128)}, f32[512,512]{1,0:T(8,128)}), (f32[512,512]{1,0:T(8,128)}, f32[512,512]{1,0:T(8,128)})) %all-reduce.23.cloned.1.call-update) | async-done | bytes 2097168
  (1135 shorter events, 472.2 us)
Async XLA Ops:
  7.2 115.0 %copy-start = (bf16[1,2048,512]{2,1,0:T(8,128)(2,1)S(1)}, bf16[1,2048,512]{2,1,0:T(8,128)(2,1)}, u32[]{:S(2)}) copy-start(bf16[1,2048,512]{2,1,0:T(8,128)(2,1)} %param.74) | copy-start | bytes 6291460
  7.2 31.4 %all-gather.7.cloned.1.call-start = ((), (), s32[]{:S(2)}) async-start(), calls=%async_computation.39 | async-start | bytes 1179648 | tf_op jit(solution)/shard_map/all_gather | solution.py:159
  8.4 132.4 %copy-start.10 = (bf16[128,512]{0,1:T(8,128)(2,1)}, bf16[128,512]{0,1:T(8,128)(2,1)S(1)}, u32[]{:S(2)}) copy-start(bf16[128,512]{0,1:T(8,128)(2,1)S(1)} %copy.249) | copy-start | bytes 393220
  11.2 87.5 %reduce-scatter.82.cloned.1.call-start = ((), (), s32[]{:S(2)}) async-start(), calls=%async_computation.57 | async-start | bytes 1179648
  13.2 166.9 %copy-start.16 = (pred[512,1024]{1,0:T(8,128)(4,1)}, pred[512,1024]{1,0:T(8,128)(4,1)S(1)}, u32[]{:S(2)}) copy-start(pred[512,1024]{1,0:T(8,128)(4,1)S(1)} %iota_compare_fusion) | copy-start | bytes 1572868
  103.9 14.2 all-to-all-start
  124.1 11.6 all-to-all-start.1
  128.5 38.1 %all-gather.9.cloned.1.call-start = ((), (), s32[]{:S(2)}) async-start(), calls=%async_computation.40 | async-start | bytes 1179648 | tf_op jit(solution)/shard_map/all_gather | solution.py:159
  142.8 83.0 %reduce-scatter.84.cloned.1.call-start = ((), (), s32[]{:S(2)}) async-start(), calls=%async_computation.58 | async-start | bytes 1179648
  231.1 14.2 all-to-all-start.2
  251.2 11.7 all-to-all-start.3
  255.8 39.6 %all-gather.11.cloned.1.call-start = ((), (), s32[]{:S(2)}) async-start(), calls=%async_computation.41 | async-start | bytes 1179648 | tf_op jit(solution)/shard_map/all_gather | solution.py:159
  271.5 84.8 %reduce-scatter.86.cloned.1.call-start = ((), (), s32[]{:S(2)}) async-start(), calls=%async_computation.59 | async-start | bytes 1179648
  361.7 14.2 all-to-all-start.4
  381.9 11.6 all-to-all-start.5
  386.3 91.7 %all-gather.13.cloned.1.call-start = ((), (), s32[]{:S(2)}) async-start(), calls=%async_computation.42 | async-start | bytes 1179648 | tf_op jit(solution)/shard_map/all_gather | solution.py:345
  454.6 106.4 %reduce-scatter.94.cloned.1.call-start = ((), (), s32[]{:S(2)}) async-start(), calls=%async_computation.63 | async-start | bytes 294912
  482.4 81.8 %reduce-scatter.88.cloned.1.call-start = ((), (), s32[]{:S(2)}) async-start(), calls=%async_computation.60 | async-start | bytes 1179648
  530.0 63.0 %reduce-scatter.90.cloned.1.call-start = ((), (), s32[]{:S(2)}) async-start(), calls=%async_computation.61 | async-start | bytes 1179648
  542.4 83.9 %reduce-scatter.92.cloned.1.call-start = ((), (), s32[]{:S(2)}) async-start(), calls=%async_computation.62 | async-start | bytes 1179648
  556.6 69.7 %copy-start.234 = (f32[128]{0:T(128)S(1)}, f32[128]{0:T(128)}, u32[]{:S(2)}) copy-start(f32[128]{0:T(128)} %copy-done.233) | copy-start | bytes 1540
  559.0 69.8 %copy-start.29 = (f32[3,128,512]{1,2,0:T(8,128)S(1)}, f32[3,128,512]{1,2,0:T(8,128)}, u32[]{:S(2)}) copy-start(f32[3,128,512]{1,2,0:T(8,128)} %copy-done.28) | copy-start | bytes 2359300
  559.0 69.8 %copy-start.214 = (f32[128]{0:T(128)S(1)}, f32[128]{0:T(128)}, u32[]{:S(2)}) copy-start(f32[128]{0:T(128)} %get-tuple-element.443) | copy-start | bytes 1540
  559.0 69.8 %copy-start.287 = (f32[128]{0:T(128)S(1)}, f32[128]{0:T(128)}, u32[]{:S(2)}) copy-start(f32[128]{0:T(128)} %get-tuple-element.442) | copy-start | bytes 1540
  559.0 69.8 %copy-start.289 = (f32[128]{0:T(128)S(1)}, f32[128]{0:T(128)}, u32[]{:S(2)}) copy-start(f32[128]{0:T(128)} %copy-done.288) | copy-start | bytes 1540
  559.0 148.5 %all-gather.15.cloned.1.call-start = ((), (), s32[]{:S(2)}) async-start(), calls=%async_computation.43 | async-start | bytes 1179648 | tf_op jit(solution)/shard_map/all_gather | solution.py:345
  684.1 107.1 %reduce-scatter.102.cloned.1.call-start = ((), (), s32[]{:S(2)}) async-start(), calls=%async_computation.67 | async-start | bytes 294912
  711.9 82.5 %reduce-scatter.96.cloned.1.call-start = ((), (), s32[]{:S(2)}) async-start(), calls=%async_computation.64 | async-start | bytes 1179648
  760.1 62.8 %reduce-scatter.98.cloned.1.call-start = ((), (), s32[]{:S(2)}) async-start(), calls=%async_computation.65 | async-start | bytes 1179648
  772.5 83.5 %reduce-scatter.100.cloned.1.call-start = ((), (), s32[]{:S(2)}) async-start(), calls=%async_computation.66 | async-start | bytes 1179648
  786.7 69.3 %copy-start.232 = (f32[128]{0:T(128)S(1)}, f32[128]{0:T(128)}, u32[]{:S(2)}) copy-start(f32[128]{0:T(128)} %copy-done.231) | copy-start | bytes 1540
  789.1 69.4 %copy-start.71 = (f32[128,512]{0,1:T(8,128)S(1)}, f32[128,512]{0,1:T(8,128)}, u32[]{:S(2)}) copy-start(f32[128,512]{0,1:T(8,128)} %copy-done.70) | copy-start | bytes 786436
  789.1 69.4 %copy-start.210 = (f32[128]{0:T(128)S(1)}, f32[128]{0:T(128)}, u32[]{:S(2)}) copy-start(f32[128]{0:T(128)} %get-tuple-element.447) | copy-start | bytes 1540
  789.1 69.4 %copy-start.253 = (f32[128]{0:T(128)S(1)}, f32[128]{0:T(128)}, u32[]{:S(2)}) copy-start(f32[128]{0:T(128)} %copy-done.252) | copy-start | bytes 1540
  789.1 69.4 %copy-start.255 = (f32[128]{0:T(128)S(1)}, f32[128]{0:T(128)}, u32[]{:S(2)}) copy-start(f32[128]{0:T(128)} %copy-done.254) | copy-start | bytes 1540
  789.2 69.4 %copy-start.257 = (f32[128]{0:T(128)S(1)}, f32[128]{0:T(128)}, u32[]{:S(2)}) copy-start(f32[128]{0:T(128)} %copy-done.256) | copy-start | bytes 1540
  789.2 69.4 %copy-start.286 = (f32[128]{0:T(128)S(1)}, f32[128]{0:T(128)}, u32[]{:S(2)}) copy-start(f32[128]{0:T(128)} %get-tuple-element.441) | copy-start | bytes 1540
  789.2 69.4 %copy-start.291 = (f32[128]{0:T(128)S(1)}, f32[128]{0:T(128)}, u32[]{:S(2)}) copy-start(f32[128]{0:T(128)} %copy-done.290) | copy-start | bytes 1540
  789.2 140.6 %all-gather.17.cloned.1.call-start = ((), (), s32[]{:S(2)}) async-start(), calls=%async_computation.44 | async-start | bytes 1179648 | tf_op jit(solution)/shard_map/all_gather | solution.py:345
  906.3 164.3 %reduce-scatter.110.cloned.1.call-start = ((), (), s32[]{:S(2)}) async-start(), calls=%async_computation.71 | async-start | bytes 294912
  932.9 142.9 %reduce-scatter.64.cloned.1.call-start = ((), (), s32[]{:S(2)}) async-start(), calls=%async_computation.48 | async-start | bytes 557056 | tf_op jit(solution)/shard_map/reduce_scatter | solution.py:409
  936.1 175.4 %reduce-scatter.66.cloned.1.call-start = ((), (), s32[]{:S(2)}) async-start(), calls=%async_computation.49 | async-start | bytes 557056 | tf_op jit(solution)/shard_map/reduce_scatter | solution.py:409
  939.1 247.5 %reduce-scatter.68.cloned.1.call-start = ((), (), s32[]{:S(2)}) async-start(), calls=%async_computation.50 | async-start | bytes 557056 | tf_op jit(solution)/shard_map/reduce_scatter | solution.py:409
  942.4 319.0 %reduce-scatter.58.cloned.1.call-start = ((), (), s32[]{:S(2)}) async-start(), calls=%async_computation.45 | async-start | bytes 557056 | tf_op jit(solution)/shard_map/reduce_scatter | solution.py:406
  945.4 391.1 %reduce-scatter.60.cloned.1.call-start = ((), (), s32[]{:S(2)}) async-start(), calls=%async_computation.46 | async-start | bytes 557056 | tf_op jit(solution)/shard_map/reduce_scatter | solution.py:406
  948.6 462.5 %reduce-scatter.62.cloned.1.call-start = ((), (), s32[]{:S(2)}) async-start(), calls=%async_computation.47 | async-start | bytes 557056 | tf_op jit(solution)/shard_map/reduce_scatter | solution.py:406
  996.0 492.4 %reduce-scatter.76.cloned.1.call-start = ((), (), s32[]{:S(2)}) async-start(), calls=%async_computation.54 | async-start | bytes 2228224 | tf_op jit(solution)/shard_map/reduce_scatter | solution.py:415
  1000.6 564.5 %reduce-scatter.78.cloned.1.call-start = ((), (), s32[]{:S(2)}) async-start(), calls=%async_computation.55 | async-start | bytes 2228224 | tf_op jit(solution)/shard_map/reduce_scatter | solution.py:415
  1005.3 636.9 %reduce-scatter.80.cloned.1.call-start = ((), (), s32[]{:S(2)}) async-start(), calls=%async_computation.56 | async-start | bytes 2228224 | tf_op jit(solution)/shard_map/reduce_scatter | solution.py:415
  1010.2 708.7 %reduce-scatter.70.cloned.1.call-start = ((), (), s32[]{:S(2)}) async-start(), calls=%async_computation.51 | async-start | bytes 2228224 | tf_op jit(solution)/shard_map/reduce_scatter | solution.py:412
  1014.3 781.7 %reduce-scatter.72.cloned.1.call-start = ((), (), s32[]{:S(2)}) async-start(), calls=%async_computation.52 | async-start | bytes 2228224 | tf_op jit(solution)/shard_map/reduce_scatter | solution.py:412
  1018.4 854.3 %reduce-scatter.74.cloned.1.call-start = ((), (), s32[]{:S(2)}) async-start(), calls=%async_computation.53 | async-start | bytes 2228224 | tf_op jit(solution)/shard_map/reduce_scatter | solution.py:412
  1022.5 882.8 %reduce-scatter.104.cloned.1.call-start = ((), (), s32[]{:S(2)}) async-start(), calls=%async_computation.68 | async-start | bytes 1179648
  1030.0 908.5 %reduce-scatter.106.cloned.1.call-start = ((), (), s32[]{:S(2)}) async-start(), calls=%async_computation.69 | async-start | bytes 1179648
  1050.2 921.4 %reduce-scatter.108.cloned.1.call-start = ((), (), s32[]{:S(2)}) async-start(), calls=%async_computation.70 | async-start | bytes 1179648
  1067.5 871.0 %copy-start.51 = (bf16[512,512]{1,0:T(8,128)(2,1)S(1)}, bf16[512,512]{1,0:T(8,128)(2,1)}, u32[]{:S(2)}) copy-start(bf16[512,512]{1,0:T(8,128)(2,1)} %param.68) | copy-start | bytes 1572868
  1069.9 901.7 %copy-start.12 = (bf16[128,512]{0,1:T(8,128)(2,1)S(1)}, bf16[128,512]{0,1:T(8,128)(2,1)}, u32[]{:S(2)}) copy-start(bf16[128,512]{0,1:T(8,128)(2,1)} %copy-done.10) | copy-start | bytes 393220
  1069.9 901.7 %copy-start.54 = (bf16[512,512]{1,0:T(8,128)(2,1)S(1)}, bf16[512,512]{1,0:T(8,128)(2,1)}, u32[]{:S(2)}) copy-start(bf16[512,512]{1,0:T(8,128)(2,1)} %param.69) | copy-start | bytes 1572868
  1069.9 901.7 %copy-start.159 = (f32[512]{0:T(512)S(1)}, f32[512]{0:T(512)}, u32[]{:S(2)}) copy-start(f32[512]{0:T(512)} %param.65) | copy-start | bytes 6148
  1069.9 1060.8 %all-reduce.23.cloned.1.call-start = ((), (), s32[]{:S(2)}) async-start(), calls=%async_computation.72 | async-start | bytes 4194304
  1073.9 899.9 %copy-start.298 = (f32[128]{0:T(128)S(1)}, f32[128]{0:T(128)}, u32[]{:S(2)}) copy-start(f32[128]{0:T(128)} %copy-done.297) | copy-start | bytes 1540
  1976.9 80.0 %copy-start.87 = (f32[128,512]{0,1:T(8,128)S(1)}, f32[128,512]{0,1:T(8,128)}, u32[]{:S(2)}) copy-start(f32[128,512]{0,1:T(8,128)} %get-tuple-element.374) | copy-start | bytes 786436
  1976.9 80.0 %copy-start.89 = (f32[128,512]{0,1:T(8,128)S(1)}, f32[128,512]{0,1:T(8,128)}, u32[]{:S(2)}) copy-start(f32[128,512]{0,1:T(8,128)} %copy-done.88) | copy-start | bytes 786436
  1977.0 80.0 %copy-start.207 = (f32[128]{0:T(128)S(1)}, f32[128]{0:T(128)}, u32[]{:S(2)}) copy-start(f32[128]{0:T(128)} %get-tuple-element.444) | copy-start | bytes 1540
  (304 other events, 3390.4 us)
Sparse Core Ops, SparseCore 0:
  11.3 27.1 all-gather.6
  69.2 29.5 reduce-scatter.81
  142.9 23.6 all-gather.8
  196.3 29.5 reduce-scatter.83
  271.6 23.7 all-gather.10
  326.8 29.4 reduce-scatter.85
  454.7 23.3 all-gather.12
  482.5 28.2 reduce-scatter.93
  530.1 29.6 reduce-scatter.87
  562.1 30.8 reduce-scatter.89
  595.5 30.7 reduce-scatter.91
  684.2 23.3 all-gather.14
  712.0 28.2 reduce-scatter.101
  760.3 29.6 reduce-scatter.95
  792.2 30.7 reduce-scatter.97
  825.2 30.7 reduce-scatter.99
  906.4 23.3 all-gather.16
  933.0 28.2 reduce-scatter.109
  964.8 72.0 reduce-scatter.63
  1040.0 71.5 reduce-scatter.65
  1115.0 71.5 reduce-scatter.67
  1189.8 71.5 reduce-scatter.57
  1264.9 71.5 reduce-scatter.59
  1339.5 71.5 reduce-scatter.61
  1414.7 73.5 reduce-scatter.75
  1491.5 73.5 reduce-scatter.77
  1568.6 73.5 reduce-scatter.79
  1645.4 73.4 reduce-scatter.69
  1722.6 73.4 reduce-scatter.71
  1799.2 73.4 reduce-scatter.73
  1875.2 30.0 reduce-scatter.103
  1907.8 30.6 reduce-scatter.105
  1940.8 30.6 reduce-scatter.107
  1978.4 152.3 all-reduce.22
where the time goes:
time: 2150 us; the launch traced here: 2140 us
  waiting for transfers between devices  1330 us (62%)
  matrix products  318 us (15%)
  other arithmetic  154 us (7%)
  blocking collectives  145 us (7%)
  local copies, waits for them, and re-layouts  139 us (6%)
  starting transfers between devices  37.7 us (2%)
    unnamed x50, waiting for transfers between devices  356 us
    reduce_scatter x3, waiting for transfers between devices, local(): lax.psum_scatter(step_ffn_out.astype(jnp.bfloat16), 'dp', scatter_dimensi...  230 us
    reduce_scatter x3, waiting for transfers between devices, local(): lax.psum_scatter(step_ffn_in.astype(jnp.bfloat16), 'dp', scatter_dimensio...  229 us
    reduce_scatter x3, waiting for transfers between devices, local(): lax.psum_scatter(step_query.astype(jnp.bfloat16), 'dp', scatter_dimension...  223 us
    reduce_scatter x3, waiting for transfers between devices, local(): lax.psum_scatter(step_out.astype(jnp.bfloat16), 'dp', scatter_dimension=1...  111 us
    unnamed x688, local copies, waits for them, and re-layouts  76.8 us
    unnamed x1, blocking collectives  72.2 us
    all_gather x3, waiting for transfers between devices, local(): group_rows = lax.all_gather(normed, 'expert', axis=0, tiled=True)  71.5 us
  transfers between devices with their start and end apart: 40, of which 34 were waited for; matrix products, arithmetic and copies ran while one was open for 16% of the time, Pallas kernels for 0%

commit v1 on v0

v1 whole, which is shorter than its diff:
```python
import functools

import jax
import jax.numpy as jnp
from jax import lax
from jax.experimental import pallas as pl
from jax.experimental.pallas import tpu as pltpu
from jax.sharding import PartitionSpec as P

F32 = jnp.float32
BF16 = jnp.bfloat16
I32 = jnp.int32

WIDTH = 512
SEQ = 1024
TOK = 128
HALF = 512
CHIPS = 4
PAIRS = 4
SLOTS = 40
SPAN = 256
FFN = 2048
UNROLL = 4
PART = 512
LANES = 128


def nn(a, b):
    return lax.dot_general(a, b, (((1,), (0,)), ((), ())), preferred_element_type=F32)


def nt(a, b):
    return lax.dot_general(a, b, (((1,), (1,)), ((), ())), preferred_element_type=F32)


def tn(a, b):
    return lax.dot_general(a, b, (((0,), (0,)), ((), ())), preferred_element_type=F32)


def iota(shape, dim):
    return lax.broadcasted_iota(I32, shape, dim)


def onehot(mask):
    return jnp.where(mask, 1.0, 0.0).astype(BF16)


def row_sum(x):
    return jnp.sum(x, -1, keepdims=True)


def norm_parts(x):
    centred = x - jnp.mean(x, -1, keepdims=True)
    rstd = lax.rsqrt(jnp.mean(centred * centred, -1, keepdims=True) + 1e-05)
    return centred * rstd, rstd


def norm_back(grad, x, gain):
    hat, rstd = norm_parts(x)
    inner = grad * gain
    out = rstd * (
        inner
        - jnp.mean(inner, -1, keepdims=True)
        - hat * jnp.mean(inner * hat, -1, keepdims=True)
    )
    return out, jnp.sum(grad * hat, 0, keepdims=True)


def column(table, index):
    return row_sum(jnp.where(iota(table.shape, 1) == index, table, 0.0))


def masked_softmax(logits, chosen):
    peak = jnp.max(jnp.where(chosen, logits, -jnp.inf), -1, keepdims=True)
    weights = jnp.where(chosen, jnp.exp(logits - peak), 0.0)
    return weights / row_sum(weights)


def named(choice, count):
    lanes = iota((choice.shape[0], LANES), 1)
    mask = lanes == choice[:, 0:1]
    for k in range(1, count):
        mask = mask | (lanes == choice[:, k : k + 1])
    return mask


def lane_of(row, lane):
    return jnp.where(iota((LANES, WIDTH), 0) == lane, row, 0.0).T


def rows_at(block):
    return pl.ds(pl.multiple_of(block * TOK, TOK), TOK)


def split_heads(pair):
    lanes = iota((1, LANES), 1)
    low = jnp.where(lanes < 64, 1.0, 0.0).astype(BF16)
    high = jnp.where(lanes < 64, 0.0, 1.0).astype(BF16)
    return jnp.concatenate([pair * low, pair * high], 0)


def join_heads(both):
    return jnp.where(iota((TOK, LANES), 1) < 64, both[:TOK], both[TOK:])


def call(name, kernel, outs, args, scratch=(), smem=(), flops=0, vmem=60, aliases=None):
    specs = [
        pl.BlockSpec(memory_space=pltpu.SMEM if i in smem else pltpu.VMEM)
        for i in range(len(args))
    ]
    moved = sum(a.size * a.dtype.itemsize for a in args) + sum(
        o.size * o.dtype.itemsize for o in outs
    )
    return pl.pallas_call(
        kernel,
        out_shape=tuple(outs),
        in_specs=specs,
        out_specs=tuple(pl.BlockSpec(memory_space=pltpu.VMEM) for _ in outs),
        scratch_shapes=list(scratch),
        input_output_aliases=aliases or {},
        compiler_params=pltpu.CompilerParams(vmem_limit_bytes=vmem * 2**20),
        cost_estimate=pl.CostEstimate(flops=flops, bytes_accessed=moved, transcendentals=0),
        name=name,
    )(*args)


def like(shape, dtype):
    return jax.ShapeDtypeStruct(shape, dtype)


ANY = pl.BlockSpec(memory_space=pl.ANY)


def copy_in(src, dst, sem):
    moving = pltpu.make_async_copy(src, dst, sem)
    moving.start()
    return moving


def call_any(name, kernel, outs, args, scratch, flops, vmem):
    moved = sum(a.size * a.dtype.itemsize for a in args) + sum(
        o.size * o.dtype.itemsize for o in outs
    )
    return pl.pallas_call(
        kernel,
        out_shape=tuple(outs),
        in_specs=[pl.BlockSpec(memory_space=pltpu.SMEM)] + [ANY] * (len(args) - 1),
        out_specs=tuple(ANY for _ in outs),
        scratch_shapes=list(scratch),
        compiler_params=pltpu.CompilerParams(vmem_limit_bytes=vmem * 2**20),
        cost_estimate=pl.CostEstimate(flops=flops, bytes_accessed=moved, transcendentals=0),
        name=name,
    )(*args)


def allowed_keys(key_pos, span, start):
    number = lax.rem(iota((span, 2 * TOK), 1), TOK) + start
    column_pos = key_pos[0:span, :]
    return jnp.concatenate([column_pos, column_pos], 1) <= number


def attend_level(span, start, keys, value_x, key_row, q_pairs, o_held, logs):
    @pl.loop(0, PAIRS, unroll=UNROLL)
    def _(i):
        pair = pl.ds(pl.multiple_of(i * LANES, LANES), LANES)
        part = nt(q_pairs[i], keys[0:span, pair])
        number = lax.rem(iota((2 * TOK, span), 0), TOK) + start
        part = jnp.where(key_row[0:1, 0:span] <= number, part, -jnp.inf)
        top = jnp.max(part, -1, keepdims=True)
        mixed = nn(jnp.exp(part - top).astype(BF16), value_x[i, 0:span, :])
        total = mixed[:, LANES : 2 * LANES]
        o_held[pl.ds(pl.multiple_of(start, TOK), TOK), pair] = join_heads(
            mixed[:, 0:LANES] / total
        ).astype(BF16)
        lanes = iota((2 * TOK, LANES), 1)
        logs[...] = jnp.where(lanes == i, top + jnp.log(total), logs[...])


def attend_kernel(*refs):
    scal = refs[0]
    same, other = refs[1:5], refs[5:9]
    sources = refs[9:19]
    outs = refs[20:24]
    rows_out, keys_out, values_out, q_out, o_out, spread_0, spread_1, lse_out, gates_out = refs[24:33]
    rows, own, keys, values, value_t = refs[33:38]
    held = refs[38:48]
    key_w, value_w, query_0, query_1, out_0, out_1, router, chosen, pos_row, pos_col = held[:10]
    key_pos = refs[48]
    queries, q_held, o_held, spread, o_spread, staged, lse, gates = refs[49:57]
    q_pairs, key_row, logs = refs[57:60]
    in_sems, row_sems, out_sems, block_sems = refs[60:64]
    query_w, out_w = (query_0, query_1), (out_0, out_1)
    blocks, chip, core = scal[0, 8], scal[0, 9], scal[0, 10]

    row_copies = []
    for hop in range(CHIPS):
        source = lax.rem(chip - hop + CHIPS, CHIPS)
        row_copies.append(
            copy_in(same[hop].at[0:TOK], rows.at[rows_at(source * 2 + core)], row_sems.at[2 * hop])
        )
        row_copies.append(
            copy_in(
                other[hop].at[0:TOK], rows.at[rows_at(source * 2 + 1 - core)], row_sems.at[2 * hop + 1]
            )
        )
    order = (0, 1, 2, 3, 6, 7, 8, 9, 4, 5)
    copies = {i: copy_in(sources[i], held[i], in_sems.at[i]) for i in order}
    key_copy = copy_in(refs[19], key_pos, in_sems.at[10])
    for moving in row_copies:
        moving.wait()
    rows_copy = copy_in(rows, rows_out, out_sems.at[0])
    for source in range(CHIPS):
        own[source * TOK : (source + 1) * TOK, :] = rows[rows_at(2 * source + core), :]
    copies[0].wait()
    copies[1].wait()

    @pl.loop(0, 4)
    def _(tile):
        at = pl.ds(pl.multiple_of(tile * 256, 256), 256)
        block = rows[at, :]
        keys[at, :] = nn(block, key_w[...]).astype(BF16)
        low = nn(block, value_w[...]).astype(BF16)
        values[at, :] = low
        for i in range(PAIRS):
            value_t[i, at, 0:LANES] = low[:, i * LANES : (i + 1) * LANES]
            value_t[i, at, LANES : 2 * LANES] = jnp.ones((256, LANES), BF16)

    keys_copy = copy_in(keys, keys_out, out_sems.at[1])
    values_copy = copy_in(values, values_out, out_sems.at[2])
    mine = own[...]
    for r in range(2):
        copies[2 + r].wait()
        full = nn(mine, query_w[r][...]).astype(BF16)
        queries[r] = full * jnp.asarray(0.125, BF16)
    copies[6].wait()
    copies[7].wait()
    weights = masked_softmax(nt(mine, router[...]), chosen[...] > 0.0)
    gates[...] = weights
    gates_copy = copy_in(gates, gates_out, out_sems.at[3])
    spread[...] = jnp.zeros_like(spread)
    copies[8].wait()
    copies[9].wait()
    key_copy.wait()
    for part in range(8):
        at = slice(part * TOK, (part + 1) * TOK)
        key_row[:, at] = key_pos[at, :].astype(F32).T[:8].astype(I32)

    @pl.loop(0, blocks)
    def _(j):
        start = j * TOK
        here = pl.ds(pl.multiple_of(start, TOK), TOK)
        take = iota((TOK, HALF), 0) + start
        packed = sum(
            nn(onehot(pos_row[r : r + 1, :] == take), queries[r]) for r in range(2)
        ).astype(BF16)
        q_held[here, :] = packed
        copy_in(q_held.at[here], q_out.at[here], block_sems.at[0, j])
        for i in range(PAIRS):
            q_pairs[i] = split_heads(packed[:, i * LANES : (i + 1) * LANES])
        for level in range(1, 5):
            pl.when(scal[0, j] == level)(
                functools.partial(
                    attend_level, level * SPAN, start, keys, value_t, key_row, q_pairs, o_held, logs
                )
            )
        lse[j] = logs[...].T[:8]
        copy_in(o_held.at[here], o_out.at[here], block_sems.at[1, j])
        block = o_held[here, :]
        put = iota((HALF, TOK), 1) + start
        for r in range(2):
            spread[r] += nn(onehot(pos_col[:, r : r + 1] == put), block)

    lse_copy = copy_in(lse, lse_out, out_sems.at[4])
    copies[4].wait()
    copies[5].wait()
    mixture = jnp.zeros((HALF, WIDTH), F32)
    for r in range(2):
        full = spread[r].astype(BF16)
        o_spread[r] = full
        expert = 2 * chip + (core if r == 0 else 1 - core)
        mixture = mixture + column(gates[...], expert) * nn(full, out_w[r][...])
    staged[...] = mixture.astype(BF16)
    final = [
        copy_in(staged.at[rows_at(lax.rem(chip + hop, CHIPS))], outs[hop], row_sems.at[hop])
        for hop in range(CHIPS)
    ]
    final.append(copy_in(o_spread.at[0], spread_0, out_sems.at[5]))
    final.append(copy_in(o_spread.at[1], spread_1, out_sems.at[6]))

    @pl.loop(0, blocks)
    def _(j):
        here = rows_at(j)
        pltpu.make_async_copy(q_held.at[here], q_out.at[here], block_sems.at[0, j]).wait()
        pltpu.make_async_copy(o_held.at[here], o_out.at[here], block_sems.at[1, j]).wait()

    for moving in [rows_copy, keys_copy, values_copy, gates_copy, lse_copy, *final]:
        moving.wait()


def attend(table, same, other, key_w, value_w, query_w, out_w, router, plan):
    outs = [like((TOK, WIDTH), BF16)] * 4 + [
        like((SEQ, WIDTH), BF16),
        like((SEQ, WIDTH), BF16),
        like((SEQ, WIDTH), BF16),
        like((SEQ, WIDTH), BF16),
        like((SEQ, WIDTH), BF16),
        like((HALF, WIDTH), BF16),
        like((HALF, WIDTH), BF16),
        like((8, 8, 2 * TOK), F32),
        like((HALF, LANES), F32),
    ]
    square = pltpu.VMEM((WIDTH, WIDTH), BF16)
    scratch = [
        pltpu.VMEM((SEQ, WIDTH), BF16),
        pltpu.VMEM((HALF, WIDTH), BF16),
        pltpu.VMEM((SEQ, WIDTH), BF16),
        pltpu.VMEM((SEQ, WIDTH), BF16),
        pltpu.VMEM((PAIRS, SEQ, 2 * LANES), BF16),
        square,
        square,
        square,
        square,
        square,
        square,
        pltpu.VMEM((LANES, WIDTH), BF16),
        pltpu.VMEM((HALF, LANES), F32),
        pltpu.VMEM((8, HALF), I32),
        pltpu.VMEM((HALF, LANES), I32),
        pltpu.VMEM((SEQ, LANES), I32),
        pltpu.VMEM((2, HALF, WIDTH), BF16),
        pltpu.VMEM((SEQ, WIDTH), BF16),
        pltpu.VMEM((SEQ, WIDTH), BF16),
        pltpu.VMEM((2, HALF, WIDTH), F32),
        pltpu.VMEM((2, HALF, WIDTH), BF16),
        pltpu.VMEM((HALF, WIDTH), BF16),
        pltpu.VMEM((8, 8, 2 * TOK), F32),
        pltpu.VMEM((HALF, LANES), F32),
        pltpu.VMEM((PAIRS, 2 * TOK, LANES), BF16),
        pltpu.VMEM((8, SEQ), I32),
        pltpu.VMEM((2 * TOK, LANES), F32),
        pltpu.SemaphoreType.DMA((11,)),
        pltpu.SemaphoreType.DMA((8,)),
        pltpu.SemaphoreType.DMA((7,)),
        pltpu.SemaphoreType.DMA((2, 8)),
    ]
    args = [
        table, *same, *other, key_w, value_w, *query_w, *out_w, router,
        plan["chosen"], plan["pos_row"], plan["pos_col"], plan["key_pos"],
    ]
    return call_any("attend", attend_kernel, outs, args, scratch, 6 * 10**9, 60)


def back_level(
    span, start, keys, values, key_pos, q_pairs, o_pairs, logs, inner, sum_k, sum_v, part_q
):
    @pl.loop(0, PAIRS, unroll=UNROLL)
    def _(i):
        pair = pl.ds(pl.multiple_of(i * LANES, LANES), LANES)
        key_block = keys[0:span, pair]
        queries, grads = q_pairs[i], o_pairs[i]
        probs = jnp.exp(nt(key_block, queries) - logs[pl.ds(i, 1), :])
        probs = jnp.where(allowed_keys(key_pos, span, start), probs, 0.0)
        grad_probs = nt(values[0:span, pair], grads)
        grad_scores = (probs * (grad_probs - inner[pl.ds(i, 1), :])).astype(BF16)
        sum_k[0:span, pair] += nn(grad_scores, queries)
        sum_v[0:span, pair] += nn(probs.astype(BF16), grads)
        part_q[i] = tn(grad_scores, key_block)


def attend_back_kernel(*refs):
    scal = refs[0]
    arrived = refs[1:5]
    sources = refs[5:26]
    same, other = refs[26:30], refs[30]
    y_out, q_out, k_out, v_out, tiny_out = refs[31:33], refs[33:35], refs[35], refs[36], refs[37]
    upstream = refs[38]
    held = refs[39:60]
    (
        out_0, out_1, gates, spread_0, spread_1, pos_row, q_held, o_held, lse, keys, values,
        key_pos, pos_col, query_0, query_1, key_w, value_w, rows, router, gain, tiny,
    ) = held
    grad_o, sum_k, sum_v, sum_q, part_q, q_pairs, o_pairs, logs, inner, own, gate_low = refs[60:71]
    grad_y, grad_q, grad_k, grad_v, same_s, other_s = refs[71:77]
    in_sems, row_sems, out_sems = refs[77:80]
    o_spread = (spread_0, spread_1)
    query_w, out_w = (query_0, query_1), (out_0, out_1)
    blocks, chip, core = scal[0, 8], scal[0, 9], scal[0, 10]

    row_copies = [
        copy_in(
            arrived[hop],
            upstream.at[rows_at(lax.rem(chip - hop + CHIPS, CHIPS))],
            row_sems.at[hop],
        )
        for hop in range(CHIPS)
    ]
    copies = [copy_in(sources[i], held[i], in_sems.at[i]) for i in range(21)]
    sum_k[...] = jnp.zeros_like(sum_k)
    sum_v[...] = jnp.zeros_like(sum_v)
    sum_q[...] = jnp.zeros_like(sum_q)
    for moving in row_copies + copies[0:5]:
        moving.wait()
    lanes = iota((HALF, LANES), 1)
    gate_grads = jnp.zeros((HALF, LANES), F32)
    for r in range(2):
        expert = 2 * chip + (core if r == 0 else 1 - core)
        gate = column(gates[...], expert)
        raw = nt(upstream[...], out_w[r][...])
        gate_grads = jnp.where(
            lanes == expert, row_sum(o_spread[r][...].astype(F32) * raw), gate_grads
        )
        grad_o[r] = (gate * raw).astype(BF16)
        grad_y[r] = (gate * upstream[...].astype(F32)).astype(BF16)
    y_copies = [copy_in(grad_y.at[r], y_out[r], out_sems.at[r]) for r in range(2)]
    weights = gates[...]
    gate_low[...] = (weights * (gate_grads - row_sum(weights * gate_grads))).astype(BF16)
    for moving in copies[5:13]:
        moving.wait()

    @pl.loop(0, blocks)
    def _(j):
        start = j * TOK
        here = pl.ds(pl.multiple_of(start, TOK), TOK)
        take = iota((TOK, HALF), 0) + start
        packed = sum(
            nn(onehot(pos_row[r : r + 1, :] == take), grad_o[r]) for r in range(2)
        ).astype(BF16)
        pair_lanes = iota((2 * TOK, LANES), 1)
        inners = jnp.zeros((2 * TOK, LANES), F32)
        for i in range(PAIRS):
            at = slice(i * LANES, (i + 1) * LANES)
            q_pairs[i] = split_heads(q_held[here, at])
            grad_pair = split_heads(packed[:, at])
            o_pairs[i] = grad_pair
            block = o_held[here, at].astype(F32)
            product = row_sum(grad_pair.astype(F32) * jnp.concatenate([block, block], 0))
            inners = jnp.where(pair_lanes == i, product, inners)
        inner[...] = inners.T[:8]
        logs[...] = lse[j]
        for level in range(1, 5):
            pl.when(scal[0, j] == level)(
                functools.partial(
                    back_level, level * SPAN, start, keys, values, key_pos, q_pairs, o_pairs, logs,
                    inner, sum_k, sum_v, part_q,
                )
            )

        block = jnp.concatenate(
            [(join_heads(part_q[i]) * 0.125).astype(BF16) for i in range(PAIRS)], 1
        )
        put = iota((HALF, TOK), 1) + start
        for r in range(2):
            sum_q[r] += nn(onehot(pos_col[:, r : r + 1] == put), block)

    for r in range(2):
        grad_q[r] = sum_q[r].astype(BF16)
    q_copies = [copy_in(grad_q.at[r], q_out[r], out_sems.at[2 + r]) for r in range(2)]
    for moving in copies[13:21]:
        moving.wait()
    for source in range(CHIPS):
        own[source * TOK : (source + 1) * TOK, :] = rows[rows_at(2 * source + core), :]
    sum_q[0] = (
        nt(grad_q[0], query_w[0][...])
        + nt(grad_q[1], query_w[1][...])
        + nn(gate_low[...], router[...])
    )
    gain_part = jnp.sum(sum_q[0] * own[...].astype(F32), 0, keepdims=True)
    sum_q[1, 0:1, :] = gain_part

    @pl.loop(0, 4)
    def _(tile):
        at = pl.ds(pl.multiple_of(tile * 256, 256), 256)
        low_k, low_v = sum_k[at, :].astype(BF16), sum_v[at, :].astype(BF16)
        grad_k[at, :] = low_k
        grad_v[at, :] = low_v
        total = nt(low_k, key_w[...]) + nt(low_v, value_w[...])
        sum_k[at, :] = total
        sum_q[1, 0:1, :] += jnp.sum(total * rows[at, :].astype(F32), 0, keepdims=True)

    k_copy = copy_in(grad_k, k_out, out_sems.at[4])
    v_copy = copy_in(grad_v, v_out, out_sems.at[5])
    final = []
    for hop in range(CHIPS):
        target = lax.rem(chip + hop, CHIPS)
        other_s[hop] = sum_k[rows_at(target * 2 + 1 - core), :].astype(BF16)
    final.append(copy_in(other_s, other, out_sems.at[6]))
    for hop in range(CHIPS):
        target = lax.rem(chip + hop, CHIPS)
        same_s[hop] = (
            sum_k[rows_at(target * 2 + core), :] + sum_q[0, rows_at(target), :]
        ).astype(BF16)
        final.append(copy_in(same_s.at[hop], same[hop], row_sems.at[hop]))
    tiny[...] += tn(own[...], gate_low[...]) + lane_of(sum_q[1, 0:1, :] / gain[...], 8)
    final.append(copy_in(tiny, tiny_out, out_sems.at[7]))
    for moving in [*y_copies, *q_copies, k_copy, v_copy, *final]:
        moving.wait()


def attend_back(table, arrived, held, key_w, value_w, query_w, out_w, plan, rest):
    outs = [like((TOK, WIDTH), BF16)] * 4 + [
        like((CHIPS, TOK, WIDTH), BF16),
        like((HALF, WIDTH), BF16),
        like((HALF, WIDTH), BF16),
        like((HALF, WIDTH), BF16),
        like((HALF, WIDTH), BF16),
        like((SEQ, WIDTH), BF16),
        like((SEQ, WIDTH), BF16),
        like((WIDTH, LANES), F32),
    ]
    keys, values, q_held, o_held, spread_0, spread_1, lse, gates = held
    sources = [
        *out_w, gates, spread_0, spread_1, plan["pos_row"], q_held, o_held, lse, keys, values,
        plan["key_pos"], plan["pos_col"], *query_w, key_w, value_w, *rest,
    ]
    scratch = [pltpu.VMEM((HALF, WIDTH), BF16)]
    scratch += [pltpu.VMEM(a.shape, a.dtype) for a in sources]
    scratch += [
        pltpu.VMEM((2, HALF, WIDTH), BF16),
        pltpu.VMEM((SEQ, WIDTH), F32),
        pltpu.VMEM((SEQ, WIDTH), F32),
        pltpu.VMEM((2, HALF, WIDTH), F32),
        pltpu.VMEM((PAIRS, 2 * TOK, LANES), F32),
        pltpu.VMEM((PAIRS, 2 * TOK, LANES), BF16),
        pltpu.VMEM((PAIRS, 2 * TOK, LANES), BF16),
        pltpu.VMEM((8, 2 * TOK), F32),
        pltpu.VMEM((8, 2 * TOK), F32),
        pltpu.VMEM((HALF, WIDTH), BF16),
        pltpu.VMEM((HALF, LANES), BF16),
        pltpu.VMEM((2, HALF, WIDTH), BF16),
        pltpu.VMEM((2, HALF, WIDTH), BF16),
        pltpu.VMEM((SEQ, WIDTH), BF16),
        pltpu.VMEM((SEQ, WIDTH), BF16),
        pltpu.VMEM((CHIPS, TOK, WIDTH), BF16),
        pltpu.VMEM((CHIPS, TOK, WIDTH), BF16),
        pltpu.SemaphoreType.DMA((21,)),
        pltpu.SemaphoreType.DMA((4,)),
        pltpu.SemaphoreType.DMA((8,)),
    ]
    args = [table, *arrived, *sources]
    return call_any("attend_back", attend_back_kernel, outs, args, scratch, 10**11, 60)


def pair_sum_kernel(*refs):
    other, outs = refs[4], refs[5:]
    for hop in range(CHIPS):
        outs[hop][...] = (refs[hop][...].astype(F32) + other[hop].astype(F32)).astype(BF16)


def pair_sum(same, other):
    return call("pair_sum", pair_sum_kernel, [like((TOK, WIDTH), BF16)] * 4, [*same, other])


def expert_weights_kernel(first, *refs):
    scal, rows = refs[0:2]
    mixes, grad_y, grad_q = refs[2:4], refs[4:6], refs[6:8]
    before = None if first else refs[8]
    after, own = refs[8 if first else 9 :]
    core = scal[0, 10]
    for side in range(2):
        for source in range(CHIPS):
            own[side, source * TOK : (source + 1) * TOK, :] = rows[
                rows_at(2 * source + (core if side == 0 else 1 - core)), :
            ]
    halves = (
        tn(own[0], grad_q[0][...]) + tn(own[1], grad_q[1][...]),
        tn(mixes[0][...], grad_y[0][...]) + tn(mixes[1][...], grad_y[1][...]),
    )
    for half, value in enumerate(halves):
        at = slice(half * WIDTH, (half + 1) * WIDTH)
        if not first:
            value = value + before[:, at]
        after[:, at] = value.astype(after.dtype)


def expert_weights(table, rows, mixes, grad_y, grad_q, before, last):
    first = before is None
    args = [table, rows, *mixes, *grad_y, *grad_q, *(() if first else (before,))]
    outs = [like((WIDTH, 2 * WIDTH), BF16 if last else F32)]
    return call(
        "expert_weights",
        functools.partial(expert_weights_kernel, first),
        outs,
        args,
        [pltpu.VMEM((2, HALF, WIDTH), BF16)],
        smem=(0,),
        flops=3 * 10**9,
    )[0]


def shared_weights_kernel(first, rows, grad_k, grad_v, *refs):
    after = refs[-1]
    for half, grad in enumerate((grad_k, grad_v)):
        at = slice(half * WIDTH, (half + 1) * WIDTH)
        value = tn(rows[...], grad[...])
        if not first:
            value = value + refs[0][:, at]
        after[:, at] = value.astype(after.dtype)
    if after.shape[1] == SHARED:
        after[:, 2 * WIDTH :] = refs[1][...].astype(after.dtype)


SHARED = 2 * WIDTH + LANES


def shared_weights(rows, grad_k, grad_v, before, tiny):
    first, last = before is None, tiny is not None
    args = [rows, grad_k, grad_v, *(() if first else (before,)), *((tiny,) if last else ())]
    return call(
        "shared_weights",
        functools.partial(shared_weights_kernel, first),
        [like((WIDTH, SHARED), BF16) if last else like((WIDTH, 2 * WIDTH), F32)],
        args,
        flops=3 * 10**9,
    )[0]


def slot_pick(shape, r, row_dim):
    row, col = iota(shape, row_dim), iota(shape, 1 - row_dim)
    skip = SLOTS * r
    for source in range(1, CHIPS):
        skip = skip + jnp.where(row >= SLOTS * source, SLOTS, 0)
    return onehot(col == row + skip)


ROWS = CHIPS * SLOTS
BLOCK = 2 * SLOTS


def gelu_parts(x):
    scale = 0.7978845608028654
    inner = scale * (x + 0.044715 * x * x * x)
    return jnp.tanh(inner), scale * (1.0 + 3.0 * 0.044715 * x * x)


def store_blocks(results, outs):
    full = sum(
        nn(slot_pick((2 * ROWS, ROWS), r, 1), results[r].astype(BF16)) for r in range(2)
    ).astype(BF16)
    for hop in range(CHIPS):
        outs[hop][...] = full[hop * BLOCK : (hop + 1) * BLOCK]


def feed_kernel(*refs):
    blocks, win, wout = refs[0:4], refs[4:6], refs[6:8]
    outs, received = refs[8:12], refs[12:14]
    total, = refs[14:]
    step = pl.program_id(0)

    @pl.when(step == 0)
    def _():
        full = jnp.concatenate([b[...] for b in blocks], 0)
        for r in range(2):
            received[r][...] = nn(slot_pick((ROWS, 2 * ROWS), r, 0), full).astype(BF16)
        total[...] = jnp.zeros_like(total)

    for r in range(2):
        pre = nn(received[r][...], win[r][...])
        bend, _ = gelu_parts(pre)
        total[r] += nn((0.5 * pre * (1.0 + bend)).astype(BF16), wout[r][...])

    @pl.when(step == pl.num_programs(0) - 1)
    def _():
        store_blocks([total[0], total[1]], outs)


def whole(shape):
    return pl.BlockSpec(shape, lambda f: (0,) * len(shape))


def feed(blocks, win, wout):
    grid = FFN // PART
    return pl.pallas_call(
        feed_kernel,
        grid=(grid,),
        in_specs=[whole((BLOCK, WIDTH))] * 4
        + [pl.BlockSpec((WIDTH, PART), lambda f: (0, f))] * 2
        + [pl.BlockSpec((PART, WIDTH), lambda f: (f, 0))] * 2,
        out_specs=tuple([whole((BLOCK, WIDTH))] * 4 + [whole((ROWS, WIDTH))] * 2),
        out_shape=tuple([like((BLOCK, WIDTH), BF16)] * 4 + [like((ROWS, WIDTH), BF16)] * 2),
        scratch_shapes=[pltpu.VMEM((2, ROWS, WIDTH), F32)],
        compiler_params=pltpu.CompilerParams(vmem_limit_bytes=60 * 2**20),
        cost_estimate=pl.CostEstimate(flops=2 * 10**9, bytes_accessed=10**7, transcendentals=10**6),
        name="feed",
    )(*blocks, *win, *wout)


def feed_back_kernel(*refs):
    blocks, received, win, wout = refs[0:4], refs[4:6], refs[6:8], refs[8:10]
    outs, grad_rows, acts, grad_pre = refs[10:14], refs[14:16], refs[16:18], refs[18:20]
    total, = refs[20:]
    step = pl.program_id(0)

    @pl.when(step == 0)
    def _():
        full = jnp.concatenate([b[...] for b in blocks], 0)
        for r in range(2):
            grad_rows[r][...] = nn(slot_pick((ROWS, 2 * ROWS), r, 0), full).astype(BF16)
        total[...] = jnp.zeros_like(total)

    for r in range(2):
        pre = nn(received[r][...], win[r][...])
        bend, slope = gelu_parts(pre)
        acts[r][...] = (0.5 * pre * (1.0 + bend)).astype(BF16)
        grad_act = nt(grad_rows[r][...], wout[r][...])
        inner = 0.5 * (1.0 + bend) + 0.5 * pre * (1.0 - bend * bend) * slope
        low = (grad_act * inner).astype(BF16)
        grad_pre[r][...] = low
        total[r] += nt(low, win[r][...])

    @pl.when(step == pl.num_programs(0) - 1)
    def _():
        store_blocks([total[0], total[1]], outs)


HIDDEN = pl.BlockSpec((ROWS, PART), lambda f: (0, f))


def feed_back(blocks, received, win, wout):
    return pl.pallas_call(
        feed_back_kernel,
        grid=(FFN // PART,),
        in_specs=[whole((BLOCK, WIDTH))] * 4
        + [whole((ROWS, WIDTH))] * 2
        + [pl.BlockSpec((WIDTH, PART), lambda f: (0, f))] * 2
        + [pl.BlockSpec((PART, WIDTH), lambda f: (f, 0))] * 2,
        out_specs=tuple([whole((BLOCK, WIDTH))] * 4 + [whole((ROWS, WIDTH))] * 2 + [HIDDEN] * 4),
        out_shape=tuple(
            [like((BLOCK, WIDTH), BF16)] * 4
            + [like((ROWS, WIDTH), BF16)] * 2
            + [like((ROWS, FFN), BF16)] * 4
        ),
        scratch_shapes=[pltpu.VMEM((2, ROWS, WIDTH), F32)],
        compiler_params=pltpu.CompilerParams(vmem_limit_bytes=60 * 2**20),
        cost_estimate=pl.CostEstimate(flops=3 * 10**9, bytes_accessed=10**7, transcendentals=10**6),
        name="feed_back",
    )(*blocks, *received, *win, *wout)


def feed_weights_kernel(*refs):
    scal = refs[0]
    received, grad_rows, acts, grad_pre = refs[1:7], refs[7:13], refs[13:19], refs[19:25]
    out_in, outs_out, total = refs[25], refs[26:30], refs[30]
    out_in[...] = sum(tn(received[s][...], grad_pre[s][...]) for s in range(6)).astype(BF16)
    total[...] = sum(tn(acts[s][...], grad_rows[s][...]) for s in range(6))
    for hop in range(4):
        outs_out[hop][...] = total[rows_at(lax.rem(scal[0, 12] + hop, 4)), :].astype(BF16)


def feed_weights(table, received, grad_rows, acts, grad_pre):
    return pl.pallas_call(
        feed_weights_kernel,
        grid=(FFN // PART,),
        in_specs=[pl.BlockSpec(memory_space=pltpu.SMEM)]
        + [whole((ROWS, WIDTH))] * 12
        + [HIDDEN] * 12,
        out_specs=tuple(
            [pl.BlockSpec((WIDTH, PART), lambda f: (0, f))]
            + [pl.BlockSpec((TOK, WIDTH), lambda f: (f, 0))] * 4
        ),
        out_shape=tuple([like((WIDTH, FFN), BF16)] + [like((4 * TOK, WIDTH), BF16)] * 4),
        scratch_shapes=[pltpu.VMEM((WIDTH, PART), F32)],
        compiler_params=pltpu.CompilerParams(vmem_limit_bytes=60 * 2**20),
        cost_estimate=pl.CostEstimate(flops=8 * 10**9, bytes_accessed=2 * 10**7, transcendentals=0),
        name="feed_weights",
    )(table, *received, *grad_rows, *acts, *grad_pre)


def fold_kernel(axes, scal, *refs):
    count = len(axes)
    for n, axis in enumerate(axes):
        parts = refs[4 * n : 4 * n + 4]
        outs = refs[4 * (count + n) : 4 * (count + n) + 4]
        total = refs[8 * count + n]
        unit = total.shape[0] // 4
        total[...] = sum(p[...].astype(F32) for p in parts)
        place = scal[0, axis]
        for hop in range(4):
            at = pl.ds(pl.multiple_of(lax.rem(place + hop, 4) * unit, unit), unit)
            outs[hop][...] = total[at, :].astype(BF16)


def fold(table, groups, axes):
    outs = []
    for parts in groups:
        rows, cols = parts[0].shape
        outs += [like((rows // 4, cols), BF16)] * 4
    scratch = [pltpu.VMEM(parts[0].shape, F32) for parts in groups]
    args = [table] + [p for parts in groups for p in parts]
    places = tuple({"x": 11, "y": 12}[axis] for axis in axes)
    res = call("fold", functools.partial(fold_kernel, places), outs, args, scratch, smem=(0,))
    return [list(res[4 * n : 4 * n + 4]) for n in range(len(groups))]


def last_sum_kernel(count, *refs):
    for n in range(count):
        total = sum(p[...].astype(F32) for p in refs[4 * n : 4 * n + 4])
        refs[4 * count + n][...] = total.astype(refs[4 * count + n].dtype)


def last_sum(groups, dtypes):
    outs = [like(parts[0].shape, dtype) for parts, dtype in zip(groups, dtypes)]
    args = [p for parts in groups for p in parts]
    return call("last_sum", functools.partial(last_sum_kernel, len(groups)), outs, args)


def first_norm_kernel(block, gain, depth, wide, normed, payload, tail):
    value = block[...].astype(F32)
    wide[...] = value
    low = (norm_parts(value)[0] * gain[...]).astype(BF16)
    normed[...] = low
    payload[0:TOK, :] = low
    tail[...] = jnp.zeros_like(tail)
    tail[0:1, 0:TOK] = depth[...].astype(F32)
    payload[TOK : TOK + 16, :] = tail[...].astype(BF16)


def first_norm(block, gain, depth):
    outs = [
        like((TOK, WIDTH), F32),
        like((TOK, WIDTH), BF16),
        like((TOK + 16, WIDTH), BF16),
    ]
    scratch = [pltpu.VMEM((16, WIDTH), F32)]
    return call("first_norm", first_norm_kernel, outs, [block, gain, depth], scratch)


def attend_plan_kernel(steps, *refs):
    place, choices = refs[0], refs[1]
    blocks = refs[2:10] if 0 not in steps else ()
    outs = refs[2 + len(blocks) :]
    outs, (spots, named_all, depth_col) = outs[: 5 * len(steps)], outs[5 * len(steps) :]
    chip, core = place[0], place[1]
    dp_row, dp_col = place[2], place[3]
    token = iota((SEQ, LANES), 0)
    lanes = iota((SEQ, LANES), 1)
    held = ((token // TOK) % 2) == core
    if blocks:
        for hop in range(CHIPS):
            source = lax.rem(chip - hop + CHIPS, CHIPS)
            for side, ref in ((core, blocks[hop]), (1 - core, blocks[CHIPS + hop])):
                rows = ref[TOK : TOK + 16, 0:TOK].astype(F32)
                rows = jnp.concatenate([rows, jnp.zeros((TOK - 16, TOK), F32)], 0)
                depth_col[rows_at(source * 2 + side), :] = rows.T
    before = onehot(iota((SEQ, SEQ), 1) < iota((SEQ, SEQ), 0))
    for n, s in enumerate(steps):
        table, chosen_out, row_out, col_out, key_out = outs[5 * n : 5 * n + 5]
        turned = jnp.concatenate([choices[s].astype(F32), jnp.zeros((4, SEQ), F32)], 0).T
        named_here = named(turned.astype(I32), 4)
        named_all[...] = jnp.where(named_here, 1.0, 0.0)
        live = held[:, 0:1]
        if blocks:
            live = live & (depth_col[:, 0:1] > s + 0.5)
        live = jnp.where(live, 1.0, 0.0)
        hits = [
            row_sum(jnp.where(lanes == 2 * chip + side, named_all[...], 0.0)) * live
            for side in (core, 1 - core)
        ]
        count = hits[0] + hits[1]
        base = nn(before, jnp.broadcast_to(count, (SEQ, LANES)).astype(BF16))
        key_out[...] = base.astype(I32)
        spot = jnp.where(
            lanes == 0,
            jnp.where(hits[0] > 0, base, -1.0),
            jnp.where(hits[1] > 0, base + hits[0], -1.0),
        )
        spots[...] = jnp.where(lanes < 2, spot, -1.0)
        for source in range(CHIPS):
            at = slice(source * TOK, (source + 1) * TOK)
            chosen_out[at, :] = named_all[rows_at(2 * source + core), :]
            part = spots[rows_at(2 * source + core), :]
            col_out[at, :] = part.astype(I32)
            row_out[:, at] = part.T[:8].astype(I32)
        reach = jnp.sum(
            jnp.where(base <= (lanes * TOK + TOK - 1).astype(F32), 1.0, 0.0), 0, keepdims=True
        )
        total = jnp.sum(count, 0, keepdims=True).astype(I32)
        line = iota((8, LANES), 1)
        chunks = (reach.astype(I32) + (SPAN - 1)) // SPAN
        packed = (total + (TOK - 1)) // TOK
        table[...] = jnp.where(
            line < 8,
            chunks,
            packed,
        )
        for lane, value in ((9, chip), (10, core), (11, dp_row), (12, dp_col)):
            table[...] = jnp.where(line == lane, value, table[...])


def attend_plan(steps, place, choices, blocks):
    outs = [
        like((8, LANES), I32),
        like((HALF, LANES), F32),
        like((8, HALF), I32),
        like((HALF, LANES), I32),
        like((SEQ, LANES), I32),
    ] * len(steps)
    scratch = [pltpu.VMEM((SEQ, LANES), F32)] * 3
    res = call(
        "attend_plan", functools.partial(attend_plan_kernel, steps), outs,
        [place, choices, *blocks], scratch, smem=(0,), flops=10**9,
    )
    names = ("table", "chosen", "pos_row", "pos_col", "key_pos")
    return [dict(zip(names, res[5 * n : 5 * n + 5])) for n in range(len(steps))]


def slot_plan_kernel(place, choices, depth, *outs):
    chip, core = place[0], place[1]
    lanes = iota((TOK, LANES), 1)
    before = onehot(iota((TOK, TOK), 1) < iota((TOK, TOK), 0))
    hop = (lanes // 2 - chip + CHIPS) % CHIPS
    start = hop * BLOCK + jnp.where(lanes % 2 == core, 0, SLOTS)
    for s in range(3):
        turned = jnp.concatenate([choices[s].astype(F32), jnp.zeros((6, TOK), F32)], 0).T
        choice = turned.astype(I32)
        live = depth[...] > s
        names = [lanes == choice[:, k : k + 1] for k in range(2)]
        hits = jnp.where((names[0] | names[1]) & live, 1.0, 0.0)
        spot = nn(before, hits.astype(BF16)) + start.astype(F32)
        table = jnp.full((TOK, LANES), -1.0, F32)
        for k in range(2):
            slot = jnp.where(live, row_sum(jnp.where(names[k], spot, 0.0)), -1.0)
            table = jnp.where(lanes == k, slot, table)
            table = jnp.where(lanes == 2 + k, choice[:, k : k + 1].astype(F32), table)
        outs[2 * s][...] = table.astype(I32)
        outs[2 * s + 1][...] = table.T[:8].astype(I32)


def slot_plan(place, choices, depth):
    outs = [like((TOK, LANES), I32), like((8, TOK), I32)] * 3
    res = call("slot_plan", slot_plan_kernel, outs, [place, choices, depth], smem=(0,))
    return res[0::2], res[1::2]


def dispatch_kernel(*refs):
    state, parts = refs[0], refs[1:5]
    gain, router, slot_row, slot_col = refs[5:9]
    mixed_out, normed_out, gates_out = refs[9:12]
    sends = refs[12:16]
    mixed = state[...] + sum(p[...].astype(F32) for p in parts)
    mixed_out[...] = mixed
    normed = (norm_parts(mixed)[0] * gain[...]).astype(BF16)
    normed_out[...] = normed
    logits = nt(normed, router[...])
    picked = [column(logits, slot_col[:, 2 + k : 3 + k]) for k in range(2)]
    peak = jnp.maximum(picked[0], picked[1])
    weights = [jnp.exp(p - peak) for p in picked]
    total = weights[0] + weights[1]
    lanes = iota((TOK, LANES), 1)
    gates_out[...] = jnp.where(
        lanes == 0, weights[0] / total, jnp.where(lanes == 1, weights[1] / total, 0.0)
    )
    slots = iota((2 * ROWS, TOK), 0)
    hit = (slot_row[0:1, :] == slots) | (slot_row[1:2, :] == slots)
    full = nn(onehot(hit), normed).astype(BF16)
    for hop in range(CHIPS):
        sends[hop][...] = full[hop * BLOCK : (hop + 1) * BLOCK]


def dispatch(state, parts, gain, router, slot_row, slot_col):
    outs = [
        like((TOK, WIDTH), F32),
        like((TOK, WIDTH), BF16),
        like((TOK, LANES), F32),
    ] + [like((BLOCK, WIDTH), BF16)] * 4
    return call("dispatch", dispatch_kernel, outs, [state, *parts, gain, router, slot_row, slot_col])


def picked_rows(slot_col, returned):
    full = jnp.concatenate([b[...] for b in returned], 0)
    slots = iota((TOK, 2 * ROWS), 1)
    return [nn(onehot(slot_col[:, k : k + 1] == slots), full) for k in range(2)]


def next_state(mixed, state, gates, slot_col, rows):
    part = gates[:, 0:1] * rows[0] + gates[:, 1:2] * rows[1]
    return jnp.where(slot_col[:, 0:1] >= 0, mixed + part, state)


def advance_kernel(*refs):
    mixed, state, gates, slot_col = refs[0:4]
    returned, gain = refs[4:8], refs[8]
    state_out, normed_out = refs[9:11]
    rows = picked_rows(slot_col[...], returned)
    new = next_state(mixed[...], state[...], gates[...], slot_col[...], rows)
    state_out[...] = new
    normed_out[...] = (norm_parts(new)[0] * gain[...]).astype(BF16)


def advance(mixed, state, gates, slot_col, returned, gain):
    outs = [like((TOK, WIDTH), F32), like((TOK, WIDTH), BF16)]
    return call("advance", advance_kernel, outs, [mixed, state, gates, slot_col, *returned, gain])


def send_grads(upstream, rows, gates, slot_row, slot_col, grad_z_out, gate_grads_out, sends):
    grad_z = jnp.where(slot_col[:, 0:1] >= 0, upstream, 0.0)
    grad_z_out[...] = grad_z
    lanes = iota((TOK, LANES), 1)
    gate_grads_out[...] = jnp.where(
        lanes == 0,
        row_sum(rows[0] * grad_z),
        jnp.where(lanes == 1, row_sum(rows[1] * grad_z), 0.0),
    )
    slots = iota((2 * ROWS, TOK), 0)
    full = sum(
        nn(onehot(slot_row[k : k + 1, :] == slots), (gates[:, k : k + 1] * grad_z).astype(BF16))
        for k in range(2)
    ).astype(BF16)
    for hop in range(CHIPS):
        sends[hop][...] = full[hop * BLOCK : (hop + 1) * BLOCK]


SEND_OUTS = [
    like((TOK, WIDTH), F32),
    like((TOK, LANES), F32),
] + [like((BLOCK, WIDTH), BF16)] * 4


def turn_kernel(*refs):
    mixed, state, gates, slot_col, slot_row = refs[0:5]
    returned = refs[5:9]
    first_state, halt, depth, cotangent = refs[9:13]
    output, coefs, tiny, upstream_out, grad_z, gate_grads = refs[13:19]
    sends = refs[19:23]
    rows = picked_rows(slot_col[...], returned)
    second = state[...]
    third = next_state(mixed[...], second, gates[...], slot_col[...], rows)
    first = first_state[...]
    vector = halt[...]
    grad = cotangent[...].astype(F32)
    p1 = jax.nn.sigmoid(row_sum(first * vector))
    p2 = jax.nn.sigmoid(row_sum(second * vector))
    a1, a2, a3 = row_sum(first * grad), row_sum(second * grad), row_sum(third * grad)
    steps = depth[...]
    one, two, three = steps == 1, steps == 2, steps == 3
    c1 = jnp.where(one, 1.0, p1)
    c2 = jnp.where(one, 0.0, jnp.where(two, 1.0 - p1, p2 * (1.0 - p1)))
    c3 = jnp.where(three, (1.0 - p1) * (1.0 - p2), 0.0)
    output[...] = c1 * first + c2 * second + c3 * third
    d1 = jnp.where(
        two, a1 - a2, jnp.where(three, a1 - p2 * a2 - (1.0 - p2) * a3, 0.0)
    ) * (p1 * (1.0 - p1))
    d2 = jnp.where(three, (1.0 - p1) * (a2 - a3), 0.0) * (p2 * (1.0 - p2))
    tiny[...] = lane_of(jnp.sum(d1 * first + d2 * second, 0, keepdims=True), 25)
    lanes = iota((TOK, LANES), 1)
    table = jnp.zeros((TOK, LANES), F32)
    for lane, value in enumerate((c1, c2, c3, d1, d2)):
        table = jnp.where(lanes == lane, value, table)
    coefs[...] = table
    upstream = c3 * grad
    upstream_out[...] = upstream
    send_grads(upstream, rows, gates[...], slot_row[...], slot_col[...], grad_z, gate_grads, sends)


def turn(mixed, state, gates, slot_col, slot_row, returned, first_state, halt, depth, cotangent):
    outs = [
        like((TOK, WIDTH), F32),
        like((TOK, LANES), F32),
        like((WIDTH, LANES), F32),
        like((TOK, WIDTH), F32),
    ] + SEND_OUTS
    args = [mixed, state, gates, slot_col, slot_row, *returned, first_state, halt, depth, cotangent]
    return call("turn", turn_kernel, outs, args)


def moe_back_kernel(*refs):
    returned, slot_col, gates, gate_grads = refs[0:4], refs[4], refs[5], refs[6]
    normed, router, mixed, gain, grad_z, tiny = refs[7:13]
    grad_mixed, grad_low, tiny_out = refs[13:]
    full = jnp.concatenate([b[...] for b in returned], 0)
    slots = iota((TOK, 2 * ROWS), 1)
    hit = (slot_col[:, 0:1] == slots) | (slot_col[:, 1:2] == slots)
    grad_normed = nn(onehot(hit), full)
    weights, grads = gates[...], gate_grads[...]
    inner = row_sum(weights * grads)
    lanes = iota((TOK, LANES), 1)
    grad_logits = jnp.zeros((TOK, LANES), F32)
    for k in range(2):
        value = weights[:, k : k + 1] * (grads[:, k : k + 1] - inner)
        grad_logits = grad_logits + jnp.where(lanes == slot_col[:, 2 + k : 3 + k], value, 0.0)
    low = grad_logits.astype(BF16)
    grad_normed = grad_normed + nn(low, router[...])
    out, gain_part = norm_back(grad_normed, mixed[...], gain[...])
    out = out + grad_z[...]
    turned = jnp.concatenate([low[:, LANES - 16 :], low[:, : LANES - 16]], 1)
    tiny_out[...] = tiny[...] + tn(normed[...], turned) + lane_of(gain_part, 24)
    grad_mixed[...] = out
    grad_low[...] = out.astype(BF16)


def moe_back(returned, slot_col, gates, gate_grads, normed, router, mixed, gain, grad_z, tiny):
    outs = [
        like((TOK, WIDTH), F32),
        like((TOK, WIDTH), BF16),
        like((WIDTH, LANES), F32),
    ]
    args = [*returned, slot_col, gates, gate_grads, normed, router, mixed, gain, grad_z, tiny]
    return call("moe_back", moe_back_kernel, outs, args)


def retreat_kernel(step, *refs):
    parts = refs[0:4]
    state, gain, slot_col, upstream, grad_mixed = refs[4:9]
    rest = refs[9:]
    total = sum(p[...].astype(F32) for p in parts)
    out, _ = norm_back(total, state[...], gain[...])
    kept = jnp.where(slot_col[:, 0:1] >= 0, 0.0, upstream[...])
    carry = kept + grad_mixed[...] + out
    if step == 0:
        rest[0][...] = carry
        return
    cotangent, halt, coefs, gates, before_col, before_row = rest[0:6]
    returned = rest[6:10]
    upstream_out, grad_z, gate_grads_out = rest[10:13]
    sends = rest[13:17]
    table = coefs[...]
    carry = carry + column(table, step - 1) * cotangent[...].astype(F32)
    carry = carry + column(table, step + 2) * halt[...]
    upstream_out[...] = carry
    rows = picked_rows(before_col[...], returned)
    send_grads(
        carry, rows, gates[...], before_row[...], before_col[...], grad_z, gate_grads_out, sends
    )


def retreat(step, parts, args, extra):
    outs = [like((TOK, WIDTH), F32)] + (SEND_OUTS if step else [])
    return call("retreat", functools.partial(retreat_kernel, step), outs, [*parts, *args, *extra])


def swap_core(rows):
    return lax.ppermute(rows, "expert", [(i, i ^ 1) for i in range(2 * CHIPS)])


def shift_chip(rows, hops):
    count = 2 * CHIPS
    return lax.ppermute(rows, "expert", [(i, (i + 2 * hops) % count) for i in range(count)])


def send_blocks(blocks):
    return [blocks[0]] + [shift_chip(blocks[d], d) for d in (1, 2, 3)]


def return_blocks(blocks):
    return [blocks[0]] + [shift_chip(blocks[d], CHIPS - d) for d in (1, 2, 3)]


def spread_rows(rows):
    return [rows] + [shift_chip(rows, d) for d in (1, 2, 3)]


def shift_x(rows, hops):
    return lax.ppermute(rows, "dp", [(i, (i + 4 * hops) % 16) for i in range(16)])


def shift_y(rows, hops):
    return lax.ppermute(rows, "dp", [(i, i // 4 * 4 + (i + hops) % 4) for i in range(16)])


def go(shift, blocks):
    return [blocks[0]] + [shift(blocks[d], d) for d in (1, 2, 3)]


def block_sum(blocks):
    return jnp.sum(blocks.astype(F32), 0)


def local(
    block_input,
    gain_one,
    gain_two,
    moa_router,
    key_proj,
    value_proj,
    query_proj,
    out_proj,
    moe_router,
    ffn_in,
    ffn_out,
    halt_weight,
    depths,
    moa_choice,
    moe_choice,
    cotangent,
):
    member = lax.axis_index("expert")
    spot = lax.axis_index("dp")
    place = jnp.stack([member // 2, member % 2, spot // 4, spot % 4]).astype(I32)
    gain_a, gain_b = gain_one[None, :], gain_two[None, :]
    halt = halt_weight[None, :]
    router_a = jnp.pad(moa_router.T, ((0, LANES - 8), (0, 0)))
    router_b = jnp.pad(moe_router.T, ((0, LANES - 8), (0, 0)))
    depth = depths[:, None]
    moa_rows, moe_rows = moa_choice.swapaxes(1, 2), moe_choice.swapaxes(1, 2)

    state, normed, payload = first_norm(block_input, gain_a, depths[None, :])
    same = spread_rows(payload)
    query_w = [query_proj[0], swap_core(query_proj[0])]
    out_w = [out_proj[0], swap_core(out_proj[0])]
    plan = attend_plan((0,), place, moa_rows, ())
    same[1], plan[0]["table"] = lax.optimization_barrier((same[1], plan[0]["table"]))
    other = [swap_core(rows) for rows in same]
    slot_cols, slot_rows = slot_plan(place, moe_rows, depth)
    win = wout = None

    kept = []
    states = [state]
    for s in range(3):
        if s:
            same = spread_rows(normed)
            other = [swap_core(rows) for rows in same]
        p = plan[s]
        res = attend(
            p["table"], same, other, key_proj, value_proj, query_w, out_w, router_a, p
        )
        parts = send_blocks(res[:4])
        if s == 0:
            win = [ffn_in[0], swap_core(ffn_in[0])]
            wout = [ffn_out[0], swap_core(ffn_out[0])]
            plan = plan + attend_plan((1, 2), place, moa_rows, (*same, *other))
            parts[1], plan[1]["table"] = lax.optimization_barrier((parts[1], plan[1]["table"]))
        mixed, normed_b, gates, *sends = dispatch(
            state, parts, gain_b, router_b, slot_rows[s], slot_cols[s]
        )
        *sends, mine, others = feed(send_blocks(sends), win, wout)
        returned = return_blocks(sends)
        *saved, spread_0, spread_1, lse, weights = res[4:]
        kept.append(
            dict(
                normed=normed, rows=saved[0], mixed=mixed, normed_b=normed_b, gates=gates,
                attend=(*saved[1:], spread_0, spread_1, lse, weights),
                mixes=(spread_0, swap_core(spread_1)),
                received=(mine, others), returned=returned, state=state,
                received_all=(mine, swap_core(others)),
            )
        )
        if s < 2:
            state, normed = advance(mixed, state, gates, slot_cols[s], returned, gain_a)
            states.append(state)

    output, coefs, tiny, upstream, grad_z, gate_grads, *sends = turn(
        mixed, state, gates, slot_cols[2], slot_rows[2], returned, states[1], halt, depth, cotangent
    )
    expert_acc = shared_acc = None
    received, acts, grad_pres, grad_rows = [], [], [], []
    for s in (2, 1, 0):
        k, p = kept[s], plan[s]
        table = p["table"]
        *sends, rows_0, rows_1, act_0, act_1, pre_0, pre_1 = feed_back(
            send_blocks(sends), k["received"], win, wout
        )
        back = return_blocks(sends)
        received += k["received_all"]
        acts += [act_0, swap_core(act_1)]
        grad_pres += [pre_0, swap_core(pre_1)]
        grad_rows += [rows_0, swap_core(rows_1)]
        grad_mixed, grad_low, tiny = moe_back(
            back, slot_cols[s], k["gates"], gate_grads, k["normed_b"], router_b, k["mixed"],
            gain_b, grad_z, tiny,
        )
        if s == 0:
            grad_in, *blocks = feed_weights(table, received, grad_rows, acts, grad_pres)
            grad_low, grad_in, *blocks = lax.optimization_barrier((grad_low, grad_in, *blocks))
            grads_out = go(shift_y, blocks)
            grad_in = lax.psum_scatter(grad_in, "dp", scatter_dimension=0, tiled=True)
        *same, other, y_0, y_1, q_0, q_1, grad_k, grad_v, tiny = attend_back(
            table, spread_rows(grad_low), k["attend"], key_proj, value_proj, query_w, out_w, p,
            (k["rows"], router_a, gain_a, tiny),
        )
        other = swap_core(other)
        if s == 0:
            other, *arrived = lax.optimization_barrier((other, *grads_out[1:]))
            grads_out[1:] = arrived
        parts = pair_sum(same, other)
        q_0, grad_k, *parts = lax.optimization_barrier((q_0, grad_k, *parts))
        parts = send_blocks(parts)
        expert_acc = expert_weights(
            table, k["rows"], k["mixes"], (y_0, swap_core(y_1)), (q_0, swap_core(q_1)),
            expert_acc, s == 0,
        )
        shared_acc = shared_weights(
            k["rows"], grad_k, grad_v, shared_acc, None if s else tiny
        )
        parts[1], shared_acc, expert_acc = lax.optimization_barrier(
            (parts[1], shared_acc, expert_acc)
        )
        args = (k["state"], gain_a, slot_cols[s], upstream, grad_mixed)
        if s:
            b = kept[s - 1]
            extra = (
                cotangent, halt, coefs, b["gates"], slot_cols[s - 1], slot_rows[s - 1],
                *b["returned"],
            )
            upstream, grad_z, gate_grads, *sends = retreat(s, parts, args, extra)
        else:
            (grad_input,) = retreat(s, parts, args, ())

    (grads_out,) = fold(table, (grads_out,), "x")
    grads_out = go(shift_x, grads_out)
    grad_qo = block_sum(
        lax.all_to_all(
            expert_acc.reshape(16, 32, 2 * WIDTH), "dp", split_axis=0, concat_axis=0, tiled=True
        )
    )
    shared = block_sum(
        lax.all_to_all(
            shared_acc.reshape(128, 4, SHARED), ("dp", "expert"), split_axis=0, concat_axis=0,
            tiled=True,
        )
    )
    tiny = shared[:, 2 * WIDTH :]
    (grad_out,) = last_sum((grads_out,), (F32,))
    return (
        output,
        grad_input,
        tiny[:, 8],
        tiny[:, 24],
        tiny[:, :8],
        shared[:, :WIDTH],
        shared[:, WIDTH : 2 * WIDTH],
        grad_qo[:, :WIDTH][None],
        grad_qo[:, WIDTH:][None],
        tiny[:, 16:24],
        grad_in.astype(F32)[None],
        grad_out[None],
        tiny[:, 25],
    )


def solution(mesh):
    in_specs = (
        P(("dp", "expert"), None),
        P(),
        P(),
        P(),
        P(),
        P(),
        P("expert", None, None),
        P("expert", None, None),
        P(),
        P("expert", None, None),
        P("expert", None, None),
        P(),
        P(("dp", "expert")),
        P(None, "dp", None),
        P(None, ("dp", "expert"), None),
        P(("dp", "expert"), None),
    )
    out_specs = (
        P(("dp", "expert"), None),
        P(("dp", "expert"), None),
        P(("dp", "expert")),
        P(("dp", "expert")),
        P(("dp", "expert"), None),
        P(("dp", "expert"), None),
        P(("dp", "expert"), None),
        P("expert", "dp", None),
        P("expert", "dp", None),
        P(("dp", "expert"), None),
        P("expert", "dp", None),
        P("expert", "dp", None),
        P(("dp", "expert")),
    )
    return jax.shard_map(local, mesh=mesh, in_specs=in_specs, out_specs=out_specs, check_vma=False)
```

time: 2150 us -> 602 us (0.28)
  waiting for transfers between devices: 1330 us -> 114 us
  matrix products: 318 us -> 0 us
  Pallas kernels: 0 us -> 273 us
  other arithmetic: 154 us -> 2.93 us
  blocking collectives: 145 us -> 0 us
  starting transfers between devices: 37.7 us -> 160 us
  local copies, waits for them, and re-layouts: 139 us -> 29 us
    reduce_scatter x12 -> x1, waiting for transfers between devices: 792 us -> 0.01 us  [local(): grad_in = lax.psum_scatter(grad_in, 'dp', scatter_dimension=0, tiled=True)]
    unnamed x50 -> x1, waiting for transfers between devices: 356 us -> 0.02 us
    dot_general x114 -> x0, matrix products: 318 us -> none  [the longest x6 52.9 us: attend_backward(): jnp.einsum('qhd,khd->hqk', upstream, value_heads, preferred_element_type=...]
    pallas_call x0 -> x40, Pallas kernels: none -> 273 us  [the longest x6 121 us: call_any(): pl.pallas_call(kernel, out_shape=tuple(outs), in_specs=[pl.BlockSpec(memo...]
    ppermute x0 -> x118, starting transfers between devices: none -> 144 us  [the longest x72 84.5 us: shift_chip(): lax.ppermute(rows, 'expert', [(i, (i + 2 * hops) % count) for i in range(...]
    all_gather x6 -> x0, waiting for transfers between devices: 141 us -> none  [the longest x3 71.5 us: local(): group_rows = lax.all_gather(normed, 'expert', axis=0, tiled=True)]
    ppermute x0 -> x118, waiting for transfers between devices: none -> 100 us  [the longest x72 81.1 us: shift_chip(): lax.ppermute(rows, 'expert', [(i, (i + 2 * hops) % count) for i in range(...]
    all_to_all x6 -> x0, blocking collectives: 73 us -> none  [the longest x3 41.1 us: local(): lax.all_to_all(grad_send.reshape(peer_count, moe_local * capacity, model_...]
  transfers between devices with their start and end apart: 40 -> 121, of which waited for: 34 -> 60; matrix products, arithmetic and copies ran while one was open for 16% -> 1% of each run, Pallas kernels for 0% -> 21%
where the time goes in v1:
time: 602 us; the launch traced here: 595 us
  Pallas kernels  273 us (45%)
  starting transfers between devices  160 us (27%)
  waiting for transfers between devices  114 us (19%)
  local copies, waits for them, and re-layouts  29 us (5%)
  between operations  15.3 us (3%)
    pallas_call x6, Pallas kernels, call_any(): pl.pallas_call(kernel, out_shape=tuple(outs), in_specs=[pl.BlockSpec(memo...  121 us
    pallas_call x27, Pallas kernels, call(): pl.pallas_call(kernel, out_shape=tuple(outs), in_specs=specs, out_specs=t...  89.3 us
    ppermute x72, starting transfers between devices, shift_chip(): lax.ppermute(rows, 'expert', [(i, (i + 2 * hops) % count) for i in range(...  84.5 us
    ppermute x72, waiting for transfers between devices, shift_chip(): lax.ppermute(rows, 'expert', [(i, (i + 2 * hops) % count) for i in range(...  81.1 us
    ppermute x40, starting transfers between devices, swap_core(): return lax.ppermute(rows, 'expert', [(i, i ^ 1) for i in range(2 * CHIPS)])  48.4 us
    pallas_call x3, Pallas kernels, feed_back(): pl.pallas_call(feed_back_kernel, grid=(FFN // PART,), in_specs=[whole((BL...  28.1 us
    unnamed x258, local copies, waits for them, and re-layouts  23.1 us
    pallas_call x3, Pallas kernels, feed(): pl.pallas_call(feed_kernel, grid=(grid,), in_specs=[whole((BLOCK, WIDTH))...  22.4 us
  transfers between devices with their start and end apart: 121, of which 60 were waited for; matrix products, arithmetic and copies ran while one was open for 1% of the time, Pallas kernels for 21%

profile of v1, /device:TPU:1, one launch (start us, length us, event | category | flops | bytes accessed | tf_op | source)
XLA Modules:
  0.0 594.5 jit_solution(6042551432027520997)
XLA Ops:
  12.4 3.3 collective-permute-start.1
  24.6 3.4 attend_plan.2
  33.3 20.2 %attend.3 = (bf16[128,512]{1,0:T(8,128)(2,1)}, bf16[128,512]{1,0:T(8,128)(2,1)}, bf16[128,512]{1,0:T(8,128)(2,1)}, bf16[128,512]{1,0:T(8,128)(2,1)}, bf16[1024,5...) custom-call(s32[8,128]{1,0:T(8,128)} %get-tuple-element.282.refs_0_., ...), custom_call_target="tpu_custom_call" | custom-call | flops 6000000000 | bytes 12668928 | tf_op jit(solution)/shard_map/attend/pallas_call | solution.py:144
  58.8 3.0 slot_plan.1
  61.7 7.2 %attend_plan.3 = (s32[8,128]{1,0:T(8,128)}, f32[512,128]{1,0:T(8,128)}, s32[8,512]{1,0:T(8,128)}, s32[512,128]{1,0:T(8,128)}, s32[1024,128]{1,0:T(8,128)}, /*ind...) custom-call(s32[4]{0:T(128)} %pad_add_fusion.refs_0_.place, ...), custom_call_target="tpu_custom_call" | custom-call | flops 1000000000 | bytes 3366928 | tf_op jit(solution)/shard_map/attend_plan/pallas_call | solution.py:114
  79.9 7.5 %feed.3 = (bf16[80,512]{1,0:T(8,128)(2,1)}, bf16[80,512]{1,0:T(8,128)(2,1)}, bf16[80,512]{1,0:T(8,128)(2,1)}, bf16[80,512]{1,0:T(8,128)(2,1)}, bf16[160,512]{1,0:T(8,128)(2,1)}, /*index=5*/bf16[160,512]{1,0:T(8,128)(2,1)}) custom-call(bf16[80,512]{1,0:T(8,128)(2,1)} %get-tuple-element.298.refs_0_, bf16[80,512]{1,0:T(8,128)(2,1)} %copy-done.35, ...), custom_call_target="tpu_custom_call" | custom-call | flops 2000000000 | bytes 10000000 | tf_op jit(solution)/shard_map/feed/pallas_call | solution.py:672
  87.4 3.4 collective-permute-start.17
  92.9 3.0 collective-permute-done.18.refs_6_.refs_17_
  103.4 2.6 collective-permute-start.23
  106.3 3.8 collective-permute-start.24
  112.7 15.9 %attend.4 = (bf16[128,512]{1,0:T(8,128)(2,1)}, bf16[128,512]{1,0:T(8,128)(2,1)}, bf16[128,512]{1,0:T(8,128)(2,1)}, bf16[128,512]{1,0:T(8,128)(2,1)}, bf16[1024,5...) custom-call(s32[8,128]{1,0:T(8,128)} %get-tuple-element.307.refs_0_,, ...), custom_call_target="tpu_custom_call" | custom-call | flops 6000000000 | bytes 12537856 | tf_op jit(solution)/shard_map/attend/pallas_call | solution.py:144
  129.2 3.0 collective-permute-start.28
  132.3 2.6 collective-permute-done.27.refs_2_
  134.8 3.7 collective-permute-done.28.refs_3_
  141.8 3.7 collective-permute-start.31
  146.4 2.9 collective-permute-done.31.refs_2_
  150.7 7.5 %feed.4 = (bf16[80,512]{1,0:T(8,128)(2,1)}, bf16[80,512]{1,0:T(8,128)(2,1)}, bf16[80,512]{1,0:T(8,128)(2,1)}, bf16[80,512]{1,0:T(8,128)(2,1)}, bf16[160,512]{1,0:T(8,128)(2,1)}, /*index=5*/bf16[160,512]{1,0:T(8,128)(2,1)}) custom-call(bf16[80,512]{1,0:T(8,128)(2,1)} %get-tuple-element.321.refs_0_, bf16[80,512]{1,0:T(8,128)(2,1)} %copy-done.38, ...), custom_call_target="tpu_custom_call" | custom-call | flops 2000000000 | bytes 10000000 | tf_op jit(solution)/shard_map/feed/pallas_call | solution.py:672
  170.5 4.8 collective-permute-start.39
  175.3 3.8 collective-permute-start.40
  181.6 14.0 %attend.5 = (bf16[128,512]{1,0:T(8,128)(2,1)}, bf16[128,512]{1,0:T(8,128)(2,1)}, bf16[128,512]{1,0:T(8,128)(2,1)}, bf16[128,512]{1,0:T(8,128)(2,1)}, bf16[1024,5...) custom-call(s32[8,128]{1,0:T(8,128)} %get-tuple-element.330.refs_0_,, ...), custom_call_target="tpu_custom_call" | custom-call | flops 6000000000 | bytes 12537856 | tf_op jit(solution)/shard_map/attend/pallas_call | solution.py:144
  196.2 3.1 collective-permute-start.44
  201.8 3.7 collective-permute-done.44.refs_3_
  209.5 3.4 collective-permute-start.47
  213.8 2.9 collective-permute-done.47.refs_2_
  218.0 7.5 %feed.5 = (bf16[80,512]{1,0:T(8,128)(2,1)}, bf16[80,512]{1,0:T(8,128)(2,1)}, bf16[80,512]{1,0:T(8,128)(2,1)}, bf16[80,512]{1,0:T(8,128)(2,1)}, bf16[160,512]{1,0:T(8,128)(2,1)}, /*index=5*/bf16[160,512]{1,0:T(8,128)(2,1)}) custom-call(bf16[80,512]{1,0:T(8,128)(2,1)} %get-tuple-element.344.refs_0_, bf16[80,512]{1,0:T(8,128)(2,1)} %copy-done.39, ...), custom_call_target="tpu_custom_call" | custom-call | flops 2000000000 | bytes 10000000 | tf_op jit(solution)/shard_map/feed/pallas_call | solution.py:672
  232.4 3.1 turn.1
  242.3 9.3 %feed_back.3 = (bf16[80,512]{1,0:T(8,128)(2,1)}, bf16[80,512]{1,0:T(8,128)(2,1)}, bf16[80,512]{1,0:T(8,128)(2,1)}, bf16[80,512]{1,0:T(8,128)(2,1)}, bf16[160,512...) custom-call(bf16[80,512]{1,0:T(8,128)(2,1)} %get-tuple-element.353.r, ...), custom_call_target="tpu_custom_call" | custom-call | flops 3000000000 | bytes 10000000 | tf_op jit(solution)/shard_map/feed_back/pallas_call | solution.py:719
  260.6 3.0 moe_back.3
  266.3 4.0 collective-permute-done.58.refs_2_
  271.5 19.9 %attend_back.3 = (bf16[128,512]{1,0:T(8,128)(2,1)}, bf16[128,512]{1,0:T(8,128)(2,1)}, bf16[128,512]{1,0:T(8,128)(2,1)}, bf16[128,512]{1,0:T(8,128)(2,1)}, bf16[4...) custom-call(s32[8,128]{1,0:T(8,128)} %get-tuple-element.330.refs_0_,, ...), custom_call_target="tpu_custom_call" | custom-call | flops 99999997952 | bytes 16996352 | tf_op jit(solution)/shard_map/attend_back/pallas_call | solution.py:144
  291.4 8.3 %collective-permute-start.61 = (bf16[4,128,512]{2,1,0:T(8,128)(2,1)}, bf16[4,128,512]{2,1,0:T(8,128)(2,1)S(1)}, u32[]{:S(2)}, u32[]{:S(2)}) collective-permute-start(bf16[4,128,512]{2,1,0:T(8,128)(2,1)} %get-tuple-element.384), channel_id=1, source_target_pairs={{0,1},{1,0},{2,3},{3,2},{4,5},{5,4},{6,7},{7,6},{8,9},{9,8},{10,11... | collective-permute-start | bytes 1572872 | tf_op jit(solution)/shard_map/ppermute | solution.py:1131
  304.8 3.2 collective-permute-start.66
  307.9 4.5 shared_weights.3.refs_0_
  313.6 4.8 expert_weights.3.refs_8_
  319.2 3.1 retreat.3
  329.4 9.3 %feed_back.4 = (bf16[80,512]{1,0:T(8,128)(2,1)}, bf16[80,512]{1,0:T(8,128)(2,1)}, bf16[80,512]{1,0:T(8,128)(2,1)}, bf16[80,512]{1,0:T(8,128)(2,1)}, bf16[160,512...) custom-call(bf16[80,512]{1,0:T(8,128)(2,1)} %get-tuple-element.403.r, ...), custom_call_target="tpu_custom_call" | custom-call | flops 3000000000 | bytes 10000000 | tf_op jit(solution)/shard_map/feed_back/pallas_call | solution.py:719
  347.7 3.0 moe_back.4
  353.4 4.0 collective-permute-done.74.refs_2_
  358.6 22.9 %attend_back.4 = (bf16[128,512]{1,0:T(8,128)(2,1)}, bf16[128,512]{1,0:T(8,128)(2,1)}, bf16[128,512]{1,0:T(8,128)(2,1)}, bf16[128,512]{1,0:T(8,128)(2,1)}, bf16[4...) custom-call(s32[8,128]{1,0:T(8,128)} %get-tuple-element.307.refs_0_,, ...), custom_call_target="tpu_custom_call" | custom-call | flops 99999997952 | bytes 16996352 | tf_op jit(solution)/shard_map/attend_back/pallas_call | solution.py:144
  381.5 5.2 collective-permute-start.77
  391.8 5.3 shared_weights.4.refs_0_
  397.9 3.3 collective-permute-start.82
  401.2 5.6 expert_weights.4.refs_8_
  407.7 3.1 retreat.4
  412.0 3.2 collective-permute-start.85
  421.2 9.4 %feed_back.5 = (bf16[80,512]{1,0:T(8,128)(2,1)}, bf16[80,512]{1,0:T(8,128)(2,1)}, bf16[80,512]{1,0:T(8,128)(2,1)}, bf16[80,512]{1,0:T(8,128)(2,1)}, bf16[160,512...) custom-call(bf16[80,512]{1,0:T(8,128)(2,1)} %get-tuple-element.454.r, ...), custom_call_target="tpu_custom_call" | custom-call | flops 3000000000 | bytes 10000000 | tf_op jit(solution)/shard_map/feed_back/pallas_call | solution.py:719
  432.5 2.7 collective-permute-done.94.refs_10_
  440.9 3.2 collective-permute-done.88.refs_2_
  444.4 4.4 collective-permute-done.89.refs_3_
  448.8 3.6 collective-permute-start.95
  452.5 3.0 moe_back.5
  456.5 11.4 %feed_weights.1 = (bf16[512,2048]{1,0:T(8,128)(2,1)}, bf16[512,512]{1,0:T(8,128)(2,1)}, bf16[512,512]{1,0:T(8,128)(2,1)}, bf16[512,512]{1,0:T(8,128)(2,1)}, bf16[512,512]{1,0:T(8,128)(2,1)}) custom-call(s32[8,128]{1,0:T(8,128)} %get-tuple-element.282.refs_0_.scal, bf16[160,512]{1,0:T(8,128)(2,1)} %get-tuple-element.357.refs_4_.refs_1_, ...), custom_call_target="tpu_custom_call" | custom-call | flops 8000000000 | bytes 20000000 | tf_op jit(solution)/shard_map/feed_weights/pallas_call | solution.py:750
  468.0 2.7 collective-permute-start.103
  471.5 3.1 collective-permute-start.107
  477.7 28.5 %attend_back.5 = (bf16[128,512]{1,0:T(8,128)(2,1)}, bf16[128,512]{1,0:T(8,128)(2,1)}, bf16[128,512]{1,0:T(8,128)(2,1)}, bf16[128,512]{1,0:T(8,128)(2,1)}, bf16[4...) custom-call(s32[8,128]{1,0:T(8,128)} %get-tuple-element.282.refs_0_., ...), custom_call_target="tpu_custom_call" | custom-call | flops 99999997952 | bytes 16996352 | tf_op jit(solution)/shard_map/attend_back/pallas_call | solution.py:144
  512.3 4.8 shared_weights.5
  518.0 5.3 expert_weights.5
  523.3 7.4 %all-to-all-start.1 = ((bf16[16,32,1024]{2,1,0:T(8,128)(2,1)}), bf16[16,32,1024]{2,1,0:T(8,128)(2,1)S(1)}, u32[]{:S(2)}, u32[]{:S(2)}) async-start(bf16[16,32,1024]{2,1,0:T(8,128)(2,1)} %bitcast.40), calls=%async_computation.1 | async-start | bytes 2097152 | tf_op jit(solution)/shard_map/all_to_all | solution.py:1300
  531.9 14.3 %all-to-all-done.1 = bf16[16,32,1024]{2,1,0:T(8,128)(2,1)S(1)} async-done(((bf16[16,32,1024]{2,1,0:T(8,128)(2,1)}), bf16[16,32,1024]{2,1,0:T(8,128)(2,1)S(1)}, u32[]{:S(2)}, u32[]{:S(2)}) %all-to-all-start.1) | async-done | bytes 1048608 | tf_op jit(solution)/shard_map/all_to_all | solution.py:1300
  546.2 9.1 %all-to-all-start = ((bf16[128,4,1152]{2,1,0:T(4,128)(2,1)}), bf16[128,4,1152]{2,1,0:T(4,128)(2,1)S(1)}, u32[]{:S(2)}, u32[]{:S(2)}) async-start(bf16[128,4,1152]{2,1,0:T(4,128)(2,1)} %reshape.32), calls=%async_computation | async-start | bytes 2359296 | tf_op jit(solution)/shard_map/all_to_all | solution.py:1305
  555.3 2.8 fold.1
  563.0 3.1 collective-permute-start.113
  566.8 6.8 %collective-permute-done.115.refs_1_ = bf16[128,512]{1,0:T(8,128)(2,1)S(1)} collective-permute-done((bf16[128,512]{1,0:T(8,128)(2,1)}, bf16[128,512]{1,0:T(8,128)(2,1)S(1)}, u32[]{:S(2)}, u32[]{:S(2)}) %collective-permute-start.115) | collective-permute-done | bytes 131104 | tf_op jit(solution)/shard_map/ppermute | solution.py:1152
  573.6 3.0 collective-permute-done.116.refs_2_
  (489 shorter events, 182.9 us)
Async XLA Ops:
  7.2 578.4 %reduce-scatter.2.cloned.1.call-start = ((), (), s32[]{:S(2)}) async-start(), calls=%async_computation.3 | async-start | bytes 2228224 | tf_op jit(solution)/shard_map/reduce_scatter | solution.py:1264
  7.2 71.3 %collective-permute-start.15 = (bf16[512,2048]{1,0:T(8,128)(2,1)}, bf16[512,2048]{1,0:T(8,128)(2,1)S(1)}, u32[]{:S(2)}, u32[]{:S(2)}) collective-permute-start(bf16[512,2048]{1,0:T(8,128)(2,1)} %bitcast.26), channel_id=1, source_target_pairs={{0,1},{1,0},{2,3},{3,2},{4,5},{5,4},{6,7},{7,6},{8,9},{9,8},{10,11... | collective-permute-start | bytes 6291464 | tf_op jit(solution)/shard_map/ppermute | solution.py:1131
  8.7 69.8 %collective-permute-start.16 = (bf16[2048,512]{1,0:T(8,128)(2,1)}, bf16[2048,512]{1,0:T(8,128)(2,1)}, u32[]{:S(2)}, u32[]{:S(2)}) collective-permute-start(bf16[2048,512]{1,0:T(8,128)(2,1)} %bitcast.33), channel_id=1, source_target_pairs={{0,1},{1,0},{2,3},{3,2},{4,5},{5,4},{6,7},{7,6},{8,9},{9,8},{10,11... | collective-permute-start | bytes 6291464 | tf_op jit(solution)/shard_map/ppermute | solution.py:1131
  10.7 7.9 %collective-permute-start = (bf16[144,512]{1,0:T(8,128)(2,1)}, bf16[144,512]{1,0:T(8,128)(2,1)S(1)}, u32[]{:S(2)}, u32[]{:S(2)}) collective-permute-start(bf16[144,512]{1,0:T(8,128)(2,1)} %get-tuple-element.280.refs_1_.refs_2_), channel_id=1, source_target_pairs={{0,2},{1,3},{2,4},{3,5},{4,6},{5,7},{6,0},{7,1},{8,10},{9,11},{10,... | collective-permute-start | bytes 442376 | tf_op jit(solution)/shard_map/ppermute | solution.py:1136
  12.4 10.2 %collective-permute-start.1 = (bf16[144,512]{1,0:T(8,128)(2,1)}, bf16[144,512]{1,0:T(8,128)(2,1)S(1)}, u32[]{:S(2)}, u32[]{:S(2)}) collective-permute-start(bf16[144,512]{1,0:T(8,128)(2,1)} %get-tuple-element.280.refs_1_.refs_2_), channel_id=1, source_target_pairs={{0,4},{1,5},{2,6},{3,7},{4,0},{5,1},{6,2},{7,3},{8,12},{9,13},{10,... | collective-permute-start | bytes 442376 | tf_op jit(solution)/shard_map/ppermute | solution.py:1136
  15.7 8.2 %collective-permute-start.2 = (bf16[144,512]{1,0:T(8,128)(2,1)}, bf16[144,512]{1,0:T(8,128)(2,1)S(1)}, u32[]{:S(2)}, u32[]{:S(2)}) collective-permute-start(bf16[144,512]{1,0:T(8,128)(2,1)} %get-tuple-element.280.refs_1_.refs_2_), channel_id=1, source_target_pairs={{0,6},{1,7},{2,0},{3,1},{4,2},{5,3},{6,4},{7,5},{8,14},{9,15},{10,... | collective-permute-start | bytes 442376 | tf_op jit(solution)/shard_map/ppermute | solution.py:1136
  18.6 9.4 %collective-permute-start.3 = (bf16[144,512]{1,0:T(8,128)(2,1)}, bf16[144,512]{1,0:T(8,128)(2,1)S(1)}, u32[]{:S(2)}, u32[]{:S(2)}) collective-permute-start(bf16[144,512]{1,0:T(8,128)(2,1)} %get-tuple-element.280.refs_1_.refs_2_), channel_id=1, source_target_pairs={{0,1},{1,0},{2,3},{3,2},{4,5},{5,4},{6,7},{7,6},{8,9},{9,8},{10,11... | collective-permute-start | bytes 442376 | tf_op jit(solution)/shard_map/ppermute | solution.py:1131
  22.6 9.7 %collective-permute-start.7 = (bf16[512,512]{1,0:T(8,128)(2,1)}, bf16[512,512]{1,0:T(8,128)(2,1)S(1)}, u32[]{:S(2)}, u32[]{:S(2)}) collective-permute-start(bf16[512,512]{1,0:T(8,128)(2,1)} %bitcast.65), channel_id=1, source_target_pairs={{0,1},{1,0},{2,3},{3,2},{4,5},{5,4},{6,7},{7,6},{8,9},{9,8},{10,11... | collective-permute-start | bytes 1572872 | tf_op jit(solution)/shard_map/ppermute | solution.py:1131
  24.5 7.7 %collective-permute-start.8 = (bf16[512,512]{1,0:T(8,128)(2,1)}, bf16[512,512]{1,0:T(8,128)(2,1)S(1)}, u32[]{:S(2)}, u32[]{:S(2)}) collective-permute-start(bf16[512,512]{1,0:T(8,128)(2,1)} %bitcast.72), channel_id=1, source_target_pairs={{0,1},{1,0},{2,3},{3,2},{4,5},{5,4},{6,7},{7,6},{8,9},{9,8},{10,11... | collective-permute-start | bytes 1572872 | tf_op jit(solution)/shard_map/ppermute | solution.py:1131
  53.4 15.5 %collective-permute-start.9 = (bf16[128,512]{1,0:T(8,128)(2,1)}, bf16[128,512]{1,0:T(8,128)(2,1)S(1)}, u32[]{:S(2)}, u32[]{:S(2)}) collective-permute-start(bf16[128,512]{1,0:T(8,128)(2,1)} %get-tuple-element.289), channel_id=1, source_target_pairs={{0,2},{1,3},{2,4},{3,5},{4,6},{5,7},{6,0},{7,1},{8,10},{9,11},{10,... | collective-permute-start | bytes 393224 | tf_op jit(solution)/shard_map/ppermute | solution.py:1136
  53.8 15.1 %collective-permute-start.10 = (bf16[128,512]{1,0:T(8,128)(2,1)}, bf16[128,512]{1,0:T(8,128)(2,1)S(1)}, u32[]{:S(2)}, u32[]{:S(2)}) collective-permute-start(bf16[128,512]{1,0:T(8,128)(2,1)} %get-tuple-element.292), channel_id=1, source_target_pairs={{0,4},{1,5},{2,6},{3,7},{4,0},{5,1},{6,2},{7,3},{8,12},{9,13},{10,... | collective-permute-start | bytes 393224 | tf_op jit(solution)/shard_map/ppermute | solution.py:1136
  55.0 13.9 %collective-permute-start.11 = (bf16[128,512]{1,0:T(8,128)(2,1)}, bf16[128,512]{1,0:T(8,128)(2,1)S(1)}, u32[]{:S(2)}, u32[]{:S(2)}) collective-permute-start(bf16[128,512]{1,0:T(8,128)(2,1)} %get-tuple-element.293), channel_id=1, source_target_pairs={{0,6},{1,7},{2,0},{3,1},{4,2},{5,3},{6,4},{7,5},{8,14},{9,15},{10,... | collective-permute-start | bytes 393224 | tf_op jit(solution)/shard_map/ppermute | solution.py:1136
  99.7 10.4 %collective-permute-start.21 = (bf16[128,512]{1,0:T(8,128)(2,1)}, bf16[128,512]{1,0:T(8,128)(2,1)S(1)}, u32[]{:S(2)}, u32[]{:S(2)}) collective-permute-start(bf16[128,512]{1,0:T(8,128)(2,1)} %get-tuple-element.308.refs_1_), channel_id=1, source_target_pairs={{0,4},{1,5},{2,6},{3,7},{4,0},{5,1},{6,2},{7,3},{8,12},{9,13},{10,... | collective-permute-start | bytes 393224 | tf_op jit(solution)/shard_map/ppermute | solution.py:1136
  101.5 8.7 %collective-permute-start.22 = (bf16[128,512]{1,0:T(8,128)(2,1)}, bf16[128,512]{1,0:T(8,128)(2,1)S(1)}, u32[]{:S(2)}, u32[]{:S(2)}) collective-permute-start(bf16[128,512]{1,0:T(8,128)(2,1)} %get-tuple-element.308.refs_1_), channel_id=1, source_target_pairs={{0,6},{1,7},{2,0},{3,1},{4,2},{5,3},{6,4},{7,5},{8,14},{9,15},{10,... | collective-permute-start | bytes 393224 | tf_op jit(solution)/shard_map/ppermute | solution.py:1136
  103.4 7.7 %collective-permute-start.23 = (bf16[128,512]{1,0:T(8,128)(2,1)}, bf16[128,512]{1,0:T(8,128)(2,1)S(1)}, u32[]{:S(2)}, u32[]{:S(2)}) collective-permute-start(bf16[128,512]{1,0:T(8,128)(2,1)} %get-tuple-element.308.refs_1_), channel_id=1, source_target_pairs={{0,1},{1,0},{2,3},{3,2},{4,5},{5,4},{6,7},{7,6},{8,9},{9,8},{10,11... | collective-permute-start | bytes 393224 | tf_op jit(solution)/shard_map/ppermute | solution.py:1131
  129.2 9.3 %collective-permute-start.28 = (bf16[128,512]{1,0:T(8,128)(2,1)}, bf16[128,512]{1,0:T(8,128)(2,1)S(1)}, u32[]{:S(2)}, u32[]{:S(2)}) collective-permute-start(bf16[128,512]{1,0:T(8,128)(2,1)} %get-tuple-element.315), channel_id=1, source_target_pairs={{0,4},{1,5},{2,6},{3,7},{4,0},{5,1},{6,2},{7,3},{8,12},{9,13},{10,... | collective-permute-start | bytes 393224 | tf_op jit(solution)/shard_map/ppermute | solution.py:1136
  141.8 7.4 %collective-permute-start.31 = (bf16[80,512]{1,0:T(8,128)(2,1)}, bf16[80,512]{1,0:T(8,128)(2,1)S(1)}, u32[]{:S(2)}, u32[]{:S(2)}) collective-permute-start(bf16[80,512]{1,0:T(8,128)(2,1)} %get-tuple-element.323), channel_id=1, source_target_pairs={{0,4},{1,5},{2,6},{3,7},{4,0},{5,1},{6,2},{7,3},{8,12},{9,13},{10,... | collective-permute-start | bytes 245768 | tf_op jit(solution)/shard_map/ppermute | solution.py:1136
  167.5 7.8 %collective-permute-start.36 = (bf16[128,512]{1,0:T(8,128)(2,1)}, bf16[128,512]{1,0:T(8,128)(2,1)S(1)}, u32[]{:S(2)}, u32[]{:S(2)}) collective-permute-start(bf16[128,512]{1,0:T(8,128)(2,1)} %get-tuple-element.331.refs_1_), channel_id=1, source_target_pairs={{0,2},{1,3},{2,4},{3,5},{4,6},{5,7},{6,0},{7,1},{8,10},{9,11},{10,... | collective-permute-start | bytes 393224 | tf_op jit(solution)/shard_map/ppermute | solution.py:1136
  168.0 11.2 %collective-permute-start.37 = (bf16[128,512]{1,0:T(8,128)(2,1)}, bf16[128,512]{1,0:T(8,128)(2,1)S(1)}, u32[]{:S(2)}, u32[]{:S(2)}) collective-permute-start(bf16[128,512]{1,0:T(8,128)(2,1)} %get-tuple-element.331.refs_1_), channel_id=1, source_target_pairs={{0,4},{1,5},{2,6},{3,7},{4,0},{5,1},{6,2},{7,3},{8,12},{9,13},{10,... | collective-permute-start | bytes 393224 | tf_op jit(solution)/shard_map/ppermute | solution.py:1136
  170.2 9.0 %collective-permute-start.38 = (bf16[128,512]{1,0:T(8,128)(2,1)}, bf16[128,512]{1,0:T(8,128)(2,1)S(1)}, u32[]{:S(2)}, u32[]{:S(2)}) collective-permute-start(bf16[128,512]{1,0:T(8,128)(2,1)} %get-tuple-element.331.refs_1_), channel_id=1, source_target_pairs={{0,6},{1,7},{2,0},{3,1},{4,2},{5,3},{6,4},{7,5},{8,14},{9,15},{10,... | collective-permute-start | bytes 393224 | tf_op jit(solution)/shard_map/ppermute | solution.py:1136
  170.5 9.5 %collective-permute-start.39 = (bf16[128,512]{1,0:T(8,128)(2,1)}, bf16[128,512]{1,0:T(8,128)(2,1)S(1)}, u32[]{:S(2)}, u32[]{:S(2)}) collective-permute-start(bf16[128,512]{1,0:T(8,128)(2,1)} %get-tuple-element.331.refs_1_), channel_id=1, source_target_pairs={{0,1},{1,0},{2,3},{3,2},{4,5},{5,4},{6,7},{7,6},{8,9},{9,8},{10,11... | collective-permute-start | bytes 393224 | tf_op jit(solution)/shard_map/ppermute | solution.py:1131
  196.2 9.4 %collective-permute-start.44 = (bf16[128,512]{1,0:T(8,128)(2,1)}, bf16[128,512]{1,0:T(8,128)(2,1)S(1)}, u32[]{:S(2)}, u32[]{:S(2)}) collective-permute-start(bf16[128,512]{1,0:T(8,128)(2,1)} %get-tuple-element.338), channel_id=1, source_target_pairs={{0,4},{1,5},{2,6},{3,7},{4,0},{5,1},{6,2},{7,3},{8,12},{9,13},{10,... | collective-permute-start | bytes 393224 | tf_op jit(solution)/shard_map/ppermute | solution.py:1136
  209.5 7.1 %collective-permute-start.47 = (bf16[80,512]{1,0:T(8,128)(2,1)}, bf16[80,512]{1,0:T(8,128)(2,1)S(1)}, u32[]{:S(2)}, u32[]{:S(2)}) collective-permute-start(bf16[80,512]{1,0:T(8,128)(2,1)} %get-tuple-element.346), channel_id=1, source_target_pairs={{0,4},{1,5},{2,6},{3,7},{4,0},{5,1},{6,2},{7,3},{8,12},{9,13},{10,... | collective-permute-start | bytes 245768 | tf_op jit(solution)/shard_map/ppermute | solution.py:1136
  263.6 6.6 %collective-permute-start.59 = (bf16[128,512]{1,0:T(8,128)(2,1)}, bf16[128,512]{1,0:T(8,128)(2,1)S(1)}, u32[]{:S(2)}, u32[]{:S(2)}) collective-permute-start(bf16[128,512]{1,0:T(8,128)(2,1)} %get-tuple-element.367.refs_1_), channel_id=1, source_target_pairs={{0,4},{1,5},{2,6},{3,7},{4,0},{5,1},{6,2},{7,3},{8,12},{9,13},{10,... | collective-permute-start | bytes 393224 | tf_op jit(solution)/shard_map/ppermute | solution.py:1136
  291.4 10.0 %collective-permute-start.61 = (bf16[4,128,512]{2,1,0:T(8,128)(2,1)}, bf16[4,128,512]{2,1,0:T(8,128)(2,1)S(1)}, u32[]{:S(2)}, u32[]{:S(2)}) collective-permute-start(bf16[4,128,512]{2,1,0:T(8,128)(2,1)} %get-tuple-element.384), channel_id=1, source_target_pairs={{0,1},{1,0},{2,3},{3,2},{4,5},{5,4},{6,7},{7,6},{8,9},{9,8},{10,11... | collective-permute-start | bytes 1572872 | tf_op jit(solution)/shard_map/ppermute | solution.py:1131
  299.7 12.8 %collective-permute-start.63 = (bf16[512,512]{1,0:T(8,128)(2,1)S(1)}, bf16[512,512]{1,0:T(8,128)(2,1)S(1)}, u32[]{:S(2)}, u32[]{:S(2)}) collective-permute-start(bf16[512,512]{1,0:T(8,128)(2,1)S(1)} %copy-done.69), channel_id=1, source_target_pairs={{0,1},{1,0},{2,3},{3,2},{4,5},{5,4},{6,7},{7,6},{8,9},{9,8},{10,11... | collective-permute-start | bytes 1572872 | tf_op jit(solution)/shard_map/ppermute | solution.py:1131
  299.8 12.8 %collective-permute-start.64 = (bf16[512,512]{1,0:T(8,128)(2,1)}, bf16[512,512]{1,0:T(8,128)(2,1)S(1)}, u32[]{:S(2)}, u32[]{:S(2)}) collective-permute-start(bf16[512,512]{1,0:T(8,128)(2,1)} %get-tuple-element.394), channel_id=1, source_target_pairs={{0,1},{1,0},{2,3},{3,2},{4,5},{5,4},{6,7},{7,6},{8,9},{9,8},{10,11... | collective-permute-start | bytes 1572872 | tf_op jit(solution)/shard_map/ppermute | solution.py:1131
  300.2 12.4 %collective-permute-start.65 = (bf16[512,512]{1,0:T(8,128)(2,1)}, bf16[512,512]{1,0:T(8,128)(2,1)S(1)}, u32[]{:S(2)}, u32[]{:S(2)}) collective-permute-start(bf16[512,512]{1,0:T(8,128)(2,1)} %get-tuple-element.396), channel_id=1, source_target_pairs={{0,1},{1,0},{2,3},{3,2},{4,5},{5,4},{6,7},{7,6},{8,9},{9,8},{10,11... | collective-permute-start | bytes 1572872 | tf_op jit(solution)/shard_map/ppermute | solution.py:1131
  304.4 14.1 %collective-permute-start.62 = (bf16[128,512]{1,0:T(8,128)(2,1)}, bf16[128,512]{1,0:T(8,128)(2,1)S(1)}, u32[]{:S(2)}, u32[]{:S(2)}) collective-permute-start(bf16[128,512]{1,0:T(8,128)(2,1)} %get-tuple-element.390), channel_id=1, source_target_pairs={{0,2},{1,3},{2,4},{3,5},{4,6},{5,7},{6,0},{7,1},{8,10},{9,11},{10,... | collective-permute-start | bytes 393224 | tf_op jit(solution)/shard_map/ppermute | solution.py:1136
  304.8 13.7 %collective-permute-start.66 = (bf16[128,512]{1,0:T(8,128)(2,1)}, bf16[128,512]{1,0:T(8,128)(2,1)S(1)}, u32[]{:S(2)}, u32[]{:S(2)}) collective-permute-start(bf16[128,512]{1,0:T(8,128)(2,1)} %get-tuple-element.398), channel_id=1, source_target_pairs={{0,4},{1,5},{2,6},{3,7},{4,0},{5,1},{6,2},{7,3},{8,12},{9,13},{10,... | collective-permute-start | bytes 393224 | tf_op jit(solution)/shard_map/ppermute | solution.py:1136
  381.5 7.0 %collective-permute-start.77 = (bf16[4,128,512]{2,1,0:T(8,128)(2,1)}, bf16[4,128,512]{2,1,0:T(8,128)(2,1)S(1)}, u32[]{:S(2)}, u32[]{:S(2)}) collective-permute-start(bf16[4,128,512]{2,1,0:T(8,128)(2,1)} %get-tuple-element.434), channel_id=1, source_target_pairs={{0,1},{1,0},{2,3},{3,2},{4,5},{5,4},{6,7},{7,6},{8,9},{9,8},{10,11... | collective-permute-start | bytes 1572872 | tf_op jit(solution)/shard_map/ppermute | solution.py:1131
  386.7 10.3 %collective-permute-start.79 = (bf16[512,512]{1,0:T(8,128)(2,1)S(1)}, bf16[512,512]{1,0:T(8,128)(2,1)S(1)}, u32[]{:S(2)}, u32[]{:S(2)}) collective-permute-start(bf16[512,512]{1,0:T(8,128)(2,1)S(1)} %copy-done.68), channel_id=1, source_target_pairs={{0,1},{1,0},{2,3},{3,2},{4,5},{5,4},{6,7},{7,6},{8,9},{9,8},{10,11... | collective-permute-start | bytes 1572872 | tf_op jit(solution)/shard_map/ppermute | solution.py:1131
  386.8 10.9 %collective-permute-start.80 = (bf16[512,512]{1,0:T(8,128)(2,1)}, bf16[512,512]{1,0:T(8,128)(2,1)S(1)}, u32[]{:S(2)}, u32[]{:S(2)}) collective-permute-start(bf16[512,512]{1,0:T(8,128)(2,1)} %get-tuple-element.445), channel_id=1, source_target_pairs={{0,1},{1,0},{2,3},{3,2},{4,5},{5,4},{6,7},{7,6},{8,9},{9,8},{10,11... | collective-permute-start | bytes 1572872 | tf_op jit(solution)/shard_map/ppermute | solution.py:1131
  387.2 10.7 %collective-permute-start.81 = (bf16[512,512]{1,0:T(8,128)(2,1)}, bf16[512,512]{1,0:T(8,128)(2,1)}, u32[]{:S(2)}, u32[]{:S(2)}) collective-permute-start(bf16[512,512]{1,0:T(8,128)(2,1)} %get-tuple-element.447), channel_id=1, source_target_pairs={{0,1},{1,0},{2,3},{3,2},{4,5},{5,4},{6,7},{7,6},{8,9},{9,8},{10,11... | collective-permute-start | bytes 1572872 | tf_op jit(solution)/shard_map/ppermute | solution.py:1131
  387.3 44.6 %collective-permute-start.96 = (bf16[160,2048]{1,0:T(8,128)(2,1)S(1)}, bf16[160,2048]{1,0:T(8,128)(2,1)S(1)}, u32[]{:S(2)}, u32[]{:S(2)}) collective-permute-start(bf16[160,2048]{1,0:T(8,128)(2,1)S(1)} %copy-done.60), channel_id=1, source_target_pairs={{0,1},{1,0},{2,3},{3,2},{4,5},{5,4},{6,7},{7,6},{8,9},{9,8},{10,11... | collective-permute-start | bytes 1966088 | tf_op jit(solution)/shard_map/ppermute | solution.py:1131
  391.4 9.8 %collective-permute-start.78 = (bf16[128,512]{1,0:T(8,128)(2,1)}, bf16[128,512]{1,0:T(8,128)(2,1)S(1)}, u32[]{:S(2)}, u32[]{:S(2)}) collective-permute-start(bf16[128,512]{1,0:T(8,128)(2,1)} %get-tuple-element.440), channel_id=1, source_target_pairs={{0,2},{1,3},{2,4},{3,5},{4,6},{5,7},{6,0},{7,1},{8,10},{9,11},{10,... | collective-permute-start | bytes 393224 | tf_op jit(solution)/shard_map/ppermute | solution.py:1136
  397.0 18.2 %collective-permute-start.92 = (bf16[160,512]{1,0:T(8,128)(2,1)S(1)}, bf16[160,512]{1,0:T(8,128)(2,1)S(1)}, u32[]{:S(2)}, u32[]{:S(2)}) collective-permute-start(bf16[160,512]{1,0:T(8,128)(2,1)S(1)} %copy-done.77), channel_id=1, source_target_pairs={{0,1},{1,0},{2,3},{3,2},{4,5},{5,4},{6,7},{7,6},{8,9},{9,8},{10,11... | collective-permute-start | bytes 491528 | tf_op jit(solution)/shard_map/ppermute | solution.py:1131
  397.8 34.5 %collective-permute-start.99 = (bf16[160,2048]{1,0:T(8,128)(2,1)S(1)}, bf16[160,2048]{1,0:T(8,128)(2,1)}, u32[]{:S(2)}, u32[]{:S(2)}) collective-permute-start(bf16[160,2048]{1,0:T(8,128)(2,1)S(1)} %copy-done.59), channel_id=1, source_target_pairs={{0,1},{1,0},{2,3},{3,2},{4,5},{5,4},{6,7},{7,6},{8,9},{9,8},{10,11... | collective-permute-start | bytes 1966088 | tf_op jit(solution)/shard_map/ppermute | solution.py:1131
  397.9 8.9 %collective-permute-start.82 = (bf16[128,512]{1,0:T(8,128)(2,1)}, bf16[128,512]{1,0:T(8,128)(2,1)S(1)}, u32[]{:S(2)}, u32[]{:S(2)}) collective-permute-start(bf16[128,512]{1,0:T(8,128)(2,1)} %get-tuple-element.450), channel_id=1, source_target_pairs={{0,4},{1,5},{2,6},{3,7},{4,0},{5,1},{6,2},{7,3},{8,12},{9,13},{10,... | collective-permute-start | bytes 393224 | tf_op jit(solution)/shard_map/ppermute | solution.py:1136
  412.0 6.9 %collective-permute-start.85 = (bf16[80,512]{1,0:T(8,128)(2,1)}, bf16[80,512]{1,0:T(8,128)(2,1)S(1)}, u32[]{:S(2)}, u32[]{:S(2)}) collective-permute-start(bf16[80,512]{1,0:T(8,128)(2,1)} %get-tuple-element.456), channel_id=1, source_target_pairs={{0,4},{1,5},{2,6},{3,7},{4,0},{5,1},{6,2},{7,3},{8,12},{9,13},{10,... | collective-permute-start | bytes 245768 | tf_op jit(solution)/shard_map/ppermute | solution.py:1136
  416.1 14.6 %collective-permute-start.91 = (bf16[160,512]{1,0:T(8,128)(2,1)S(1)}, bf16[160,512]{1,0:T(8,128)(2,1)S(1)}, u32[]{:S(2)}, u32[]{:S(2)}) collective-permute-start(bf16[160,512]{1,0:T(8,128)(2,1)S(1)} %copy-done.78), channel_id=1, source_target_pairs={{0,1},{1,0},{2,3},{3,2},{4,5},{5,4},{6,7},{7,6},{8,9},{9,8},{10,11... | collective-permute-start | bytes 491528 | tf_op jit(solution)/shard_map/ppermute | solution.py:1131
  418.9 12.2 %collective-permute-start.90 = (bf16[160,512]{1,0:T(8,128)(2,1)}, bf16[160,512]{1,0:T(8,128)(2,1)S(1)}, u32[]{:S(2)}, u32[]{:S(2)}) collective-permute-start(bf16[160,512]{1,0:T(8,128)(2,1)} %get-tuple-element.358.refs_5_), channel_id=1, source_target_pairs={{0,1},{1,0},{2,3},{3,2},{4,5},{5,4},{6,7},{7,6},{8,9},{9,8},{10,11... | collective-permute-start | bytes 491528 | tf_op jit(solution)/shard_map/ppermute | solution.py:1131
  420.6 10.8 %collective-permute-start.93 = (bf16[160,512]{1,0:T(8,128)(2,1)}, bf16[160,512]{1,0:T(8,128)(2,1)}, u32[]{:S(2)}, u32[]{:S(2)}) collective-permute-start(bf16[160,512]{1,0:T(8,128)(2,1)} %get-tuple-element.470), channel_id=1, source_target_pairs={{0,1},{1,0},{2,3},{3,2},{4,5},{5,4},{6,7},{7,6},{8,9},{9,8},{10,11... | collective-permute-start | bytes 491528 | tf_op jit(solution)/shard_map/ppermute | solution.py:1131
  430.7 24.8 %collective-permute-start.100 = (bf16[160,2048]{1,0:T(8,128)(2,1)S(1)}, bf16[160,2048]{1,0:T(8,128)(2,1)}, u32[]{:S(2)}, u32[]{:S(2)}) collective-permute-start(bf16[160,2048]{1,0:T(8,128)(2,1)S(1)} %copy-done.62), channel_id=1, source_target_pairs={{0,1},{1,0},{2,3},{3,2},{4,5},{5,4},{6,7},{7,6},{8,9},{9,8},{10,11... | collective-permute-start | bytes 1966088 | tf_op jit(solution)/shard_map/ppermute | solution.py:1131
  431.1 24.4 %collective-permute-start.97 = (bf16[160,2048]{1,0:T(8,128)(2,1)S(1)}, bf16[160,2048]{1,0:T(8,128)(2,1)}, u32[]{:S(2)}, u32[]{:S(2)}) collective-permute-start(bf16[160,2048]{1,0:T(8,128)(2,1)S(1)} %copy-done.61), channel_id=1, source_target_pairs={{0,1},{1,0},{2,3},{3,2},{4,5},{5,4},{6,7},{7,6},{8,9},{9,8},{10,11... | collective-permute-start | bytes 1966088 | tf_op jit(solution)/shard_map/ppermute | solution.py:1131
  431.8 23.8 %collective-permute-start.101 = (bf16[160,2048]{1,0:T(8,128)(2,1)}, bf16[160,2048]{1,0:T(8,128)(2,1)S(1)}, u32[]{:S(2)}, u32[]{:S(2)}) collective-permute-start(bf16[160,2048]{1,0:T(8,128)(2,1)} %get-tuple-element.486), channel_id=1, source_target_pairs={{0,1},{1,0},{2,3},{3,2},{4,5},{5,4},{6,7},{7,6},{8,9},{9,8},{10,11... | collective-permute-start | bytes 1966088 | tf_op jit(solution)/shard_map/ppermute | solution.py:1131
  431.9 23.6 %collective-permute-start.98 = (bf16[160,2048]{1,0:T(8,128)(2,1)}, bf16[160,2048]{1,0:T(8,128)(2,1)}, u32[]{:S(2)}, u32[]{:S(2)}) collective-permute-start(bf16[160,2048]{1,0:T(8,128)(2,1)} %get-tuple-element.480), channel_id=1, source_target_pairs={{0,1},{1,0},{2,3},{3,2},{4,5},{5,4},{6,7},{7,6},{8,9},{9,8},{10,11... | collective-permute-start | bytes 1966088 | tf_op jit(solution)/shard_map/ppermute | solution.py:1131
  448.8 6.7 %collective-permute-start.95 = (bf16[160,512]{1,0:T(8,128)(2,1)}, bf16[160,512]{1,0:T(8,128)(2,1)S(1)}, u32[]{:S(2)}, u32[]{:S(2)}) collective-permute-start(bf16[160,512]{1,0:T(8,128)(2,1)} %get-tuple-element.474), channel_id=1, source_target_pairs={{0,1},{1,0},{2,3},{3,2},{4,5},{5,4},{6,7},{7,6},{8,9},{9,8},{10,11... | collective-permute-start | bytes 491528 | tf_op jit(solution)/shard_map/ppermute | solution.py:1131
  467.9 6.8 %collective-permute-start.102 = (bf16[128,512]{1,0:T(8,128)(2,1)S(1)}, bf16[128,512]{1,0:T(8,128)(2,1)S(1)}, u32[]{:S(2)}, u32[]{:S(2)}) collective-permute-start(bf16[128,512]{1,0:T(8,128)(2,1)S(1)} %copy-done.93), channel_id=1, source_target_pairs={{0,2},{1,3},{2,4},{3,5},{4,6},{5,7},{6,0},{7,1},{8,10},{9,11},{10,... | collective-permute-start | bytes 393224 | tf_op jit(solution)/shard_map/ppermute | solution.py:1136
  468.0 8.9 %collective-permute-start.103 = (bf16[128,512]{1,0:T(8,128)(2,1)S(1)}, bf16[128,512]{1,0:T(8,128)(2,1)S(1)}, u32[]{:S(2)}, u32[]{:S(2)}) collective-permute-start(bf16[128,512]{1,0:T(8,128)(2,1)S(1)} %copy-done.93), channel_id=1, source_target_pairs={{0,4},{1,5},{2,6},{3,7},{4,0},{5,1},{6,2},{7,3},{8,12},{9,13},{10,... | collective-permute-start | bytes 393224 | tf_op jit(solution)/shard_map/ppermute | solution.py:1136
  470.8 36.0 %collective-permute-start.106 = (bf16[512,512]{1,0:T(8,128)(2,1)}, bf16[512,512]{1,0:T(8,128)(2,1)S(1)}, u32[]{:S(2)}, u32[]{:S(2)}) collective-permute-start(bf16[512,512]{1,0:T(8,128)(2,1)} %get-tuple-element.510), channel_id=1, source_target_pairs={{0,8},{8,16},{16,24},{24,0},{32,40},{40,48},{48,56},{56,32},{64,72... | collective-permute-start | bytes 1572872 | tf_op jit(solution)/shard_map/ppermute | solution.py:1156
  471.5 35.3 %collective-permute-start.107 = (bf16[512,512]{1,0:T(8,128)(2,1)}, bf16[512,512]{1,0:T(8,128)(2,1)S(1)}, u32[]{:S(2)}, u32[]{:S(2)}) collective-permute-start(bf16[512,512]{1,0:T(8,128)(2,1)} %get-tuple-element.511), channel_id=1, source_target_pairs={{0,16},{8,24},{16,0},{24,8},{32,48},{40,56},{48,32},{56,40},{64,80... | collective-permute-start | bytes 1572872 | tf_op jit(solution)/shard_map/ppermute | solution.py:1156
  474.7 32.8 %collective-permute-start.108 = (bf16[512,512]{1,0:T(8,128)(2,1)S(1)}, bf16[512,512]{1,0:T(8,128)(2,1)S(1)}, u32[]{:S(2)}, u32[]{:S(2)}) collective-permute-start(bf16[512,512]{1,0:T(8,128)(2,1)S(1)} %copy-done.70), channel_id=1, source_target_pairs={{0,24},{8,0},{16,8},{24,16},{32,56},{40,32},{48,40},{56,48},{64,88... | collective-permute-start | bytes 1572872 | tf_op jit(solution)/shard_map/ppermute | solution.py:1156
  506.3 10.9 %collective-permute-start.110 = (bf16[512,512]{1,0:T(8,128)(2,1)S(1)}, bf16[512,512]{1,0:T(8,128)(2,1)S(1)}, u32[]{:S(2)}, u32[]{:S(2)}) collective-permute-start(bf16[512,512]{1,0:T(8,128)(2,1)S(1)} %copy-done.65), channel_id=1, source_target_pairs={{0,1},{1,0},{2,3},{3,2},{4,5},{5,4},{6,7},{7,6},{8,9},{9,8},{10,11... | collective-permute-start | bytes 1572872 | tf_op jit(solution)/shard_map/ppermute | solution.py:1131
  506.8 10.4 %collective-permute-start.111 = (bf16[512,512]{1,0:T(8,128)(2,1)}, bf16[512,512]{1,0:T(8,128)(2,1)}, u32[]{:S(2)}, u32[]{:S(2)}) collective-permute-start(bf16[512,512]{1,0:T(8,128)(2,1)} %get-tuple-element.525), channel_id=1, source_target_pairs={{0,1},{1,0},{2,3},{3,2},{4,5},{5,4},{6,7},{7,6},{8,9},{9,8},{10,11... | collective-permute-start | bytes 1572872 | tf_op jit(solution)/shard_map/ppermute | solution.py:1131
  506.9 10.3 %collective-permute-start.112 = (bf16[512,512]{1,0:T(8,128)(2,1)}, bf16[512,512]{1,0:T(8,128)(2,1)}, u32[]{:S(2)}, u32[]{:S(2)}) collective-permute-start(bf16[512,512]{1,0:T(8,128)(2,1)} %get-tuple-element.527), channel_id=1, source_target_pairs={{0,1},{1,0},{2,3},{3,2},{4,5},{5,4},{6,7},{7,6},{8,9},{9,8},{10,11... | collective-permute-start | bytes 1572872 | tf_op jit(solution)/shard_map/ppermute | solution.py:1131
  511.4 11.9 %collective-permute-start.109 = (bf16[128,512]{1,0:T(8,128)(2,1)}, bf16[128,512]{1,0:T(8,128)(2,1)S(1)}, u32[]{:S(2)}, u32[]{:S(2)}) collective-permute-start(bf16[128,512]{1,0:T(8,128)(2,1)} %get-tuple-element.519), channel_id=1, source_target_pairs={{0,2},{1,3},{2,4},{3,5},{4,6},{5,7},{6,0},{7,1},{8,10},{9,11},{10,... | collective-permute-start | bytes 393224 | tf_op jit(solution)/shard_map/ppermute | solution.py:1136
  523.3 22.9 %all-to-all-start.1 = ((bf16[16,32,1024]{2,1,0:T(8,128)(2,1)}), bf16[16,32,1024]{2,1,0:T(8,128)(2,1)S(1)}, u32[]{:S(2)}, u32[]{:S(2)}) async-start(bf16[16,32,1024]{2,1,0:T(8,128)(2,1)} %bitcast.40), calls=%async_computation.1 | async-start | bytes 2097152 | tf_op jit(solution)/shard_map/all_to_all | solution.py:1300
  546.2 36.9 %all-to-all-start = ((bf16[128,4,1152]{2,1,0:T(4,128)(2,1)}), bf16[128,4,1152]{2,1,0:T(4,128)(2,1)S(1)}, u32[]{:S(2)}, u32[]{:S(2)}) async-start(bf16[128,4,1152]{2,1,0:T(4,128)(2,1)} %reshape.32), calls=%async_computation | async-start | bytes 2359296 | tf_op jit(solution)/shard_map/all_to_all | solution.py:1305
  558.1 15.5 %collective-permute-start.115 = (bf16[128,512]{1,0:T(8,128)(2,1)}, bf16[128,512]{1,0:T(8,128)(2,1)S(1)}, u32[]{:S(2)}, u32[]{:S(2)}) collective-permute-start(bf16[128,512]{1,0:T(8,128)(2,1)} %get-tuple-element.542), channel_id=1, source_target_pairs={{0,32},{8,40},{16,48},{24,56},{32,64},{40,72},{48,80},{56,88},{64,... | collective-permute-start | bytes 393224 | tf_op jit(solution)/shard_map/ppermute | solution.py:1152
  559.5 17.1 %collective-permute-start.116 = (bf16[128,512]{1,0:T(8,128)(2,1)}, bf16[128,512]{1,0:T(8,128)(2,1)S(1)}, u32[]{:S(2)}, u32[]{:S(2)}) collective-permute-start(bf16[128,512]{1,0:T(8,128)(2,1)} %get-tuple-element.543), channel_id=1, source_target_pairs={{0,64},{8,72},{16,80},{24,88},{32,96},{40,104},{48,112},{56,120},{... | collective-permute-start | bytes 393224 | tf_op jit(solution)/shard_map/ppermute | solution.py:1152
  561.9 14.7 %collective-permute-start.117 = (bf16[128,512]{1,0:T(8,128)(2,1)}, bf16[128,512]{1,0:T(8,128)(2,1)S(1)}, u32[]{:S(2)}, u32[]{:S(2)}) collective-permute-start(bf16[128,512]{1,0:T(8,128)(2,1)} %get-tuple-element.544), channel_id=1, source_target_pairs={{0,96},{8,104},{16,112},{24,120},{32,0},{40,8},{48,16},{56,24},{64... | collective-permute-start | bytes 393224 | tf_op jit(solution)/shard_map/ppermute | solution.py:1152
  563.0 16.1 %collective-permute-start.113 = (bf16[128,512]{1,0:T(8,128)(2,1)S(1)}, bf16[128,512]{1,0:T(8,128)(2,1)S(1)}, u32[]{:S(2)}, u32[]{:S(2)}) collective-permute-start(bf16[128,512]{1,0:T(8,128)(2,1)S(1)} %copy-done.95), channel_id=1, source_target_pairs={{0,4},{1,5},{2,6},{3,7},{4,0},{5,1},{6,2},{7,3},{8,12},{9,13},{10,... | collective-permute-start | bytes 393224 | tf_op jit(solution)/shard_map/ppermute | solution.py:1136
  566.2 13.0 %collective-permute-start.114 = (bf16[128,512]{1,0:T(8,128)(2,1)S(1)}, bf16[128,512]{1,0:T(8,128)(2,1)S(1)}, u32[]{:S(2)}, u32[]{:S(2)}) collective-permute-start(bf16[128,512]{1,0:T(8,128)(2,1)S(1)} %copy-done.94), channel_id=1, source_target_pairs={{0,6},{1,7},{2,0},{3,1},{4,2},{5,3},{6,4},{7,5},{8,14},{9,15},{10,... | collective-permute-start | bytes 393224 | tf_op jit(solution)/shard_map/ppermute | solution.py:1136
  (186 other events, 910.2 us)
Sparse Core Ops, SparseCore 0:
  474.8 80.2 reduce-scatter.1

commit v2 on v1

--- a/solution.py
+++ b/solution.py
@@ -103,49 +103,79 @@
     return jnp.where(iota((TOK, LANES), 1) < 64, both[:TOK], both[TOK:])
 
 
-def call(name, kernel, outs, args, scratch=(), smem=(), flops=0, vmem=60, aliases=None):
-    specs = [
-        pl.BlockSpec(memory_space=pltpu.SMEM if i in smem else pltpu.VMEM)
-        for i in range(len(args))
-    ]
+def call(name, kernel, outs, args, scratch=(), smem=(), near=(), near_out=(), raw=(), flops=0, vmem=20):
+    far = [i for i in range(len(args)) if i not in smem and i not in near and i not in raw]
+    far_out = [i for i in range(len(outs)) if i not in near_out]
+    count, total = len(args), len(args) + len(outs)
+
+    def body(*refs):
+        held = refs[total : total + len(far) + len(far_out)]
+        in_sems, out_sems = refs[-2:]
+        given, results = list(refs[:count]), list(refs[count:total])
+        moving = []
+        for n, i in enumerate(far):
+            moving.append(pltpu.make_async_copy(given[i], held[n], in_sems.at[n]))
+            moving[-1].start()
+            given[i] = held[n]
+        for n, i in enumerate(far_out):
+            results[i] = held[len(far) + n]
+        for copy in moving:
+            copy.wait()
+        kernel(*given, *results, *refs[total + len(far) + len(far_out) : -2])
+        leaving = []
+        for n, i in enumerate(far_out):
+            leaving.append(pltpu.make_async_copy(results[i], refs[count + i], out_sems.at[n]))
+            leaving[-1].start()
+        for copy in leaving:
+            copy.wait()
+
+    def spec(i, places, nearby):
+        if i in places:
+            return pl.BlockSpec(memory_space=pltpu.SMEM)
+        return pl.BlockSpec(memory_space=pltpu.VMEM if i in nearby else pltpu.HBM)
+
+    moved = sum(a.size * a.dtype.itemsize for a in args) + sum(
+        o.size * o.dtype.itemsize for o in outs
+    )
+    return pl.pallas_call(
+        body,
+        out_shape=tuple(outs),
+        in_specs=[spec(i, smem, near) for i in range(count)],
+        out_specs=tuple(spec(i, (), near_out) for i in range(len(outs))),
+        scratch_shapes=[pltpu.VMEM(args[i].shape, args[i].dtype) for i in far]
+        + [pltpu.VMEM(outs[i].shape, outs[i].dtype) for i in far_out]
+        + list(scratch)
+        + [pltpu.SemaphoreType.DMA((max(1, len(far)),)), pltpu.SemaphoreType.DMA((max(1, len(far_out)),))],
+        compiler_params=pltpu.CompilerParams(vmem_limit_bytes=vmem * 2**20),
+        cost_estimate=pl.CostEstimate(flops=flops, bytes_accessed=moved, transcendentals=0),
+        name=name,
+    )(*args)
+
+
+def like(shape, dtype):
+    return jax.ShapeDtypeStruct(shape, dtype)
+
+
+ANY = pl.BlockSpec(memory_space=pl.ANY)
+FAR = pl.BlockSpec(memory_space=pltpu.HBM)
+
+
+def copy_in(src, dst, sem):
+    moving = pltpu.make_async_copy(src, dst, sem)
+    moving.start()
+    return moving
+
+
+def call_any(name, kernel, outs, args, scratch, flops, vmem, near, near_out):
     moved = sum(a.size * a.dtype.itemsize for a in args) + sum(
         o.size * o.dtype.itemsize for o in outs
     )
     return pl.pallas_call(
         kernel,
         out_shape=tuple(outs),
-        in_specs=specs,
-        out_specs=tuple(pl.BlockSpec(memory_space=pltpu.VMEM) for _ in outs),
-        scratch_shapes=list(scratch),
-        input_output_aliases=aliases or {},
-        compiler_params=pltpu.CompilerParams(vmem_limit_bytes=vmem * 2**20),
-        cost_estimate=pl.CostEstimate(flops=flops, bytes_accessed=moved, transcendentals=0),
-        name=name,
-    )(*args)
-
-
-def like(shape, dtype):
-    return jax.ShapeDtypeStruct(shape, dtype)
-
-
-ANY = pl.BlockSpec(memory_space=pl.ANY)
-
-
-def copy_in(src, dst, sem):
-    moving = pltpu.make_async_copy(src, dst, sem)
-    moving.start()
-    return moving
-
-
-def call_any(name, kernel, outs, args, scratch, flops, vmem):
-    moved = sum(a.size * a.dtype.itemsize for a in args) + sum(
-        o.size * o.dtype.itemsize for o in outs
-    )
-    return pl.pallas_call(
-        kernel,
-        out_shape=tuple(outs),
-        in_specs=[pl.BlockSpec(memory_space=pltpu.SMEM)] + [ANY] * (len(args) - 1),
-        out_specs=tuple(ANY for _ in outs),
+        in_specs=[pl.BlockSpec(memory_space=pltpu.SMEM)]
+        + [ANY if i in near else FAR for i in range(1, len(args))],
+        out_specs=tuple(ANY if i in near_out else FAR for i in range(len(outs))),
         scratch_shapes=list(scratch),
         compiler_params=pltpu.CompilerParams(vmem_limit_bytes=vmem * 2**20),
         cost_estimate=pl.CostEstimate(flops=flops, bytes_accessed=moved, transcendentals=0),
@@ -297,7 +327,7 @@
         moving.wait()
 
 
-def attend(table, same, other, key_w, value_w, query_w, out_w, router, plan):
+def attend(table, same, other, key_w, value_w, query_w, out_w, router, plan, vmem):
     outs = [like((TOK, WIDTH), BF16)] * 4 + [
         like((SEQ, WIDTH), BF16),
         like((SEQ, WIDTH), BF16),
@@ -347,7 +377,7 @@
         table, *same, *other, key_w, value_w, *query_w, *out_w, router,
         plan["chosen"], plan["pos_row"], plan["pos_col"], plan["key_pos"],
     ]
-    return call_any("attend", attend_kernel, outs, args, scratch, 6 * 10**9, 60)
+    return call_any("attend", attend_kernel, outs, args, scratch, 6 * 10**9, vmem, range(1, 9), range(4))
 
 
 def back_level(
@@ -496,7 +526,7 @@
         moving.wait()
 
 
-def attend_back(table, arrived, held, key_w, value_w, query_w, out_w, plan, rest):
+def attend_back(table, arrived, held, key_w, value_w, query_w, out_w, plan, rest, vmem):
     outs = [like((TOK, WIDTH), BF16)] * 4 + [
         like((CHIPS, TOK, WIDTH), BF16),
         like((HALF, WIDTH), BF16),
@@ -537,7 +567,7 @@
         pltpu.SemaphoreType.DMA((8,)),
     ]
     args = [table, *arrived, *sources]
-    return call_any("attend_back", attend_back_kernel, outs, args, scratch, 10**11, 60)
+    return call_any("attend_back", attend_back_kernel, outs, args, scratch, 10**11, vmem, range(1, 5), range(5))
 
 
 def pair_sum_kernel(*refs):
@@ -546,8 +576,8 @@
         outs[hop][...] = (refs[hop][...].astype(F32) + other[hop].astype(F32)).astype(BF16)
 
 
-def pair_sum(same, other):
-    return call("pair_sum", pair_sum_kernel, [like((TOK, WIDTH), BF16)] * 4, [*same, other])
+def pair_sum(same, other, vmem):
+    return call("pair_sum", pair_sum_kernel, [like((TOK, WIDTH), BF16)] * 4, [*same, other], near=range(5), near_out=range(4), vmem=vmem)
 
 
 def expert_weights_kernel(first, *refs):
@@ -572,7 +602,7 @@
         after[:, at] = value.astype(after.dtype)
 
 
-def expert_weights(table, rows, mixes, grad_y, grad_q, before, last):
+def expert_weights(table, rows, mixes, grad_y, grad_q, before, last, vmem):
     first = before is None
     args = [table, rows, *mixes, *grad_y, *grad_q, *(() if first else (before,))]
     outs = [like((WIDTH, 2 * WIDTH), BF16 if last else F32)]
@@ -584,6 +614,7 @@
         [pltpu.VMEM((2, HALF, WIDTH), BF16)],
         smem=(0,),
         flops=3 * 10**9,
+        vmem=vmem,
     )[0]
 
 
@@ -595,23 +626,33 @@
         if not first:
             value = value + refs[0][:, at]
         after[:, at] = value.astype(after.dtype)
-    if after.shape[1] == SHARED:
-        after[:, 2 * WIDTH :] = refs[1][...].astype(after.dtype)
+
+
+def shared_weights_last_kernel(rows, grad_k, grad_v, before, tiny, experts, after):
+    after[:, 0 : 2 * WIDTH] = experts[...]
+    for half, grad in enumerate((grad_k, grad_v)):
+        at = slice(half * WIDTH, (half + 1) * WIDTH)
+        there = slice((2 + half) * WIDTH, (3 + half) * WIDTH)
+        after[:, there] = (tn(rows[...], grad[...]) + before[:, at]).astype(BF16)
+    after[:, 4 * WIDTH :] = tiny[...].astype(BF16)
 
 
 SHARED = 2 * WIDTH + LANES
 
 
-def shared_weights(rows, grad_k, grad_v, before, tiny):
-    first, last = before is None, tiny is not None
-    args = [rows, grad_k, grad_v, *(() if first else (before,)), *((tiny,) if last else ())]
-    return call(
-        "shared_weights",
-        functools.partial(shared_weights_kernel, first),
-        [like((WIDTH, SHARED), BF16) if last else like((WIDTH, 2 * WIDTH), F32)],
-        args,
-        flops=3 * 10**9,
-    )[0]
+def shared_weights(rows, grad_k, grad_v, before):
+    first = before is None
+    args = [rows, grad_k, grad_v, *(() if first else (before,))]
+    outs = [like((WIDTH, 2 * WIDTH), F32)]
+    kernel = functools.partial(shared_weights_kernel, first)
+    return call("shared_weights", kernel, outs, args, flops=3 * 10**9)[0]
+
+
+def shared_weights_last(rows, grad_k, grad_v, before, tiny, experts):
+    args = [rows, grad_k, grad_v, before, tiny, experts]
+    outs = [like((WIDTH, 2 * WIDTH + SHARED), BF16)]
+    kernel = shared_weights_last_kernel
+    return call("shared_weights", kernel, outs, args, flops=3 * 10**9, vmem=60)[0]
 
 
 def slot_pick(shape, r, row_dim):
@@ -640,129 +681,185 @@
         outs[hop][...] = full[hop * BLOCK : (hop + 1) * BLOCK]
 
 
+def hidden_at(step):
+    return slice(step * PART, (step + 1) * PART)
+
+
+def fetch_weights(win, wout, win_far, wout_far, sems):
+    copies = []
+    for step in range(FFN // PART):
+        at = hidden_at(step)
+        now = []
+        for r in range(2):
+            now.append((win_far[r].at[:, at], win.at[r, :, at]))
+            now.append((wout_far[r].at[at, :], wout.at[r, at, :]))
+        copies.append([copy_in(src, dst, sems.at[step, n]) for n, (src, dst) in enumerate(now)])
+    return copies
+
+
 def feed_kernel(*refs):
-    blocks, win, wout = refs[0:4], refs[4:6], refs[6:8]
-    outs, received = refs[8:12], refs[12:14]
-    total, = refs[14:]
-    step = pl.program_id(0)
-
-    @pl.when(step == 0)
-    def _():
-        full = jnp.concatenate([b[...] for b in blocks], 0)
+    blocks, win_far, wout_far = refs[0:4], refs[4:6], refs[6:8]
+    outs, received_out = refs[8:12], refs[12:14]
+    win, wout, received, weight_sems, out_sems = refs[14:]
+    copies = fetch_weights(win, wout, win_far, wout_far, weight_sems)
+    full = jnp.concatenate([b[...] for b in blocks], 0)
+    leaving = []
+    for r in range(2):
+        received[r] = nn(slot_pick((ROWS, 2 * ROWS), r, 0), full).astype(BF16)
+        leaving.append(copy_in(received.at[r], received_out[r], out_sems.at[r]))
+    total = [jnp.zeros((ROWS, WIDTH), F32)] * 2
+    for step in range(FFN // PART):
+        at = hidden_at(step)
+        for copy in copies[step]:
+            copy.wait()
         for r in range(2):
-            received[r][...] = nn(slot_pick((ROWS, 2 * ROWS), r, 0), full).astype(BF16)
-        total[...] = jnp.zeros_like(total)
-
-    for r in range(2):
-        pre = nn(received[r][...], win[r][...])
-        bend, _ = gelu_parts(pre)
-        total[r] += nn((0.5 * pre * (1.0 + bend)).astype(BF16), wout[r][...])
-
-    @pl.when(step == pl.num_programs(0) - 1)
-    def _():
-        store_blocks([total[0], total[1]], outs)
-
-
-def whole(shape):
-    return pl.BlockSpec(shape, lambda f: (0,) * len(shape))
+            pre = nn(received[r], win[r, :, at])
+            bend, _ = gelu_parts(pre)
+            total[r] = total[r] + nn((0.5 * pre * (1.0 + bend)).astype(BF16), wout[r, at, :])
+    store_blocks(total, outs)
+    for copy in leaving:
+        copy.wait()
+
+
+NEAR = pl.BlockSpec(memory_space=pltpu.VMEM)
 
 
 def feed(blocks, win, wout):
-    grid = FFN // PART
     return pl.pallas_call(
         feed_kernel,
-        grid=(grid,),
-        in_specs=[whole((BLOCK, WIDTH))] * 4
-        + [pl.BlockSpec((WIDTH, PART), lambda f: (0, f))] * 2
-        + [pl.BlockSpec((PART, WIDTH), lambda f: (f, 0))] * 2,
-        out_specs=tuple([whole((BLOCK, WIDTH))] * 4 + [whole((ROWS, WIDTH))] * 2),
+        in_specs=[NEAR] * 4 + [FAR] * 4,
+        out_specs=tuple([NEAR] * 4 + [FAR] * 2),
         out_shape=tuple([like((BLOCK, WIDTH), BF16)] * 4 + [like((ROWS, WIDTH), BF16)] * 2),
-        scratch_shapes=[pltpu.VMEM((2, ROWS, WIDTH), F32)],
-        compiler_params=pltpu.CompilerParams(vmem_limit_bytes=60 * 2**20),
+        scratch_shapes=[
+            pltpu.VMEM((2, WIDTH, FFN), BF16),
+            pltpu.VMEM((2, FFN, WIDTH), BF16),
+            pltpu.VMEM((2, ROWS, WIDTH), BF16),
+            pltpu.SemaphoreType.DMA((FFN // PART, 4)),
+            pltpu.SemaphoreType.DMA((2,)),
+        ],
+        compiler_params=pltpu.CompilerParams(vmem_limit_bytes=24 * 2**20),
         cost_estimate=pl.CostEstimate(flops=2 * 10**9, bytes_accessed=10**7, transcendentals=10**6),
         name="feed",
     )(*blocks, *win, *wout)
 
 
 def feed_back_kernel(*refs):
-    blocks, received, win, wout = refs[0:4], refs[4:6], refs[6:8], refs[8:10]
-    outs, grad_rows, acts, grad_pre = refs[10:14], refs[14:16], refs[16:18], refs[18:20]
-    total, = refs[20:]
-    step = pl.program_id(0)
-
-    @pl.when(step == 0)
-    def _():
-        full = jnp.concatenate([b[...] for b in blocks], 0)
+    blocks, received_far, win_far, wout_far = refs[0:4], refs[4:6], refs[6:8], refs[8:10]
+    outs, rows_out, acts_out, pre_out = refs[10:14], refs[14:16], refs[16:18], refs[18:20]
+    win, wout, received, grad_rows, acts, grad_pre = refs[20:26]
+    weight_sems, in_sems, out_sems = refs[26:]
+    arriving = [copy_in(received_far[r], received.at[r], in_sems.at[r]) for r in range(2)]
+    copies = fetch_weights(win, wout, win_far, wout_far, weight_sems)
+    full = jnp.concatenate([b[...] for b in blocks], 0)
+    leaving = []
+    for r in range(2):
+        grad_rows[r] = nn(slot_pick((ROWS, 2 * ROWS), r, 0), full).astype(BF16)
+        leaving.append(copy_in(grad_rows.at[r], rows_out[r], out_sems.at[r]))
+    for copy in arriving:
+        copy.wait()
+    total = [jnp.zeros((ROWS, WIDTH), F32)] * 2
+    for step in range(FFN // PART):
+        at = hidden_at(step)
+        for copy in copies[step]:
+            copy.wait()
         for r in range(2):
-            grad_rows[r][...] = nn(slot_pick((ROWS, 2 * ROWS), r, 0), full).astype(BF16)
-        total[...] = jnp.zeros_like(total)
-
+            pre = nn(received[r], win[r, :, at])
+            bend, slope = gelu_parts(pre)
+            acts[r, :, at] = (0.5 * pre * (1.0 + bend)).astype(BF16)
+            grad_act = nt(grad_rows[r], wout[r, at, :])
+            inner = 0.5 * (1.0 + bend) + 0.5 * pre * (1.0 - bend * bend) * slope
+            low = (grad_act * inner).astype(BF16)
+            grad_pre[r, :, at] = low
+            total[r] = total[r] + nt(low, win[r, :, at])
     for r in range(2):
-        pre = nn(received[r][...], win[r][...])
-        bend, slope = gelu_parts(pre)
-        acts[r][...] = (0.5 * pre * (1.0 + bend)).astype(BF16)
-        grad_act = nt(grad_rows[r][...], wout[r][...])
-        inner = 0.5 * (1.0 + bend) + 0.5 * pre * (1.0 - bend * bend) * slope
-        low = (grad_act * inner).astype(BF16)
-        grad_pre[r][...] = low
-        total[r] += nt(low, win[r][...])
-
-    @pl.when(step == pl.num_programs(0) - 1)
-    def _():
-        store_blocks([total[0], total[1]], outs)
-
-
-HIDDEN = pl.BlockSpec((ROWS, PART), lambda f: (0, f))
+        leaving.append(copy_in(acts.at[r], acts_out[r], out_sems.at[2 + r]))
+        leaving.append(copy_in(grad_pre.at[r], pre_out[r], out_sems.at[4 + r]))
+    store_blocks(total, outs)
+    for copy in leaving:
+        copy.wait()
 
 
 def feed_back(blocks, received, win, wout):
     return pl.pallas_call(
         feed_back_kernel,
-        grid=(FFN // PART,),
-        in_specs=[whole((BLOCK, WIDTH))] * 4
-        + [whole((ROWS, WIDTH))] * 2
-        + [pl.BlockSpec((WIDTH, PART), lambda f: (0, f))] * 2
-        + [pl.BlockSpec((PART, WIDTH), lambda f: (f, 0))] * 2,
-        out_specs=tuple([whole((BLOCK, WIDTH))] * 4 + [whole((ROWS, WIDTH))] * 2 + [HIDDEN] * 4),
+        in_specs=[NEAR] * 4 + [FAR] * 6,
+        out_specs=tuple([NEAR] * 4 + [FAR] * 6),
         out_shape=tuple(
             [like((BLOCK, WIDTH), BF16)] * 4
             + [like((ROWS, WIDTH), BF16)] * 2
             + [like((ROWS, FFN), BF16)] * 4
         ),
-        scratch_shapes=[pltpu.VMEM((2, ROWS, WIDTH), F32)],
-        compiler_params=pltpu.CompilerParams(vmem_limit_bytes=60 * 2**20),
+        scratch_shapes=[
+            pltpu.VMEM((2, WIDTH, FFN), BF16),
+            pltpu.VMEM((2, FFN, WIDTH), BF16),
+            pltpu.VMEM((2, ROWS, WIDTH), BF16),
+            pltpu.VMEM((2, ROWS, WIDTH), BF16),
+            pltpu.VMEM((2, ROWS, FFN), BF16),
+            pltpu.VMEM((2, ROWS, FFN), BF16),
+            pltpu.SemaphoreType.DMA((FFN // PART, 4)),
+            pltpu.SemaphoreType.DMA((2,)),
+            pltpu.SemaphoreType.DMA((6,)),
+        ],
+        compiler_params=pltpu.CompilerParams(vmem_limit_bytes=28 * 2**20),
         cost_estimate=pl.CostEstimate(flops=3 * 10**9, bytes_accessed=10**7, transcendentals=10**6),
         name="feed_back",
     )(*blocks, *received, *win, *wout)
 
 
 def feed_weights_kernel(*refs):
-    scal = refs[0]
-    received, grad_rows, acts, grad_pre = refs[1:7], refs[7:13], refs[13:19], refs[19:25]
-    out_in, outs_out, total = refs[25], refs[26:30], refs[30]
-    out_in[...] = sum(tn(received[s][...], grad_pre[s][...]) for s in range(6)).astype(BF16)
-    total[...] = sum(tn(acts[s][...], grad_rows[s][...]) for s in range(6))
+    scal, far = refs[0], refs[1:25]
+    outs_in, outs_out = refs[25:29], refs[29:33]
+    received, grad_rows, acts, grad_pre, total_in, total_out, in_sems, out_sems = refs[33:]
+    held = (received, grad_pre, grad_rows, acts)
+    copies = [
+        [
+            copy_in(far[6 * n + s], held[n].at[ROWS * s : ROWS * (s + 1)], in_sems.at[n, s])
+            for s in range(6)
+        ]
+        for n in range(4)
+    ]
+    row, col = scal[0, 11], scal[0, 12]
+    leaving = []
+    for copy in copies[0] + copies[1]:
+        copy.wait()
+    for step in range(FFN // PART):
+        at = hidden_at(step)
+        total_in[:, at] = tn(received[...], grad_pre[:, at]).astype(BF16)
     for hop in range(4):
-        outs_out[hop][...] = total[rows_at(lax.rem(scal[0, 12] + hop, 4)), :].astype(BF16)
+        there = rows_at(lax.rem(row + hop, 4))
+        leaving.append(copy_in(total_in.at[there], outs_in[hop], out_sems.at[0, hop]))
+    for copy in copies[2] + copies[3]:
+        copy.wait()
+    for step in range(FFN // PART):
+        total_out[step] = tn(acts[:, hidden_at(step)], grad_rows[...]).astype(BF16)
+        for hop in range(4):
+            there = rows_at(lax.rem(col + hop, 4))
+            out = outs_out[hop].at[step * TOK : (step + 1) * TOK]
+            leaving.append(copy_in(total_out.at[step, there], out, out_sems.at[1 + step, hop]))
+    for copy in leaving:
+        copy.wait()
 
 
 def feed_weights(table, received, grad_rows, acts, grad_pre):
     return pl.pallas_call(
         feed_weights_kernel,
-        grid=(FFN // PART,),
-        in_specs=[pl.BlockSpec(memory_space=pltpu.SMEM)]
-        + [whole((ROWS, WIDTH))] * 12
-        + [HIDDEN] * 12,
-        out_specs=tuple(
-            [pl.BlockSpec((WIDTH, PART), lambda f: (0, f))]
-            + [pl.BlockSpec((TOK, WIDTH), lambda f: (f, 0))] * 4
-        ),
-        out_shape=tuple([like((WIDTH, FFN), BF16)] + [like((4 * TOK, WIDTH), BF16)] * 4),
-        scratch_shapes=[pltpu.VMEM((WIDTH, PART), F32)],
+        in_specs=[pl.BlockSpec(memory_space=pltpu.SMEM)] + [FAR] * 24,
+        out_specs=tuple([FAR] * 8),
+        out_shape=tuple([like((TOK, FFN), BF16)] * 4 + [like((4 * TOK, WIDTH), BF16)] * 4),
+        scratch_shapes=[
+            pltpu.VMEM((6 * ROWS, WIDTH), BF16),
+            pltpu.VMEM((6 * ROWS, WIDTH), BF16),
+            pltpu.VMEM((6 * ROWS, FFN), BF16),
+            pltpu.VMEM((6 * ROWS, FFN), BF16),
+            pltpu.VMEM((WIDTH, FFN), BF16),
+            pltpu.VMEM((4, PART, WIDTH), BF16),
+            pltpu.SemaphoreType.DMA((4, 6)),
+            pltpu.SemaphoreType.DMA((5, 4)),
+        ],
         compiler_params=pltpu.CompilerParams(vmem_limit_bytes=60 * 2**20),
         cost_estimate=pl.CostEstimate(flops=8 * 10**9, bytes_accessed=2 * 10**7, transcendentals=0),
         name="feed_weights",
-    )(table, *received, *grad_rows, *acts, *grad_pre)
+    )(table, *received, *grad_pre, *grad_rows, *acts)
 
 
 def fold_kernel(axes, scal, *refs):
@@ -787,7 +884,7 @@
     scratch = [pltpu.VMEM(parts[0].shape, F32) for parts in groups]
     args = [table] + [p for parts in groups for p in parts]
     places = tuple({"x": 11, "y": 12}[axis] for axis in axes)
-    res = call("fold", functools.partial(fold_kernel, places), outs, args, scratch, smem=(0,))
+    res = call("fold", functools.partial(fold_kernel, places), outs, args, scratch, smem=(0,), vmem=60)
     return [list(res[4 * n : 4 * n + 4]) for n in range(len(groups))]
 
 
@@ -800,7 +897,7 @@
 def last_sum(groups, dtypes):
     outs = [like(parts[0].shape, dtype) for parts, dtype in zip(groups, dtypes)]
     args = [p for parts in groups for p in parts]
-    return call("last_sum", functools.partial(last_sum_kernel, len(groups)), outs, args)
+    return call("last_sum", functools.partial(last_sum_kernel, len(groups)), outs, args, vmem=60)
 
 
 def first_norm_kernel(block, gain, depth, wide, normed, payload, tail):
@@ -821,24 +918,31 @@
         like((TOK + 16, WIDTH), BF16),
     ]
     scratch = [pltpu.VMEM((16, WIDTH), F32)]
-    return call("first_norm", first_norm_kernel, outs, [block, gain, depth], scratch)
+    args = [block, gain, depth]
+    return call("first_norm", first_norm_kernel, outs, args, scratch, near_out=(2,), vmem=60)
 
 
 def attend_plan_kernel(steps, *refs):
     place, choices = refs[0], refs[1]
     blocks = refs[2:10] if 0 not in steps else ()
     outs = refs[2 + len(blocks) :]
-    outs, (spots, named_all, depth_col) = outs[: 5 * len(steps)], outs[5 * len(steps) :]
+    outs, (spots, named_all, depth_col, tails, sems) = outs[: 5 * len(steps)], outs[5 * len(steps) :]
     chip, core = place[0], place[1]
     dp_row, dp_col = place[2], place[3]
     token = iota((SEQ, LANES), 0)
     lanes = iota((SEQ, LANES), 1)
     held = ((token // TOK) % 2) == core
     if blocks:
+        copies = [
+            copy_in(ref.at[TOK : TOK + 16, 0:TOK], tails.at[n], sems.at[n])
+            for n, ref in enumerate(blocks)
+        ]
+        for copy in copies:
+            copy.wait()
         for hop in range(CHIPS):
             source = lax.rem(chip - hop + CHIPS, CHIPS)
-            for side, ref in ((core, blocks[hop]), (1 - core, blocks[CHIPS + hop])):
-                rows = ref[TOK : TOK + 16, 0:TOK].astype(F32)
+            for side, n in ((core, hop), (1 - core, CHIPS + hop)):
+                rows = tails[n].astype(F32)
                 rows = jnp.concatenate([rows, jnp.zeros((TOK - 16, TOK), F32)], 0)
                 depth_col[rows_at(source * 2 + side), :] = rows.T
     before = onehot(iota((SEQ, SEQ), 1) < iota((SEQ, SEQ), 0))
@@ -895,9 +999,10 @@
         like((SEQ, LANES), I32),
     ] * len(steps)
     scratch = [pltpu.VMEM((SEQ, LANES), F32)] * 3
+    scratch += [pltpu.VMEM((8, 16, TOK), BF16), pltpu.SemaphoreType.DMA((8,))]
     res = call(
         "attend_plan", functools.partial(attend_plan_kernel, steps), outs,
-        [place, choices, *blocks], scratch, smem=(0,), flops=10**9,
+        [place, choices, *blocks], scratch, smem=(0,), raw=range(2, 10), flops=10**9, vmem=60,
     )
     names = ("table", "chosen", "pos_row", "pos_col", "key_pos")
     return [dict(zip(names, res[5 * n : 5 * n + 5])) for n in range(len(steps))]
@@ -927,8 +1032,8 @@
 
 def slot_plan(place, choices, depth):
     outs = [like((TOK, LANES), I32), like((8, TOK), I32)] * 3
-    res = call("slot_plan", slot_plan_kernel, outs, [place, choices, depth], smem=(0,))
-    return res[0::2], res[1::2]
+    res = call("slot_plan", slot_plan_kernel, outs, [place, choices, depth], smem=(0,), vmem=60)
+    return list(res[0::2]), list(res[1::2])
 
 
 def dispatch_kernel(*refs):
@@ -962,7 +1067,7 @@
         like((TOK, WIDTH), BF16),
         like((TOK, LANES), F32),
     ] + [like((BLOCK, WIDTH), BF16)] * 4
-    return call("dispatch", dispatch_kernel, outs, [state, *parts, gain, router, slot_row, slot_col])
+    return call("dispatch", dispatch_kernel, outs, [state, *parts, gain, router, slot_row, slot_col], near=range(1, 5), near_out=range(3, 7))
 
 
 def picked_rows(slot_col, returned):
@@ -988,7 +1093,7 @@
 
 def advance(mixed, state, gates, slot_col, returned, gain):
     outs = [like((TOK, WIDTH), F32), like((TOK, WIDTH), BF16)]
-    return call("advance", advance_kernel, outs, [mixed, state, gates, slot_col, *returned, gain])
+    return call("advance", advance_kernel, outs, [mixed, state, gates, slot_col, *returned, gain], near=range(4, 8), near_out=(1,))
 
 
 def send_grads(upstream, rows, gates, slot_row, slot_col, grad_z_out, gate_grads_out, sends):
@@ -1059,7 +1164,7 @@
         like((TOK, WIDTH), F32),
     ] + SEND_OUTS
     args = [mixed, state, gates, slot_col, slot_row, *returned, first_state, halt, depth, cotangent]
-    return call("turn", turn_kernel, outs, args)
+    return call("turn", turn_kernel, outs, args, near=range(5, 9), near_out=range(6, 10))
 
 
 def moe_back_kernel(*refs):
@@ -1094,7 +1199,7 @@
         like((WIDTH, LANES), F32),
     ]
     args = [*returned, slot_col, gates, gate_grads, normed, router, mixed, gain, grad_z, tiny]
-    return call("moe_back", moe_back_kernel, outs, args)
+    return call("moe_back", moe_back_kernel, outs, args, near=range(4), near_out=(1,))
 
 
 def retreat_kernel(step, *refs):
@@ -1124,7 +1229,10 @@
 
 def retreat(step, parts, args, extra):
     outs = [like((TOK, WIDTH), F32)] + (SEND_OUTS if step else [])
-    return call("retreat", functools.partial(retreat_kernel, step), outs, [*parts, *args, *extra])
+    return call(
+        "retreat", functools.partial(retreat_kernel, step), outs, [*parts, *args, *extra],
+        near=range(4), near_out=range(3, 7),
+    )
 
 
 def swap_core(rows):
@@ -1138,6 +1246,10 @@
 
 def send_blocks(blocks):
     return [blocks[0]] + [shift_chip(blocks[d], d) for d in (1, 2, 3)]
+
+
+def after(value, other):
+    return lax.optimization_barrier((value, other))
 
 
 def return_blocks(blocks):
@@ -1194,12 +1306,12 @@
 
     state, normed, payload = first_norm(block_input, gain_a, depths[None, :])
     same = spread_rows(payload)
+    plan = attend_plan((0,), place, moa_rows, ())
+    same[1], plan[0]["table"] = after(same[1], plan[0]["table"])
     query_w = [query_proj[0], swap_core(query_proj[0])]
     out_w = [out_proj[0], swap_core(out_proj[0])]
-    plan = attend_plan((0,), place, moa_rows, ())
-    same[1], plan[0]["table"] = lax.optimization_barrier((same[1], plan[0]["table"]))
     other = [swap_core(rows) for rows in same]
-    slot_cols, slot_rows = slot_plan(place, moe_rows, depth)
+    slot_cols = slot_rows = None
     win = wout = None
 
     kept = []
@@ -1210,18 +1322,29 @@
             other = [swap_core(rows) for rows in same]
         p = plan[s]
         res = attend(
-            p["table"], same, other, key_proj, value_proj, query_w, out_w, router_a, p
+            p["table"], same, other, key_proj, value_proj, query_w, out_w, router_a, p,
+            32 if s else 60,
         )
-        parts = send_blocks(res[:4])
+        parts = list(res[:4])
         if s == 0:
+            parts[0], place_late = after(parts[0], place)
+            slot_cols, slot_rows = slot_plan(place_late, moe_rows, depth)
+            parts[3], slot_cols[0] = after(parts[3], slot_cols[0])
             win = [ffn_in[0], swap_core(ffn_in[0])]
             wout = [ffn_out[0], swap_core(ffn_out[0])]
-            plan = plan + attend_plan((1, 2), place, moa_rows, (*same, *other))
-            parts[1], plan[1]["table"] = lax.optimization_barrier((parts[1], plan[1]["table"]))
+            tails = (*same, *other)
+        parts = send_blocks(parts)
         mixed, normed_b, gates, *sends = dispatch(
             state, parts, gain_b, router_b, slot_rows[s], slot_cols[s]
         )
-        *sends, mine, others = feed(send_blocks(sends), win, wout)
+        if s == 0:
+            plan = plan + attend_plan((1,), place, moa_rows, tails)
+            sends[3], plan[1]["table"] = after(sends[3], plan[1]["table"])
+        sends = send_blocks(sends)
+        *sends, mine, others = feed(sends, win, wout)
+        if s == 0:
+            plan = plan + attend_plan((2,), place, moa_rows, tails)
+            sends[3], plan[2]["table"] = after(sends[3], plan[2]["table"])
         returned = return_blocks(sends)
         *saved, spread_0, spread_1, lse, weights = res[4:]
         kept.append(
@@ -1257,32 +1380,50 @@
             back, slot_cols[s], k["gates"], gate_grads, k["normed_b"], router_b, k["mixed"],
             gain_b, grad_z, tiny,
         )
+        limit = 20 if s else 60
         if s == 0:
-            grad_in, *blocks = feed_weights(table, received, grad_rows, acts, grad_pres)
-            grad_low, grad_in, *blocks = lax.optimization_barrier((grad_low, grad_in, *blocks))
-            grads_out = go(shift_y, blocks)
-            grad_in = lax.psum_scatter(grad_in, "dp", scatter_dimension=0, tiled=True)
+            blocks = feed_weights(table, received, grad_rows, acts, grad_pres)
+            grad_low, *blocks = lax.optimization_barrier((grad_low, *blocks))
+            grads_in, grads_out = go(shift_x, blocks[:4]), go(shift_y, blocks[4:])
         *same, other, y_0, y_1, q_0, q_1, grad_k, grad_v, tiny = attend_back(
             table, spread_rows(grad_low), k["attend"], key_proj, value_proj, query_w, out_w, p,
-            (k["rows"], router_a, gain_a, tiny),
+            (k["rows"], router_a, gain_a, tiny), 36 if s else 60,
         )
+        if s == 0:
+            other, y_1, q_0, q_1, grad_k, *arrived = lax.optimization_barrier(
+                (other, y_1, q_0, q_1, grad_k, *grads_in[1:], *grads_out[1:])
+            )
+            grads_in[1:], grads_out[1:] = arrived[:3], arrived[3:]
         other = swap_core(other)
-        if s == 0:
-            other, *arrived = lax.optimization_barrier((other, *grads_out[1:]))
-            grads_out[1:] = arrived
-        parts = pair_sum(same, other)
-        q_0, grad_k, *parts = lax.optimization_barrier((q_0, grad_k, *parts))
-        parts = send_blocks(parts)
+        if s:
+            parts = pair_sum(same, other, limit)
+            q_0, grad_k, *parts = lax.optimization_barrier((q_0, grad_k, *parts))
         expert_acc = expert_weights(
             table, k["rows"], k["mixes"], (y_0, swap_core(y_1)), (q_0, swap_core(q_1)),
-            expert_acc, s == 0,
+            expert_acc, s == 0, limit,
         )
-        shared_acc = shared_weights(
-            k["rows"], grad_k, grad_v, shared_acc, None if s else tiny
-        )
-        parts[1], shared_acc, expert_acc = lax.optimization_barrier(
-            (parts[1], shared_acc, expert_acc)
-        )
+        if s:
+            shared_acc = shared_weights(k["rows"], grad_k, grad_v, shared_acc)
+            parts = send_blocks(parts)
+            *parts, shared_acc, expert_acc = lax.optimization_barrier(
+                (*parts, shared_acc, expert_acc)
+            )
+        else:
+            weights_last = shared_weights_last(
+                k["rows"], grad_k, grad_v, shared_acc, tiny, expert_acc
+            )
+            other, weights_last = lax.optimization_barrier((other, weights_last))
+            moved = lax.all_to_all(
+                weights_last.reshape(16, 32, -1), "dp", split_axis=0, concat_axis=0, tiled=True
+            )
+            parts = send_blocks(pair_sum(same, other, limit))
+        if s == 0:
+            summed = block_sum(moved)
+            low = summed[:, 2 * WIDTH :].astype(BF16)
+            parts[1], low = after(parts[1], low)
+            shared = lax.all_to_all(
+                low.reshape(8, 4, SHARED), "expert", split_axis=0, concat_axis=0, tiled=True
+            )
         args = (k["state"], gain_a, slot_cols[s], upstream, grad_mixed)
         if s:
             b = kept[s - 1]
@@ -1294,21 +1435,12 @@
         else:
             (grad_input,) = retreat(s, parts, args, ())
 
-    (grads_out,) = fold(table, (grads_out,), "x")
-    grads_out = go(shift_x, grads_out)
-    grad_qo = block_sum(
-        lax.all_to_all(
-            expert_acc.reshape(16, 32, 2 * WIDTH), "dp", split_axis=0, concat_axis=0, tiled=True
-        )
-    )
-    shared = block_sum(
-        lax.all_to_all(
-            shared_acc.reshape(128, 4, SHARED), ("dp", "expert"), split_axis=0, concat_axis=0,
-            tiled=True,
-        )
-    )
+    grads_in, grads_out = fold(table, (grads_in, grads_out), "yx")
+    grads_in, grads_out = go(shift_y, grads_in), go(shift_x, grads_out)
+    grads_in[1], low = after(grads_in[1], low)
+    shared = block_sum(shared)
     tiny = shared[:, 2 * WIDTH :]
-    (grad_out,) = last_sum((grads_out,), (F32,))
+    grad_in, grad_out = last_sum((grads_in, grads_out), (F32, F32))
     return (
         output,
         grad_input,
@@ -1317,10 +1449,10 @@
         tiny[:, :8],
         shared[:, :WIDTH],
         shared[:, WIDTH : 2 * WIDTH],
-        grad_qo[:, :WIDTH][None],
-        grad_qo[:, WIDTH:][None],
+        summed[:, :WIDTH][None],
+        summed[:, WIDTH : 2 * WIDTH][None],
         tiny[:, 16:24],
-        grad_in.astype(F32)[None],
+        grad_in[None],
         grad_out[None],
         tiny[:, 25],
     )

time: 602 us -> 566 us (0.940)
  Pallas kernels: 273 us -> 235 us
  starting transfers between devices: 160 us -> 176 us
  between operations: 15.3 us -> 3.01 us
    pallas_call x34 -> x35, Pallas kernels: 151 us -> 117 us  [the longest x28 68.4 us: call(): pl.pallas_call(body, out_shape=tuple(outs), in_specs=[spec(i, smem, near)...]
    ppermute x3 -> x6, starting transfers between devices: 6.02 us -> 14 us  [shift_y(): lax.ppermute(rows, 'dp', [(i, i // 4 * 4 + (i + hops) % 4) for i in range...]
    ppermute x3 -> x6, starting transfers between devices: 4.96 us -> 12.4 us  [shift_x(): lax.ppermute(rows, 'dp', [(i, (i + 4 * hops) % 16) for i in range(16)])]
    ppermute x3 -> x6, waiting for transfers between devices: 9.8 us -> 2.82 us  [shift_x(): lax.ppermute(rows, 'dp', [(i, (i + 4 * hops) % 16) for i in range(16)])]
    unnamed x258 -> x332, local copies, waits for them, and re-layouts: 23.1 us -> 25.6 us
  transfers between devices with their start and end apart: 121 -> 126, of which waited for: 60 -> 63; matrix products, arithmetic and copies ran while one was open for 1% -> 1% of each run, Pallas kernels for 21% -> 20%
where the time goes in v2:
time: 566 us; the launch traced here: 559 us
  Pallas kernels  235 us (42%)
  starting transfers between devices  176 us (31%)
  waiting for transfers between devices  113 us (20%)
  local copies, waits for them, and re-layouts  30.3 us (5%)
    pallas_call x6, Pallas kernels, call_any(): pl.pallas_call(kernel, out_shape=tuple(outs), in_specs=[pl.BlockSpec(memo...  118 us
    ppermute x72, waiting for transfers between devices, shift_chip(): lax.ppermute(rows, 'expert', [(i, (i + 2 * hops) % count) for i in range(...  80.8 us
    ppermute x72, starting transfers between devices, shift_chip(): lax.ppermute(rows, 'expert', [(i, (i + 2 * hops) % count) for i in range(...  79 us
    pallas_call x28, Pallas kernels, call(): pl.pallas_call(body, out_shape=tuple(outs), in_specs=[spec(i, smem, near)...  68.4 us
    ppermute x40, starting transfers between devices, swap_core(): return lax.ppermute(rows, 'expert', [(i, i ^ 1) for i in range(2 * CHIPS)])  50.4 us
    unnamed x332, local copies, waits for them, and re-layouts  25.6 us
    pallas_call x3, Pallas kernels, feed_back(): pl.pallas_call(feed_back_kernel, in_specs=[NEAR] * 4 + [FAR] * 6, out_spe...  24.5 us
    all_to_all x1, waiting for transfers between devices, local(): lax.all_to_all(weights_last.reshape(16, 32, -1), 'dp', split_axis=0, conc...  16.8 us
  transfers between devices with their start and end apart: 126, of which 63 were waited for; matrix products, arithmetic and copies ran while one was open for 1% of the time, Pallas kernels for 20%

profile of v2, /device:TPU:1, one launch (start us, length us, event | category | flops | bytes accessed | tf_op | source)
XLA Modules:
  0.0 559.0 jit_solution(8190078979029302340)
XLA Ops:
  2.3 2.5 first_norm.1
  6.5 3.3 collective-permute-start.1
  14.3 2.5 collective-permute-done.1.refs_3_.refs_4_
  18.1 4.2 attend_plan.3
  28.1 20.2 %attend.3 = (bf16[128,512]{1,0:T(8,128)(2,1)}, bf16[128,512]{1,0:T(8,128)(2,1)}, bf16[128,512]{1,0:T(8,128)(2,1)}, bf16[128,512]{1,0:T(8,128)(2,1)}, bf16[1024,5...) custom-call(s32[8,128]{1,0:T(8,128)} %get-tuple-element.309.refs_0_,, ...), custom_call_target="tpu_custom_call" | custom-call | flops 6000000000 | bytes 12668928 | tf_op jit(solution)/shard_map/attend/pallas_call | solution.py:173
  48.3 3.8 slot_plan.1
  53.7 5.3 attend_plan.4
  59.0 2.7 collective-permute-done.9.refs_2_
  65.9 5.2 attend_plan.5
  72.9 4.9 feed.3
  83.2 2.6 collective-permute-done.18.refs_6_.refs_17_
  90.3 3.3 collective-permute-start.23
  99.1 16.7 %attend.4 = (bf16[128,512]{1,0:T(8,128)(2,1)S(1)}, bf16[128,512]{1,0:T(8,128)(2,1)S(1)}, bf16[128,512]{1,0:T(8,128)(2,1)S(1)}, bf16[128,512]{1,0:T(8,128)(2,1)S(...) custom-call(s32[8,128]{1,0:T(8,128)S(1)} %copy-done.124, ...), custom_call_target="tpu_custom_call" | custom-call | flops 6000000000 | bytes 12537856 | tf_op jit(solution)/shard_map/attend/pallas_call | solution.py:173
  117.6 2.6 collective-permute-start.28
  122.0 3.7 collective-permute-done.28.refs_3_
  128.6 2.6 collective-permute-start.31
  131.9 2.7 collective-permute-done.31.refs_2_
  135.7 4.9 feed.4
  148.8 2.5 collective-permute-start.37
  151.3 5.9 %collective-permute-start.39 = (bf16[128,512]{1,0:T(8,128)(2,1)S(1)}, bf16[128,512]{1,0:T(8,128)(2,1)S(1)}, u32[]{:S(2)}, u32[]{:S(2)}) collective-permute-start(bf16[128,512]{1,0:T(8,128)(2,1)S(1)} %get-tuple-element.364.refs_1_), channel_id=1, source_target_pairs={{0,1},{1,0},{2,3},{3,2},{4,5},{5,4},{6,7},{7,6},{8,9},{9,8},{10,11... | collective-permute-start | bytes 393224 | tf_op jit(solution)/shard_map/ppermute | solution.py:1239
  157.2 2.8 collective-permute-start.40
  161.9 14.6 %attend.5 = (bf16[128,512]{1,0:T(8,128)(2,1)S(1)}, bf16[128,512]{1,0:T(8,128)(2,1)S(1)}, bf16[128,512]{1,0:T(8,128)(2,1)S(1)}, bf16[128,512]{1,0:T(8,128)(2,1)S(...) custom-call(s32[8,128]{1,0:T(8,128)S(1)} %copy-done.125, ...), custom_call_target="tpu_custom_call" | custom-call | flops 6000000000 | bytes 12537856 | tf_op jit(solution)/shard_map/attend/pallas_call | solution.py:173
  183.5 3.4 collective-permute-done.44.refs_3_
  189.6 2.6 collective-permute-start.47
  192.9 2.7 collective-permute-done.47.refs_2_
  196.3 4.9 feed.5
  204.7 2.9 collective-permute-done.50.refs_7_
  213.4 2.4 collective-permute-done.52.refs_1_
  216.5 8.2 %feed_back.3 = (bf16[80,512]{1,0:T(8,128)(2,1)S(1)}, bf16[80,512]{1,0:T(8,128)(2,1)S(1)}, bf16[80,512]{1,0:T(8,128)(2,1)S(1)}, bf16[80,512]{1,0:T(8,128)(2,1)S(1...) custom-call(bf16[80,512]{1,0:T(8,128)(2,1)S(1)} %get-tuple-element.3, ...), custom_call_target="tpu_custom_call" | custom-call | flops 3000000000 | bytes 10000000 | tf_op jit(solution)/shard_map/feed_back/pallas_call | solution.py:783
  229.4 2.6 collective-permute-done.56.refs_2_
  237.1 3.1 collective-permute-done.58.refs_2_
  242.6 17.7 %attend_back.3 = (bf16[128,512]{1,0:T(8,128)(2,1)S(1)}, bf16[128,512]{1,0:T(8,128)(2,1)S(1)}, bf16[128,512]{1,0:T(8,128)(2,1)S(1)}, bf16[128,512]{1,0:T(8,128)(2...) custom-call(s32[8,128]{1,0:T(8,128)S(1)} %copy-done.125, ...), custom_call_target="tpu_custom_call" | custom-call | flops 99999997952 | bytes 16996352 | tf_op jit(solution)/shard_map/attend_back/pallas_call | solution.py:173
  261.3 8.2 %collective-permute-start.61 = (bf16[4,128,512]{2,1,0:T(8,128)(2,1)S(1)}, bf16[4,128,512]{2,1,0:T(8,128)(2,1)S(1)}, u32[]{:S(2)}, u32[]{:S(2)}) collective-permute-start(bf16[4,128,512]{2,1,0:T(8,128)(2,1)S(1)} %get-tuple-element.417), channel_id=1, source_target_pairs={{0,1},{1,0},{2,3},{3,2},{4,5},{5,4},{6,7},{7,6},{8,9},{9,8},{10,11... | collective-permute-start | bytes 1572872 | tf_op jit(solution)/shard_map/ppermute | solution.py:1239
  278.6 2.4 expert_weights.3.refs_8_
  284.8 2.8 collective-permute-start.69
  291.3 8.2 %feed_back.4 = (bf16[80,512]{1,0:T(8,128)(2,1)S(1)}, bf16[80,512]{1,0:T(8,128)(2,1)S(1)}, bf16[80,512]{1,0:T(8,128)(2,1)S(1)}, bf16[80,512]{1,0:T(8,128)(2,1)S(1...) custom-call(bf16[80,512]{1,0:T(8,128)(2,1)S(1)} %get-tuple-element.4, ...), custom_call_target="tpu_custom_call" | custom-call | flops 3000000000 | bytes 10000000 | tf_op jit(solution)/shard_map/feed_back/pallas_call | solution.py:783
  303.7 3.1 collective-permute-done.72.refs_2_
  312.4 3.2 collective-permute-done.74.refs_2_
  319.5 19.8 %attend_back.4 = (bf16[128,512]{1,0:T(8,128)(2,1)S(1)}, bf16[128,512]{1,0:T(8,128)(2,1)S(1)}, bf16[128,512]{1,0:T(8,128)(2,1)S(1)}, bf16[128,512]{1,0:T(8,128)(2...) custom-call(s32[8,128]{1,0:T(8,128)S(1)} %copy-done.124, ...), custom_call_target="tpu_custom_call" | custom-call | flops 99999997952 | bytes 16996352 | tf_op jit(solution)/shard_map/attend_back/pallas_call | solution.py:173
  341.1 7.1 %collective-permute-start.77 = (bf16[4,128,512]{2,1,0:T(8,128)(2,1)S(1)}, bf16[4,128,512]{2,1,0:T(8,128)(2,1)S(1)}, u32[]{:S(2)}, u32[]{:S(2)}) collective-permute-start(bf16[4,128,512]{2,1,0:T(8,128)(2,1)S(1)} %get-tuple-element.470), channel_id=1, source_target_pairs={{0,1},{1,0},{2,3},{3,2},{4,5},{5,4},{6,7},{7,6},{8,9},{9,8},{10,11... | collective-permute-start | bytes 1572872 | tf_op jit(solution)/shard_map/ppermute | solution.py:1239
  358.6 3.0 collective-permute-start.79
  362.7 2.6 expert_weights.4.refs_8_
  370.9 3.1 collective-permute-start.85
  379.6 8.1 %feed_back.5 = (bf16[80,512]{1,0:T(8,128)(2,1)S(1)}, bf16[80,512]{1,0:T(8,128)(2,1)S(1)}, bf16[80,512]{1,0:T(8,128)(2,1)S(1)}, bf16[80,512]{1,0:T(8,128)(2,1)S(1...) custom-call(bf16[80,512]{1,0:T(8,128)(2,1)S(1)} %get-tuple-element.4, ...), custom_call_target="tpu_custom_call" | custom-call | flops 3000000000 | bytes 10000000 | tf_op jit(solution)/shard_map/feed_back/pallas_call | solution.py:783
  389.1 3.8 collective-permute-done.97.refs_16_
  398.0 3.6 collective-permute-done.88.refs_2_
  402.1 4.2 collective-permute-done.89.refs_3_
  406.3 3.2 collective-permute-start.98
  413.4 9.2 %feed_weights.1 = (bf16[128,2048]{1,0:T(8,128)(2,1)}, bf16[128,2048]{1,0:T(8,128)(2,1)}, bf16[128,2048]{1,0:T(8,128)(2,1)}, bf16[128,2048]{1,0:T(8,128)(2,1)}, b...) custom-call(s32[8,128]{1,0:T(8,128)} %get-tuple-element.309.refs_0_, ...), custom_call_target="tpu_custom_call" | custom-call | flops 8000000000 | bytes 20000000 | tf_op jit(solution)/shard_map/feed_weights/pallas_call | solution.py:844
  424.8 2.7 collective-permute-start.103
  427.6 2.6 collective-permute-start.106
  433.7 2.8 collective-permute-start.108
  438.7 4.3 collective-permute-start.110
  443.0 28.7 %attend_back.5 = (bf16[128,512]{1,0:T(8,128)(2,1)}, bf16[128,512]{1,0:T(8,128)(2,1)}, bf16[128,512]{1,0:T(8,128)(2,1)}, bf16[128,512]{1,0:T(8,128)(2,1)}, bf16[4...) custom-call(s32[8,128]{1,0:T(8,128)} %get-tuple-element.309.refs_0_,, ...), custom_call_target="tpu_custom_call" | custom-call | flops 99999997952 | bytes 16996352 | tf_op jit(solution)/shard_map/attend_back/pallas_call | solution.py:173
  476.6 5.9 %expert_weights.5.refs_5_ = bf16[512,1024]{1,0:T(8,128)(2,1)} custom-call(s32[8,128]{1,0:T(8,128)} %get-tuple-element.309.refs_0_, bf16[1024,512]{1,0:T(8,128)(2,1)} %get-tuple-element.543.refs_22_.refs_1_.refs_0_, bf16[512,512]{1,0:T(8,128)(2,1)} %get-tuple-element.536.refs_8_.refs_2_, bf16[512,512]{1,0:T(8,128)(2,1)} %collective-permute-done.112.refs_3_, ...), custom_call_target="tpu_custom_call" | custom-call | flops 3000000000 | bytes 7344128 | tf_op jit(solution)/shard_map/expert_weights/pallas_call | solution.py:140
  482.6 5.7 %shared_weights.5 = bf16[512,2176]{1,0:T(8,128)(2,1)} custom-call(bf16[1024,512]{1,0:T(8,128)(2,1)} %get-tuple-element.543.refs_22_.refs_1_.refs_0_, bf16[1024,512]{1,0:T(8,128)(2,1)} %get-tuple-element.561.refs_1_, bf16[1024,512]{1,0:T(8,128)(2,1)} %get-tuple-element.562.refs_2_, f32[512,1024]{1,0:T(8,128)} %copy-done.60, ...), custom_call_target="tpu_custom_call" | custom-call | flops 3000000000 | bytes 8781824 | tf_op jit(solution)/shard_map/shared_weights/pallas_call | solution.py:140
  489.1 14.0 %all-to-all-start = ((bf16[16,32,2176]{2,1,0:T(8,128)(2,1)}), bf16[16,32,2176]{2,1,0:T(8,128)(2,1)}, u32[]{:S(2)}, u32[]{:S(2)}) async-start(bf16[16,32,2176]{2,1,0:T(8,128)(2,1)} %bitcast.70), calls=%async_computation | async-start | bytes 4456448 | tf_op jit(solution)/shard_map/all_to_all | solution.py:1416
  503.0 5.0 fold.1
  508.1 2.4 collective-permute-start.118
  514.1 2.7 collective-permute-start.116
  516.8 16.8 %all-to-all-done = bf16[16,32,2176]{2,1,0:T(8,128)(2,1)} async-done(((bf16[16,32,2176]{2,1,0:T(8,128)(2,1)}), bf16[16,32,2176]{2,1,0:T(8,128)(2,1)}, u32[]{:S(2)}, u32[]{:S(2)}) %all-to-all-start) | async-done | bytes 2228256 | tf_op jit(solution)/shard_map/all_to_all | solution.py:1416
  537.5 6.0 %all-to-all-start.1 = ((bf16[8,4,1152]{2,1,0:T(4,128)(2,1)}), bf16[8,4,1152]{2,1,0:T(4,128)(2,1)S(1)}, u32[]{:S(2)}, u32[]{:S(2)}) async-start(bf16[8,4,1152]{2,1,0:T(4,128)(2,1)} %reshape.33), calls=%async_computation.1 | async-start | bytes 147456 | tf_op jit(solution)/shard_map/all_to_all | solution.py:1424
  544.2 3.1 collective-permute-start.122
  551.3 2.6 collective-permute-done.122.refs_6_
  (573 shorter events, 184.9 us)
Async XLA Ops:
  0.7 70.5 %collective-permute-start.15 = (bf16[512,2048]{1,0:T(8,128)(2,1)}, bf16[512,2048]{1,0:T(8,128)(2,1)}, u32[]{:S(2)}, u32[]{:S(2)}) collective-permute-start(bf16[512,2048]{1,0:T(8,128)(2,1)} %bitcast.24), channel_id=1, source_target_pairs={{0,1},{1,0},{2,3},{3,2},{4,5},{5,4},{6,7},{7,6},{8,9},{9,8},{10,11... | collective-permute-start | bytes 6291464 | tf_op jit(solution)/shard_map/ppermute | solution.py:1239
  2.2 69.0 %collective-permute-start.16 = (bf16[2048,512]{1,0:T(8,128)(2,1)}, bf16[2048,512]{1,0:T(8,128)(2,1)}, u32[]{:S(2)}, u32[]{:S(2)}) collective-permute-start(bf16[2048,512]{1,0:T(8,128)(2,1)} %bitcast.31), channel_id=1, source_target_pairs={{0,1},{1,0},{2,3},{3,2},{4,5},{5,4},{6,7},{7,6},{8,9},{9,8},{10,11... | collective-permute-start | bytes 6291464 | tf_op jit(solution)/shard_map/ppermute | solution.py:1239
  4.7 8.0 %collective-permute-start = (bf16[144,512]{1,0:T(8,128)(2,1)}, bf16[144,512]{1,0:T(8,128)(2,1)S(1)}, u32[]{:S(2)}, u32[]{:S(2)}) collective-permute-start(bf16[144,512]{1,0:T(8,128)(2,1)} %get-tuple-element.307.refs_1_.refs_2_), channel_id=1, source_target_pairs={{0,2},{1,3},{2,4},{3,5},{4,6},{5,7},{6,0},{7,1},{8,10},{9,11},{10,... | collective-permute-start | bytes 442376 | tf_op jit(solution)/shard_map/ppermute | solution.py:1244
  6.5 10.2 %collective-permute-start.1 = (bf16[144,512]{1,0:T(8,128)(2,1)}, bf16[144,512]{1,0:T(8,128)(2,1)S(1)}, u32[]{:S(2)}, u32[]{:S(2)}) collective-permute-start(bf16[144,512]{1,0:T(8,128)(2,1)} %get-tuple-element.307.refs_1_.refs_2_), channel_id=1, source_target_pairs={{0,4},{1,5},{2,6},{3,7},{4,0},{5,1},{6,2},{7,3},{8,12},{9,13},{10,... | collective-permute-start | bytes 442376 | tf_op jit(solution)/shard_map/ppermute | solution.py:1244
  9.8 8.2 %collective-permute-start.2 = (bf16[144,512]{1,0:T(8,128)(2,1)}, bf16[144,512]{1,0:T(8,128)(2,1)S(1)}, u32[]{:S(2)}, u32[]{:S(2)}) collective-permute-start(bf16[144,512]{1,0:T(8,128)(2,1)} %get-tuple-element.307.refs_1_.refs_2_), channel_id=1, source_target_pairs={{0,6},{1,7},{2,0},{3,1},{4,2},{5,3},{6,4},{7,5},{8,14},{9,15},{10,... | collective-permute-start | bytes 442376 | tf_op jit(solution)/shard_map/ppermute | solution.py:1244
  12.7 9.6 %collective-permute-start.3 = (bf16[144,512]{1,0:T(8,128)(2,1)}, bf16[144,512]{1,0:T(8,128)(2,1)S(1)}, u32[]{:S(2)}, u32[]{:S(2)}) collective-permute-start(bf16[144,512]{1,0:T(8,128)(2,1)} %get-tuple-element.307.refs_1_.refs_2_), channel_id=1, source_target_pairs={{0,1},{1,0},{2,3},{3,2},{4,5},{5,4},{6,7},{7,6},{8,9},{9,8},{10,11... | collective-permute-start | bytes 442376 | tf_op jit(solution)/shard_map/ppermute | solution.py:1239
  16.8 10.3 %collective-permute-start.7 = (bf16[512,512]{1,0:T(8,128)(2,1)}, bf16[512,512]{1,0:T(8,128)(2,1)S(1)}, u32[]{:S(2)}, u32[]{:S(2)}) collective-permute-start(bf16[512,512]{1,0:T(8,128)(2,1)} %bitcast.56), channel_id=1, source_target_pairs={{0,1},{1,0},{2,3},{3,2},{4,5},{5,4},{6,7},{7,6},{8,9},{9,8},{10,11... | collective-permute-start | bytes 1572872 | tf_op jit(solution)/shard_map/ppermute | solution.py:1239
  18.0 9.0 %collective-permute-start.8 = (bf16[512,512]{1,0:T(8,128)(2,1)}, bf16[512,512]{1,0:T(8,128)(2,1)S(1)}, u32[]{:S(2)}, u32[]{:S(2)}) collective-permute-start(bf16[512,512]{1,0:T(8,128)(2,1)} %bitcast.63), channel_id=1, source_target_pairs={{0,1},{1,0},{2,3},{3,2},{4,5},{5,4},{6,7},{7,6},{8,9},{9,8},{10,11... | collective-permute-start | bytes 1572872 | tf_op jit(solution)/shard_map/ppermute | solution.py:1239
  52.2 6.8 %collective-permute-start.11 = (bf16[128,512]{1,0:T(8,128)(2,1)}, bf16[128,512]{1,0:T(8,128)(2,1)S(1)}, u32[]{:S(2)}, u32[]{:S(2)}) collective-permute-start(bf16[128,512]{1,0:T(8,128)(2,1)} %get-tuple-element.322), channel_id=1, source_target_pairs={{0,6},{1,7},{2,0},{3,1},{4,2},{5,3},{6,4},{7,5},{8,14},{9,15},{10,... | collective-permute-start | bytes 393224 | tf_op jit(solution)/shard_map/ppermute | solution.py:1244
  52.2 6.8 %collective-permute-start.10 = (bf16[128,512]{1,0:T(8,128)(2,1)}, bf16[128,512]{1,0:T(8,128)(2,1)S(1)}, u32[]{:S(2)}, u32[]{:S(2)}) collective-permute-start(bf16[128,512]{1,0:T(8,128)(2,1)} %get-tuple-element.318), channel_id=1, source_target_pairs={{0,4},{1,5},{2,6},{3,7},{4,0},{5,1},{6,2},{7,3},{8,12},{9,13},{10,... | collective-permute-start | bytes 393224 | tf_op jit(solution)/shard_map/ppermute | solution.py:1244
  52.4 9.4 %collective-permute-start.9 = (bf16[128,512]{1,0:T(8,128)(2,1)}, bf16[128,512]{1,0:T(8,128)(2,1)S(1)}, u32[]{:S(2)}, u32[]{:S(2)}) collective-permute-start(bf16[128,512]{1,0:T(8,128)(2,1)} %get-tuple-element.317), channel_id=1, source_target_pairs={{0,2},{1,3},{2,4},{3,5},{4,6},{5,7},{6,0},{7,1},{8,10},{9,11},{10,... | collective-permute-start | bytes 393224 | tf_op jit(solution)/shard_map/ppermute | solution.py:1244
  62.9 8.3 %collective-permute-start.14 = (bf16[80,512]{1,0:T(8,128)(2,1)S(1)}, bf16[80,512]{1,0:T(8,128)(2,1)S(1)}, u32[]{:S(2)}, u32[]{:S(2)}) collective-permute-start(bf16[80,512]{1,0:T(8,128)(2,1)S(1)} %get-tuple-element.332), channel_id=1, source_target_pairs={{0,6},{1,7},{2,0},{3,1},{4,2},{5,3},{6,4},{7,5},{8,14},{9,15},{10,... | collective-permute-start | bytes 245768 | tf_op jit(solution)/shard_map/ppermute | solution.py:1244
  64.2 7.0 %collective-permute-start.12 = (bf16[80,512]{1,0:T(8,128)(2,1)S(1)}, bf16[80,512]{1,0:T(8,128)(2,1)S(1)}, u32[]{:S(2)}, u32[]{:S(2)}) collective-permute-start(bf16[80,512]{1,0:T(8,128)(2,1)S(1)} %get-tuple-element.328), channel_id=1, source_target_pairs={{0,2},{1,3},{2,4},{3,5},{4,6},{5,7},{6,0},{7,1},{8,10},{9,11},{10,... | collective-permute-start | bytes 245768 | tf_op jit(solution)/shard_map/ppermute | solution.py:1244
  86.6 6.9 %collective-permute-start.20 = (bf16[128,512]{1,0:T(8,128)(2,1)S(1)}, bf16[128,512]{1,0:T(8,128)(2,1)S(1)}, u32[]{:S(2)}, u32[]{:S(2)}) collective-permute-start(bf16[128,512]{1,0:T(8,128)(2,1)S(1)} %get-tuple-element.341.refs_1_), channel_id=1, source_target_pairs={{0,2},{1,3},{2,4},{3,5},{4,6},{5,7},{6,0},{7,1},{8,10},{9,11},{10,... | collective-permute-start | bytes 393224 | tf_op jit(solution)/shard_map/ppermute | solution.py:1244
  87.8 7.8 %collective-permute-start.21 = (bf16[128,512]{1,0:T(8,128)(2,1)S(1)}, bf16[128,512]{1,0:T(8,128)(2,1)S(1)}, u32[]{:S(2)}, u32[]{:S(2)}) collective-permute-start(bf16[128,512]{1,0:T(8,128)(2,1)S(1)} %get-tuple-element.341.refs_1_), channel_id=1, source_target_pairs={{0,4},{1,5},{2,6},{3,7},{4,0},{5,1},{6,2},{7,3},{8,12},{9,13},{10,... | collective-permute-start | bytes 393224 | tf_op jit(solution)/shard_map/ppermute | solution.py:1244
  88.6 8.7 %collective-permute-start.22 = (bf16[128,512]{1,0:T(8,128)(2,1)S(1)}, bf16[128,512]{1,0:T(8,128)(2,1)S(1)}, u32[]{:S(2)}, u32[]{:S(2)}) collective-permute-start(bf16[128,512]{1,0:T(8,128)(2,1)S(1)} %get-tuple-element.341.refs_1_), channel_id=1, source_target_pairs={{0,6},{1,7},{2,0},{3,1},{4,2},{5,3},{6,4},{7,5},{8,14},{9,15},{10,... | collective-permute-start | bytes 393224 | tf_op jit(solution)/shard_map/ppermute | solution.py:1244
  90.3 7.6 %collective-permute-start.23 = (bf16[128,512]{1,0:T(8,128)(2,1)S(1)}, bf16[128,512]{1,0:T(8,128)(2,1)S(1)}, u32[]{:S(2)}, u32[]{:S(2)}) collective-permute-start(bf16[128,512]{1,0:T(8,128)(2,1)S(1)} %get-tuple-element.341.refs_1_), channel_id=1, source_target_pairs={{0,1},{1,0},{2,3},{3,2},{4,5},{5,4},{6,7},{7,6},{8,9},{9,8},{10,11... | collective-permute-start | bytes 393224 | tf_op jit(solution)/shard_map/ppermute | solution.py:1239
  117.6 8.2 %collective-permute-start.28 = (bf16[128,512]{1,0:T(8,128)(2,1)S(1)}, bf16[128,512]{1,0:T(8,128)(2,1)S(1)}, u32[]{:S(2)}, u32[]{:S(2)}) collective-permute-start(bf16[128,512]{1,0:T(8,128)(2,1)S(1)} %get-tuple-element.348), channel_id=1, source_target_pairs={{0,4},{1,5},{2,6},{3,7},{4,0},{5,1},{6,2},{7,3},{8,12},{9,13},{10,... | collective-permute-start | bytes 393224 | tf_op jit(solution)/shard_map/ppermute | solution.py:1244
  148.3 9.0 %collective-permute-start.36 = (bf16[128,512]{1,0:T(8,128)(2,1)S(1)}, bf16[128,512]{1,0:T(8,128)(2,1)S(1)}, u32[]{:S(2)}, u32[]{:S(2)}) collective-permute-start(bf16[128,512]{1,0:T(8,128)(2,1)S(1)} %get-tuple-element.364.refs_1_), channel_id=1, source_target_pairs={{0,2},{1,3},{2,4},{3,5},{4,6},{5,7},{6,0},{7,1},{8,10},{9,11},{10,... | collective-permute-start | bytes 393224 | tf_op jit(solution)/shard_map/ppermute | solution.py:1244
  148.8 11.2 %collective-permute-start.37 = (bf16[128,512]{1,0:T(8,128)(2,1)S(1)}, bf16[128,512]{1,0:T(8,128)(2,1)S(1)}, u32[]{:S(2)}, u32[]{:S(2)}) collective-permute-start(bf16[128,512]{1,0:T(8,128)(2,1)S(1)} %get-tuple-element.364.refs_1_), channel_id=1, source_target_pairs={{0,4},{1,5},{2,6},{3,7},{4,0},{5,1},{6,2},{7,3},{8,12},{9,13},{10,... | collective-permute-start | bytes 393224 | tf_op jit(solution)/shard_map/ppermute | solution.py:1244
  151.3 8.7 %collective-permute-start.38 = (bf16[128,512]{1,0:T(8,128)(2,1)S(1)}, bf16[128,512]{1,0:T(8,128)(2,1)S(1)}, u32[]{:S(2)}, u32[]{:S(2)}) collective-permute-start(bf16[128,512]{1,0:T(8,128)(2,1)S(1)} %get-tuple-element.364.refs_1_), channel_id=1, source_target_pairs={{0,6},{1,7},{2,0},{3,1},{4,2},{5,3},{6,4},{7,5},{8,14},{9,15},{10,... | collective-permute-start | bytes 393224 | tf_op jit(solution)/shard_map/ppermute | solution.py:1244
  151.3 9.5 %collective-permute-start.39 = (bf16[128,512]{1,0:T(8,128)(2,1)S(1)}, bf16[128,512]{1,0:T(8,128)(2,1)S(1)}, u32[]{:S(2)}, u32[]{:S(2)}) collective-permute-start(bf16[128,512]{1,0:T(8,128)(2,1)S(1)} %get-tuple-element.364.refs_1_), channel_id=1, source_target_pairs={{0,1},{1,0},{2,3},{3,2},{4,5},{5,4},{6,7},{7,6},{8,9},{9,8},{10,11... | collective-permute-start | bytes 393224 | tf_op jit(solution)/shard_map/ppermute | solution.py:1239
  178.5 8.4 %collective-permute-start.44 = (bf16[128,512]{1,0:T(8,128)(2,1)S(1)}, bf16[128,512]{1,0:T(8,128)(2,1)S(1)}, u32[]{:S(2)}, u32[]{:S(2)}) collective-permute-start(bf16[128,512]{1,0:T(8,128)(2,1)S(1)} %get-tuple-element.371), channel_id=1, source_target_pairs={{0,4},{1,5},{2,6},{3,7},{4,0},{5,1},{6,2},{7,3},{8,12},{9,13},{10,... | collective-permute-start | bytes 393224 | tf_op jit(solution)/shard_map/ppermute | solution.py:1244
  234.5 6.9 %collective-permute-start.59 = (bf16[128,512]{1,0:T(8,128)(2,1)S(1)}, bf16[128,512]{1,0:T(8,128)(2,1)S(1)}, u32[]{:S(2)}, u32[]{:S(2)}) collective-permute-start(bf16[128,512]{1,0:T(8,128)(2,1)S(1)} %get-tuple-element.400.refs_1_), channel_id=1, source_target_pairs={{0,4},{1,5},{2,6},{3,7},{4,0},{5,1},{6,2},{7,3},{8,12},{9,13},{10,... | collective-permute-start | bytes 393224 | tf_op jit(solution)/shard_map/ppermute | solution.py:1244
  261.3 9.7 %collective-permute-start.61 = (bf16[4,128,512]{2,1,0:T(8,128)(2,1)S(1)}, bf16[4,128,512]{2,1,0:T(8,128)(2,1)S(1)}, u32[]{:S(2)}, u32[]{:S(2)}) collective-permute-start(bf16[4,128,512]{2,1,0:T(8,128)(2,1)S(1)} %get-tuple-element.417), channel_id=1, source_target_pairs={{0,1},{1,0},{2,3},{3,2},{4,5},{5,4},{6,7},{7,6},{8,9},{9,8},{10,11... | collective-permute-start | bytes 1572872 | tf_op jit(solution)/shard_map/ppermute | solution.py:1239
  269.5 8.7 %collective-permute-start.65 = (bf16[512,512]{1,0:T(8,128)(2,1)S(1)}, bf16[512,512]{1,0:T(8,128)(2,1)S(1)}, u32[]{:S(2)}, u32[]{:S(2)}) collective-permute-start(bf16[512,512]{1,0:T(8,128)(2,1)S(1)} %get-tuple-element.403.refs_9_), channel_id=1, source_target_pairs={{0,1},{1,0},{2,3},{3,2},{4,5},{5,4},{6,7},{7,6},{8,9},{9,8},{10,11... | collective-permute-start | bytes 1572872 | tf_op jit(solution)/shard_map/ppermute | solution.py:1239
  269.5 9.1 %collective-permute-start.66 = (bf16[512,512]{1,0:T(8,128)(2,1)S(1)}, bf16[512,512]{1,0:T(8,128)(2,1)S(1)}, u32[]{:S(2)}, u32[]{:S(2)}) collective-permute-start(bf16[512,512]{1,0:T(8,128)(2,1)S(1)} %get-tuple-element.429), channel_id=1, source_target_pairs={{0,1},{1,0},{2,3},{3,2},{4,5},{5,4},{6,7},{7,6},{8,9},{9,8},{10,11... | collective-permute-start | bytes 1572872 | tf_op jit(solution)/shard_map/ppermute | solution.py:1239
  270.0 8.6 %collective-permute-start.67 = (bf16[512,512]{1,0:T(8,128)(2,1)S(1)}, bf16[512,512]{1,0:T(8,128)(2,1)S(1)}, u32[]{:S(2)}, u32[]{:S(2)}) collective-permute-start(bf16[512,512]{1,0:T(8,128)(2,1)S(1)} %get-tuple-element.431), channel_id=1, source_target_pairs={{0,1},{1,0},{2,3},{3,2},{4,5},{5,4},{6,7},{7,6},{8,9},{9,8},{10,11... | collective-permute-start | bytes 1572872 | tf_op jit(solution)/shard_map/ppermute | solution.py:1239
  271.2 9.9 %collective-permute-start.62 = (bf16[128,512]{1,0:T(8,128)(2,1)S(1)}, bf16[128,512]{1,0:T(8,128)(2,1)S(1)}, u32[]{:S(2)}, u32[]{:S(2)}) collective-permute-start(bf16[128,512]{1,0:T(8,128)(2,1)S(1)} %get-tuple-element.423), channel_id=1, source_target_pairs={{0,2},{1,3},{2,4},{3,5},{4,6},{5,7},{6,0},{7,1},{8,10},{9,11},{10,... | collective-permute-start | bytes 393224 | tf_op jit(solution)/shard_map/ppermute | solution.py:1244
  271.9 9.2 %collective-permute-start.63 = (bf16[128,512]{1,0:T(8,128)(2,1)S(1)}, bf16[128,512]{1,0:T(8,128)(2,1)S(1)}, u32[]{:S(2)}, u32[]{:S(2)}) collective-permute-start(bf16[128,512]{1,0:T(8,128)(2,1)S(1)} %get-tuple-element.424), channel_id=1, source_target_pairs={{0,4},{1,5},{2,6},{3,7},{4,0},{5,1},{6,2},{7,3},{8,12},{9,13},{10,... | collective-permute-start | bytes 393224 | tf_op jit(solution)/shard_map/ppermute | solution.py:1244
  341.1 8.7 %collective-permute-start.77 = (bf16[4,128,512]{2,1,0:T(8,128)(2,1)S(1)}, bf16[4,128,512]{2,1,0:T(8,128)(2,1)S(1)}, u32[]{:S(2)}, u32[]{:S(2)}) collective-permute-start(bf16[4,128,512]{2,1,0:T(8,128)(2,1)S(1)} %get-tuple-element.470), channel_id=1, source_target_pairs={{0,1},{1,0},{2,3},{3,2},{4,5},{5,4},{6,7},{7,6},{8,9},{9,8},{10,11... | collective-permute-start | bytes 1572872 | tf_op jit(solution)/shard_map/ppermute | solution.py:1239
  348.2 9.5 %collective-permute-start.81 = (bf16[512,512]{1,0:T(8,128)(2,1)S(1)}, bf16[512,512]{1,0:T(8,128)(2,1)S(1)}, u32[]{:S(2)}, u32[]{:S(2)}) collective-permute-start(bf16[512,512]{1,0:T(8,128)(2,1)S(1)} %copy-done.42), channel_id=1, source_target_pairs={{0,1},{1,0},{2,3},{3,2},{4,5},{5,4},{6,7},{7,6},{8,9},{9,8},{10,11... | collective-permute-start | bytes 1572872 | tf_op jit(solution)/shard_map/ppermute | solution.py:1239
  348.2 10.2 %collective-permute-start.82 = (bf16[512,512]{1,0:T(8,128)(2,1)S(1)}, bf16[512,512]{1,0:T(8,128)(2,1)S(1)}, u32[]{:S(2)}, u32[]{:S(2)}) collective-permute-start(bf16[512,512]{1,0:T(8,128)(2,1)S(1)} %get-tuple-element.483), channel_id=1, source_target_pairs={{0,1},{1,0},{2,3},{3,2},{4,5},{5,4},{6,7},{7,6},{8,9},{9,8},{10,11... | collective-permute-start | bytes 1572872 | tf_op jit(solution)/shard_map/ppermute | solution.py:1239
  348.8 9.8 %collective-permute-start.83 = (bf16[512,512]{1,0:T(8,128)(2,1)S(1)}, bf16[512,512]{1,0:T(8,128)(2,1)S(1)}, u32[]{:S(2)}, u32[]{:S(2)}) collective-permute-start(bf16[512,512]{1,0:T(8,128)(2,1)S(1)} %get-tuple-element.485), channel_id=1, source_target_pairs={{0,1},{1,0},{2,3},{3,2},{4,5},{5,4},{6,7},{7,6},{8,9},{9,8},{10,11... | collective-permute-start | bytes 1572872 | tf_op jit(solution)/shard_map/ppermute | solution.py:1239
  348.8 39.8 %collective-permute-start.93 = (bf16[160,2048]{1,0:T(8,128)(2,1)S(1)}, bf16[160,2048]{1,0:T(8,128)(2,1)S(1)}, u32[]{:S(2)}, u32[]{:S(2)}) collective-permute-start(bf16[160,2048]{1,0:T(8,128)(2,1)S(1)} %get-tuple-element.509), channel_id=1, source_target_pairs={{0,1},{1,0},{2,3},{3,2},{4,5},{5,4},{6,7},{7,6},{8,9},{9,8},{10,11... | collective-permute-start | bytes 1966088 | tf_op jit(solution)/shard_map/ppermute | solution.py:1239
  349.9 11.6 %collective-permute-start.78 = (bf16[128,512]{1,0:T(8,128)(2,1)S(1)}, bf16[128,512]{1,0:T(8,128)(2,1)S(1)}, u32[]{:S(2)}, u32[]{:S(2)}) collective-permute-start(bf16[128,512]{1,0:T(8,128)(2,1)S(1)} %get-tuple-element.476), channel_id=1, source_target_pairs={{0,2},{1,3},{2,4},{3,5},{4,6},{5,7},{6,0},{7,1},{8,10},{9,11},{10,... | collective-permute-start | bytes 393224 | tf_op jit(solution)/shard_map/ppermute | solution.py:1244
  357.7 16.2 %collective-permute-start.92 = (bf16[160,512]{1,0:T(8,128)(2,1)S(1)}, bf16[160,512]{1,0:T(8,128)(2,1)S(1)}, u32[]{:S(2)}, u32[]{:S(2)}) collective-permute-start(bf16[160,512]{1,0:T(8,128)(2,1)S(1)} %copy-done.47), channel_id=1, source_target_pairs={{0,1},{1,0},{2,3},{3,2},{4,5},{5,4},{6,7},{7,6},{8,9},{9,8},{10,11... | collective-permute-start | bytes 491528 | tf_op jit(solution)/shard_map/ppermute | solution.py:1239
  358.5 30.4 %collective-permute-start.99 = (bf16[160,2048]{1,0:T(8,128)(2,1)S(1)}, bf16[160,2048]{1,0:T(8,128)(2,1)S(1)}, u32[]{:S(2)}, u32[]{:S(2)}) collective-permute-start(bf16[160,2048]{1,0:T(8,128)(2,1)S(1)} %get-tuple-element.521), channel_id=1, source_target_pairs={{0,1},{1,0},{2,3},{3,2},{4,5},{5,4},{6,7},{7,6},{8,9},{9,8},{10,11... | collective-permute-start | bytes 1966088 | tf_op jit(solution)/shard_map/ppermute | solution.py:1239
  374.6 13.1 %collective-permute-start.91 = (bf16[160,512]{1,0:T(8,128)(2,1)S(1)}, bf16[160,512]{1,0:T(8,128)(2,1)S(1)}, u32[]{:S(2)}, u32[]{:S(2)}) collective-permute-start(bf16[160,512]{1,0:T(8,128)(2,1)S(1)} %copy-done.51), channel_id=1, source_target_pairs={{0,1},{1,0},{2,3},{3,2},{4,5},{5,4},{6,7},{7,6},{8,9},{9,8},{10,11... | collective-permute-start | bytes 491528 | tf_op jit(solution)/shard_map/ppermute | solution.py:1239
  377.5 10.5 %collective-permute-start.90 = (bf16[160,512]{1,0:T(8,128)(2,1)S(1)}, bf16[160,512]{1,0:T(8,128)(2,1)S(1)}, u32[]{:S(2)}, u32[]{:S(2)}) collective-permute-start(bf16[160,512]{1,0:T(8,128)(2,1)S(1)} %copy-done.54), channel_id=1, source_target_pairs={{0,1},{1,0},{2,3},{3,2},{4,5},{5,4},{6,7},{7,6},{8,9},{9,8},{10,11... | collective-permute-start | bytes 491528 | tf_op jit(solution)/shard_map/ppermute | solution.py:1239
  379.1 9.2 %collective-permute-start.96 = (bf16[160,512]{1,0:T(8,128)(2,1)S(1)}, bf16[160,512]{1,0:T(8,128)(2,1)S(1)}, u32[]{:S(2)}, u32[]{:S(2)}) collective-permute-start(bf16[160,512]{1,0:T(8,128)(2,1)S(1)} %copy-done.56), channel_id=1, source_target_pairs={{0,1},{1,0},{2,3},{3,2},{4,5},{5,4},{6,7},{7,6},{8,9},{9,8},{10,11... | collective-permute-start | bytes 491528 | tf_op jit(solution)/shard_map/ppermute | solution.py:1239
  387.7 24.0 %collective-permute-start.100 = (bf16[160,2048]{1,0:T(8,128)(2,1)S(1)}, bf16[160,2048]{1,0:T(8,128)(2,1)S(1)}, u32[]{:S(2)}, u32[]{:S(2)}) collective-permute-start(bf16[160,2048]{1,0:T(8,128)(2,1)S(1)} %get-tuple-element.523), channel_id=1, source_target_pairs={{0,1},{1,0},{2,3},{3,2},{4,5},{5,4},{6,7},{7,6},{8,9},{9,8},{10,11... | collective-permute-start | bytes 1966088 | tf_op jit(solution)/shard_map/ppermute | solution.py:1239
  388.0 23.7 %collective-permute-start.94 = (bf16[160,2048]{1,0:T(8,128)(2,1)S(1)}, bf16[160,2048]{1,0:T(8,128)(2,1)S(1)}, u32[]{:S(2)}, u32[]{:S(2)}) collective-permute-start(bf16[160,2048]{1,0:T(8,128)(2,1)S(1)} %get-tuple-element.511), channel_id=1, source_target_pairs={{0,1},{1,0},{2,3},{3,2},{4,5},{5,4},{6,7},{7,6},{8,9},{9,8},{10,11... | collective-permute-start | bytes 1966088 | tf_op jit(solution)/shard_map/ppermute | solution.py:1239
  388.4 23.4 %collective-permute-start.101 = (bf16[160,2048]{1,0:T(8,128)(2,1)S(1)}, bf16[160,2048]{1,0:T(8,128)(2,1)S(1)}, u32[]{:S(2)}, u32[]{:S(2)}) collective-permute-start(bf16[160,2048]{1,0:T(8,128)(2,1)S(1)} %get-tuple-element.525), channel_id=1, source_target_pairs={{0,1},{1,0},{2,3},{3,2},{4,5},{5,4},{6,7},{7,6},{8,9},{9,8},{10,11... | collective-permute-start | bytes 1966088 | tf_op jit(solution)/shard_map/ppermute | solution.py:1239
  388.5 23.2 %collective-permute-start.95 = (bf16[160,2048]{1,0:T(8,128)(2,1)S(1)}, bf16[160,2048]{1,0:T(8,128)(2,1)S(1)}, u32[]{:S(2)}, u32[]{:S(2)}) collective-permute-start(bf16[160,2048]{1,0:T(8,128)(2,1)S(1)} %get-tuple-element.513), channel_id=1, source_target_pairs={{0,1},{1,0},{2,3},{3,2},{4,5},{5,4},{6,7},{7,6},{8,9},{9,8},{10,11... | collective-permute-start | bytes 1966088 | tf_op jit(solution)/shard_map/ppermute | solution.py:1239
  422.6 16.1 %collective-permute-start.105 = (bf16[128,2048]{1,0:T(8,128)(2,1)}, bf16[128,2048]{1,0:T(8,128)(2,1)S(1)}, u32[]{:S(2)}, u32[]{:S(2)}) collective-permute-start(bf16[128,2048]{1,0:T(8,128)(2,1)} %get-tuple-element.554), channel_id=1, source_target_pairs={{0,32},{8,40},{16,48},{24,56},{32,64},{40,72},{48,80},{56,88},{64,... | collective-permute-start | bytes 1572872 | tf_op jit(solution)/shard_map/ppermute | solution.py:1264
  424.8 8.9 %collective-permute-start.103 = (bf16[128,512]{1,0:T(8,128)(2,1)S(1)}, bf16[128,512]{1,0:T(8,128)(2,1)S(1)}, u32[]{:S(2)}, u32[]{:S(2)}) collective-permute-start(bf16[128,512]{1,0:T(8,128)(2,1)S(1)} %get-tuple-element.534.refs_1_), channel_id=1, source_target_pairs={{0,4},{1,5},{2,6},{3,7},{4,0},{5,1},{6,2},{7,3},{8,12},{9,13},{10,... | collective-permute-start | bytes 393224 | tf_op jit(solution)/shard_map/ppermute | solution.py:1244
  427.6 8.9 %collective-permute-start.104 = (bf16[128,512]{1,0:T(8,128)(2,1)S(1)}, bf16[128,512]{1,0:T(8,128)(2,1)S(1)}, u32[]{:S(2)}, u32[]{:S(2)}) collective-permute-start(bf16[128,512]{1,0:T(8,128)(2,1)S(1)} %get-tuple-element.534.refs_1_), channel_id=1, source_target_pairs={{0,6},{1,7},{2,0},{3,1},{4,2},{5,3},{6,4},{7,5},{8,14},{9,15},{10,... | collective-permute-start | bytes 393224 | tf_op jit(solution)/shard_map/ppermute | solution.py:1244
  427.6 44.1 %collective-permute-start.106 = (bf16[128,2048]{1,0:T(8,128)(2,1)}, bf16[128,2048]{1,0:T(8,128)(2,1)S(1)}, u32[]{:S(2)}, u32[]{:S(2)}) collective-permute-start(bf16[128,2048]{1,0:T(8,128)(2,1)} %get-tuple-element.555), channel_id=1, source_target_pairs={{0,64},{8,72},{16,80},{24,88},{32,96},{40,104},{48,112},{56,120},{... | collective-permute-start | bytes 1572872 | tf_op jit(solution)/shard_map/ppermute | solution.py:1264
  430.9 41.6 %collective-permute-start.107 = (bf16[128,2048]{1,0:T(8,128)(2,1)}, bf16[128,2048]{1,0:T(8,128)(2,1)S(1)}, u32[]{:S(2)}, u32[]{:S(2)}) collective-permute-start(bf16[128,2048]{1,0:T(8,128)(2,1)} %get-tuple-element.556), channel_id=1, source_target_pairs={{0,96},{8,104},{16,112},{24,120},{32,0},{40,8},{48,16},{56,24},{64... | collective-permute-start | bytes 1572872 | tf_op jit(solution)/shard_map/ppermute | solution.py:1264
  433.7 38.8 %collective-permute-start.108 = (bf16[512,512]{1,0:T(8,128)(2,1)}, bf16[512,512]{1,0:T(8,128)(2,1)S(1)}, u32[]{:S(2)}, u32[]{:S(2)}) collective-permute-start(bf16[512,512]{1,0:T(8,128)(2,1)} %get-tuple-element.557), channel_id=1, source_target_pairs={{0,8},{8,16},{16,24},{24,0},{32,40},{40,48},{48,56},{56,32},{64,72... | collective-permute-start | bytes 1572872 | tf_op jit(solution)/shard_map/ppermute | solution.py:1268
  436.5 36.0 %collective-permute-start.109 = (bf16[512,512]{1,0:T(8,128)(2,1)}, bf16[512,512]{1,0:T(8,128)(2,1)}, u32[]{:S(2)}, u32[]{:S(2)}) collective-permute-start(bf16[512,512]{1,0:T(8,128)(2,1)} %get-tuple-element.558), channel_id=1, source_target_pairs={{0,16},{8,24},{16,0},{24,8},{32,48},{40,56},{48,32},{56,40},{64,80... | collective-permute-start | bytes 1572872 | tf_op jit(solution)/shard_map/ppermute | solution.py:1268
  438.7 33.8 %collective-permute-start.110 = (bf16[512,512]{1,0:T(8,128)(2,1)}, bf16[512,512]{1,0:T(8,128)(2,1)}, u32[]{:S(2)}, u32[]{:S(2)}) collective-permute-start(bf16[512,512]{1,0:T(8,128)(2,1)} %get-tuple-element.559), channel_id=1, source_target_pairs={{0,24},{8,0},{16,8},{24,16},{32,56},{40,32},{48,40},{56,48},{64,88... | collective-permute-start | bytes 1572872 | tf_op jit(solution)/shard_map/ppermute | solution.py:1268
  473.1 15.1 %collective-permute-start.111 = (bf16[4,128,512]{2,1,0:T(8,128)(2,1)}, bf16[4,128,512]{2,1,0:T(8,128)(2,1)S(1)}, u32[]{:S(2)}, u32[]{:S(2)}) collective-permute-start(bf16[4,128,512]{2,1,0:T(8,128)(2,1)} %get-tuple-element.560), channel_id=1, source_target_pairs={{0,1},{1,0},{2,3},{3,2},{4,5},{5,4},{6,7},{7,6},{8,9},{9,8},{10,11... | collective-permute-start | bytes 1572872 | tf_op jit(solution)/shard_map/ppermute | solution.py:1239
  489.1 44.5 %all-to-all-start = ((bf16[16,32,2176]{2,1,0:T(8,128)(2,1)}), bf16[16,32,2176]{2,1,0:T(8,128)(2,1)}, u32[]{:S(2)}, u32[]{:S(2)}) async-start(bf16[16,32,2176]{2,1,0:T(8,128)(2,1)} %bitcast.70), calls=%async_computation | async-start | bytes 4456448 | tf_op jit(solution)/shard_map/all_to_all | solution.py:1416
  508.1 35.4 %collective-permute-start.118 = (bf16[32,2048]{1,0:T(8,128)(2,1)}, bf16[32,2048]{1,0:T(8,128)(2,1)S(1)}, u32[]{:S(2)}, u32[]{:S(2)}) collective-permute-start(bf16[32,2048]{1,0:T(8,128)(2,1)} %get-tuple-element.589), channel_id=1, source_target_pairs={{0,8},{8,16},{16,24},{24,0},{32,40},{40,48},{48,56},{56,32},{64,72... | collective-permute-start | bytes 393224 | tf_op jit(solution)/shard_map/ppermute | solution.py:1268
  510.5 40.8 %collective-permute-start.119 = (bf16[32,2048]{1,0:T(8,128)(2,1)}, bf16[32,2048]{1,0:T(8,128)(2,1)S(1)}, u32[]{:S(2)}, u32[]{:S(2)}) collective-permute-start(bf16[32,2048]{1,0:T(8,128)(2,1)} %get-tuple-element.591), channel_id=1, source_target_pairs={{0,16},{8,24},{16,0},{24,8},{32,48},{40,56},{48,32},{56,40},{64,80... | collective-permute-start | bytes 393224 | tf_op jit(solution)/shard_map/ppermute | solution.py:1268
  514.0 21.6 %collective-permute-start.115 = (bf16[128,512]{1,0:T(8,128)(2,1)}, bf16[128,512]{1,0:T(8,128)(2,1)S(1)}, u32[]{:S(2)}, u32[]{:S(2)}) collective-permute-start(bf16[128,512]{1,0:T(8,128)(2,1)} %get-tuple-element.572), channel_id=1, source_target_pairs={{0,2},{1,3},{2,4},{3,5},{4,6},{5,7},{6,0},{7,1},{8,10},{9,11},{10,... | collective-permute-start | bytes 393224 | tf_op jit(solution)/shard_map/ppermute | solution.py:1244
  514.1 30.1 %collective-permute-start.116 = (bf16[128,512]{1,0:T(8,128)(2,1)}, bf16[128,512]{1,0:T(8,128)(2,1)S(1)}, u32[]{:S(2)}, u32[]{:S(2)}) collective-permute-start(bf16[128,512]{1,0:T(8,128)(2,1)} %get-tuple-element.575), channel_id=1, source_target_pairs={{0,4},{1,5},{2,6},{3,7},{4,0},{5,1},{6,2},{7,3},{8,12},{9,13},{10,... | collective-permute-start | bytes 393224 | tf_op jit(solution)/shard_map/ppermute | solution.py:1244
  516.8 30.5 %collective-permute-start.117 = (bf16[128,512]{1,0:T(8,128)(2,1)}, bf16[128,512]{1,0:T(8,128)(2,1)S(1)}, u32[]{:S(2)}, u32[]{:S(2)}) collective-permute-start(bf16[128,512]{1,0:T(8,128)(2,1)} %get-tuple-element.576), channel_id=1, source_target_pairs={{0,6},{1,7},{2,0},{3,1},{4,2},{5,3},{6,4},{7,5},{8,14},{9,15},{10,... | collective-permute-start | bytes 393224 | tf_op jit(solution)/shard_map/ppermute | solution.py:1244
  535.6 15.6 %collective-permute-start.120 = (bf16[32,2048]{1,0:T(8,128)(2,1)S(1)}, bf16[32,2048]{1,0:T(8,128)(2,1)S(1)}, u32[]{:S(2)}, u32[]{:S(2)}) collective-permute-start(bf16[32,2048]{1,0:T(8,128)(2,1)S(1)} %copy-done.162), channel_id=1, source_target_pairs={{0,24},{8,0},{16,8},{24,16},{32,56},{40,32},{48,40},{56,48},{64,88... | collective-permute-start | bytes 393224 | tf_op jit(solution)/shard_map/ppermute | solution.py:1268
  537.5 19.4 %all-to-all-start.1 = ((bf16[8,4,1152]{2,1,0:T(4,128)(2,1)}), bf16[8,4,1152]{2,1,0:T(4,128)(2,1)S(1)}, u32[]{:S(2)}, u32[]{:S(2)}) async-start(bf16[8,4,1152]{2,1,0:T(4,128)(2,1)} %reshape.33), calls=%async_computation.1 | async-start | bytes 147456 | tf_op jit(solution)/shard_map/all_to_all | solution.py:1424
  543.5 7.8 %collective-permute-start.121 = (bf16[128,512]{1,0:T(8,128)(2,1)S(1)}, bf16[128,512]{1,0:T(8,128)(2,1)S(1)}, u32[]{:S(2)}, u32[]{:S(2)}) collective-permute-start(bf16[128,512]{1,0:T(8,128)(2,1)S(1)} %copy-done.161), channel_id=1, source_target_pairs={{0,32},{8,40},{16,48},{24,56},{32,64},{40,72},{48,80},{56,88},{64,... | collective-permute-start | bytes 393224 | tf_op jit(solution)/shard_map/ppermute | solution.py:1264
  544.2 9.7 %collective-permute-start.122 = (bf16[128,512]{1,0:T(8,128)(2,1)S(1)}, bf16[128,512]{1,0:T(8,128)(2,1)S(1)}, u32[]{:S(2)}, u32[]{:S(2)}) collective-permute-start(bf16[128,512]{1,0:T(8,128)(2,1)S(1)} %copy-done.160), channel_id=1, source_target_pairs={{0,64},{8,72},{16,80},{24,88},{32,96},{40,104},{48,112},{56,120},{... | collective-permute-start | bytes 393224 | tf_op jit(solution)/shard_map/ppermute | solution.py:1264
  (228 other events, 3029.6 us)

commit v3 on v2

--- a/solution.py
+++ b/solution.py
@@ -88,6 +88,11 @@
     return jnp.where(iota((LANES, WIDTH), 0) == lane, row, 0.0).T
 
 
+def turned_row(row):
+    wide = jnp.concatenate([row.astype(F32), jnp.zeros((7, TOK), F32)], 0)
+    return wide.T[:, 0:1].astype(I32)
+
+
 def rows_at(block):
     return pl.ds(pl.multiple_of(block * TOK, TOK), TOK)
 
@@ -99,8 +104,8 @@
     return jnp.concatenate([pair * low, pair * high], 0)
 
 
-def join_heads(both):
-    return jnp.where(iota((TOK, LANES), 1) < 64, both[:TOK], both[TOK:])
+def join_heads(both, rows):
+    return jnp.where(iota((rows, LANES), 1) < 64, both[:rows], both[rows:])
 
 
 def call(name, kernel, outs, args, scratch=(), smem=(), near=(), near_out=(), raw=(), flops=0, vmem=20):
@@ -183,27 +188,43 @@
     )(*args)
 
 
-def allowed_keys(key_pos, span, start):
-    number = lax.rem(iota((span, 2 * TOK), 1), TOK) + start
+def allowed_keys(key_pos, span, start, rows):
+    number = lax.rem(iota((span, 2 * rows), 1), rows) + start
     column_pos = key_pos[0:span, :]
-    return jnp.concatenate([column_pos, column_pos], 1) <= number
-
-
-def attend_level(span, start, keys, value_x, key_row, q_pairs, o_held, logs):
+    if rows == TOK:
+        column_pos = jnp.concatenate([column_pos, column_pos], 1)
+    return column_pos <= number
+
+
+def packed_rows(start, rows):
+    return pl.ds(pl.multiple_of(start, TOK), rows)
+
+
+def attend_level(rows, span, start, keys, value_x, key_row, q_held, o_held, logs):
+    here = packed_rows(start, rows)
+
     @pl.loop(0, PAIRS, unroll=UNROLL)
     def _(i):
         pair = pl.ds(pl.multiple_of(i * LANES, LANES), LANES)
-        part = nt(q_pairs[i], keys[0:span, pair])
-        number = lax.rem(iota((2 * TOK, span), 0), TOK) + start
+        part = nt(split_heads(q_held[here, pair]), keys[0:span, pair])
+        number = lax.rem(iota((2 * rows, span), 0), rows) + start
         part = jnp.where(key_row[0:1, 0:span] <= number, part, -jnp.inf)
         top = jnp.max(part, -1, keepdims=True)
         mixed = nn(jnp.exp(part - top).astype(BF16), value_x[i, 0:span, :])
         total = mixed[:, LANES : 2 * LANES]
-        o_held[pl.ds(pl.multiple_of(start, TOK), TOK), pair] = join_heads(
-            mixed[:, 0:LANES] / total
-        ).astype(BF16)
-        lanes = iota((2 * TOK, LANES), 1)
-        logs[...] = jnp.where(lanes == i, top + jnp.log(total), logs[...])
+        o_held[here, pair] = join_heads(mixed[:, 0:LANES] / total, rows).astype(BF16)
+        lanes = iota((2 * rows, LANES), 1)
+        logs[0 : 2 * rows, :] = jnp.where(
+            lanes == i, top + jnp.log(total), logs[0 : 2 * rows, :]
+        )
+
+    if rows < TOK:
+        rest = pl.ds(pl.multiple_of(start + rows, rows), TOK - rows)
+        o_held[rest, :] = jnp.zeros((TOK - rows, WIDTH), BF16)
+
+
+SMALL = 5
+LEVELS = [(TOK, level * SPAN, level) for level in range(1, 5)] + [(TOK // 2, SEQ, SMALL)]
 
 
 def attend_kernel(*refs):
@@ -217,8 +238,8 @@
     key_w, value_w, query_0, query_1, out_0, out_1, router, chosen, pos_row, pos_col = held[:10]
     key_pos = refs[48]
     queries, q_held, o_held, spread, o_spread, staged, lse, gates = refs[49:57]
-    q_pairs, key_row, logs = refs[57:60]
-    in_sems, row_sems, out_sems, block_sems = refs[60:64]
+    key_row, logs = refs[57:59]
+    in_sems, row_sems, out_sems, block_sems = refs[59:63]
     query_w, out_w = (query_0, query_1), (out_0, out_1)
     blocks, chip, core = scal[0, 8], scal[0, 9], scal[0, 10]
 
@@ -285,12 +306,10 @@
         ).astype(BF16)
         q_held[here, :] = packed
         copy_in(q_held.at[here], q_out.at[here], block_sems.at[0, j])
-        for i in range(PAIRS):
-            q_pairs[i] = split_heads(packed[:, i * LANES : (i + 1) * LANES])
-        for level in range(1, 5):
+        for rows_now, span, level in LEVELS:
             pl.when(scal[0, j] == level)(
                 functools.partial(
-                    attend_level, level * SPAN, start, keys, value_t, key_row, q_pairs, o_held, logs
+                    attend_level, rows_now, span, start, keys, value_t, key_row, q_held, o_held, logs
                 )
             )
         lse[j] = logs[...].T[:8]
@@ -365,7 +384,6 @@
         pltpu.VMEM((HALF, WIDTH), BF16),
         pltpu.VMEM((8, 8, 2 * TOK), F32),
         pltpu.VMEM((HALF, LANES), F32),
-        pltpu.VMEM((PAIRS, 2 * TOK, LANES), BF16),
         pltpu.VMEM((8, SEQ), I32),
         pltpu.VMEM((2 * TOK, LANES), F32),
         pltpu.SemaphoreType.DMA((11,)),
@@ -381,20 +399,37 @@
 
 
 def back_level(
-    span, start, keys, values, key_pos, q_pairs, o_pairs, logs, inner, sum_k, sum_v, part_q
+    rows, span, start, keys, values, key_pos, q_held, o_held, packed, logs, inner,
+    sum_k, sum_v, part_q, block,
 ):
+    here = packed_rows(start, rows)
+    lanes = iota((2 * rows, LANES), 1)
+    inners = jnp.zeros((2 * rows, LANES), F32)
+    for i in range(PAIRS):
+        at = slice(i * LANES, (i + 1) * LANES)
+        held = o_held[here, at].astype(F32)
+        grads = split_heads(packed[0:rows, at]).astype(F32)
+        inners = jnp.where(lanes == i, row_sum(grads * jnp.concatenate([held, held], 0)), inners)
+    inner[:, 0 : 2 * rows] = inners.T[:8]
+
     @pl.loop(0, PAIRS, unroll=UNROLL)
     def _(i):
         pair = pl.ds(pl.multiple_of(i * LANES, LANES), LANES)
         key_block = keys[0:span, pair]
-        queries, grads = q_pairs[i], o_pairs[i]
-        probs = jnp.exp(nt(key_block, queries) - logs[pl.ds(i, 1), :])
-        probs = jnp.where(allowed_keys(key_pos, span, start), probs, 0.0)
+        queries, grads = split_heads(q_held[here, pair]), split_heads(packed[0:rows, pair])
+        probs = jnp.exp(nt(key_block, queries) - logs[pl.ds(i, 1), 0 : 2 * rows])
+        probs = jnp.where(allowed_keys(key_pos, span, start, rows), probs, 0.0)
         grad_probs = nt(values[0:span, pair], grads)
-        grad_scores = (probs * (grad_probs - inner[pl.ds(i, 1), :])).astype(BF16)
+        grad_scores = (probs * (grad_probs - inner[pl.ds(i, 1), 0 : 2 * rows])).astype(BF16)
         sum_k[0:span, pair] += nn(grad_scores, queries)
         sum_v[0:span, pair] += nn(probs.astype(BF16), grads)
-        part_q[i] = tn(grad_scores, key_block)
+        part_q[i, 0 : 2 * rows] = tn(grad_scores, key_block)
+
+    for i in range(PAIRS):
+        at = slice(i * LANES, (i + 1) * LANES)
+        block[0:rows, at] = (join_heads(part_q[i, 0 : 2 * rows], rows) * 0.125).astype(BF16)
+    if rows < TOK:
+        block[rows:TOK, :] = jnp.zeros((TOK - rows, WIDTH), BF16)
 
 
 def attend_back_kernel(*refs):
@@ -409,7 +444,7 @@
         out_0, out_1, gates, spread_0, spread_1, pos_row, q_held, o_held, lse, keys, values,
         key_pos, pos_col, query_0, query_1, key_w, value_w, rows, router, gain, tiny,
     ) = held
-    grad_o, sum_k, sum_v, sum_q, part_q, q_pairs, o_pairs, logs, inner, own, gate_low = refs[60:71]
+    grad_o, sum_k, sum_v, sum_q, part_q, packed_s, block_q, logs, inner, own, gate_low = refs[60:71]
     grad_y, grad_q, grad_k, grad_v, same_s, other_s = refs[71:77]
     in_sems, row_sems, out_sems = refs[77:80]
     o_spread = (spread_0, spread_1)
@@ -455,29 +490,17 @@
         packed = sum(
             nn(onehot(pos_row[r : r + 1, :] == take), grad_o[r]) for r in range(2)
         ).astype(BF16)
-        pair_lanes = iota((2 * TOK, LANES), 1)
-        inners = jnp.zeros((2 * TOK, LANES), F32)
-        for i in range(PAIRS):
-            at = slice(i * LANES, (i + 1) * LANES)
-            q_pairs[i] = split_heads(q_held[here, at])
-            grad_pair = split_heads(packed[:, at])
-            o_pairs[i] = grad_pair
-            block = o_held[here, at].astype(F32)
-            product = row_sum(grad_pair.astype(F32) * jnp.concatenate([block, block], 0))
-            inners = jnp.where(pair_lanes == i, product, inners)
-        inner[...] = inners.T[:8]
+        packed_s[...] = packed
         logs[...] = lse[j]
-        for level in range(1, 5):
+        for rows_now, span, level in LEVELS:
             pl.when(scal[0, j] == level)(
                 functools.partial(
-                    back_level, level * SPAN, start, keys, values, key_pos, q_pairs, o_pairs, logs,
-                    inner, sum_k, sum_v, part_q,
+                    back_level, rows_now, span, start, keys, values, key_pos, q_held, o_held,
+                    packed_s, logs, inner, sum_k, sum_v, part_q, block_q,
                 )
             )
 
-        block = jnp.concatenate(
-            [(join_heads(part_q[i]) * 0.125).astype(BF16) for i in range(PAIRS)], 1
-        )
+        block = block_q[...]
         put = iota((HALF, TOK), 1) + start
         for r in range(2):
             sum_q[r] += nn(onehot(pos_col[:, r : r + 1] == put), block)
@@ -550,8 +573,8 @@
         pltpu.VMEM((SEQ, WIDTH), F32),
         pltpu.VMEM((2, HALF, WIDTH), F32),
         pltpu.VMEM((PAIRS, 2 * TOK, LANES), F32),
-        pltpu.VMEM((PAIRS, 2 * TOK, LANES), BF16),
-        pltpu.VMEM((PAIRS, 2 * TOK, LANES), BF16),
+        pltpu.VMEM((TOK, WIDTH), BF16),
+        pltpu.VMEM((TOK, WIDTH), BF16),
         pltpu.VMEM((8, 2 * TOK), F32),
         pltpu.VMEM((8, 2 * TOK), F32),
         pltpu.VMEM((HALF, WIDTH), BF16),
@@ -628,31 +651,114 @@
         after[:, at] = value.astype(after.dtype)
 
 
-def shared_weights_last_kernel(rows, grad_k, grad_v, before, tiny, experts, after):
-    after[:, 0 : 2 * WIDTH] = experts[...]
-    for half, grad in enumerate((grad_k, grad_v)):
-        at = slice(half * WIDTH, (half + 1) * WIDTH)
-        there = slice((2 + half) * WIDTH, (3 + half) * WIDTH)
-        after[:, there] = (tn(rows[...], grad[...]) + before[:, at]).astype(BF16)
-    after[:, 4 * WIDTH :] = tiny[...].astype(BF16)
+def shared_last_kernel(*refs):
+    scal, far, outs = refs[0], refs[1:6], refs[6:8]
+    held, (total, packed, in_sems, out_sems) = refs[8:13], refs[13:]
+    rows, grad_k, before, grad_v, tiny = held
+    copies = [copy_in(far[n], held[n], in_sems.at[n]) for n in range(5)]
+    for n in range(3):
+        copies[n].wait()
+    total[:, 0:WIDTH] = (tn(rows[...], grad_k[...]) + before[:, 0:WIDTH]).astype(BF16)
+    copies[3].wait()
+    copies[4].wait()
+    total[:, WIDTH : 2 * WIDTH] = (
+        tn(rows[...], grad_v[...]) + before[:, WIDTH : 2 * WIDTH]
+    ).astype(BF16)
+    total[:, 2 * WIDTH :] = tiny[...].astype(BF16)
+    row = iota((WIDTH, WIDTH), 0)
+    side, hop, spot = row >> 8, (row >> 6) & 3, (row >> 2) & 15
+    owner = ((scal[0, 9] + hop) & 3) * 2 + (side ^ scal[0, 10])
+    source = spot * 32 + owner * 4 + (row & 3)
+    pick = onehot(source == iota((WIDTH, WIDTH), 1))
+    packed[...] = nn(pick, total[...]).astype(BF16).reshape(2, CHIPS, 64, SHARED)
+    leaving = [copy_in(packed.at[n], outs[n], out_sems.at[n]) for n in range(2)]
+    for copy in leaving:
+        copy.wait()
+
+
+def shared_last(table, rows, grad_k, grad_v, before, tiny):
+    args = [rows, grad_k, before, grad_v, tiny]
+    scratch = [pltpu.VMEM(a.shape, a.dtype) for a in args] + [
+        pltpu.VMEM((WIDTH, SHARED), BF16),
+        pltpu.VMEM((2, CHIPS, 64, SHARED), BF16),
+        pltpu.SemaphoreType.DMA((5,)),
+        pltpu.SemaphoreType.DMA((2,)),
+    ]
+    outs = [like((CHIPS, 64, SHARED), BF16)] * 2
+    return call_any(
+        "shared_last", shared_last_kernel, outs, [table, *args], scratch, 4 * 10**9, 60, (), ()
+    )
+
+
+def core_sum_kernel(mine, other, *outs):
+    for hop in range(CHIPS):
+        outs[hop][...] = (mine[hop].astype(F32) + other[hop].astype(F32)).astype(BF16)
+
+
+def core_sum(mine, other):
+    outs = [like((64, SHARED), BF16)] * CHIPS
+    return call("core_sum", core_sum_kernel, outs, [mine, other], vmem=60)
+
+
+def last_weights_kernel(*refs):
+    scal, far, out = refs[0], refs[1:13], refs[13]
+    held, (own, total, in_sems, out_sem) = refs[14:26], refs[26:]
+    rows, q_0, q_1, expert_acc, mix_0, y_0, mix_1, y_1 = held[:8]
+    parts = held[8:]
+    copies = [copy_in(far[n], held[n], in_sems.at[n]) for n in range(12)]
+    core = scal[0, 10]
+    copies[0].wait()
+    for side in range(2):
+        for source in range(CHIPS):
+            own[side, source * TOK : (source + 1) * TOK, :] = rows[
+                rows_at(2 * source + (core if side == 0 else 1 - core)), :
+            ]
+    for n in range(1, 4):
+        copies[n].wait()
+    value = tn(own[0], q_0[...]) + tn(own[1], q_1[...]) + expert_acc[:, 0:WIDTH]
+    total[:, 0:32, :] = value.astype(BF16).reshape(16, 32, WIDTH)
+    for n in range(4, 8):
+        copies[n].wait()
+    value = tn(mix_0[...], y_0[...]) + tn(mix_1[...], y_1[...]) + expert_acc[:, WIDTH : 2 * WIDTH]
+    total[:, 32:64, :] = value.astype(BF16).reshape(16, 32, WIDTH)
+    for n in range(8, 12):
+        copies[n].wait()
+    summed = sum(p[...].astype(F32) for p in parts).astype(BF16)
+    small = jnp.concatenate(
+        [summed[:, 2 * WIDTH :], jnp.zeros((64, WIDTH - LANES), BF16)], 1
+    )
+    row, col = iota((256, 64), 0), iota((256, 64), 1)
+    spread = jnp.zeros((256, WIDTH), F32)
+    for n, value in enumerate((summed[:, 0:WIDTH], summed[:, WIDTH : 2 * WIDTH], small)):
+        pick = onehot(((row >> 4) * 4 + (row & 15) - 4 * n == col) & (((row >> 2) & 3) == n))
+        spread = spread + nn(pick, value)
+    total[:, 64:80, :] = spread.astype(BF16).reshape(16, 16, WIDTH)
+    copy_in(total, out, out_sem.at[0]).wait()
+
+
+def last_weights(table, rows, mixes, grad_y, grad_q, expert_acc, parts):
+    args = [rows, *grad_q, expert_acc, mixes[0], grad_y[0], mixes[1], grad_y[1], *parts]
+    scratch = [pltpu.VMEM(a.shape, a.dtype) for a in args] + [
+        pltpu.VMEM((2, HALF, WIDTH), BF16),
+        pltpu.VMEM((16, 80, WIDTH), BF16),
+        pltpu.SemaphoreType.DMA((12,)),
+        pltpu.SemaphoreType.DMA((1,)),
+    ]
+    outs = [like((16, 80, WIDTH), BF16)]
+    return call_any(
+        "last_weights", last_weights_kernel, outs, [table, *args], scratch, 4 * 10**9, 60, (), ()
+    )[0]
 
 
 SHARED = 2 * WIDTH + LANES
 
 
-def shared_weights(rows, grad_k, grad_v, before):
+def shared_weights(rows, grad_k, grad_v, before, vmem=20):
     first = before is None
     args = [rows, grad_k, grad_v, *(() if first else (before,))]
     outs = [like((WIDTH, 2 * WIDTH), F32)]
     kernel = functools.partial(shared_weights_kernel, first)
-    return call("shared_weights", kernel, outs, args, flops=3 * 10**9)[0]
-
-
-def shared_weights_last(rows, grad_k, grad_v, before, tiny, experts):
-    args = [rows, grad_k, grad_v, before, tiny, experts]
-    outs = [like((WIDTH, 2 * WIDTH + SHARED), BF16)]
-    kernel = shared_weights_last_kernel
-    return call("shared_weights", kernel, outs, args, flops=3 * 10**9, vmem=60)[0]
+    return call("shared_weights", kernel, outs, args, flops=3 * 10**9, vmem=vmem)[0]
 
 
 def slot_pick(shape, r, row_dim):
@@ -807,9 +913,8 @@
 
 
 def feed_weights_kernel(*refs):
-    scal, far = refs[0], refs[1:25]
-    outs_in, outs_out = refs[25:29], refs[29:33]
-    received, grad_rows, acts, grad_pre, total_in, total_out, in_sems, out_sems = refs[33:]
+    far, out = refs[0:24], refs[24]
+    received, grad_rows, acts, grad_pre, total, in_sems, out_sem = refs[25:]
     held = (received, grad_pre, grad_rows, acts)
     copies = [
         [
@@ -818,86 +923,39 @@
         ]
         for n in range(4)
     ]
-    row, col = scal[0, 11], scal[0, 12]
-    leaving = []
     for copy in copies[0] + copies[1]:
         copy.wait()
     for step in range(FFN // PART):
-        at = hidden_at(step)
-        total_in[:, at] = tn(received[...], grad_pre[:, at]).astype(BF16)
-    for hop in range(4):
-        there = rows_at(lax.rem(row + hop, 4))
-        leaving.append(copy_in(total_in.at[there], outs_in[hop], out_sems.at[0, hop]))
+        value = tn(received[...], grad_pre[:, hidden_at(step)]).astype(BF16)
+        total[:, step * 32 : (step + 1) * 32, :] = value.reshape(16, 32, PART)
     for copy in copies[2] + copies[3]:
         copy.wait()
     for step in range(FFN // PART):
-        total_out[step] = tn(acts[:, hidden_at(step)], grad_rows[...]).astype(BF16)
-        for hop in range(4):
-            there = rows_at(lax.rem(col + hop, 4))
-            out = outs_out[hop].at[step * TOK : (step + 1) * TOK]
-            leaving.append(copy_in(total_out.at[step, there], out, out_sems.at[1 + step, hop]))
-    for copy in leaving:
-        copy.wait()
-
-
-def feed_weights(table, received, grad_rows, acts, grad_pre):
+        value = tn(acts[:, hidden_at(step)], grad_rows[...]).astype(BF16)
+        total[4 * step : 4 * step + 4, TOK : 2 * TOK, :] = value.reshape(4, TOK, WIDTH)
+    leaving = copy_in(total, out, out_sem.at[0])
+    leaving.wait()
+
+
+def feed_weights(received, grad_rows, acts, grad_pre):
     return pl.pallas_call(
         feed_weights_kernel,
-        in_specs=[pl.BlockSpec(memory_space=pltpu.SMEM)] + [FAR] * 24,
-        out_specs=tuple([FAR] * 8),
-        out_shape=tuple([like((TOK, FFN), BF16)] * 4 + [like((4 * TOK, WIDTH), BF16)] * 4),
+        in_specs=[FAR] * 24,
+        out_specs=FAR,
+        out_shape=like((16, 2 * TOK, WIDTH), BF16),
         scratch_shapes=[
             pltpu.VMEM((6 * ROWS, WIDTH), BF16),
             pltpu.VMEM((6 * ROWS, WIDTH), BF16),
             pltpu.VMEM((6 * ROWS, FFN), BF16),
             pltpu.VMEM((6 * ROWS, FFN), BF16),
-            pltpu.VMEM((WIDTH, FFN), BF16),
-            pltpu.VMEM((4, PART, WIDTH), BF16),
+            pltpu.VMEM((16, 2 * TOK, WIDTH), BF16),
             pltpu.SemaphoreType.DMA((4, 6)),
-            pltpu.SemaphoreType.DMA((5, 4)),
+            pltpu.SemaphoreType.DMA((1,)),
         ],
         compiler_params=pltpu.CompilerParams(vmem_limit_bytes=60 * 2**20),
         cost_estimate=pl.CostEstimate(flops=8 * 10**9, bytes_accessed=2 * 10**7, transcendentals=0),
         name="feed_weights",
-    )(table, *received, *grad_pre, *grad_rows, *acts)
-
-
-def fold_kernel(axes, scal, *refs):
-    count = len(axes)
-    for n, axis in enumerate(axes):
-        parts = refs[4 * n : 4 * n + 4]
-        outs = refs[4 * (count + n) : 4 * (count + n) + 4]
-        total = refs[8 * count + n]
-        unit = total.shape[0] // 4
-        total[...] = sum(p[...].astype(F32) for p in parts)
-        place = scal[0, axis]
-        for hop in range(4):
-            at = pl.ds(pl.multiple_of(lax.rem(place + hop, 4) * unit, unit), unit)
-            outs[hop][...] = total[at, :].astype(BF16)
-
-
-def fold(table, groups, axes):
-    outs = []
-    for parts in groups:
-        rows, cols = parts[0].shape
-        outs += [like((rows // 4, cols), BF16)] * 4
-    scratch = [pltpu.VMEM(parts[0].shape, F32) for parts in groups]
-    args = [table] + [p for parts in groups for p in parts]
-    places = tuple({"x": 11, "y": 12}[axis] for axis in axes)
-    res = call("fold", functools.partial(fold_kernel, places), outs, args, scratch, smem=(0,), vmem=60)
-    return [list(res[4 * n : 4 * n + 4]) for n in range(len(groups))]
-
-
-def last_sum_kernel(count, *refs):
-    for n in range(count):
-        total = sum(p[...].astype(F32) for p in refs[4 * n : 4 * n + 4])
-        refs[4 * count + n][...] = total.astype(refs[4 * count + n].dtype)
-
-
-def last_sum(groups, dtypes):
-    outs = [like(parts[0].shape, dtype) for parts, dtype in zip(groups, dtypes)]
-    args = [p for parts in groups for p in parts]
-    return call("last_sum", functools.partial(last_sum_kernel, len(groups)), outs, args, vmem=60)
+    )(*received, *grad_pre, *grad_rows, *acts)
 
 
 def first_norm_kernel(block, gain, depth, wide, normed, payload, tail):
@@ -981,6 +1039,8 @@
         line = iota((8, LANES), 1)
         chunks = (reach.astype(I32) + (SPAN - 1)) // SPAN
         packed = (total + (TOK - 1)) // TOK
+        short = (line == packed - 1) & (total - (packed - 1) * TOK <= TOK // 2)
+        chunks = jnp.where(short, SMALL, chunks)
         table[...] = jnp.where(
             line < 8,
             chunks,
@@ -1010,6 +1070,7 @@
 
 def slot_plan_kernel(place, choices, depth, *outs):
     chip, core = place[0], place[1]
+    depth_col = turned_row(depth[...])
     lanes = iota((TOK, LANES), 1)
     before = onehot(iota((TOK, TOK), 1) < iota((TOK, TOK), 0))
     hop = (lanes // 2 - chip + CHIPS) % CHIPS
@@ -1017,7 +1078,7 @@
     for s in range(3):
         turned = jnp.concatenate([choices[s].astype(F32), jnp.zeros((6, TOK), F32)], 0).T
         choice = turned.astype(I32)
-        live = depth[...] > s
+        live = depth_col > s
         names = [lanes == choice[:, k : k + 1] for k in range(2)]
         hits = jnp.where((names[0] | names[1]) & live, 1.0, 0.0)
         spot = nn(before, hits.astype(BF16)) + start.astype(F32)
@@ -1032,7 +1093,7 @@
 
 def slot_plan(place, choices, depth):
     outs = [like((TOK, LANES), I32), like((8, TOK), I32)] * 3
-    res = call("slot_plan", slot_plan_kernel, outs, [place, choices, depth], smem=(0,), vmem=60)
+    res = call("slot_plan", slot_plan_kernel, outs, [place, choices, depth], smem=(0,))
     return list(res[0::2]), list(res[1::2])
 
 
@@ -1135,7 +1196,7 @@
     p1 = jax.nn.sigmoid(row_sum(first * vector))
     p2 = jax.nn.sigmoid(row_sum(second * vector))
     a1, a2, a3 = row_sum(first * grad), row_sum(second * grad), row_sum(third * grad)
-    steps = depth[...]
+    steps = turned_row(depth[...])
     one, two, three = steps == 1, steps == 2, steps == 3
     c1 = jnp.where(one, 1.0, p1)
     c2 = jnp.where(one, 0.0, jnp.where(two, 1.0 - p1, p2 * (1.0 - p1)))
@@ -1260,16 +1321,8 @@
     return [rows] + [shift_chip(rows, d) for d in (1, 2, 3)]
 
 
-def shift_x(rows, hops):
-    return lax.ppermute(rows, "dp", [(i, (i + 4 * hops) % 16) for i in range(16)])
-
-
-def shift_y(rows, hops):
-    return lax.ppermute(rows, "dp", [(i, i // 4 * 4 + (i + hops) % 4) for i in range(16)])
-
-
-def go(shift, blocks):
-    return [blocks[0]] + [shift(blocks[d], d) for d in (1, 2, 3)]
+def dp_move(blocks):
+    return lax.all_to_all(blocks, "dp", split_axis=0, concat_axis=0, tiled=True)
 
 
 def block_sum(blocks):
@@ -1301,13 +1354,14 @@
     halt = halt_weight[None, :]
     router_a = jnp.pad(moa_router.T, ((0, LANES - 8), (0, 0)))
     router_b = jnp.pad(moe_router.T, ((0, LANES - 8), (0, 0)))
-    depth = depths[:, None]
+    depth = depths[None, :]
     moa_rows, moe_rows = moa_choice.swapaxes(1, 2), moe_choice.swapaxes(1, 2)
 
-    state, normed, payload = first_norm(block_input, gain_a, depths[None, :])
+    state, normed, payload = first_norm(block_input, gain_a, depth)
     same = spread_rows(payload)
-    plan = attend_plan((0,), place, moa_rows, ())
-    same[1], plan[0]["table"] = after(same[1], plan[0]["table"])
+    same[1], place_late = after(same[1], place)
+    plan = attend_plan((0,), place_late, moa_rows, ())
+    same[2], plan[0]["table"] = after(same[2], plan[0]["table"])
     query_w = [query_proj[0], swap_core(query_proj[0])]
     out_w = [out_proj[0], swap_core(out_proj[0])]
     other = [swap_core(rows) for rows in same]
@@ -1323,29 +1377,25 @@
         p = plan[s]
         res = attend(
             p["table"], same, other, key_proj, value_proj, query_w, out_w, router_a, p,
-            32 if s else 60,
+            60,
         )
-        parts = list(res[:4])
+        parts = send_blocks(res[:4])
         if s == 0:
-            parts[0], place_late = after(parts[0], place)
+            parts[1], place_late = after(parts[1], place)
             slot_cols, slot_rows = slot_plan(place_late, moe_rows, depth)
-            parts[3], slot_cols[0] = after(parts[3], slot_cols[0])
+            parts[2], slot_cols[0] = after(parts[2], slot_cols[0])
             win = [ffn_in[0], swap_core(ffn_in[0])]
             wout = [ffn_out[0], swap_core(ffn_out[0])]
             tails = (*same, *other)
-        parts = send_blocks(parts)
         mixed, normed_b, gates, *sends = dispatch(
             state, parts, gain_b, router_b, slot_rows[s], slot_cols[s]
         )
-        if s == 0:
-            plan = plan + attend_plan((1,), place, moa_rows, tails)
-            sends[3], plan[1]["table"] = after(sends[3], plan[1]["table"])
-        sends = send_blocks(sends)
-        *sends, mine, others = feed(sends, win, wout)
-        if s == 0:
-            plan = plan + attend_plan((2,), place, moa_rows, tails)
-            sends[3], plan[2]["table"] = after(sends[3], plan[2]["table"])
+        *sends, mine, others = feed(send_blocks(sends), win, wout)
         returned = return_blocks(sends)
+        if s < 2:
+            returned[1], place_late = after(returned[1], place)
+            plan = plan + attend_plan((s + 1,), place_late, moa_rows, tails)
+            returned[2], plan[s + 1]["table"] = after(returned[2], plan[s + 1]["table"])
         *saved, spread_0, spread_1, lse, weights = res[4:]
         kept.append(
             dict(
@@ -1363,7 +1413,7 @@
     output, coefs, tiny, upstream, grad_z, gate_grads, *sends = turn(
         mixed, state, gates, slot_cols[2], slot_rows[2], returned, states[1], halt, depth, cotangent
     )
-    expert_acc = shared_acc = None
+    expert_acc = shared_acc = pending = None
     received, acts, grad_pres, grad_rows = [], [], [], []
     for s in (2, 1, 0):
         k, p = kept[s], plan[s]
@@ -1372,58 +1422,55 @@
             send_blocks(sends), k["received"], win, wout
         )
         back = return_blocks(sends)
+        if pending and s:
+            back[1], grad_k = after(back[1], pending[1])
+            shared_acc = shared_weights(pending[0], grad_k, pending[2], shared_acc)
+            back[2], shared_acc = after(back[2], shared_acc)
         received += k["received_all"]
         acts += [act_0, swap_core(act_1)]
         grad_pres += [pre_0, swap_core(pre_1)]
         grad_rows += [rows_0, swap_core(rows_1)]
+        if s == 0:
+            feed_grads = feed_weights(received, grad_rows, acts, grad_pres)
+            back[2], feed_grads = after(back[2], feed_grads)
+            feed_grads = dp_move(feed_grads)
         grad_mixed, grad_low, tiny = moe_back(
             back, slot_cols[s], k["gates"], gate_grads, k["normed_b"], router_b, k["mixed"],
             gain_b, grad_z, tiny,
         )
         limit = 20 if s else 60
+        arrived = spread_rows(grad_low)
         if s == 0:
-            blocks = feed_weights(table, received, grad_rows, acts, grad_pres)
-            grad_low, *blocks = lax.optimization_barrier((grad_low, *blocks))
-            grads_in, grads_out = go(shift_x, blocks[:4]), go(shift_y, blocks[4:])
+            arrived[1], grad_k = after(arrived[1], pending[1])
+            shared_acc = shared_weights(pending[0], grad_k, pending[2], shared_acc, 60)
+            arrived[2], shared_acc = after(arrived[2], shared_acc)
         *same, other, y_0, y_1, q_0, q_1, grad_k, grad_v, tiny = attend_back(
-            table, spread_rows(grad_low), k["attend"], key_proj, value_proj, query_w, out_w, p,
+            table, arrived, k["attend"], key_proj, value_proj, query_w, out_w, p,
             (k["rows"], router_a, gain_a, tiny), 36 if s else 60,
         )
-        if s == 0:
-            other, y_1, q_0, q_1, grad_k, *arrived = lax.optimization_barrier(
-                (other, y_1, q_0, q_1, grad_k, *grads_in[1:], *grads_out[1:])
-            )
-            grads_in[1:], grads_out[1:] = arrived[:3], arrived[3:]
         other = swap_core(other)
         if s:
-            parts = pair_sum(same, other, limit)
-            q_0, grad_k, *parts = lax.optimization_barrier((q_0, grad_k, *parts))
-        expert_acc = expert_weights(
-            table, k["rows"], k["mixes"], (y_0, swap_core(y_1)), (q_0, swap_core(q_1)),
-            expert_acc, s == 0, limit,
-        )
+            parts = send_blocks(pair_sum(same, other, limit))
+            parts[1], q_0 = after(parts[1], q_0)
         if s:
-            shared_acc = shared_weights(k["rows"], grad_k, grad_v, shared_acc)
-            parts = send_blocks(parts)
-            *parts, shared_acc, expert_acc = lax.optimization_barrier(
-                (*parts, shared_acc, expert_acc)
+            expert_acc = expert_weights(
+                table, k["rows"], k["mixes"], (y_0, swap_core(y_1)), (q_0, swap_core(q_1)),
+                expert_acc, False, 20,
             )
+            parts[2], expert_acc = after(parts[2], expert_acc)
+            pending = (k["rows"], grad_k, grad_v)
         else:
-            weights_last = shared_weights_last(
-                k["rows"], grad_k, grad_v, shared_acc, tiny, expert_acc
+            mine, others = shared_last(table, k["rows"], grad_k, grad_v, shared_acc, tiny)
+            shared = send_blocks(core_sum(mine, swap_core(others)))
+            parts = send_blocks(pair_sum(same, other, limit))
+            weights_last = last_weights(
+                table, k["rows"], k["mixes"], (y_0, swap_core(y_1)), (q_0, swap_core(q_1)),
+                expert_acc, shared,
             )
-            other, weights_last = lax.optimization_barrier((other, weights_last))
-            moved = lax.all_to_all(
-                weights_last.reshape(16, 32, -1), "dp", split_axis=0, concat_axis=0, tiled=True
+            weights_last, feed_grads, *parts = lax.optimization_barrier(
+                (weights_last, feed_grads, *parts)
             )
-            parts = send_blocks(pair_sum(same, other, limit))
-        if s == 0:
-            summed = block_sum(moved)
-            low = summed[:, 2 * WIDTH :].astype(BF16)
-            parts[1], low = after(parts[1], low)
-            shared = lax.all_to_all(
-                low.reshape(8, 4, SHARED), "expert", split_axis=0, concat_axis=0, tiled=True
-            )
+            moved = dp_move(weights_last)
         args = (k["state"], gain_a, slot_cols[s], upstream, grad_mixed)
         if s:
             b = kept[s - 1]
@@ -1435,22 +1482,21 @@
         else:
             (grad_input,) = retreat(s, parts, args, ())
 
-    grads_in, grads_out = fold(table, (grads_in, grads_out), "yx")
-    grads_in, grads_out = go(shift_y, grads_in), go(shift_x, grads_out)
-    grads_in[1], low = after(grads_in[1], low)
-    shared = block_sum(shared)
-    tiny = shared[:, 2 * WIDTH :]
-    grad_in, grad_out = last_sum((grads_in, grads_out), (F32, F32))
+    summed = block_sum(moved)
+    tiny = summed[72:76]
+    feed_grads = block_sum(feed_grads)
+    grad_in = feed_grads[:TOK].reshape(4, 32, PART).swapaxes(0, 1).reshape(32, FFN)
+    grad_out = feed_grads[TOK:]
     return (
         output,
         grad_input,
         tiny[:, 8],
         tiny[:, 24],
         tiny[:, :8],
-        shared[:, :WIDTH],
-        shared[:, WIDTH : 2 * WIDTH],
-        summed[:, :WIDTH][None],
-        summed[:, WIDTH : 2 * WIDTH][None],
+        summed[64:68],
+        summed[68:72],
+        summed[0:32][None],
+        summed[32:64][None],
         tiny[:, 16:24],
         grad_in[None],
         grad_out[None],

time: 566 us -> 524 us (0.926)
  waiting for transfers between devices: 113 us -> 85.9 us
  starting transfers between devices: 176 us -> 160 us
  Pallas kernels: 235 us -> 227 us
    ppermute x12 -> x0, starting transfers between devices: 26.4 us -> none  [the longest x6 14 us: shift_y(): lax.ppermute(rows, 'dp', [(i, i // 4 * 4 + (i + hops) % 4) for i in range...]
    ppermute x72 -> x75, waiting for transfers between devices: 80.8 us -> 64.7 us  [shift_chip(): lax.ppermute(rows, 'expert', [(i, (i + 2 * hops) % count) for i in range(...]
    pallas_call x28 -> x25, Pallas kernels: 68.4 us -> 53.6 us  [call(): pl.pallas_call(body, out_shape=tuple(outs), in_specs=[spec(i, smem, near)...]
    ppermute x72 -> x75, starting transfers between devices: 79 us -> 92.1 us  [shift_chip(): lax.ppermute(rows, 'expert', [(i, (i + 2 * hops) % count) for i in range(...]
    pallas_call x6 -> x8, Pallas kernels: 118 us -> 124 us  [call_any(): pl.pallas_call(kernel, out_shape=tuple(outs), in_specs=[pl.BlockSpec(memo...]
    unnamed x332 -> x330, local copies, waits for them, and re-layouts: 25.6 us -> 28.9 us
    ppermute x40 -> x41, waiting for transfers between devices: 12.3 us -> 9.48 us  [swap_core(): return lax.ppermute(rows, 'expert', [(i, i ^ 1) for i in range(2 * CHIPS)])]
    ppermute x40 -> x41, starting transfers between devices: 50.4 us -> 52.1 us  [swap_core(): return lax.ppermute(rows, 'expert', [(i, i ^ 1) for i in range(2 * CHIPS)])]
  transfers between devices with their start and end apart: 126 -> 118, of which waited for: 63 -> 56; matrix products, arithmetic and copies ran while one was open for 1% -> 1% of each run, Pallas kernels for 20% -> 23%
where the time goes in v3:
time: 524 us; the launch traced here: 514 us
  Pallas kernels  227 us (43%)
  starting transfers between devices  160 us (31%)
  waiting for transfers between devices  85.9 us (16%)
  local copies, waits for them, and re-layouts  34 us (6%)
    pallas_call x8, Pallas kernels, call_any(): pl.pallas_call(kernel, out_shape=tuple(outs), in_specs=[pl.BlockSpec(memo...  124 us
    ppermute x75, starting transfers between devices, shift_chip(): lax.ppermute(rows, 'expert', [(i, (i + 2 * hops) % count) for i in range(...  92.1 us
    ppermute x75, waiting for transfers between devices, shift_chip(): lax.ppermute(rows, 'expert', [(i, (i + 2 * hops) % count) for i in range(...  64.7 us
    pallas_call x25, Pallas kernels, call(): pl.pallas_call(body, out_shape=tuple(outs), in_specs=[spec(i, smem, near)...  53.6 us
    ppermute x41, starting transfers between devices, swap_core(): return lax.ppermute(rows, 'expert', [(i, i ^ 1) for i in range(2 * CHIPS)])  52.1 us
    unnamed x330, local copies, waits for them, and re-layouts  28.9 us
    pallas_call x3, Pallas kernels, feed_back(): pl.pallas_call(feed_back_kernel, in_specs=[NEAR] * 4 + [FAR] * 6, out_spe...  24.6 us
    all_to_all x2, starting transfers between devices, dp_move(): return lax.all_to_all(blocks, 'dp', split_axis=0, concat_axis=0, tiled=True)  16.2 us
  transfers between devices with their start and end apart: 118, of which 56 were waited for; matrix products, arithmetic and copies ran while one was open for 1% of the time, Pallas kernels for 23%

profile of v3, /device:TPU:1, one launch (start us, length us, event | category | flops | bytes accessed | tf_op | source)
XLA Modules:
  0.0 513.8 jit_solution(16278852513592132687)
XLA Ops:
  2.3 2.5 first_norm.1
  6.5 3.3 collective-permute-start
  14.2 2.5 collective-permute-done.refs_3_.refs_4_
  18.1 4.3 attend_plan.3
  27.8 19.3 %attend.3 = (bf16[128,512]{1,0:T(8,128)(2,1)}, bf16[128,512]{1,0:T(8,128)(2,1)}, bf16[128,512]{1,0:T(8,128)(2,1)}, bf16[128,512]{1,0:T(8,128)(2,1)}, bf16[1024,5...) custom-call(s32[8,128]{1,0:T(8,128)} %get-tuple-element.279.refs_0_,, ...), custom_call_target="tpu_custom_call" | custom-call | flops 6000000000 | bytes 12668928 | tf_op jit(solution)/shard_map/attend/pallas_call | solution.py:178
  51.1 3.4 collective-permute-done.9.refs_2_
  54.5 2.4 slot_plan.1
  61.4 2.4 collective-permute-start.13
  64.4 2.9 collective-permute-done.13.refs_2_
  69.1 4.9 feed.3
  78.0 5.3 %attend_plan.4 = (s32[8,128]{1,0:T(8,128)}, f32[512,128]{1,0:T(8,128)}, s32[8,512]{1,0:T(8,128)}, s32[512,128]{1,0:T(8,128)}, s32[1024,128]{1,0:T(8,128)}) custom-call(s32[4]{0:T(128)} %pad_add_fusion.refs_0_, s32[3,4,1024]{2,1,0:T(4,128)} %bitcast.79, bf16[144,512]{1,0:T(8,128)(2,1)} %get-tuple-element.276.refs_1_.refs_2_, bf16[144,512]{1,0:T(8,128)(2,1)} %copy-done.138, ...), custom_call_target="tpu_custom_call" | custom-call | flops 1000000000 | bytes 2297872 | tf_op jit(solution)/shard_map/attend_plan/pallas_call | solution.py:145
  84.9 3.0 collective-permute-start.21
  88.2 5.8 %collective-permute-start.23 = (bf16[128,512]{1,0:T(8,128)(2,1)S(1)}, bf16[128,512]{1,0:T(8,128)(2,1)S(1)}, u32[]{:S(2)}, u32[]{:S(2)}) collective-permute-start(bf16[128,512]{1,0:T(8,128)(2,1)S(1)} %get-tuple-element.312.refs_1_), channel_id=1, source_target_pairs={{0,1},{1,0},{2,3},{3,2},{4,5},{5,4},{6,7},{7,6},{8,9},{9,8},{10,11... | collective-permute-start | bytes 393224 | tf_op jit(solution)/shard_map/ppermute | solution.py:1300
  95.5 2.9 collective-permute-start.25
  100.6 15.7 %attend.4 = (bf16[128,512]{1,0:T(8,128)(2,1)}, bf16[128,512]{1,0:T(8,128)(2,1)}, bf16[128,512]{1,0:T(8,128)(2,1)}, bf16[128,512]{1,0:T(8,128)(2,1)}, bf16[1024,5...) custom-call(s32[8,128]{1,0:T(8,128)} %get-tuple-element.311.refs_0_,, ...), custom_call_target="tpu_custom_call" | custom-call | flops 6000000000 | bytes 12537856 | tf_op jit(solution)/shard_map/attend/pallas_call | solution.py:178
  116.4 2.4 collective-permute-start.28
  122.1 3.0 collective-permute-done.28.refs_3_
  127.4 2.3 collective-permute-start.30
  129.6 2.4 collective-permute-start.31
  132.7 2.6 collective-permute-done.31.refs_2_
  137.8 5.5 %feed.4 = (bf16[80,512]{1,0:T(8,128)(2,1)S(1)}, bf16[80,512]{1,0:T(8,128)(2,1)S(1)}, bf16[80,512]{1,0:T(8,128)(2,1)}, bf16[80,512]{1,0:T(8,128)(2,1)S(1)}, bf16[...) custom-call(bf16[80,512]{1,0:T(8,128)(2,1)S(1)} %get-tuple-element.325.refs_0_, ...), custom_call_target="tpu_custom_call" | custom-call | flops 2000000000 | bytes 10000000 | tf_op jit(solution)/shard_map/feed/pallas_call | solution.py:834
  148.7 5.3 %attend_plan.5 = (s32[8,128]{1,0:T(8,128)}, f32[512,128]{1,0:T(8,128)}, s32[8,512]{1,0:T(8,128)}, s32[512,128]{1,0:T(8,128)}, s32[1024,128]{1,0:T(8,128)}) custom-call(s32[4]{0:T(128)} %pad_add_fusion.refs_0_, s32[3,4,1024]{2,1,0:T(4,128)} %bitcast.80, bf16[144,512]{1,0:T(8,128)(2,1)} %get-tuple-element.276.refs_1_.refs_2_, bf16[144,512]{1,0:T(8,128)(2,1)} %copy-done.138, ...), custom_call_target="tpu_custom_call" | custom-call | flops 1000000000 | bytes 2297872 | tf_op jit(solution)/shard_map/attend_plan/pallas_call | solution.py:145
  155.3 3.9 collective-permute-start.37
  159.2 3.3 collective-permute-start.39
  162.5 2.6 collective-permute-start.40
  169.1 13.1 %attend.5 = (bf16[128,512]{1,0:T(8,128)(2,1)}, bf16[128,512]{1,0:T(8,128)(2,1)}, bf16[128,512]{1,0:T(8,128)(2,1)}, bf16[128,512]{1,0:T(8,128)(2,1)}, bf16[1024,5...) custom-call(s32[8,128]{1,0:T(8,128)} %get-tuple-element.338.refs_0_,, ...), custom_call_target="tpu_custom_call" | custom-call | flops 6000000000 | bytes 12537856 | tf_op jit(solution)/shard_map/attend/pallas_call | solution.py:178
  182.3 2.6 collective-permute-start.44
  186.3 2.6 collective-permute-done.43.refs_2_
  193.5 2.4 collective-permute-start.46
  198.7 2.8 collective-permute-done.47.refs_2_
  203.7 4.9 feed.5
  208.6 2.2 collective-permute-start.49
  213.1 2.6 collective-permute-done.50.refs_7_
  221.3 2.4 collective-permute-done.52.refs_1_
  224.5 8.3 %feed_back.3 = (bf16[80,512]{1,0:T(8,128)(2,1)S(1)}, bf16[80,512]{1,0:T(8,128)(2,1)S(1)}, bf16[80,512]{1,0:T(8,128)(2,1)S(1)}, bf16[80,512]{1,0:T(8,128)(2,1)S(1...) custom-call(bf16[80,512]{1,0:T(8,128)(2,1)S(1)} %get-tuple-element.3, ...), custom_call_target="tpu_custom_call" | custom-call | flops 3000000000 | bytes 10000000 | tf_op jit(solution)/shard_map/feed_back/pallas_call | solution.py:889
  232.9 2.4 collective-permute-start.55
  237.6 2.6 collective-permute-done.56.refs_2_
  245.3 2.4 collective-permute-done.58.refs_2_
  250.9 17.7 %attend_back.3 = (bf16[128,512]{1,0:T(8,128)(2,1)S(1)}, bf16[128,512]{1,0:T(8,128)(2,1)S(1)}, bf16[128,512]{1,0:T(8,128)(2,1)S(1)}, bf16[128,512]{1,0:T(8,128)(2...) custom-call(s32[8,128]{1,0:T(8,128)S(1)} %copy-done.115, ...), custom_call_target="tpu_custom_call" | custom-call | flops 99999997952 | bytes 16996352 | tf_op jit(solution)/shard_map/attend_back/pallas_call | solution.py:178
  269.6 7.4 %collective-permute-start.61 = (bf16[4,128,512]{2,1,0:T(8,128)(2,1)S(1)}, bf16[4,128,512]{2,1,0:T(8,128)(2,1)S(1)}, u32[]{:S(2)}, u32[]{:S(2)}) collective-permute-start(bf16[4,128,512]{2,1,0:T(8,128)(2,1)S(1)} %get-tuple-element.391), channel_id=1, source_target_pairs={{0,1},{1,0},{2,3},{3,2},{4,5},{5,4},{6,7},{7,6},{8,9},{9,8},{10,11... | collective-permute-start | bytes 1572872 | tf_op jit(solution)/shard_map/ppermute | solution.py:1300
  279.8 2.5 collective-permute-start.63
  282.3 2.3 collective-permute-done.62.refs_1_
  285.9 2.4 expert_weights.2.refs_8_
  288.8 2.2 retreat.3
  291.1 3.3 collective-permute-start.69
  298.0 8.2 %feed_back.4 = (bf16[80,512]{1,0:T(8,128)(2,1)S(1)}, bf16[80,512]{1,0:T(8,128)(2,1)S(1)}, bf16[80,512]{1,0:T(8,128)(2,1)S(1)}, bf16[80,512]{1,0:T(8,128)(2,1)S(1...) custom-call(bf16[80,512]{1,0:T(8,128)(2,1)S(1)} %get-tuple-element.4, ...), custom_call_target="tpu_custom_call" | custom-call | flops 3000000000 | bytes 10000000 | tf_op jit(solution)/shard_map/feed_back/pallas_call | solution.py:889
  317.2 3.5 collective-permute-start.75
  321.8 2.6 collective-permute-done.75.refs_3_
  324.6 19.3 %attend_back.4 = (bf16[128,512]{1,0:T(8,128)(2,1)S(1)}, bf16[128,512]{1,0:T(8,128)(2,1)S(1)}, bf16[128,512]{1,0:T(8,128)(2,1)S(1)}, bf16[128,512]{1,0:T(8,128)(2...) custom-call(s32[8,128]{1,0:T(8,128)S(1)} %copy-done.114, ...), custom_call_target="tpu_custom_call" | custom-call | flops 99999997952 | bytes 16996352 | tf_op jit(solution)/shard_map/attend_back/pallas_call | solution.py:178
  344.0 6.9 %collective-permute-start.77 = (bf16[4,128,512]{2,1,0:T(8,128)(2,1)S(1)}, bf16[4,128,512]{2,1,0:T(8,128)(2,1)S(1)}, u32[]{:S(2)}, u32[]{:S(2)}) collective-permute-start(bf16[4,128,512]{2,1,0:T(8,128)(2,1)S(1)} %get-tuple-element.440), channel_id=1, source_target_pairs={{0,1},{1,0},{2,3},{3,2},{4,5},{5,4},{6,7},{7,6},{8,9},{9,8},{10,11... | collective-permute-start | bytes 1572872 | tf_op jit(solution)/shard_map/ppermute | solution.py:1300
  355.3 3.3 collective-permute-done.78.refs_1_
  363.1 2.6 expert_weights.3.refs_4_
  367.1 2.2 retreat.4
  380.1 8.1 %feed_back.5 = (bf16[80,512]{1,0:T(8,128)(2,1)S(1)}, bf16[80,512]{1,0:T(8,128)(2,1)S(1)}, bf16[80,512]{1,0:T(8,128)(2,1)S(1)}, bf16[80,512]{1,0:T(8,128)(2,1)S(1...) custom-call(bf16[80,512]{1,0:T(8,128)(2,1)S(1)} %get-tuple-element.4, ...), custom_call_target="tpu_custom_call" | custom-call | flops 3000000000 | bytes 10000000 | tf_op jit(solution)/shard_map/feed_back/pallas_call | solution.py:889
  392.2 2.4 collective-permute-done.96.refs_15_
  400.0 9.5 %feed_weights.1 = bf16[16,256,512]{2,1,0:T(8,128)(2,1)} custom-call(bf16[160,512]{1,0:T(8,128)(2,1)} %copy-done.66, bf16[160,512]{1,0:T(8,128)(2,1)} %copy-done.134, bf16[160,512]{1,0:T(8,128)(2,1)} %copy-done.62, bf16[160,512]{1,0:T(8,128)(2,1)} %copy-done.133, bf16[160,512]{1,0:T(8,128)(2,1)} %copy-done.58, bf16[160,512]{1,0:T(8,128)(2,1)} %copy-done.132, ...), custom_call_target="tpu_custom_call" | custom-call | flops 8000000000 | bytes 20000000 | tf_op jit(solution)/shard_map/feed_weights/pallas_call | solution.py:941
  414.6 8.6 %all-to-all-start = ((bf16[16,256,512]{2,1,0:T(8,128)(2,1)}), bf16[16,256,512]{2,1,0:T(8,128)(2,1)}, u32[]{:S(2)}, u32[]{:S(2)}) async-start(bf16[16,256,512]{2,1,0:T(8,128)(2,1)} %feed_weights.1), calls=%async_computation | async-start | bytes 8388608 | tf_op jit(solution)/shard_map/all_to_all | solution.py:1325
  423.2 5.2 %shared_weights.3.refs_3_ = f32[512,1024]{1,0:T(8,128)} custom-call(bf16[1024,512]{1,0:T(8,128)(2,1)} %get-tuple-element.434.refs_22_.refs_1_.refs_0_, bf16[1024,512]{1,0:T(8,128)(2,1)} %copy-done.87, bf16[1024,512]{1,0:T(8,128)(2,1)} %copy-done.88, f32[512,1024]{1,0:T(8,128)} %copy-done.83), custom_call_target="tpu_custom_call" | custom-call | flops 3000000000 | bytes 7340032 | tf_op jit(solution)/shard_map/shared_weights/pallas_call | solution.py:145
  429.2 26.0 %attend_back.5 = (bf16[128,512]{1,0:T(8,128)(2,1)}, bf16[128,512]{1,0:T(8,128)(2,1)}, bf16[128,512]{1,0:T(8,128)(2,1)}, bf16[128,512]{1,0:T(8,128)(2,1)}, bf16[4...) custom-call(s32[8,128]{1,0:T(8,128)} %get-tuple-element.279.refs_0_,, ...), custom_call_target="tpu_custom_call" | custom-call | flops 99999997952 | bytes 16996352 | tf_op jit(solution)/shard_map/attend_back/pallas_call | solution.py:178
  455.3 6.7 %shared_last.1 = (bf16[4,64,1152]{2,1,0:T(8,128)(2,1)}, bf16[4,64,1152]{2,1,0:T(8,128)(2,1)}) custom-call(s32[8,128]{1,0:T(8,128)} %get-tuple-element.279.refs_0_, bf16[1024,512]{1,0:T(8,128)(2,1)} %get-tuple-element.361.refs_22_.refs_1_, bf16[1024,512]{1,0:T(8,128)(2,1)} %get-tuple-element.509.refs_2_, f32[512,1024]{1,0:T(8,128)} %shared_weights.3.refs_3_, ...), custom_call_target="tpu_custom_call" | custom-call | flops 4000000000 | bytes 6688768 | tf_op jit(solution)/shard_map/shared_last/pallas_call | solution.py:178
  479.6 6.1 %last_weights.1 = bf16[16,80,512]{2,1,0:T(8,128)(2,1)} custom-call(s32[8,128]{1,0:T(8,128)} %get-tuple-element.279.refs_0_, bf16[1024,512]{1,0:T(8,128)(2,1)} %get-tuple-element.361.refs_22_.refs_1_, bf16[512,512]{1,0:T(8,128)(2,1)} %get-tuple-element.504.refs_2_, bf16[512,512]{1,0:T(8,128)(2,1)} %collective-permute-done.105.refs_3_, ...), custom_call_target="tpu_custom_call" | custom-call | flops 4000000000 | bytes 8196096 | tf_op jit(solution)/shard_map/last_weights/pallas_call | solution.py:178
  485.7 7.5 %all-to-all-start.1 = ((bf16[16,80,512]{2,1,0:T(8,128)(2,1)}), bf16[16,80,512]{2,1,0:T(8,128)(2,1)S(1)}, u32[]{:S(2)}, u32[]{:S(2)}) async-start(bf16[16,80,512]{2,1,0:T(8,128)(2,1)} %last_weights.1), calls=%async_computation.1 | async-start | bytes 2621440 | tf_op jit(solution)/shard_map/all_to_all | solution.py:1325
  493.2 2.8 convert_reduce_fusion
  499.1 11.7 %all-to-all-done.1 = bf16[16,80,512]{2,1,0:T(8,128)(2,1)S(1)} async-done(((bf16[16,80,512]{2,1,0:T(8,128)(2,1)}), bf16[16,80,512]{2,1,0:T(8,128)(2,1)S(1)}, u32[]{:S(2)}, u32[]{:S(2)}) %all-to-all-start.1) | async-done | bytes 1310752 | tf_op jit(solution)/shard_map/all_to_all | solution.py:1325
  (554 shorter events, 164.5 us)
Async XLA Ops:
  0.7 66.9 %collective-permute-start.15 = (bf16[512,2048]{1,0:T(8,128)(2,1)}, bf16[512,2048]{1,0:T(8,128)(2,1)}, u32[]{:S(2)}, u32[]{:S(2)}) collective-permute-start(bf16[512,2048]{1,0:T(8,128)(2,1)} %bitcast.25), channel_id=1, source_target_pairs={{0,1},{1,0},{2,3},{3,2},{4,5},{5,4},{6,7},{7,6},{8,9},{9,8},{10,11... | collective-permute-start | bytes 6291464 | tf_op jit(solution)/shard_map/ppermute | solution.py:1300
  2.2 65.4 %collective-permute-start.16 = (bf16[2048,512]{1,0:T(8,128)(2,1)}, bf16[2048,512]{1,0:T(8,128)(2,1)}, u32[]{:S(2)}, u32[]{:S(2)}) collective-permute-start(bf16[2048,512]{1,0:T(8,128)(2,1)} %bitcast.32), channel_id=1, source_target_pairs={{0,1},{1,0},{2,3},{3,2},{4,5},{5,4},{6,7},{7,6},{8,9},{9,8},{10,11... | collective-permute-start | bytes 6291464 | tf_op jit(solution)/shard_map/ppermute | solution.py:1300
  4.7 8.0 %collective-permute-start.1 = (bf16[144,512]{1,0:T(8,128)(2,1)}, bf16[144,512]{1,0:T(8,128)(2,1)S(1)}, u32[]{:S(2)}, u32[]{:S(2)}) collective-permute-start(bf16[144,512]{1,0:T(8,128)(2,1)} %get-tuple-element.276.refs_1_.refs_2_), channel_id=1, source_target_pairs={{0,2},{1,3},{2,4},{3,5},{4,6},{5,7},{6,0},{7,1},{8,10},{9,11},{10,... | collective-permute-start | bytes 442376 | tf_op jit(solution)/shard_map/ppermute | solution.py:1305
  6.5 10.2 %collective-permute-start = (bf16[144,512]{1,0:T(8,128)(2,1)}, bf16[144,512]{1,0:T(8,128)(2,1)S(1)}, u32[]{:S(2)}, u32[]{:S(2)}) collective-permute-start(bf16[144,512]{1,0:T(8,128)(2,1)} %get-tuple-element.276.refs_1_.refs_2_), channel_id=1, source_target_pairs={{0,4},{1,5},{2,6},{3,7},{4,0},{5,1},{6,2},{7,3},{8,12},{9,13},{10,... | collective-permute-start | bytes 442376 | tf_op jit(solution)/shard_map/ppermute | solution.py:1305
  9.8 8.2 %collective-permute-start.2 = (bf16[144,512]{1,0:T(8,128)(2,1)}, bf16[144,512]{1,0:T(8,128)(2,1)S(1)}, u32[]{:S(2)}, u32[]{:S(2)}) collective-permute-start(bf16[144,512]{1,0:T(8,128)(2,1)} %get-tuple-element.276.refs_1_.refs_2_), channel_id=1, source_target_pairs={{0,6},{1,7},{2,0},{3,1},{4,2},{5,3},{6,4},{7,5},{8,14},{9,15},{10,... | collective-permute-start | bytes 442376 | tf_op jit(solution)/shard_map/ppermute | solution.py:1305
  12.7 9.6 %collective-permute-start.3 = (bf16[144,512]{1,0:T(8,128)(2,1)}, bf16[144,512]{1,0:T(8,128)(2,1)S(1)}, u32[]{:S(2)}, u32[]{:S(2)}) collective-permute-start(bf16[144,512]{1,0:T(8,128)(2,1)} %get-tuple-element.276.refs_1_.refs_2_), channel_id=1, source_target_pairs={{0,1},{1,0},{2,3},{3,2},{4,5},{5,4},{6,7},{7,6},{8,9},{9,8},{10,11... | collective-permute-start | bytes 442376 | tf_op jit(solution)/shard_map/ppermute | solution.py:1300
  16.7 9.9 %collective-permute-start.7 = (bf16[512,512]{1,0:T(8,128)(2,1)}, bf16[512,512]{1,0:T(8,128)(2,1)S(1)}, u32[]{:S(2)}, u32[]{:S(2)}) collective-permute-start(bf16[512,512]{1,0:T(8,128)(2,1)} %bitcast.61), channel_id=1, source_target_pairs={{0,1},{1,0},{2,3},{3,2},{4,5},{5,4},{6,7},{7,6},{8,9},{9,8},{10,11... | collective-permute-start | bytes 1572872 | tf_op jit(solution)/shard_map/ppermute | solution.py:1300
  18.0 8.6 %collective-permute-start.8 = (bf16[512,512]{1,0:T(8,128)(2,1)}, bf16[512,512]{1,0:T(8,128)(2,1)S(1)}, u32[]{:S(2)}, u32[]{:S(2)}) collective-permute-start(bf16[512,512]{1,0:T(8,128)(2,1)} %bitcast.68), channel_id=1, source_target_pairs={{0,1},{1,0},{2,3},{3,2},{4,5},{5,4},{6,7},{7,6},{8,9},{9,8},{10,11... | collective-permute-start | bytes 1572872 | tf_op jit(solution)/shard_map/ppermute | solution.py:1300
  47.2 7.4 %collective-permute-start.9 = (bf16[128,512]{1,0:T(8,128)(2,1)}, bf16[128,512]{1,0:T(8,128)(2,1)S(1)}, u32[]{:S(2)}, u32[]{:S(2)}) collective-permute-start(bf16[128,512]{1,0:T(8,128)(2,1)} %get-tuple-element.287), channel_id=1, source_target_pairs={{0,2},{1,3},{2,4},{3,5},{4,6},{5,7},{6,0},{7,1},{8,10},{9,11},{10,... | collective-permute-start | bytes 393224 | tf_op jit(solution)/shard_map/ppermute | solution.py:1305
  47.3 9.7 %collective-permute-start.10 = (bf16[128,512]{1,0:T(8,128)(2,1)}, bf16[128,512]{1,0:T(8,128)(2,1)S(1)}, u32[]{:S(2)}, u32[]{:S(2)}) collective-permute-start(bf16[128,512]{1,0:T(8,128)(2,1)} %get-tuple-element.289), channel_id=1, source_target_pairs={{0,4},{1,5},{2,6},{3,7},{4,0},{5,1},{6,2},{7,3},{8,12},{9,13},{10,... | collective-permute-start | bytes 393224 | tf_op jit(solution)/shard_map/ppermute | solution.py:1305
  49.4 7.6 %collective-permute-start.11 = (bf16[128,512]{1,0:T(8,128)(2,1)}, bf16[128,512]{1,0:T(8,128)(2,1)S(1)}, u32[]{:S(2)}, u32[]{:S(2)}) collective-permute-start(bf16[128,512]{1,0:T(8,128)(2,1)} %get-tuple-element.293), channel_id=1, source_target_pairs={{0,6},{1,7},{2,0},{3,1},{4,2},{5,3},{6,4},{7,5},{8,14},{9,15},{10,... | collective-permute-start | bytes 393224 | tf_op jit(solution)/shard_map/ppermute | solution.py:1305
  75.9 7.4 %collective-permute-start.18 = (bf16[80,512]{1,0:T(8,128)(2,1)S(1)}, bf16[80,512]{1,0:T(8,128)(2,1)S(1)}, u32[]{:S(2)}, u32[]{:S(2)}) collective-permute-start(bf16[80,512]{1,0:T(8,128)(2,1)S(1)} %get-tuple-element.305), channel_id=1, source_target_pairs={{0,4},{1,5},{2,6},{3,7},{4,0},{5,1},{6,2},{7,3},{8,12},{9,13},{10,... | collective-permute-start | bytes 245768 | tf_op jit(solution)/shard_map/ppermute | solution.py:1305
  76.7 6.7 %collective-permute-start.19 = (bf16[80,512]{1,0:T(8,128)(2,1)S(1)}, bf16[80,512]{1,0:T(8,128)(2,1)S(1)}, u32[]{:S(2)}, u32[]{:S(2)}) collective-permute-start(bf16[80,512]{1,0:T(8,128)(2,1)S(1)} %get-tuple-element.309), channel_id=1, source_target_pairs={{0,2},{1,3},{2,4},{3,5},{4,6},{5,7},{6,0},{7,1},{8,10},{9,11},{10,... | collective-permute-start | bytes 245768 | tf_op jit(solution)/shard_map/ppermute | solution.py:1305
  84.3 9.7 %collective-permute-start.20 = (bf16[128,512]{1,0:T(8,128)(2,1)S(1)}, bf16[128,512]{1,0:T(8,128)(2,1)S(1)}, u32[]{:S(2)}, u32[]{:S(2)}) collective-permute-start(bf16[128,512]{1,0:T(8,128)(2,1)S(1)} %get-tuple-element.312.refs_1_), channel_id=1, source_target_pairs={{0,2},{1,3},{2,4},{3,5},{4,6},{5,7},{6,0},{7,1},{8,10},{9,11},{10,... | collective-permute-start | bytes 393224 | tf_op jit(solution)/shard_map/ppermute | solution.py:1305
  84.9 10.6 %collective-permute-start.21 = (bf16[128,512]{1,0:T(8,128)(2,1)S(1)}, bf16[128,512]{1,0:T(8,128)(2,1)S(1)}, u32[]{:S(2)}, u32[]{:S(2)}) collective-permute-start(bf16[128,512]{1,0:T(8,128)(2,1)S(1)} %get-tuple-element.312.refs_1_), channel_id=1, source_target_pairs={{0,4},{1,5},{2,6},{3,7},{4,0},{5,1},{6,2},{7,3},{8,12},{9,13},{10,... | collective-permute-start | bytes 393224 | tf_op jit(solution)/shard_map/ppermute | solution.py:1305
  87.9 10.4 %collective-permute-start.22 = (bf16[128,512]{1,0:T(8,128)(2,1)S(1)}, bf16[128,512]{1,0:T(8,128)(2,1)S(1)}, u32[]{:S(2)}, u32[]{:S(2)}) collective-permute-start(bf16[128,512]{1,0:T(8,128)(2,1)S(1)} %get-tuple-element.312.refs_1_), channel_id=1, source_target_pairs={{0,6},{1,7},{2,0},{3,1},{4,2},{5,3},{6,4},{7,5},{8,14},{9,15},{10,... | collective-permute-start | bytes 393224 | tf_op jit(solution)/shard_map/ppermute | solution.py:1305
  88.2 10.8 %collective-permute-start.23 = (bf16[128,512]{1,0:T(8,128)(2,1)S(1)}, bf16[128,512]{1,0:T(8,128)(2,1)S(1)}, u32[]{:S(2)}, u32[]{:S(2)}) collective-permute-start(bf16[128,512]{1,0:T(8,128)(2,1)S(1)} %get-tuple-element.312.refs_1_), channel_id=1, source_target_pairs={{0,1},{1,0},{2,3},{3,2},{4,5},{5,4},{6,7},{7,6},{8,9},{9,8},{10,11... | collective-permute-start | bytes 393224 | tf_op jit(solution)/shard_map/ppermute | solution.py:1300
  116.4 8.7 %collective-permute-start.28 = (bf16[128,512]{1,0:T(8,128)(2,1)}, bf16[128,512]{1,0:T(8,128)(2,1)S(1)}, u32[]{:S(2)}, u32[]{:S(2)}) collective-permute-start(bf16[128,512]{1,0:T(8,128)(2,1)} %get-tuple-element.319), channel_id=1, source_target_pairs={{0,4},{1,5},{2,6},{3,7},{4,0},{5,1},{6,2},{7,3},{8,12},{9,13},{10,... | collective-permute-start | bytes 393224 | tf_op jit(solution)/shard_map/ppermute | solution.py:1305
  146.4 7.5 %collective-permute-start.34 = (bf16[80,512]{1,0:T(8,128)(2,1)}, bf16[80,512]{1,0:T(8,128)(2,1)S(1)}, u32[]{:S(2)}, u32[]{:S(2)}) collective-permute-start(bf16[80,512]{1,0:T(8,128)(2,1)} %get-tuple-element.332), channel_id=1, source_target_pairs={{0,4},{1,5},{2,6},{3,7},{4,0},{5,1},{6,2},{7,3},{8,12},{9,13},{10,... | collective-permute-start | bytes 245768 | tf_op jit(solution)/shard_map/ppermute | solution.py:1305
  146.4 7.6 %collective-permute-start.35 = (bf16[80,512]{1,0:T(8,128)(2,1)S(1)}, bf16[80,512]{1,0:T(8,128)(2,1)S(1)}, u32[]{:S(2)}, u32[]{:S(2)}) collective-permute-start(bf16[80,512]{1,0:T(8,128)(2,1)S(1)} %get-tuple-element.336), channel_id=1, source_target_pairs={{0,2},{1,3},{2,4},{3,5},{4,6},{5,7},{6,0},{7,1},{8,10},{9,11},{10,... | collective-permute-start | bytes 245768 | tf_op jit(solution)/shard_map/ppermute | solution.py:1305
  154.8 7.6 %collective-permute-start.36 = (bf16[128,512]{1,0:T(8,128)(2,1)S(1)}, bf16[128,512]{1,0:T(8,128)(2,1)S(1)}, u32[]{:S(2)}, u32[]{:S(2)}) collective-permute-start(bf16[128,512]{1,0:T(8,128)(2,1)S(1)} %get-tuple-element.339.refs_1_), channel_id=1, source_target_pairs={{0,2},{1,3},{2,4},{3,5},{4,6},{5,7},{6,0},{7,1},{8,10},{9,11},{10,... | collective-permute-start | bytes 393224 | tf_op jit(solution)/shard_map/ppermute | solution.py:1305
  155.3 9.8 %collective-permute-start.37 = (bf16[128,512]{1,0:T(8,128)(2,1)S(1)}, bf16[128,512]{1,0:T(8,128)(2,1)S(1)}, u32[]{:S(2)}, u32[]{:S(2)}) collective-permute-start(bf16[128,512]{1,0:T(8,128)(2,1)S(1)} %get-tuple-element.339.refs_1_), channel_id=1, source_target_pairs={{0,4},{1,5},{2,6},{3,7},{4,0},{5,1},{6,2},{7,3},{8,12},{9,13},{10,... | collective-permute-start | bytes 393224 | tf_op jit(solution)/shard_map/ppermute | solution.py:1305
  159.2 7.6 %collective-permute-start.38 = (bf16[128,512]{1,0:T(8,128)(2,1)S(1)}, bf16[128,512]{1,0:T(8,128)(2,1)S(1)}, u32[]{:S(2)}, u32[]{:S(2)}) collective-permute-start(bf16[128,512]{1,0:T(8,128)(2,1)S(1)} %get-tuple-element.339.refs_1_), channel_id=1, source_target_pairs={{0,6},{1,7},{2,0},{3,1},{4,2},{5,3},{6,4},{7,5},{8,14},{9,15},{10,... | collective-permute-start | bytes 393224 | tf_op jit(solution)/shard_map/ppermute | solution.py:1305
  159.2 8.2 %collective-permute-start.39 = (bf16[128,512]{1,0:T(8,128)(2,1)S(1)}, bf16[128,512]{1,0:T(8,128)(2,1)S(1)}, u32[]{:S(2)}, u32[]{:S(2)}) collective-permute-start(bf16[128,512]{1,0:T(8,128)(2,1)S(1)} %get-tuple-element.339.refs_1_), channel_id=1, source_target_pairs={{0,1},{1,0},{2,3},{3,2},{4,5},{5,4},{6,7},{7,6},{8,9},{9,8},{10,11... | collective-permute-start | bytes 393224 | tf_op jit(solution)/shard_map/ppermute | solution.py:1300
  182.2 6.7 %collective-permute-start.43 = (bf16[128,512]{1,0:T(8,128)(2,1)}, bf16[128,512]{1,0:T(8,128)(2,1)S(1)}, u32[]{:S(2)}, u32[]{:S(2)}) collective-permute-start(bf16[128,512]{1,0:T(8,128)(2,1)} %get-tuple-element.345), channel_id=1, source_target_pairs={{0,2},{1,3},{2,4},{3,5},{4,6},{5,7},{6,0},{7,1},{8,10},{9,11},{10,... | collective-permute-start | bytes 393224 | tf_op jit(solution)/shard_map/ppermute | solution.py:1305
  182.3 8.5 %collective-permute-start.44 = (bf16[128,512]{1,0:T(8,128)(2,1)}, bf16[128,512]{1,0:T(8,128)(2,1)S(1)}, u32[]{:S(2)}, u32[]{:S(2)}) collective-permute-start(bf16[128,512]{1,0:T(8,128)(2,1)} %get-tuple-element.346), channel_id=1, source_target_pairs={{0,4},{1,5},{2,6},{3,7},{4,0},{5,1},{6,2},{7,3},{8,12},{9,13},{10,... | collective-permute-start | bytes 393224 | tf_op jit(solution)/shard_map/ppermute | solution.py:1305
  269.6 8.9 %collective-permute-start.61 = (bf16[4,128,512]{2,1,0:T(8,128)(2,1)S(1)}, bf16[4,128,512]{2,1,0:T(8,128)(2,1)S(1)}, u32[]{:S(2)}, u32[]{:S(2)}) collective-permute-start(bf16[4,128,512]{2,1,0:T(8,128)(2,1)S(1)} %get-tuple-element.391), channel_id=1, source_target_pairs={{0,1},{1,0},{2,3},{3,2},{4,5},{5,4},{6,7},{7,6},{8,9},{9,8},{10,11... | collective-permute-start | bytes 1572872 | tf_op jit(solution)/shard_map/ppermute | solution.py:1300
  277.0 8.9 %collective-permute-start.64 = (bf16[512,512]{1,0:T(8,128)(2,1)S(1)}, bf16[512,512]{1,0:T(8,128)(2,1)S(1)}, u32[]{:S(2)}, u32[]{:S(2)}) collective-permute-start(bf16[512,512]{1,0:T(8,128)(2,1)S(1)} %copy-done.56), channel_id=1, source_target_pairs={{0,1},{1,0},{2,3},{3,2},{4,5},{5,4},{6,7},{7,6},{8,9},{9,8},{10,11... | collective-permute-start | bytes 1572872 | tf_op jit(solution)/shard_map/ppermute | solution.py:1300
  277.0 8.9 %collective-permute-start.65 = (bf16[512,512]{1,0:T(8,128)(2,1)S(1)}, bf16[512,512]{1,0:T(8,128)(2,1)S(1)}, u32[]{:S(2)}, u32[]{:S(2)}) collective-permute-start(bf16[512,512]{1,0:T(8,128)(2,1)S(1)} %get-tuple-element.398), channel_id=1, source_target_pairs={{0,1},{1,0},{2,3},{3,2},{4,5},{5,4},{6,7},{7,6},{8,9},{9,8},{10,11... | collective-permute-start | bytes 1572872 | tf_op jit(solution)/shard_map/ppermute | solution.py:1300
  277.5 8.4 %collective-permute-start.66 = (bf16[512,512]{1,0:T(8,128)(2,1)S(1)}, bf16[512,512]{1,0:T(8,128)(2,1)S(1)}, u32[]{:S(2)}, u32[]{:S(2)}) collective-permute-start(bf16[512,512]{1,0:T(8,128)(2,1)S(1)} %get-tuple-element.400), channel_id=1, source_target_pairs={{0,1},{1,0},{2,3},{3,2},{4,5},{5,4},{6,7},{7,6},{8,9},{9,8},{10,11... | collective-permute-start | bytes 1572872 | tf_op jit(solution)/shard_map/ppermute | solution.py:1300
  279.8 8.6 %collective-permute-start.63 = (bf16[128,512]{1,0:T(8,128)(2,1)S(1)}, bf16[128,512]{1,0:T(8,128)(2,1)S(1)}, u32[]{:S(2)}, u32[]{:S(2)}) collective-permute-start(bf16[128,512]{1,0:T(8,128)(2,1)S(1)} %get-tuple-element.396), channel_id=1, source_target_pairs={{0,4},{1,5},{2,6},{3,7},{4,0},{5,1},{6,2},{7,3},{8,12},{9,13},{10,... | collective-permute-start | bytes 393224 | tf_op jit(solution)/shard_map/ppermute | solution.py:1305
  317.2 7.2 %collective-permute-start.75 = (bf16[128,512]{1,0:T(8,128)(2,1)S(1)}, bf16[128,512]{1,0:T(8,128)(2,1)S(1)}, u32[]{:S(2)}, u32[]{:S(2)}) collective-permute-start(bf16[128,512]{1,0:T(8,128)(2,1)S(1)} %get-tuple-element.425.refs_1_), channel_id=1, source_target_pairs={{0,4},{1,5},{2,6},{3,7},{4,0},{5,1},{6,2},{7,3},{8,12},{9,13},{10,... | collective-permute-start | bytes 393224 | tf_op jit(solution)/shard_map/ppermute | solution.py:1305
  344.0 8.4 %collective-permute-start.77 = (bf16[4,128,512]{2,1,0:T(8,128)(2,1)S(1)}, bf16[4,128,512]{2,1,0:T(8,128)(2,1)S(1)}, u32[]{:S(2)}, u32[]{:S(2)}) collective-permute-start(bf16[4,128,512]{2,1,0:T(8,128)(2,1)S(1)} %get-tuple-element.440), channel_id=1, source_target_pairs={{0,1},{1,0},{2,3},{3,2},{4,5},{5,4},{6,7},{7,6},{8,9},{9,8},{10,11... | collective-permute-start | bytes 1572872 | tf_op jit(solution)/shard_map/ppermute | solution.py:1300
  350.9 9.7 %collective-permute-start.80 = (bf16[512,512]{1,0:T(8,128)(2,1)S(1)}, bf16[512,512]{1,0:T(8,128)(2,1)S(1)}, u32[]{:S(2)}, u32[]{:S(2)}) collective-permute-start(bf16[512,512]{1,0:T(8,128)(2,1)S(1)} %copy-done.55), channel_id=1, source_target_pairs={{0,1},{1,0},{2,3},{3,2},{4,5},{5,4},{6,7},{7,6},{8,9},{9,8},{10,11... | collective-permute-start | bytes 1572872 | tf_op jit(solution)/shard_map/ppermute | solution.py:1300
  351.0 9.7 %collective-permute-start.81 = (bf16[512,512]{1,0:T(8,128)(2,1)S(1)}, bf16[512,512]{1,0:T(8,128)(2,1)S(1)}, u32[]{:S(2)}, u32[]{:S(2)}) collective-permute-start(bf16[512,512]{1,0:T(8,128)(2,1)S(1)} %get-tuple-element.447), channel_id=1, source_target_pairs={{0,1},{1,0},{2,3},{3,2},{4,5},{5,4},{6,7},{7,6},{8,9},{9,8},{10,11... | collective-permute-start | bytes 1572872 | tf_op jit(solution)/shard_map/ppermute | solution.py:1300
  351.4 9.7 %collective-permute-start.82 = (bf16[512,512]{1,0:T(8,128)(2,1)S(1)}, bf16[512,512]{1,0:T(8,128)(2,1)S(1)}, u32[]{:S(2)}, u32[]{:S(2)}) collective-permute-start(bf16[512,512]{1,0:T(8,128)(2,1)S(1)} %get-tuple-element.449), channel_id=1, source_target_pairs={{0,1},{1,0},{2,3},{3,2},{4,5},{5,4},{6,7},{7,6},{8,9},{9,8},{10,11... | collective-permute-start | bytes 1572872 | tf_op jit(solution)/shard_map/ppermute | solution.py:1300
  353.8 7.6 %collective-permute-start.79 = (bf16[128,512]{1,0:T(8,128)(2,1)S(1)}, bf16[128,512]{1,0:T(8,128)(2,1)S(1)}, u32[]{:S(2)}, u32[]{:S(2)}) collective-permute-start(bf16[128,512]{1,0:T(8,128)(2,1)S(1)} %get-tuple-element.445), channel_id=1, source_target_pairs={{0,4},{1,5},{2,6},{3,7},{4,0},{5,1},{6,2},{7,3},{8,12},{9,13},{10,... | collective-permute-start | bytes 393224 | tf_op jit(solution)/shard_map/ppermute | solution.py:1305
  358.6 33.0 %collective-permute-start.92 = (bf16[160,2048]{1,0:T(8,128)(2,1)S(1)}, bf16[160,2048]{1,0:T(8,128)(2,1)S(1)}, u32[]{:S(2)}, u32[]{:S(2)}) collective-permute-start(bf16[160,2048]{1,0:T(8,128)(2,1)S(1)} %get-tuple-element.465), channel_id=1, source_target_pairs={{0,1},{1,0},{2,3},{3,2},{4,5},{5,4},{6,7},{7,6},{8,9},{9,8},{10,11... | collective-permute-start | bytes 1966088 | tf_op jit(solution)/shard_map/ppermute | solution.py:1300
  360.6 10.7 %collective-permute-start.91 = (bf16[160,512]{1,0:T(8,128)(2,1)S(1)}, bf16[160,512]{1,0:T(8,128)(2,1)S(1)}, u32[]{:S(2)}, u32[]{:S(2)}) collective-permute-start(bf16[160,512]{1,0:T(8,128)(2,1)S(1)} %copy-done.61), channel_id=1, source_target_pairs={{0,1},{1,0},{2,3},{3,2},{4,5},{5,4},{6,7},{7,6},{8,9},{9,8},{10,11... | collective-permute-start | bytes 491528 | tf_op jit(solution)/shard_map/ppermute | solution.py:1300
  360.7 12.8 %collective-permute-start.90 = (bf16[160,512]{1,0:T(8,128)(2,1)S(1)}, bf16[160,512]{1,0:T(8,128)(2,1)S(1)}, u32[]{:S(2)}, u32[]{:S(2)}) collective-permute-start(bf16[160,512]{1,0:T(8,128)(2,1)S(1)} %copy-done.65), channel_id=1, source_target_pairs={{0,1},{1,0},{2,3},{3,2},{4,5},{5,4},{6,7},{7,6},{8,9},{9,8},{10,11... | collective-permute-start | bytes 491528 | tf_op jit(solution)/shard_map/ppermute | solution.py:1300
  361.1 13.3 %collective-permute-start.89 = (bf16[160,512]{1,0:T(8,128)(2,1)S(1)}, bf16[160,512]{1,0:T(8,128)(2,1)S(1)}, u32[]{:S(2)}, u32[]{:S(2)}) collective-permute-start(bf16[160,512]{1,0:T(8,128)(2,1)S(1)} %copy-done.68), channel_id=1, source_target_pairs={{0,1},{1,0},{2,3},{3,2},{4,5},{5,4},{6,7},{7,6},{8,9},{9,8},{10,11... | collective-permute-start | bytes 491528 | tf_op jit(solution)/shard_map/ppermute | solution.py:1300
  374.4 17.3 %collective-permute-start.98 = (bf16[160,2048]{1,0:T(8,128)(2,1)S(1)}, bf16[160,2048]{1,0:T(8,128)(2,1)S(1)}, u32[]{:S(2)}, u32[]{:S(2)}) collective-permute-start(bf16[160,2048]{1,0:T(8,128)(2,1)S(1)} %get-tuple-element.477), channel_id=1, source_target_pairs={{0,1},{1,0},{2,3},{3,2},{4,5},{5,4},{6,7},{7,6},{8,9},{9,8},{10,11... | collective-permute-start | bytes 1966088 | tf_op jit(solution)/shard_map/ppermute | solution.py:1300
  376.5 14.8 %collective-permute-start.95 = (bf16[160,512]{1,0:T(8,128)(2,1)S(1)}, bf16[160,512]{1,0:T(8,128)(2,1)S(1)}, u32[]{:S(2)}, u32[]{:S(2)}) collective-permute-start(bf16[160,512]{1,0:T(8,128)(2,1)S(1)} %get-tuple-element.471), channel_id=1, source_target_pairs={{0,1},{1,0},{2,3},{3,2},{4,5},{5,4},{6,7},{7,6},{8,9},{9,8},{10,11... | collective-permute-start | bytes 491528 | tf_op jit(solution)/shard_map/ppermute | solution.py:1300
  377.7 17.1 %collective-permute-start.93 = (bf16[160,2048]{1,0:T(8,128)(2,1)S(1)}, bf16[160,2048]{1,0:T(8,128)(2,1)S(1)}, u32[]{:S(2)}, u32[]{:S(2)}) collective-permute-start(bf16[160,2048]{1,0:T(8,128)(2,1)S(1)} %get-tuple-element.467), channel_id=1, source_target_pairs={{0,1},{1,0},{2,3},{3,2},{4,5},{5,4},{6,7},{7,6},{8,9},{9,8},{10,11... | collective-permute-start | bytes 1966088 | tf_op jit(solution)/shard_map/ppermute | solution.py:1300
  379.7 16.5 %collective-permute-start.99 = (bf16[160,2048]{1,0:T(8,128)(2,1)S(1)}, bf16[160,2048]{1,0:T(8,128)(2,1)S(1)}, u32[]{:S(2)}, u32[]{:S(2)}) collective-permute-start(bf16[160,2048]{1,0:T(8,128)(2,1)S(1)} %get-tuple-element.479), channel_id=1, source_target_pairs={{0,1},{1,0},{2,3},{3,2},{4,5},{5,4},{6,7},{7,6},{8,9},{9,8},{10,11... | collective-permute-start | bytes 1966088 | tf_op jit(solution)/shard_map/ppermute | solution.py:1300
  391.2 7.7 %collective-permute-start.100 = (bf16[160,2048]{1,0:T(8,128)(2,1)S(1)}, bf16[160,2048]{1,0:T(8,128)(2,1)S(1)}, u32[]{:S(2)}, u32[]{:S(2)}) collective-permute-start(bf16[160,2048]{1,0:T(8,128)(2,1)S(1)} %get-tuple-element.481), channel_id=1, source_target_pairs={{0,1},{1,0},{2,3},{3,2},{4,5},{5,4},{6,7},{7,6},{8,9},{9,8},{10,11... | collective-permute-start | bytes 1966088 | tf_op jit(solution)/shard_map/ppermute | solution.py:1300
  391.6 7.4 %collective-permute-start.94 = (bf16[160,2048]{1,0:T(8,128)(2,1)S(1)}, bf16[160,2048]{1,0:T(8,128)(2,1)S(1)}, u32[]{:S(2)}, u32[]{:S(2)}) collective-permute-start(bf16[160,2048]{1,0:T(8,128)(2,1)S(1)} %get-tuple-element.469), channel_id=1, source_target_pairs={{0,1},{1,0},{2,3},{3,2},{4,5},{5,4},{6,7},{7,6},{8,9},{9,8},{10,11... | collective-permute-start | bytes 1966088 | tf_op jit(solution)/shard_map/ppermute | solution.py:1300
  394.8 14.7 %collective-permute-start.88 = (bf16[80,512]{1,0:T(8,128)(2,1)S(1)}, bf16[80,512]{1,0:T(8,128)(2,1)S(1)}, u32[]{:S(2)}, u32[]{:S(2)}) collective-permute-start(bf16[80,512]{1,0:T(8,128)(2,1)S(1)} %get-tuple-element.463), channel_id=1, source_target_pairs={{0,4},{1,5},{2,6},{3,7},{4,0},{5,1},{6,2},{7,3},{8,12},{9,13},{10,... | collective-permute-start | bytes 245768 | tf_op jit(solution)/shard_map/ppermute | solution.py:1305
  396.3 13.3 %collective-permute-start.101 = (bf16[80,512]{1,0:T(8,128)(2,1)S(1)}, bf16[80,512]{1,0:T(8,128)(2,1)S(1)}, u32[]{:S(2)}, u32[]{:S(2)}) collective-permute-start(bf16[80,512]{1,0:T(8,128)(2,1)S(1)} %get-tuple-element.483), channel_id=1, source_target_pairs={{0,2},{1,3},{2,4},{3,5},{4,6},{5,7},{6,0},{7,1},{8,10},{9,11},{10,... | collective-permute-start | bytes 245768 | tf_op jit(solution)/shard_map/ppermute | solution.py:1305
  397.3 12.2 %collective-permute-start.87 = (bf16[80,512]{1,0:T(8,128)(2,1)S(1)}, bf16[80,512]{1,0:T(8,128)(2,1)S(1)}, u32[]{:S(2)}, u32[]{:S(2)}) collective-permute-start(bf16[80,512]{1,0:T(8,128)(2,1)S(1)} %get-tuple-element.462), channel_id=1, source_target_pairs={{0,6},{1,7},{2,0},{3,1},{4,2},{5,3},{6,4},{7,5},{8,14},{9,15},{10,... | collective-permute-start | bytes 245768 | tf_op jit(solution)/shard_map/ppermute | solution.py:1305
  411.9 11.3 %collective-permute-start.102 = (bf16[128,512]{1,0:T(8,128)(2,1)S(1)}, bf16[128,512]{1,0:T(8,128)(2,1)S(1)}, u32[]{:S(2)}, u32[]{:S(2)}) collective-permute-start(bf16[128,512]{1,0:T(8,128)(2,1)S(1)} %get-tuple-element.488.refs_1_), channel_id=1, source_target_pairs={{0,2},{1,3},{2,4},{3,5},{4,6},{5,7},{6,0},{7,1},{8,10},{9,11},{10,... | collective-permute-start | bytes 393224 | tf_op jit(solution)/shard_map/ppermute | solution.py:1305
  411.9 16.6 %collective-permute-start.103 = (bf16[128,512]{1,0:T(8,128)(2,1)S(1)}, bf16[128,512]{1,0:T(8,128)(2,1)S(1)}, u32[]{:S(2)}, u32[]{:S(2)}) collective-permute-start(bf16[128,512]{1,0:T(8,128)(2,1)S(1)} %get-tuple-element.488.refs_1_), channel_id=1, source_target_pairs={{0,4},{1,5},{2,6},{3,7},{4,0},{5,1},{6,2},{7,3},{8,12},{9,13},{10,... | collective-permute-start | bytes 393224 | tf_op jit(solution)/shard_map/ppermute | solution.py:1305
  413.2 15.3 %collective-permute-start.104 = (bf16[128,512]{1,0:T(8,128)(2,1)S(1)}, bf16[128,512]{1,0:T(8,128)(2,1)S(1)}, u32[]{:S(2)}, u32[]{:S(2)}) collective-permute-start(bf16[128,512]{1,0:T(8,128)(2,1)S(1)} %get-tuple-element.488.refs_1_), channel_id=1, source_target_pairs={{0,6},{1,7},{2,0},{3,1},{4,2},{5,3},{6,4},{7,5},{8,14},{9,15},{10,... | collective-permute-start | bytes 393224 | tf_op jit(solution)/shard_map/ppermute | solution.py:1305
  414.6 71.1 %all-to-all-start = ((bf16[16,256,512]{2,1,0:T(8,128)(2,1)}), bf16[16,256,512]{2,1,0:T(8,128)(2,1)}, u32[]{:S(2)}, u32[]{:S(2)}) async-start(bf16[16,256,512]{2,1,0:T(8,128)(2,1)} %feed_weights.1), calls=%async_computation | async-start | bytes 8388608 | tf_op jit(solution)/shard_map/all_to_all | solution.py:1325
  464.2 7.0 %collective-permute-start.112 = (bf16[4,128,512]{2,1,0:T(8,128)(2,1)}, bf16[4,128,512]{2,1,0:T(8,128)(2,1)S(1)}, u32[]{:S(2)}, u32[]{:S(2)}) collective-permute-start(bf16[4,128,512]{2,1,0:T(8,128)(2,1)} %get-tuple-element.524), channel_id=1, source_target_pairs={{0,1},{1,0},{2,3},{3,2},{4,5},{5,4},{6,7},{7,6},{8,9},{9,8},{10,11... | collective-permute-start | bytes 1572872 | tf_op jit(solution)/shard_map/ppermute | solution.py:1300
  464.6 10.8 %collective-permute-start.105 = (bf16[512,512]{1,0:T(8,128)(2,1)S(1)}, bf16[512,512]{1,0:T(8,128)(2,1)}, u32[]{:S(2)}, u32[]{:S(2)}) collective-permute-start(bf16[512,512]{1,0:T(8,128)(2,1)S(1)} %copy-done.131), channel_id=1, source_target_pairs={{0,1},{1,0},{2,3},{3,2},{4,5},{5,4},{6,7},{7,6},{8,9},{9,8},{10,11... | collective-permute-start | bytes 1572872 | tf_op jit(solution)/shard_map/ppermute | solution.py:1300
  464.7 10.7 %collective-permute-start.107 = (bf16[512,512]{1,0:T(8,128)(2,1)S(1)}, bf16[512,512]{1,0:T(8,128)(2,1)}, u32[]{:S(2)}, u32[]{:S(2)}) collective-permute-start(bf16[512,512]{1,0:T(8,128)(2,1)S(1)} %copy-done.129), channel_id=1, source_target_pairs={{0,1},{1,0},{2,3},{3,2},{4,5},{5,4},{6,7},{7,6},{8,9},{9,8},{10,11... | collective-permute-start | bytes 1572872 | tf_op jit(solution)/shard_map/ppermute | solution.py:1300
  468.9 8.5 %collective-permute-start.109 = (bf16[64,1152]{1,0:T(8,128)(2,1)}, bf16[64,1152]{1,0:T(8,128)(2,1)S(1)}, u32[]{:S(2)}, u32[]{:S(2)}) collective-permute-start(bf16[64,1152]{1,0:T(8,128)(2,1)} %get-tuple-element.516), channel_id=1, source_target_pairs={{0,2},{1,3},{2,4},{3,5},{4,6},{5,7},{6,0},{7,1},{8,10},{9,11},{10,... | collective-permute-start | bytes 442376 | tf_op jit(solution)/shard_map/ppermute | solution.py:1305
  469.0 9.4 %collective-permute-start.110 = (bf16[64,1152]{1,0:T(8,128)(2,1)}, bf16[64,1152]{1,0:T(8,128)(2,1)S(1)}, u32[]{:S(2)}, u32[]{:S(2)}) collective-permute-start(bf16[64,1152]{1,0:T(8,128)(2,1)} %get-tuple-element.517), channel_id=1, source_target_pairs={{0,4},{1,5},{2,6},{3,7},{4,0},{5,1},{6,2},{7,3},{8,12},{9,13},{10,... | collective-permute-start | bytes 442376 | tf_op jit(solution)/shard_map/ppermute | solution.py:1305
  471.1 7.7 %collective-permute-start.111 = (bf16[64,1152]{1,0:T(8,128)(2,1)}, bf16[64,1152]{1,0:T(8,128)(2,1)S(1)}, u32[]{:S(2)}, u32[]{:S(2)}) collective-permute-start(bf16[64,1152]{1,0:T(8,128)(2,1)} %get-tuple-element.518), channel_id=1, source_target_pairs={{0,6},{1,7},{2,0},{3,1},{4,2},{5,3},{6,4},{7,5},{8,14},{9,15},{10,... | collective-permute-start | bytes 442376 | tf_op jit(solution)/shard_map/ppermute | solution.py:1305
  475.3 10.3 %collective-permute-start.113 = (bf16[128,512]{1,0:T(8,128)(2,1)}, bf16[128,512]{1,0:T(8,128)(2,1)S(1)}, u32[]{:S(2)}, u32[]{:S(2)}) collective-permute-start(bf16[128,512]{1,0:T(8,128)(2,1)} %get-tuple-element.526), channel_id=1, source_target_pairs={{0,2},{1,3},{2,4},{3,5},{4,6},{5,7},{6,0},{7,1},{8,10},{9,11},{10,... | collective-permute-start | bytes 393224 | tf_op jit(solution)/shard_map/ppermute | solution.py:1305
  475.4 10.2 %collective-permute-start.114 = (bf16[128,512]{1,0:T(8,128)(2,1)}, bf16[128,512]{1,0:T(8,128)(2,1)S(1)}, u32[]{:S(2)}, u32[]{:S(2)}) collective-permute-start(bf16[128,512]{1,0:T(8,128)(2,1)} %get-tuple-element.527), channel_id=1, source_target_pairs={{0,4},{1,5},{2,6},{3,7},{4,0},{5,1},{6,2},{7,3},{8,12},{9,13},{10,... | collective-permute-start | bytes 393224 | tf_op jit(solution)/shard_map/ppermute | solution.py:1305
  477.4 8.2 %collective-permute-start.115 = (bf16[128,512]{1,0:T(8,128)(2,1)}, bf16[128,512]{1,0:T(8,128)(2,1)S(1)}, u32[]{:S(2)}, u32[]{:S(2)}) collective-permute-start(bf16[128,512]{1,0:T(8,128)(2,1)} %get-tuple-element.528), channel_id=1, source_target_pairs={{0,6},{1,7},{2,0},{3,1},{4,2},{5,3},{6,4},{7,5},{8,14},{9,15},{10,... | collective-permute-start | bytes 393224 | tf_op jit(solution)/shard_map/ppermute | solution.py:1305
  485.7 25.1 %all-to-all-start.1 = ((bf16[16,80,512]{2,1,0:T(8,128)(2,1)}), bf16[16,80,512]{2,1,0:T(8,128)(2,1)S(1)}, u32[]{:S(2)}, u32[]{:S(2)}) async-start(bf16[16,80,512]{2,1,0:T(8,128)(2,1)} %last_weights.1), calls=%async_computation.1 | async-start | bytes 2621440 | tf_op jit(solution)/shard_map/all_to_all | solution.py:1325
  (219 other events, 2128.0 us)

commit v4 on v3

--- a/solution.py
+++ b/solution.py
@@ -652,18 +652,18 @@
 
 
 def shared_last_kernel(*refs):
-    scal, far, outs = refs[0], refs[1:6], refs[6:8]
-    held, (total, packed, in_sems, out_sems) = refs[8:13], refs[13:]
-    rows, grad_k, before, grad_v, tiny = held
-    copies = [copy_in(far[n], held[n], in_sems.at[n]) for n in range(5)]
-    for n in range(3):
+    scal, far, outs = refs[0], refs[1:9], refs[9:11]
+    held, (total, packed, in_sems, out_sems) = refs[11:19], refs[19:]
+    rows_1, grad_k1, rows_0, grad_k0, before, grad_v1, grad_v0, tiny = held
+    copies = [copy_in(far[n], held[n], in_sems.at[n]) for n in range(8)]
+    for n in range(5):
         copies[n].wait()
-    total[:, 0:WIDTH] = (tn(rows[...], grad_k[...]) + before[:, 0:WIDTH]).astype(BF16)
-    copies[3].wait()
-    copies[4].wait()
-    total[:, WIDTH : 2 * WIDTH] = (
-        tn(rows[...], grad_v[...]) + before[:, WIDTH : 2 * WIDTH]
-    ).astype(BF16)
+    value = tn(rows_1[...], grad_k1[...]) + tn(rows_0[...], grad_k0[...])
+    total[:, 0:WIDTH] = (value + before[:, 0:WIDTH]).astype(BF16)
+    for n in range(5, 8):
+        copies[n].wait()
+    value = tn(rows_1[...], grad_v1[...]) + tn(rows_0[...], grad_v0[...])
+    total[:, WIDTH : 2 * WIDTH] = (value + before[:, WIDTH : 2 * WIDTH]).astype(BF16)
     total[:, 2 * WIDTH :] = tiny[...].astype(BF16)
     row = iota((WIDTH, WIDTH), 0)
     side, hop, spot = row >> 8, (row >> 6) & 3, (row >> 2) & 15
@@ -676,12 +676,13 @@
         copy.wait()
 
 
-def shared_last(table, rows, grad_k, grad_v, before, tiny):
-    args = [rows, grad_k, before, grad_v, tiny]
+def shared_last(table, step_1, step_0, before, tiny):
+    (rows_1, grad_k1, grad_v1), (rows_0, grad_k0, grad_v0) = step_1, step_0
+    args = [rows_1, grad_k1, rows_0, grad_k0, before, grad_v1, grad_v0, tiny]
     scratch = [pltpu.VMEM(a.shape, a.dtype) for a in args] + [
         pltpu.VMEM((WIDTH, SHARED), BF16),
         pltpu.VMEM((2, CHIPS, 64, SHARED), BF16),
-        pltpu.SemaphoreType.DMA((5,)),
+        pltpu.SemaphoreType.DMA((8,)),
         pltpu.SemaphoreType.DMA((2,)),
     ]
     outs = [like((CHIPS, 64, SHARED), BF16)] * 2
@@ -1440,10 +1441,6 @@
         )
         limit = 20 if s else 60
         arrived = spread_rows(grad_low)
-        if s == 0:
-            arrived[1], grad_k = after(arrived[1], pending[1])
-            shared_acc = shared_weights(pending[0], grad_k, pending[2], shared_acc, 60)
-            arrived[2], shared_acc = after(arrived[2], shared_acc)
         *same, other, y_0, y_1, q_0, q_1, grad_k, grad_v, tiny = attend_back(
             table, arrived, k["attend"], key_proj, value_proj, query_w, out_w, p,
             (k["rows"], router_a, gain_a, tiny), 36 if s else 60,
@@ -1460,7 +1457,9 @@
             parts[2], expert_acc = after(parts[2], expert_acc)
             pending = (k["rows"], grad_k, grad_v)
         else:
-            mine, others = shared_last(table, k["rows"], grad_k, grad_v, shared_acc, tiny)
+            mine, others = shared_last(
+                table, pending, (k["rows"], grad_k, grad_v), shared_acc, tiny
+            )
             shared = send_blocks(core_sum(mine, swap_core(others)))
             parts = send_blocks(pair_sum(same, other, limit))
             weights_last = last_weights(

time: 524 us -> 522 us (level)
    pallas_call x25 -> x24, Pallas kernels: 53.6 us -> 48.4 us  [call(): pl.pallas_call(body, out_shape=tuple(outs), in_specs=[spec(i, smem, near)...]
  transfers between devices with their start and end apart: 118 -> 118, of which waited for: 56 -> 55; matrix products, arithmetic and copies ran while one was open for 1% -> 1% of each run, Pallas kernels for 23% -> 22%
where the time goes in v4:
time: 522 us; the launch traced here: 513 us
  Pallas kernels  223 us (43%)
  starting transfers between devices  159 us (30%)
  waiting for transfers between devices  88.2 us (17%)
  local copies, waits for them, and re-layouts  36.4 us (7%)
    pallas_call x8, Pallas kernels, call_any(): pl.pallas_call(kernel, out_shape=tuple(outs), in_specs=[pl.BlockSpec(memo...  125 us
    ppermute x75, starting transfers between devices, shift_chip(): lax.ppermute(rows, 'expert', [(i, (i + 2 * hops) % count) for i in range(...  96.3 us
    ppermute x75, waiting for transfers between devices, shift_chip(): lax.ppermute(rows, 'expert', [(i, (i + 2 * hops) % count) for i in range(...  66.8 us
    pallas_call x24, Pallas kernels, call(): pl.pallas_call(body, out_shape=tuple(outs), in_specs=[spec(i, smem, near)...  48.4 us
    ppermute x41, starting transfers between devices, swap_core(): return lax.ppermute(rows, 'expert', [(i, i ^ 1) for i in range(2 * CHIPS)])  47 us
    unnamed x330, local copies, waits for them, and re-layouts  31.3 us
    pallas_call x3, Pallas kernels, feed_back(): pl.pallas_call(feed_back_kernel, in_specs=[NEAR] * 4 + [FAR] * 6, out_spe...  24.6 us
    all_to_all x2, starting transfers between devices, dp_move(): return lax.all_to_all(blocks, 'dp', split_axis=0, concat_axis=0, tiled=True)  16 us
  transfers between devices with their start and end apart: 118, of which 55 were waited for; matrix products, arithmetic and copies ran while one was open for 1% of the time, Pallas kernels for 22%

profile of v4, /device:TPU:1, one launch (start us, length us, event | category | flops | bytes accessed | tf_op | source)
XLA Modules:
  0.0 513.5 jit_solution(5452462238883554903)
XLA Ops:
  2.3 2.5 first_norm.1
  6.5 3.3 collective-permute-start
  10.6 2.2 collective-permute-done.1.refs_2_.refs_3_
  14.2 2.5 collective-permute-done.refs_3_.refs_4_
  18.1 4.2 attend_plan.3
  27.7 18.6 %attend.3 = (bf16[128,512]{1,0:T(8,128)(2,1)}, bf16[128,512]{1,0:T(8,128)(2,1)}, bf16[128,512]{1,0:T(8,128)(2,1)}, bf16[128,512]{1,0:T(8,128)(2,1)}, bf16[1024,5...) custom-call(s32[8,128]{1,0:T(8,128)} %get-tuple-element.275.refs_0_,, ...), custom_call_target="tpu_custom_call" | custom-call | flops 6000000000 | bytes 12668928 | tf_op jit(solution)/shard_map/attend/pallas_call | solution.py:178
  46.8 3.2 collective-permute-start.10
  52.5 2.4 slot_plan.1
  60.2 2.2 collective-permute-start.13
  68.4 4.9 feed.3
  78.3 5.3 %attend_plan.4 = (s32[8,128]{1,0:T(8,128)}, f32[512,128]{1,0:T(8,128)}, s32[8,512]{1,0:T(8,128)}, s32[512,128]{1,0:T(8,128)}, s32[1024,128]{1,0:T(8,128)}) custom-call(s32[4]{0:T(128)} %pad_add_fusion.refs_0_, s32[3,4,1024]{2,1,0:T(4,128)} %bitcast.79, bf16[144,512]{1,0:T(8,128)(2,1)} %get-tuple-element.272.refs_1_.refs_2_, bf16[144,512]{1,0:T(8,128)(2,1)} %copy-done.138, ...), custom_call_target="tpu_custom_call" | custom-call | flops 1000000000 | bytes 2297872 | tf_op jit(solution)/shard_map/attend_plan/pallas_call | solution.py:145
  85.0 3.9 collective-permute-start.21
  88.9 4.3 collective-permute-start.23
  94.8 2.8 collective-permute-start.25
  99.9 16.0 %attend.4 = (bf16[128,512]{1,0:T(8,128)(2,1)}, bf16[128,512]{1,0:T(8,128)(2,1)}, bf16[128,512]{1,0:T(8,128)(2,1)}, bf16[128,512]{1,0:T(8,128)(2,1)}, bf16[1024,5...) custom-call(s32[8,128]{1,0:T(8,128)} %get-tuple-element.307.refs_0_,, ...), custom_call_target="tpu_custom_call" | custom-call | flops 6000000000 | bytes 12537856 | tf_op jit(solution)/shard_map/attend/pallas_call | solution.py:178
  119.2 6.1 %collective-permute-done.27.refs_2_ = bf16[128,512]{1,0:T(8,128)(2,1)S(1)} collective-permute-done((bf16[128,512]{1,0:T(8,128)(2,1)}, bf16[128,512]{1,0:T(8,128)(2,1)S(1)}, u32[]{:S(2)}, u32[]{:S(2)}) %collective-permute-start.27) | collective-permute-done | bytes 131104 | tf_op jit(solution)/shard_map/ppermute | solution.py:1306
  128.8 3.0 collective-permute-start.31
  132.5 2.9 collective-permute-done.31.refs_2_
  137.4 5.5 %feed.4 = (bf16[80,512]{1,0:T(8,128)(2,1)S(1)}, bf16[80,512]{1,0:T(8,128)(2,1)S(1)}, bf16[80,512]{1,0:T(8,128)(2,1)}, bf16[80,512]{1,0:T(8,128)(2,1)S(1)}, bf16[...) custom-call(bf16[80,512]{1,0:T(8,128)(2,1)S(1)} %get-tuple-element.321.refs_0_, ...), custom_call_target="tpu_custom_call" | custom-call | flops 2000000000 | bytes 10000000 | tf_op jit(solution)/shard_map/feed/pallas_call | solution.py:835
  144.3 2.6 collective-permute-start.33
  148.9 5.3 %attend_plan.5 = (s32[8,128]{1,0:T(8,128)}, f32[512,128]{1,0:T(8,128)}, s32[8,512]{1,0:T(8,128)}, s32[512,128]{1,0:T(8,128)}, s32[1024,128]{1,0:T(8,128)}) custom-call(s32[4]{0:T(128)} %pad_add_fusion.refs_0_, s32[3,4,1024]{2,1,0:T(4,128)} %bitcast.80, bf16[144,512]{1,0:T(8,128)(2,1)} %get-tuple-element.272.refs_1_.refs_2_, bf16[144,512]{1,0:T(8,128)(2,1)} %copy-done.138, ...), custom_call_target="tpu_custom_call" | custom-call | flops 1000000000 | bytes 2297872 | tf_op jit(solution)/shard_map/attend_plan/pallas_call | solution.py:145
  155.7 4.4 collective-permute-start.37
  160.1 2.5 collective-permute-start.39
  162.7 2.9 collective-permute-start.40
  169.4 12.9 %attend.5 = (bf16[128,512]{1,0:T(8,128)(2,1)}, bf16[128,512]{1,0:T(8,128)(2,1)}, bf16[128,512]{1,0:T(8,128)(2,1)}, bf16[128,512]{1,0:T(8,128)(2,1)}, bf16[1024,5...) custom-call(s32[8,128]{1,0:T(8,128)} %get-tuple-element.334.refs_0_,, ...), custom_call_target="tpu_custom_call" | custom-call | flops 6000000000 | bytes 12537856 | tf_op jit(solution)/shard_map/attend/pallas_call | solution.py:178
  182.5 3.1 collective-permute-start.44
  186.3 2.4 collective-permute-done.43.refs_2_
  188.8 3.5 collective-permute-done.44.refs_3_
  196.0 2.4 collective-permute-start.47
  199.0 2.9 collective-permute-done.47.refs_2_
  203.9 4.9 feed.5
  213.2 2.6 collective-permute-done.50.refs_7_
  221.5 2.4 collective-permute-done.52.refs_1_
  224.6 8.3 %feed_back.3 = (bf16[80,512]{1,0:T(8,128)(2,1)S(1)}, bf16[80,512]{1,0:T(8,128)(2,1)S(1)}, bf16[80,512]{1,0:T(8,128)(2,1)S(1)}, bf16[80,512]{1,0:T(8,128)(2,1)S(1...) custom-call(bf16[80,512]{1,0:T(8,128)(2,1)S(1)} %get-tuple-element.3, ...), custom_call_target="tpu_custom_call" | custom-call | flops 3000000000 | bytes 10000000 | tf_op jit(solution)/shard_map/feed_back/pallas_call | solution.py:890
  233.0 2.4 collective-permute-start.55
  237.7 2.6 collective-permute-done.56.refs_2_
  245.4 2.3 collective-permute-done.58.refs_2_
  250.9 17.7 %attend_back.3 = (bf16[128,512]{1,0:T(8,128)(2,1)S(1)}, bf16[128,512]{1,0:T(8,128)(2,1)S(1)}, bf16[128,512]{1,0:T(8,128)(2,1)S(1)}, bf16[128,512]{1,0:T(8,128)(2...) custom-call(s32[8,128]{1,0:T(8,128)S(1)} %copy-done.115, ...), custom_call_target="tpu_custom_call" | custom-call | flops 99999997952 | bytes 16996352 | tf_op jit(solution)/shard_map/attend_back/pallas_call | solution.py:178
  269.6 7.3 %collective-permute-start.61 = (bf16[4,128,512]{2,1,0:T(8,128)(2,1)S(1)}, bf16[4,128,512]{2,1,0:T(8,128)(2,1)S(1)}, u32[]{:S(2)}, u32[]{:S(2)}) collective-permute-start(bf16[4,128,512]{2,1,0:T(8,128)(2,1)S(1)} %get-tuple-element.387), channel_id=1, source_target_pairs={{0,1},{1,0},{2,3},{3,2},{4,5},{5,4},{6,7},{7,6},{8,9},{9,8},{10,11... | collective-permute-start | bytes 1572872 | tf_op jit(solution)/shard_map/ppermute | solution.py:1301
  279.8 2.5 collective-permute-start.63
  282.3 2.3 collective-permute-done.62.refs_1_
  285.9 2.4 expert_weights.2.refs_8_
  288.8 2.2 retreat.3
  291.1 3.3 collective-permute-start.69
  297.9 8.2 %feed_back.4 = (bf16[80,512]{1,0:T(8,128)(2,1)S(1)}, bf16[80,512]{1,0:T(8,128)(2,1)S(1)}, bf16[80,512]{1,0:T(8,128)(2,1)S(1)}, bf16[80,512]{1,0:T(8,128)(2,1)S(1...) custom-call(bf16[80,512]{1,0:T(8,128)(2,1)S(1)} %get-tuple-element.4, ...), custom_call_target="tpu_custom_call" | custom-call | flops 3000000000 | bytes 10000000 | tf_op jit(solution)/shard_map/feed_back/pallas_call | solution.py:890
  317.2 3.5 collective-permute-start.75
  321.8 2.6 collective-permute-done.75.refs_3_
  327.0 20.1 %attend_back.4 = (bf16[128,512]{1,0:T(8,128)(2,1)S(1)}, bf16[128,512]{1,0:T(8,128)(2,1)S(1)}, bf16[128,512]{1,0:T(8,128)(2,1)S(1)}, bf16[128,512]{1,0:T(8,128)(2...) custom-call(s32[8,128]{1,0:T(8,128)S(1)} %copy-done.114, ...), custom_call_target="tpu_custom_call" | custom-call | flops 99999997952 | bytes 16996352 | tf_op jit(solution)/shard_map/attend_back/pallas_call | solution.py:178
  347.1 5.3 %collective-permute-start.77 = (bf16[4,128,512]{2,1,0:T(8,128)(2,1)S(1)}, bf16[4,128,512]{2,1,0:T(8,128)(2,1)S(1)}, u32[]{:S(2)}, u32[]{:S(2)}) collective-permute-start(bf16[4,128,512]{2,1,0:T(8,128)(2,1)S(1)} %get-tuple-element.436), channel_id=1, source_target_pairs={{0,1},{1,0},{2,3},{3,2},{4,5},{5,4},{6,7},{7,6},{8,9},{9,8},{10,11... | collective-permute-start | bytes 1572872 | tf_op jit(solution)/shard_map/ppermute | solution.py:1301
  356.2 2.3 collective-permute-start.79
  358.5 2.4 collective-permute-done.78.refs_1_
  366.3 2.6 expert_weights.3.refs_4_
  370.3 2.2 retreat.4
  383.1 8.1 %feed_back.5 = (bf16[80,512]{1,0:T(8,128)(2,1)S(1)}, bf16[80,512]{1,0:T(8,128)(2,1)S(1)}, bf16[80,512]{1,0:T(8,128)(2,1)S(1)}, bf16[80,512]{1,0:T(8,128)(2,1)S(1...) custom-call(bf16[80,512]{1,0:T(8,128)(2,1)S(1)} %get-tuple-element.4, ...), custom_call_target="tpu_custom_call" | custom-call | flops 3000000000 | bytes 10000000 | tf_op jit(solution)/shard_map/feed_back/pallas_call | solution.py:890
  395.3 2.3 collective-permute-done.96.refs_15_
  403.2 9.6 %feed_weights.1 = bf16[16,256,512]{2,1,0:T(8,128)(2,1)} custom-call(bf16[160,512]{1,0:T(8,128)(2,1)} %copy-done.66, bf16[160,512]{1,0:T(8,128)(2,1)} %copy-done.134, bf16[160,512]{1,0:T(8,128)(2,1)} %copy-done.62, bf16[160,512]{1,0:T(8,128)(2,1)} %copy-done.133, bf16[160,512]{1,0:T(8,128)(2,1)} %copy-done.58, bf16[160,512]{1,0:T(8,128)(2,1)} %copy-done.132, ...), custom_call_target="tpu_custom_call" | custom-call | flops 8000000000 | bytes 20000000 | tf_op jit(solution)/shard_map/feed_weights/pallas_call | solution.py:942
  417.8 8.1 %all-to-all-start = ((bf16[16,256,512]{2,1,0:T(8,128)(2,1)}), bf16[16,256,512]{2,1,0:T(8,128)(2,1)}, u32[]{:S(2)}, u32[]{:S(2)}) async-start(bf16[16,256,512]{2,1,0:T(8,128)(2,1)} %feed_weights.1), calls=%async_computation | async-start | bytes 8388608 | tf_op jit(solution)/shard_map/all_to_all | solution.py:1326
  426.7 25.4 %attend_back.5 = (bf16[128,512]{1,0:T(8,128)(2,1)}, bf16[128,512]{1,0:T(8,128)(2,1)}, bf16[128,512]{1,0:T(8,128)(2,1)}, bf16[128,512]{1,0:T(8,128)(2,1)}, bf16[4...) custom-call(s32[8,128]{1,0:T(8,128)} %get-tuple-element.275.refs_0_,, ...), custom_call_target="tpu_custom_call" | custom-call | flops 99999997952 | bytes 16996352 | tf_op jit(solution)/shard_map/attend_back/pallas_call | solution.py:178
  452.2 8.4 %shared_last.1 = (bf16[4,64,1152]{2,1,0:T(8,128)(2,1)}, bf16[4,64,1152]{2,1,0:T(8,128)(2,1)}) custom-call(s32[8,128]{1,0:T(8,128)} %get-tuple-element.275.refs_0_, bf16[1024,512]{1,0:T(8,128)(2,1)} %get-tuple-element.430.refs_22_.refs_1_, bf16[1024,512]{1,0:T(8,128)(2,1)} %copy-done.99, bf16[1024,512]{1,0:T(8,128)(2,1)} %get-tuple-element.357.refs_22_.refs_3_.refs_1_, ...), custom_call_target="tpu_custom_call" | custom-call | flops 4000000000 | bytes 9834496 | tf_op jit(solution)/shard_map/shared_last/pallas_call | solution.py:178
  467.5 3.3 collective-permute-start.110
  478.8 6.0 %last_weights.1 = bf16[16,80,512]{2,1,0:T(8,128)(2,1)} custom-call(s32[8,128]{1,0:T(8,128)} %get-tuple-element.275.refs_0_, bf16[1024,512]{1,0:T(8,128)(2,1)} %get-tuple-element.357.refs_22_.refs_3_.refs_1_, bf16[512,512]{1,0:T(8,128)(2,1)} %get-tuple-element.494.refs_2_, bf16[512,512]{1,0:T(8,128)(2,1)} %collective-permute-done.105.refs_3_, ...), custom_call_target="tpu_custom_call" | custom-call | flops 4000000000 | bytes 8196096 | tf_op jit(solution)/shard_map/last_weights/pallas_call | solution.py:178
  484.8 7.9 %all-to-all-start.1 = ((bf16[16,80,512]{2,1,0:T(8,128)(2,1)}), bf16[16,80,512]{2,1,0:T(8,128)(2,1)S(1)}, u32[]{:S(2)}, u32[]{:S(2)}) async-start(bf16[16,80,512]{2,1,0:T(8,128)(2,1)} %last_weights.1), calls=%async_computation.1 | async-start | bytes 2621440 | tf_op jit(solution)/shard_map/all_to_all | solution.py:1326
  492.7 2.8 convert_reduce_fusion
  498.7 11.8 %all-to-all-done.1 = bf16[16,80,512]{2,1,0:T(8,128)(2,1)S(1)} async-done(((bf16[16,80,512]{2,1,0:T(8,128)(2,1)}), bf16[16,80,512]{2,1,0:T(8,128)(2,1)S(1)}, u32[]{:S(2)}, u32[]{:S(2)}) %all-to-all-start.1) | async-done | bytes 1310752 | tf_op jit(solution)/shard_map/all_to_all | solution.py:1326
  (553 shorter events, 163.5 us)
Async XLA Ops:
  0.7 66.1 %collective-permute-start.15 = (bf16[512,2048]{1,0:T(8,128)(2,1)}, bf16[512,2048]{1,0:T(8,128)(2,1)}, u32[]{:S(2)}, u32[]{:S(2)}) collective-permute-start(bf16[512,2048]{1,0:T(8,128)(2,1)} %bitcast.25), channel_id=1, source_target_pairs={{0,1},{1,0},{2,3},{3,2},{4,5},{5,4},{6,7},{7,6},{8,9},{9,8},{10,11... | collective-permute-start | bytes 6291464 | tf_op jit(solution)/shard_map/ppermute | solution.py:1301
  2.2 64.6 %collective-permute-start.16 = (bf16[2048,512]{1,0:T(8,128)(2,1)}, bf16[2048,512]{1,0:T(8,128)(2,1)}, u32[]{:S(2)}, u32[]{:S(2)}) collective-permute-start(bf16[2048,512]{1,0:T(8,128)(2,1)} %bitcast.32), channel_id=1, source_target_pairs={{0,1},{1,0},{2,3},{3,2},{4,5},{5,4},{6,7},{7,6},{8,9},{9,8},{10,11... | collective-permute-start | bytes 6291464 | tf_op jit(solution)/shard_map/ppermute | solution.py:1301
  4.7 8.0 %collective-permute-start.1 = (bf16[144,512]{1,0:T(8,128)(2,1)}, bf16[144,512]{1,0:T(8,128)(2,1)S(1)}, u32[]{:S(2)}, u32[]{:S(2)}) collective-permute-start(bf16[144,512]{1,0:T(8,128)(2,1)} %get-tuple-element.272.refs_1_.refs_2_), channel_id=1, source_target_pairs={{0,2},{1,3},{2,4},{3,5},{4,6},{5,7},{6,0},{7,1},{8,10},{9,11},{10,... | collective-permute-start | bytes 442376 | tf_op jit(solution)/shard_map/ppermute | solution.py:1306
  6.5 10.2 %collective-permute-start = (bf16[144,512]{1,0:T(8,128)(2,1)}, bf16[144,512]{1,0:T(8,128)(2,1)S(1)}, u32[]{:S(2)}, u32[]{:S(2)}) collective-permute-start(bf16[144,512]{1,0:T(8,128)(2,1)} %get-tuple-element.272.refs_1_.refs_2_), channel_id=1, source_target_pairs={{0,4},{1,5},{2,6},{3,7},{4,0},{5,1},{6,2},{7,3},{8,12},{9,13},{10,... | collective-permute-start | bytes 442376 | tf_op jit(solution)/shard_map/ppermute | solution.py:1306
  9.8 8.2 %collective-permute-start.2 = (bf16[144,512]{1,0:T(8,128)(2,1)}, bf16[144,512]{1,0:T(8,128)(2,1)S(1)}, u32[]{:S(2)}, u32[]{:S(2)}) collective-permute-start(bf16[144,512]{1,0:T(8,128)(2,1)} %get-tuple-element.272.refs_1_.refs_2_), channel_id=1, source_target_pairs={{0,6},{1,7},{2,0},{3,1},{4,2},{5,3},{6,4},{7,5},{8,14},{9,15},{10,... | collective-permute-start | bytes 442376 | tf_op jit(solution)/shard_map/ppermute | solution.py:1306
  12.7 9.6 %collective-permute-start.3 = (bf16[144,512]{1,0:T(8,128)(2,1)}, bf16[144,512]{1,0:T(8,128)(2,1)S(1)}, u32[]{:S(2)}, u32[]{:S(2)}) collective-permute-start(bf16[144,512]{1,0:T(8,128)(2,1)} %get-tuple-element.272.refs_1_.refs_2_), channel_id=1, source_target_pairs={{0,1},{1,0},{2,3},{3,2},{4,5},{5,4},{6,7},{7,6},{8,9},{9,8},{10,11... | collective-permute-start | bytes 442376 | tf_op jit(solution)/shard_map/ppermute | solution.py:1301
  16.7 9.9 %collective-permute-start.7 = (bf16[512,512]{1,0:T(8,128)(2,1)}, bf16[512,512]{1,0:T(8,128)(2,1)S(1)}, u32[]{:S(2)}, u32[]{:S(2)}) collective-permute-start(bf16[512,512]{1,0:T(8,128)(2,1)} %bitcast.61), channel_id=1, source_target_pairs={{0,1},{1,0},{2,3},{3,2},{4,5},{5,4},{6,7},{7,6},{8,9},{9,8},{10,11... | collective-permute-start | bytes 1572872 | tf_op jit(solution)/shard_map/ppermute | solution.py:1301
  18.0 8.6 %collective-permute-start.8 = (bf16[512,512]{1,0:T(8,128)(2,1)}, bf16[512,512]{1,0:T(8,128)(2,1)S(1)}, u32[]{:S(2)}, u32[]{:S(2)}) collective-permute-start(bf16[512,512]{1,0:T(8,128)(2,1)} %bitcast.68), channel_id=1, source_target_pairs={{0,1},{1,0},{2,3},{3,2},{4,5},{5,4},{6,7},{7,6},{8,9},{9,8},{10,11... | collective-permute-start | bytes 1572872 | tf_op jit(solution)/shard_map/ppermute | solution.py:1301
  46.8 9.5 %collective-permute-start.10 = (bf16[128,512]{1,0:T(8,128)(2,1)}, bf16[128,512]{1,0:T(8,128)(2,1)S(1)}, u32[]{:S(2)}, u32[]{:S(2)}) collective-permute-start(bf16[128,512]{1,0:T(8,128)(2,1)} %get-tuple-element.285), channel_id=1, source_target_pairs={{0,4},{1,5},{2,6},{3,7},{4,0},{5,1},{6,2},{7,3},{8,12},{9,13},{10,... | collective-permute-start | bytes 393224 | tf_op jit(solution)/shard_map/ppermute | solution.py:1306
  76.1 7.6 %collective-permute-start.18 = (bf16[80,512]{1,0:T(8,128)(2,1)S(1)}, bf16[80,512]{1,0:T(8,128)(2,1)S(1)}, u32[]{:S(2)}, u32[]{:S(2)}) collective-permute-start(bf16[80,512]{1,0:T(8,128)(2,1)S(1)} %get-tuple-element.301), channel_id=1, source_target_pairs={{0,4},{1,5},{2,6},{3,7},{4,0},{5,1},{6,2},{7,3},{8,12},{9,13},{10,... | collective-permute-start | bytes 245768 | tf_op jit(solution)/shard_map/ppermute | solution.py:1306
  76.1 7.6 %collective-permute-start.19 = (bf16[80,512]{1,0:T(8,128)(2,1)S(1)}, bf16[80,512]{1,0:T(8,128)(2,1)S(1)}, u32[]{:S(2)}, u32[]{:S(2)}) collective-permute-start(bf16[80,512]{1,0:T(8,128)(2,1)S(1)} %get-tuple-element.305), channel_id=1, source_target_pairs={{0,2},{1,3},{2,4},{3,5},{4,6},{5,7},{6,0},{7,1},{8,10},{9,11},{10,... | collective-permute-start | bytes 245768 | tf_op jit(solution)/shard_map/ppermute | solution.py:1306
  84.6 8.7 %collective-permute-start.20 = (bf16[128,512]{1,0:T(8,128)(2,1)S(1)}, bf16[128,512]{1,0:T(8,128)(2,1)S(1)}, u32[]{:S(2)}, u32[]{:S(2)}) collective-permute-start(bf16[128,512]{1,0:T(8,128)(2,1)S(1)} %get-tuple-element.308.refs_1_), channel_id=1, source_target_pairs={{0,2},{1,3},{2,4},{3,5},{4,6},{5,7},{6,0},{7,1},{8,10},{9,11},{10,... | collective-permute-start | bytes 393224 | tf_op jit(solution)/shard_map/ppermute | solution.py:1306
  85.0 9.8 %collective-permute-start.21 = (bf16[128,512]{1,0:T(8,128)(2,1)S(1)}, bf16[128,512]{1,0:T(8,128)(2,1)S(1)}, u32[]{:S(2)}, u32[]{:S(2)}) collective-permute-start(bf16[128,512]{1,0:T(8,128)(2,1)S(1)} %get-tuple-element.308.refs_1_), channel_id=1, source_target_pairs={{0,4},{1,5},{2,6},{3,7},{4,0},{5,1},{6,2},{7,3},{8,12},{9,13},{10,... | collective-permute-start | bytes 393224 | tf_op jit(solution)/shard_map/ppermute | solution.py:1306
  88.9 8.7 %collective-permute-start.22 = (bf16[128,512]{1,0:T(8,128)(2,1)S(1)}, bf16[128,512]{1,0:T(8,128)(2,1)S(1)}, u32[]{:S(2)}, u32[]{:S(2)}) collective-permute-start(bf16[128,512]{1,0:T(8,128)(2,1)S(1)} %get-tuple-element.308.refs_1_), channel_id=1, source_target_pairs={{0,6},{1,7},{2,0},{3,1},{4,2},{5,3},{6,4},{7,5},{8,14},{9,15},{10,... | collective-permute-start | bytes 393224 | tf_op jit(solution)/shard_map/ppermute | solution.py:1306
  88.9 9.3 %collective-permute-start.23 = (bf16[128,512]{1,0:T(8,128)(2,1)S(1)}, bf16[128,512]{1,0:T(8,128)(2,1)S(1)}, u32[]{:S(2)}, u32[]{:S(2)}) collective-permute-start(bf16[128,512]{1,0:T(8,128)(2,1)S(1)} %get-tuple-element.308.refs_1_), channel_id=1, source_target_pairs={{0,1},{1,0},{2,3},{3,2},{4,5},{5,4},{6,7},{7,6},{8,9},{9,8},{10,11... | collective-permute-start | bytes 393224 | tf_op jit(solution)/shard_map/ppermute | solution.py:1301
  115.9 9.4 %collective-permute-start.27 = (bf16[128,512]{1,0:T(8,128)(2,1)}, bf16[128,512]{1,0:T(8,128)(2,1)S(1)}, u32[]{:S(2)}, u32[]{:S(2)}) collective-permute-start(bf16[128,512]{1,0:T(8,128)(2,1)} %get-tuple-element.314), channel_id=1, source_target_pairs={{0,2},{1,3},{2,4},{3,5},{4,6},{5,7},{6,0},{7,1},{8,10},{9,11},{10,... | collective-permute-start | bytes 393224 | tf_op jit(solution)/shard_map/ppermute | solution.py:1306
  116.0 9.4 %collective-permute-start.28 = (bf16[128,512]{1,0:T(8,128)(2,1)}, bf16[128,512]{1,0:T(8,128)(2,1)S(1)}, u32[]{:S(2)}, u32[]{:S(2)}) collective-permute-start(bf16[128,512]{1,0:T(8,128)(2,1)} %get-tuple-element.315), channel_id=1, source_target_pairs={{0,4},{1,5},{2,6},{3,7},{4,0},{5,1},{6,2},{7,3},{8,12},{9,13},{10,... | collective-permute-start | bytes 393224 | tf_op jit(solution)/shard_map/ppermute | solution.py:1306
  118.0 7.6 %collective-permute-start.29 = (bf16[128,512]{1,0:T(8,128)(2,1)}, bf16[128,512]{1,0:T(8,128)(2,1)S(1)}, u32[]{:S(2)}, u32[]{:S(2)}) collective-permute-start(bf16[128,512]{1,0:T(8,128)(2,1)} %get-tuple-element.316), channel_id=1, source_target_pairs={{0,6},{1,7},{2,0},{3,1},{4,2},{5,3},{6,4},{7,5},{8,14},{9,15},{10,... | collective-permute-start | bytes 393224 | tf_op jit(solution)/shard_map/ppermute | solution.py:1306
  146.9 7.3 %collective-permute-start.34 = (bf16[80,512]{1,0:T(8,128)(2,1)}, bf16[80,512]{1,0:T(8,128)(2,1)S(1)}, u32[]{:S(2)}, u32[]{:S(2)}) collective-permute-start(bf16[80,512]{1,0:T(8,128)(2,1)} %get-tuple-element.328), channel_id=1, source_target_pairs={{0,4},{1,5},{2,6},{3,7},{4,0},{5,1},{6,2},{7,3},{8,12},{9,13},{10,... | collective-permute-start | bytes 245768 | tf_op jit(solution)/shard_map/ppermute | solution.py:1306
  146.9 7.3 %collective-permute-start.35 = (bf16[80,512]{1,0:T(8,128)(2,1)S(1)}, bf16[80,512]{1,0:T(8,128)(2,1)S(1)}, u32[]{:S(2)}, u32[]{:S(2)}) collective-permute-start(bf16[80,512]{1,0:T(8,128)(2,1)S(1)} %get-tuple-element.332), channel_id=1, source_target_pairs={{0,2},{1,3},{2,4},{3,5},{4,6},{5,7},{6,0},{7,1},{8,10},{9,11},{10,... | collective-permute-start | bytes 245768 | tf_op jit(solution)/shard_map/ppermute | solution.py:1306
  155.0 7.6 %collective-permute-start.36 = (bf16[128,512]{1,0:T(8,128)(2,1)S(1)}, bf16[128,512]{1,0:T(8,128)(2,1)S(1)}, u32[]{:S(2)}, u32[]{:S(2)}) collective-permute-start(bf16[128,512]{1,0:T(8,128)(2,1)S(1)} %get-tuple-element.335.refs_1_), channel_id=1, source_target_pairs={{0,2},{1,3},{2,4},{3,5},{4,6},{5,7},{6,0},{7,1},{8,10},{9,11},{10,... | collective-permute-start | bytes 393224 | tf_op jit(solution)/shard_map/ppermute | solution.py:1306
  155.7 9.8 %collective-permute-start.37 = (bf16[128,512]{1,0:T(8,128)(2,1)S(1)}, bf16[128,512]{1,0:T(8,128)(2,1)S(1)}, u32[]{:S(2)}, u32[]{:S(2)}) collective-permute-start(bf16[128,512]{1,0:T(8,128)(2,1)S(1)} %get-tuple-element.335.refs_1_), channel_id=1, source_target_pairs={{0,4},{1,5},{2,6},{3,7},{4,0},{5,1},{6,2},{7,3},{8,12},{9,13},{10,... | collective-permute-start | bytes 393224 | tf_op jit(solution)/shard_map/ppermute | solution.py:1306
  160.1 7.3 %collective-permute-start.38 = (bf16[128,512]{1,0:T(8,128)(2,1)S(1)}, bf16[128,512]{1,0:T(8,128)(2,1)S(1)}, u32[]{:S(2)}, u32[]{:S(2)}) collective-permute-start(bf16[128,512]{1,0:T(8,128)(2,1)S(1)} %get-tuple-element.335.refs_1_), channel_id=1, source_target_pairs={{0,6},{1,7},{2,0},{3,1},{4,2},{5,3},{6,4},{7,5},{8,14},{9,15},{10,... | collective-permute-start | bytes 393224 | tf_op jit(solution)/shard_map/ppermute | solution.py:1306
  160.1 7.5 %collective-permute-start.39 = (bf16[128,512]{1,0:T(8,128)(2,1)S(1)}, bf16[128,512]{1,0:T(8,128)(2,1)S(1)}, u32[]{:S(2)}, u32[]{:S(2)}) collective-permute-start(bf16[128,512]{1,0:T(8,128)(2,1)S(1)} %get-tuple-element.335.refs_1_), channel_id=1, source_target_pairs={{0,1},{1,0},{2,3},{3,2},{4,5},{5,4},{6,7},{7,6},{8,9},{9,8},{10,11... | collective-permute-start | bytes 393224 | tf_op jit(solution)/shard_map/ppermute | solution.py:1301
  182.5 9.8 %collective-permute-start.44 = (bf16[128,512]{1,0:T(8,128)(2,1)}, bf16[128,512]{1,0:T(8,128)(2,1)S(1)}, u32[]{:S(2)}, u32[]{:S(2)}) collective-permute-start(bf16[128,512]{1,0:T(8,128)(2,1)} %get-tuple-element.342), channel_id=1, source_target_pairs={{0,4},{1,5},{2,6},{3,7},{4,0},{5,1},{6,2},{7,3},{8,12},{9,13},{10,... | collective-permute-start | bytes 393224 | tf_op jit(solution)/shard_map/ppermute | solution.py:1306
  269.6 8.9 %collective-permute-start.61 = (bf16[4,128,512]{2,1,0:T(8,128)(2,1)S(1)}, bf16[4,128,512]{2,1,0:T(8,128)(2,1)S(1)}, u32[]{:S(2)}, u32[]{:S(2)}) collective-permute-start(bf16[4,128,512]{2,1,0:T(8,128)(2,1)S(1)} %get-tuple-element.387), channel_id=1, source_target_pairs={{0,1},{1,0},{2,3},{3,2},{4,5},{5,4},{6,7},{7,6},{8,9},{9,8},{10,11... | collective-permute-start | bytes 1572872 | tf_op jit(solution)/shard_map/ppermute | solution.py:1301
  277.0 8.9 %collective-permute-start.64 = (bf16[512,512]{1,0:T(8,128)(2,1)S(1)}, bf16[512,512]{1,0:T(8,128)(2,1)S(1)}, u32[]{:S(2)}, u32[]{:S(2)}) collective-permute-start(bf16[512,512]{1,0:T(8,128)(2,1)S(1)} %copy-done.56), channel_id=1, source_target_pairs={{0,1},{1,0},{2,3},{3,2},{4,5},{5,4},{6,7},{7,6},{8,9},{9,8},{10,11... | collective-permute-start | bytes 1572872 | tf_op jit(solution)/shard_map/ppermute | solution.py:1301
  277.0 8.9 %collective-permute-start.65 = (bf16[512,512]{1,0:T(8,128)(2,1)S(1)}, bf16[512,512]{1,0:T(8,128)(2,1)S(1)}, u32[]{:S(2)}, u32[]{:S(2)}) collective-permute-start(bf16[512,512]{1,0:T(8,128)(2,1)S(1)} %get-tuple-element.394), channel_id=1, source_target_pairs={{0,1},{1,0},{2,3},{3,2},{4,5},{5,4},{6,7},{7,6},{8,9},{9,8},{10,11... | collective-permute-start | bytes 1572872 | tf_op jit(solution)/shard_map/ppermute | solution.py:1301
  277.5 8.4 %collective-permute-start.66 = (bf16[512,512]{1,0:T(8,128)(2,1)S(1)}, bf16[512,512]{1,0:T(8,128)(2,1)S(1)}, u32[]{:S(2)}, u32[]{:S(2)}) collective-permute-start(bf16[512,512]{1,0:T(8,128)(2,1)S(1)} %get-tuple-element.396), channel_id=1, source_target_pairs={{0,1},{1,0},{2,3},{3,2},{4,5},{5,4},{6,7},{7,6},{8,9},{9,8},{10,11... | collective-permute-start | bytes 1572872 | tf_op jit(solution)/shard_map/ppermute | solution.py:1301
  279.8 8.6 %collective-permute-start.63 = (bf16[128,512]{1,0:T(8,128)(2,1)S(1)}, bf16[128,512]{1,0:T(8,128)(2,1)S(1)}, u32[]{:S(2)}, u32[]{:S(2)}) collective-permute-start(bf16[128,512]{1,0:T(8,128)(2,1)S(1)} %get-tuple-element.392), channel_id=1, source_target_pairs={{0,4},{1,5},{2,6},{3,7},{4,0},{5,1},{6,2},{7,3},{8,12},{9,13},{10,... | collective-permute-start | bytes 393224 | tf_op jit(solution)/shard_map/ppermute | solution.py:1306
  317.2 7.2 %collective-permute-start.75 = (bf16[128,512]{1,0:T(8,128)(2,1)S(1)}, bf16[128,512]{1,0:T(8,128)(2,1)S(1)}, u32[]{:S(2)}, u32[]{:S(2)}) collective-permute-start(bf16[128,512]{1,0:T(8,128)(2,1)S(1)} %get-tuple-element.421.refs_1_), channel_id=1, source_target_pairs={{0,4},{1,5},{2,6},{3,7},{4,0},{5,1},{6,2},{7,3},{8,12},{9,13},{10,... | collective-permute-start | bytes 393224 | tf_op jit(solution)/shard_map/ppermute | solution.py:1306
  347.1 6.8 %collective-permute-start.77 = (bf16[4,128,512]{2,1,0:T(8,128)(2,1)S(1)}, bf16[4,128,512]{2,1,0:T(8,128)(2,1)S(1)}, u32[]{:S(2)}, u32[]{:S(2)}) collective-permute-start(bf16[4,128,512]{2,1,0:T(8,128)(2,1)S(1)} %get-tuple-element.436), channel_id=1, source_target_pairs={{0,1},{1,0},{2,3},{3,2},{4,5},{5,4},{6,7},{7,6},{8,9},{9,8},{10,11... | collective-permute-start | bytes 1572872 | tf_op jit(solution)/shard_map/ppermute | solution.py:1301
  352.4 9.4 %collective-permute-start.80 = (bf16[512,512]{1,0:T(8,128)(2,1)S(1)}, bf16[512,512]{1,0:T(8,128)(2,1)S(1)}, u32[]{:S(2)}, u32[]{:S(2)}) collective-permute-start(bf16[512,512]{1,0:T(8,128)(2,1)S(1)} %copy-done.55), channel_id=1, source_target_pairs={{0,1},{1,0},{2,3},{3,2},{4,5},{5,4},{6,7},{7,6},{8,9},{9,8},{10,11... | collective-permute-start | bytes 1572872 | tf_op jit(solution)/shard_map/ppermute | solution.py:1301
  352.5 9.4 %collective-permute-start.81 = (bf16[512,512]{1,0:T(8,128)(2,1)S(1)}, bf16[512,512]{1,0:T(8,128)(2,1)S(1)}, u32[]{:S(2)}, u32[]{:S(2)}) collective-permute-start(bf16[512,512]{1,0:T(8,128)(2,1)S(1)} %get-tuple-element.443), channel_id=1, source_target_pairs={{0,1},{1,0},{2,3},{3,2},{4,5},{5,4},{6,7},{7,6},{8,9},{9,8},{10,11... | collective-permute-start | bytes 1572872 | tf_op jit(solution)/shard_map/ppermute | solution.py:1301
  352.9 9.4 %collective-permute-start.82 = (bf16[512,512]{1,0:T(8,128)(2,1)S(1)}, bf16[512,512]{1,0:T(8,128)(2,1)S(1)}, u32[]{:S(2)}, u32[]{:S(2)}) collective-permute-start(bf16[512,512]{1,0:T(8,128)(2,1)S(1)} %get-tuple-element.445), channel_id=1, source_target_pairs={{0,1},{1,0},{2,3},{3,2},{4,5},{5,4},{6,7},{7,6},{8,9},{9,8},{10,11... | collective-permute-start | bytes 1572872 | tf_op jit(solution)/shard_map/ppermute | solution.py:1301
  356.2 8.4 %collective-permute-start.79 = (bf16[128,512]{1,0:T(8,128)(2,1)S(1)}, bf16[128,512]{1,0:T(8,128)(2,1)S(1)}, u32[]{:S(2)}, u32[]{:S(2)}) collective-permute-start(bf16[128,512]{1,0:T(8,128)(2,1)S(1)} %get-tuple-element.441), channel_id=1, source_target_pairs={{0,4},{1,5},{2,6},{3,7},{4,0},{5,1},{6,2},{7,3},{8,12},{9,13},{10,... | collective-permute-start | bytes 393224 | tf_op jit(solution)/shard_map/ppermute | solution.py:1306
  360.9 33.8 %collective-permute-start.92 = (bf16[160,2048]{1,0:T(8,128)(2,1)S(1)}, bf16[160,2048]{1,0:T(8,128)(2,1)S(1)}, u32[]{:S(2)}, u32[]{:S(2)}) collective-permute-start(bf16[160,2048]{1,0:T(8,128)(2,1)S(1)} %get-tuple-element.461), channel_id=1, source_target_pairs={{0,1},{1,0},{2,3},{3,2},{4,5},{5,4},{6,7},{7,6},{8,9},{9,8},{10,11... | collective-permute-start | bytes 1966088 | tf_op jit(solution)/shard_map/ppermute | solution.py:1301
  361.8 12.7 %collective-permute-start.91 = (bf16[160,512]{1,0:T(8,128)(2,1)S(1)}, bf16[160,512]{1,0:T(8,128)(2,1)S(1)}, u32[]{:S(2)}, u32[]{:S(2)}) collective-permute-start(bf16[160,512]{1,0:T(8,128)(2,1)S(1)} %copy-done.61), channel_id=1, source_target_pairs={{0,1},{1,0},{2,3},{3,2},{4,5},{5,4},{6,7},{7,6},{8,9},{9,8},{10,11... | collective-permute-start | bytes 491528 | tf_op jit(solution)/shard_map/ppermute | solution.py:1301
  361.9 14.1 %collective-permute-start.90 = (bf16[160,512]{1,0:T(8,128)(2,1)S(1)}, bf16[160,512]{1,0:T(8,128)(2,1)S(1)}, u32[]{:S(2)}, u32[]{:S(2)}) collective-permute-start(bf16[160,512]{1,0:T(8,128)(2,1)S(1)} %copy-done.65), channel_id=1, source_target_pairs={{0,1},{1,0},{2,3},{3,2},{4,5},{5,4},{6,7},{7,6},{8,9},{9,8},{10,11... | collective-permute-start | bytes 491528 | tf_op jit(solution)/shard_map/ppermute | solution.py:1301
  362.3 15.3 %collective-permute-start.89 = (bf16[160,512]{1,0:T(8,128)(2,1)S(1)}, bf16[160,512]{1,0:T(8,128)(2,1)S(1)}, u32[]{:S(2)}, u32[]{:S(2)}) collective-permute-start(bf16[160,512]{1,0:T(8,128)(2,1)S(1)} %copy-done.68), channel_id=1, source_target_pairs={{0,1},{1,0},{2,3},{3,2},{4,5},{5,4},{6,7},{7,6},{8,9},{9,8},{10,11... | collective-permute-start | bytes 491528 | tf_op jit(solution)/shard_map/ppermute | solution.py:1301
  376.0 6.9 %collective-permute-start.86 = (bf16[80,512]{1,0:T(8,128)(2,1)S(1)}, bf16[80,512]{1,0:T(8,128)(2,1)S(1)}, u32[]{:S(2)}, u32[]{:S(2)}) collective-permute-start(bf16[80,512]{1,0:T(8,128)(2,1)S(1)} %get-tuple-element.454), channel_id=1, source_target_pairs={{0,6},{1,7},{2,0},{3,1},{4,2},{5,3},{6,4},{7,5},{8,14},{9,15},{10,... | collective-permute-start | bytes 245768 | tf_op jit(solution)/shard_map/ppermute | solution.py:1306
  377.6 17.2 %collective-permute-start.98 = (bf16[160,2048]{1,0:T(8,128)(2,1)S(1)}, bf16[160,2048]{1,0:T(8,128)(2,1)S(1)}, u32[]{:S(2)}, u32[]{:S(2)}) collective-permute-start(bf16[160,2048]{1,0:T(8,128)(2,1)S(1)} %get-tuple-element.473), channel_id=1, source_target_pairs={{0,1},{1,0},{2,3},{3,2},{4,5},{5,4},{6,7},{7,6},{8,9},{9,8},{10,11... | collective-permute-start | bytes 1966088 | tf_op jit(solution)/shard_map/ppermute | solution.py:1301
  379.7 14.6 %collective-permute-start.95 = (bf16[160,512]{1,0:T(8,128)(2,1)S(1)}, bf16[160,512]{1,0:T(8,128)(2,1)S(1)}, u32[]{:S(2)}, u32[]{:S(2)}) collective-permute-start(bf16[160,512]{1,0:T(8,128)(2,1)S(1)} %get-tuple-element.467), channel_id=1, source_target_pairs={{0,1},{1,0},{2,3},{3,2},{4,5},{5,4},{6,7},{7,6},{8,9},{9,8},{10,11... | collective-permute-start | bytes 491528 | tf_op jit(solution)/shard_map/ppermute | solution.py:1301
  380.8 17.1 %collective-permute-start.93 = (bf16[160,2048]{1,0:T(8,128)(2,1)S(1)}, bf16[160,2048]{1,0:T(8,128)(2,1)S(1)}, u32[]{:S(2)}, u32[]{:S(2)}) collective-permute-start(bf16[160,2048]{1,0:T(8,128)(2,1)S(1)} %get-tuple-element.463), channel_id=1, source_target_pairs={{0,1},{1,0},{2,3},{3,2},{4,5},{5,4},{6,7},{7,6},{8,9},{9,8},{10,11... | collective-permute-start | bytes 1966088 | tf_op jit(solution)/shard_map/ppermute | solution.py:1301
  382.9 16.4 %collective-permute-start.99 = (bf16[160,2048]{1,0:T(8,128)(2,1)S(1)}, bf16[160,2048]{1,0:T(8,128)(2,1)S(1)}, u32[]{:S(2)}, u32[]{:S(2)}) collective-permute-start(bf16[160,2048]{1,0:T(8,128)(2,1)S(1)} %get-tuple-element.475), channel_id=1, source_target_pairs={{0,1},{1,0},{2,3},{3,2},{4,5},{5,4},{6,7},{7,6},{8,9},{9,8},{10,11... | collective-permute-start | bytes 1966088 | tf_op jit(solution)/shard_map/ppermute | solution.py:1301
  394.2 7.8 %collective-permute-start.100 = (bf16[160,2048]{1,0:T(8,128)(2,1)S(1)}, bf16[160,2048]{1,0:T(8,128)(2,1)S(1)}, u32[]{:S(2)}, u32[]{:S(2)}) collective-permute-start(bf16[160,2048]{1,0:T(8,128)(2,1)S(1)} %get-tuple-element.477), channel_id=1, source_target_pairs={{0,1},{1,0},{2,3},{3,2},{4,5},{5,4},{6,7},{7,6},{8,9},{9,8},{10,11... | collective-permute-start | bytes 1966088 | tf_op jit(solution)/shard_map/ppermute | solution.py:1301
  394.7 7.3 %collective-permute-start.94 = (bf16[160,2048]{1,0:T(8,128)(2,1)S(1)}, bf16[160,2048]{1,0:T(8,128)(2,1)S(1)}, u32[]{:S(2)}, u32[]{:S(2)}) collective-permute-start(bf16[160,2048]{1,0:T(8,128)(2,1)S(1)} %get-tuple-element.465), channel_id=1, source_target_pairs={{0,1},{1,0},{2,3},{3,2},{4,5},{5,4},{6,7},{7,6},{8,9},{9,8},{10,11... | collective-permute-start | bytes 1966088 | tf_op jit(solution)/shard_map/ppermute | solution.py:1301
  397.9 14.8 %collective-permute-start.88 = (bf16[80,512]{1,0:T(8,128)(2,1)S(1)}, bf16[80,512]{1,0:T(8,128)(2,1)S(1)}, u32[]{:S(2)}, u32[]{:S(2)}) collective-permute-start(bf16[80,512]{1,0:T(8,128)(2,1)S(1)} %get-tuple-element.459), channel_id=1, source_target_pairs={{0,4},{1,5},{2,6},{3,7},{4,0},{5,1},{6,2},{7,3},{8,12},{9,13},{10,... | collective-permute-start | bytes 245768 | tf_op jit(solution)/shard_map/ppermute | solution.py:1306
  399.3 13.4 %collective-permute-start.101 = (bf16[80,512]{1,0:T(8,128)(2,1)S(1)}, bf16[80,512]{1,0:T(8,128)(2,1)S(1)}, u32[]{:S(2)}, u32[]{:S(2)}) collective-permute-start(bf16[80,512]{1,0:T(8,128)(2,1)S(1)} %get-tuple-element.479), channel_id=1, source_target_pairs={{0,2},{1,3},{2,4},{3,5},{4,6},{5,7},{6,0},{7,1},{8,10},{9,11},{10,... | collective-permute-start | bytes 245768 | tf_op jit(solution)/shard_map/ppermute | solution.py:1306
  400.3 12.5 %collective-permute-start.87 = (bf16[80,512]{1,0:T(8,128)(2,1)S(1)}, bf16[80,512]{1,0:T(8,128)(2,1)S(1)}, u32[]{:S(2)}, u32[]{:S(2)}) collective-permute-start(bf16[80,512]{1,0:T(8,128)(2,1)S(1)} %get-tuple-element.458), channel_id=1, source_target_pairs={{0,6},{1,7},{2,0},{3,1},{4,2},{5,3},{6,4},{7,5},{8,14},{9,15},{10,... | collective-permute-start | bytes 245768 | tf_op jit(solution)/shard_map/ppermute | solution.py:1306
  415.1 10.8 %collective-permute-start.102 = (bf16[128,512]{1,0:T(8,128)(2,1)S(1)}, bf16[128,512]{1,0:T(8,128)(2,1)S(1)}, u32[]{:S(2)}, u32[]{:S(2)}) collective-permute-start(bf16[128,512]{1,0:T(8,128)(2,1)S(1)} %get-tuple-element.484.refs_1_), channel_id=1, source_target_pairs={{0,2},{1,3},{2,4},{3,5},{4,6},{5,7},{6,0},{7,1},{8,10},{9,11},{10,... | collective-permute-start | bytes 393224 | tf_op jit(solution)/shard_map/ppermute | solution.py:1306
  415.1 10.8 %collective-permute-start.103 = (bf16[128,512]{1,0:T(8,128)(2,1)S(1)}, bf16[128,512]{1,0:T(8,128)(2,1)S(1)}, u32[]{:S(2)}, u32[]{:S(2)}) collective-permute-start(bf16[128,512]{1,0:T(8,128)(2,1)S(1)} %get-tuple-element.484.refs_1_), channel_id=1, source_target_pairs={{0,4},{1,5},{2,6},{3,7},{4,0},{5,1},{6,2},{7,3},{8,12},{9,13},{10,... | collective-permute-start | bytes 393224 | tf_op jit(solution)/shard_map/ppermute | solution.py:1306
  416.3 9.6 %collective-permute-start.104 = (bf16[128,512]{1,0:T(8,128)(2,1)S(1)}, bf16[128,512]{1,0:T(8,128)(2,1)S(1)}, u32[]{:S(2)}, u32[]{:S(2)}) collective-permute-start(bf16[128,512]{1,0:T(8,128)(2,1)S(1)} %get-tuple-element.484.refs_1_), channel_id=1, source_target_pairs={{0,6},{1,7},{2,0},{3,1},{4,2},{5,3},{6,4},{7,5},{8,14},{9,15},{10,... | collective-permute-start | bytes 393224 | tf_op jit(solution)/shard_map/ppermute | solution.py:1306
  417.8 67.0 %all-to-all-start = ((bf16[16,256,512]{2,1,0:T(8,128)(2,1)}), bf16[16,256,512]{2,1,0:T(8,128)(2,1)}, u32[]{:S(2)}, u32[]{:S(2)}) async-start(bf16[16,256,512]{2,1,0:T(8,128)(2,1)} %feed_weights.1), calls=%async_computation | async-start | bytes 8388608 | tf_op jit(solution)/shard_map/all_to_all | solution.py:1326
  462.7 8.1 %collective-permute-start.112 = (bf16[4,128,512]{2,1,0:T(8,128)(2,1)}, bf16[4,128,512]{2,1,0:T(8,128)(2,1)S(1)}, u32[]{:S(2)}, u32[]{:S(2)}) collective-permute-start(bf16[4,128,512]{2,1,0:T(8,128)(2,1)} %get-tuple-element.516), channel_id=1, source_target_pairs={{0,1},{1,0},{2,3},{3,2},{4,5},{5,4},{6,7},{7,6},{8,9},{9,8},{10,11... | collective-permute-start | bytes 1572872 | tf_op jit(solution)/shard_map/ppermute | solution.py:1301
  463.1 11.9 %collective-permute-start.105 = (bf16[512,512]{1,0:T(8,128)(2,1)S(1)}, bf16[512,512]{1,0:T(8,128)(2,1)}, u32[]{:S(2)}, u32[]{:S(2)}) collective-permute-start(bf16[512,512]{1,0:T(8,128)(2,1)S(1)} %copy-done.131), channel_id=1, source_target_pairs={{0,1},{1,0},{2,3},{3,2},{4,5},{5,4},{6,7},{7,6},{8,9},{9,8},{10,11... | collective-permute-start | bytes 1572872 | tf_op jit(solution)/shard_map/ppermute | solution.py:1301
  463.2 11.8 %collective-permute-start.107 = (bf16[512,512]{1,0:T(8,128)(2,1)S(1)}, bf16[512,512]{1,0:T(8,128)(2,1)}, u32[]{:S(2)}, u32[]{:S(2)}) collective-permute-start(bf16[512,512]{1,0:T(8,128)(2,1)S(1)} %copy-done.129), channel_id=1, source_target_pairs={{0,1},{1,0},{2,3},{3,2},{4,5},{5,4},{6,7},{7,6},{8,9},{9,8},{10,11... | collective-permute-start | bytes 1572872 | tf_op jit(solution)/shard_map/ppermute | solution.py:1301
  467.4 9.6 %collective-permute-start.109 = (bf16[64,1152]{1,0:T(8,128)(2,1)}, bf16[64,1152]{1,0:T(8,128)(2,1)S(1)}, u32[]{:S(2)}, u32[]{:S(2)}) collective-permute-start(bf16[64,1152]{1,0:T(8,128)(2,1)} %get-tuple-element.508), channel_id=1, source_target_pairs={{0,2},{1,3},{2,4},{3,5},{4,6},{5,7},{6,0},{7,1},{8,10},{9,11},{10,... | collective-permute-start | bytes 442376 | tf_op jit(solution)/shard_map/ppermute | solution.py:1306
  467.5 10.6 %collective-permute-start.110 = (bf16[64,1152]{1,0:T(8,128)(2,1)}, bf16[64,1152]{1,0:T(8,128)(2,1)S(1)}, u32[]{:S(2)}, u32[]{:S(2)}) collective-permute-start(bf16[64,1152]{1,0:T(8,128)(2,1)} %get-tuple-element.509), channel_id=1, source_target_pairs={{0,4},{1,5},{2,6},{3,7},{4,0},{5,1},{6,2},{7,3},{8,12},{9,13},{10,... | collective-permute-start | bytes 442376 | tf_op jit(solution)/shard_map/ppermute | solution.py:1306
  470.8 7.3 %collective-permute-start.111 = (bf16[64,1152]{1,0:T(8,128)(2,1)}, bf16[64,1152]{1,0:T(8,128)(2,1)S(1)}, u32[]{:S(2)}, u32[]{:S(2)}) collective-permute-start(bf16[64,1152]{1,0:T(8,128)(2,1)} %get-tuple-element.510), channel_id=1, source_target_pairs={{0,6},{1,7},{2,0},{3,1},{4,2},{5,3},{6,4},{7,5},{8,14},{9,15},{10,... | collective-permute-start | bytes 442376 | tf_op jit(solution)/shard_map/ppermute | solution.py:1306
  474.9 9.8 %collective-permute-start.113 = (bf16[128,512]{1,0:T(8,128)(2,1)}, bf16[128,512]{1,0:T(8,128)(2,1)S(1)}, u32[]{:S(2)}, u32[]{:S(2)}) collective-permute-start(bf16[128,512]{1,0:T(8,128)(2,1)} %get-tuple-element.518), channel_id=1, source_target_pairs={{0,2},{1,3},{2,4},{3,5},{4,6},{5,7},{6,0},{7,1},{8,10},{9,11},{10,... | collective-permute-start | bytes 393224 | tf_op jit(solution)/shard_map/ppermute | solution.py:1306
  475.0 9.7 %collective-permute-start.114 = (bf16[128,512]{1,0:T(8,128)(2,1)}, bf16[128,512]{1,0:T(8,128)(2,1)S(1)}, u32[]{:S(2)}, u32[]{:S(2)}) collective-permute-start(bf16[128,512]{1,0:T(8,128)(2,1)} %get-tuple-element.519), channel_id=1, source_target_pairs={{0,4},{1,5},{2,6},{3,7},{4,0},{5,1},{6,2},{7,3},{8,12},{9,13},{10,... | collective-permute-start | bytes 393224 | tf_op jit(solution)/shard_map/ppermute | solution.py:1306
  477.0 7.8 %collective-permute-start.115 = (bf16[128,512]{1,0:T(8,128)(2,1)}, bf16[128,512]{1,0:T(8,128)(2,1)S(1)}, u32[]{:S(2)}, u32[]{:S(2)}) collective-permute-start(bf16[128,512]{1,0:T(8,128)(2,1)} %get-tuple-element.520), channel_id=1, source_target_pairs={{0,6},{1,7},{2,0},{3,1},{4,2},{5,3},{6,4},{7,5},{8,14},{9,15},{10,... | collective-permute-start | bytes 393224 | tf_op jit(solution)/shard_map/ppermute | solution.py:1306
  484.8 25.6 %all-to-all-start.1 = ((bf16[16,80,512]{2,1,0:T(8,128)(2,1)}), bf16[16,80,512]{2,1,0:T(8,128)(2,1)S(1)}, u32[]{:S(2)}, u32[]{:S(2)}) async-start(bf16[16,80,512]{2,1,0:T(8,128)(2,1)} %last_weights.1), calls=%async_computation.1 | async-start | bytes 2621440 | tf_op jit(solution)/shard_map/all_to_all | solution.py:1326
  (219 other events, 2099.8 us)
